TPU v7x, 512 devices: a whole 4x8x8 slice. The times are simulated.
512 devices in a mesh: tm: 16 (over z, core), space: 32 (over y, x).
Axes of the slice: x: 4, y: 8, z: 8, core: 2. Of those that a mesh axis runs over, the one named last changes fastest.
Arguments:
- forward_states: bfloat16 [64, 4, 128, 8, 128], P('tm', None, 'space'), may hold values from -3 to 3
- adjoint_source: float32 [64, 4, 128, 8, 128], P('tm', None, 'space'), may hold values from -6 to 6
- source_gain: float32 [4, 128, 8, 128], P(None, 'space'), may hold values from -4 to 0.3
- guess_pairs: float32 [16, 2, 4, 128, 8, 128], P('tm', None, None, 'space'), may hold values from -6 to 6
Outputs:
- corrected: float32 [16, 2, 4, 128, 8, 128], P('tm', None, None, 'space')
- gradient: float32 [4, 128, 8, 128], P(None, 'space')
All inputs are finite; a program needn't handle non-finite values.
Results may differ from a plain program's by a relative error of at most 0.0003.
Values sent between devices are 32-bit elements; how exact they have to be, the bound alone decides.
No kernel may reach another device: no remote copies, remote signals or barrier semaphores. Data moves between devices by JAX's collectives and lax.ppermute only.
A program may use at most 64 MiB of HBM per device.

v0:
```python
import jax
import jax.numpy as jnp
from jax import lax
from jax.sharding import PartitionSpec as P

SWEEPS = 4


diffusion = (2.4, 1.2, 0.6, 4.0)
fibre_weight = 128.0
reaction = (
    (-14.4, 7.2, -4.8, 2.4),
    (4.8, -19.2, 7.2, -4.8),
    (-7.2, 2.4, -12.0, 7.2),
    (4.8, -7.2, 2.4, -38.4),
)
self_rates = (-14.4, -19.2, -12.0, -38.4)
masses = (1.0, 1.0, 1.0, 0.0)
fine_rate = 3.0
coarse_rate = 0.75
time_step = 0.5
operator_scale = 0.0078125
state_weight = 0.1
gain_weight = 0.25


def with_halo(cells, sides, width):
    for axis, dim in sides:
        count = lax.axis_size(axis)
        ends = count - 1
        head = lax.slice_in_dim(cells, 0, width, axis=dim)
        tail = lax.slice_in_dim(cells, cells.shape[dim] - width, cells.shape[dim], axis=dim)
        cells = jnp.concatenate(
            [
                lax.ppermute(tail, axis, [(i, (i + 1) % count) for i in range(ends)]),
                cells,
                lax.ppermute(head, axis, [((i + 1) % count, i) for i in range(ends)]),
            ],
            axis=dim,
        )
    return cells


def passed_along(value, axis, steps):
    count = lax.axis_size(axis)
    initial, last = (max(0, -steps), min(count, count - steps))
    return lax.ppermute(value, axis, [(source, source + steps) for source in range(initial, last)])


def column(values):
    return jnp.array(values, jnp.float32).reshape(4, 1, 1, 1)


def from_below(field, axis):
    extent = field.shape[axis]
    retained = lax.slice_in_dim(field, 0, extent - 1, axis=axis)
    widths = [(0, 0)] * field.ndim
    widths[axis] = (1, 0)
    return jnp.pad(retained, widths)


def from_above(field, axis):
    extent = field.shape[axis]
    retained = lax.slice_in_dim(field, 1, extent, axis=axis)
    widths = [(0, 0)] * field.ndim
    widths[axis] = (0, 1)
    return jnp.pad(retained, widths)


def neighbours(field):
    running = fibre_weight * (from_below(field, 1) + from_above(field, 1))
    running = running + from_below(field, 2) + from_above(field, 2)
    return running + from_below(field, 3) + from_above(field, 3)


def coupling(field):
    stacked_rows = []
    for target in range(4):
        running = jnp.zeros_like(field[0])
        for source in range(4):
            if source != target:
                running = running + reaction[source][target] * field[source]
        stacked_rows.append(running)
    return jnp.stack(stacked_rows)


def jacobi_sweep(field, right_side, diagonal):
    spread = column(diffusion) * neighbours(field) + coupling(field)
    return (right_side + operator_scale * spread) / diagonal


def make_diagonal(state, source_gain, rate):
    stencil_total = (2.0 * fibre_weight + 4.0) * column(diffusion)
    spatial = operator_scale * (stencil_total - column(self_rates))
    return (
        rate * column(masses) + spatial + state_weight * state * state - gain_weight * source_gain
    )


def inside_mask(thickness):
    start_cell = lax.axis_index("space") * thickness - SWEEPS
    cell_index = start_cell + jnp.arange(thickness + 2 * SWEEPS, dtype=jnp.int32)
    return ((cell_index >= 0) & (cell_index < thickness * lax.axis_size("space"))).reshape(
        1, -1, 1, 1
    )


def guarded(wide_diagonal, inside):
    return jnp.where(inside, wide_diagonal, 1.0)


def relax(wide_right, safe_diagonal, inside):
    thickness = wide_right.shape[1] - 2 * SWEEPS
    iterate = jnp.where(inside, wide_right / safe_diagonal, 0.0)
    for sweep_count in range(SWEEPS):
        iterate = jnp.where(inside, jacobi_sweep(iterate, wide_right, safe_diagonal), 0.0)
    return iterate[:, SWEEPS : SWEEPS + thickness]


def implicit_solve(right_side, diagonal_info):
    thickness = right_side.shape[1]
    inside = inside_mask(thickness)
    widened = with_halo(jnp.stack([right_side, diagonal_info]), (("space", 2),), SWEEPS)
    return relax(widened[0], guarded(widened[1], inside), inside)


def coarse_step(pair, diagonal_info):
    solved = implicit_solve(column(masses) * (pair[0] - 0.25 * pair[1]), diagonal_info)
    return jnp.stack([solved, 0.5 * (solved + pair[0])])


def on_device(forward_states, adjoint_source, source_gain, guess_pairs):
    states = forward_states.astype(jnp.float32)
    mass = column(masses)
    local_steps = forward_states.shape[0]
    fine_diagonals = [
        make_diagonal(states[offset], source_gain, fine_rate) for offset in range(local_steps)
    ]
    coarse_diagonal = make_diagonal(states[0], source_gain, coarse_rate)
    later = passed_along(guess_pairs[0], "tm", -1)
    ahead_one, ahead_two = (later[0], later[1])
    adjoints = [None] * local_steps
    for offset in range(local_steps - 1, -1, -1):
        right_side = adjoint_source[offset] + mass * (4.0 * ahead_one - ahead_two)
        current = implicit_solve(right_side, fine_diagonals[offset])
        adjoints[offset] = current
        ahead_two, ahead_one = (ahead_one, current)
    running = adjoints[0] * states[0]
    for offset in range(1, local_steps):
        running = running + adjoints[offset] * states[offset]
    gradient = lax.psum(time_step * running, "tm")
    relaxed = jnp.stack([adjoints[0], adjoints[1]])
    following = passed_along(relaxed, "tm", -1)
    offsets = relaxed - coarse_step(following, coarse_diagonal)
    tm_count = lax.axis_size("tm")

    def advance(step_index, carried):
        incoming = passed_along(carried, "tm", -1)
        return coarse_step(incoming, coarse_diagonal) + offsets

    corrected = lax.fori_loop(0, tm_count, advance, jnp.zeros_like(offsets))
    return (corrected[None], gradient)


def solution(mesh):
    placed = (
        P("tm", None, "space", None, None),
        P("tm", None, "space", None, None),
        P(None, "space", None, None),
        P("tm", None, None, "space", None, None),
    )
    return jax.shard_map(
        on_device,
        mesh=mesh,
        in_specs=placed,
        out_specs=(P("tm", None, None, "space", None, None), P(None, "space", None, None)),
        check_vma=False,
    )
```

profile of v0, /device:TPU:225, one launch (start us, length us, event | category | flops | bytes accessed | tf_op | source)
XLA Modules:
  0.0 527.8 jit_solution(11160475156981937752)
XLA Ops:
  19.2 5.5 %collective-permute-start.5 = (f32[2,4,4,8,128]{4,3,2,1,0:T(8,128)S(1)}, f32[2,4,4,8,128]{4,3,2,1,0:T(8,128)S(1)}, u32[]{:S(2)}, u32[]{:S(2)}) collective-permute-start(f32[2,4,4,8,128]{4,3,2,1,0:T(8,128)S(1)} %pad_maximum_fusion.14), channel_id=1, source_target_pairs={{1,0},{2,1},{3,2},{4,3},{5,4},{6,5},{7,6},{8,7},{9,8},{10,9},{11,1... | collective-permute-start | bytes 393224 | tf_op jit(solution)/shard_map/ppermute | solution.py:37
  31.1 7.1 %collective-permute-start.7 = (f32[2,4,4,8,128]{4,3,2,1,0:T(8,128)S(1)}, f32[2,4,4,8,128]{4,3,2,1,0:T(8,128)S(1)}, u32[]{:S(2)}, u32[]{:S(2)}) collective-permute-start(f32[2,4,4,8,128]{4,3,2,1,0:T(8,128)S(1)} %pad_maximum_fusion.15), channel_id=1, source_target_pairs={{1,0},{2,1},{3,2},{4,3},{5,4},{6,5},{7,6},{8,7},{9,8},{10,9},{11,1... | collective-permute-start | bytes 393224 | tf_op jit(solution)/shard_map/ppermute | solution.py:37
  44.0 7.1 %collective-permute-start.9 = (f32[2,4,4,8,128]{4,3,2,1,0:T(8,128)S(1)}, f32[2,4,4,8,128]{4,3,2,1,0:T(8,128)S(1)}, u32[]{:S(2)}, u32[]{:S(2)}) collective-permute-start(f32[2,4,4,8,128]{4,3,2,1,0:T(8,128)S(1)} %pad_maximum_fusion.16), channel_id=1, source_target_pairs={{1,0},{2,1},{3,2},{4,3},{5,4},{6,5},{7,6},{8,7},{9,8},{10,9},{11,1... | collective-permute-start | bytes 393224 | tf_op jit(solution)/shard_map/ppermute | solution.py:37
  58.1 7.2 %collective-permute-start.11 = (f32[2,4,4,8,128]{4,3,2,1,0:T(8,128)S(1)}, f32[2,4,4,8,128]{4,3,2,1,0:T(8,128)S(1)}, u32[]{:S(2)}, u32[]{:S(2)}) collective-permute-start(f32[2,4,4,8,128]{4,3,2,1,0:T(8,128)S(1)} %pad_maximum_fusion.17), channel_id=1, source_target_pairs={{1,0},{2,1},{3,2},{4,3},{5,4},{6,5},{7,6},{8,7},{9,8},{10,9},{11,1... | collective-permute-start | bytes 393224 | tf_op jit(solution)/shard_map/ppermute | solution.py:37
  73.4 5.8 %collective-permute-done.12 = f32[2,4,4,8,128]{4,3,2,1,0:T(8,128)S(1)} collective-permute-done((f32[2,4,4,8,128]{4,3,2,1,0:T(8,128)S(1)}, f32[2,4,4,8,128]{4,3,2,1,0:T(8,128)S(1)}, u32[]{:S(2)}, u32[]{:S(2)}) %collective-permute-start.12) | collective-permute-done | bytes 131104 | tf_op jit(solution)/shard_map/ppermute | solution.py:47
  81.2 7.4 %collective-permute-start.14 = (f32[2,4,4,8,128]{4,3,2,1,0:T(8,128)S(1)}, f32[2,4,4,8,128]{4,3,2,1,0:T(8,128)S(1)}, u32[]{:S(2)}, u32[]{:S(2)}) collective-permute-start(f32[2,4,4,8,128]{4,3,2,1,0:T(8,128)S(1)} %pad_maximum_fusion.19), channel_id=1, source_target_pairs={{1,0},{2,1},{3,2},{4,3},{5,4},{6,5},{7,6},{8,7},{9,8},{10,9},{11,1... | collective-permute-start | bytes 393224 | tf_op jit(solution)/shard_map/ppermute | solution.py:37
  92.5 98.0 %all-reduce.146.cloned.1.call-done = f32[4,4,8,128]{3,2,1,0:T(8,128)} async-done(((f32[4,4,8,128]{3,2,1,0:T(8,128)}), f32[4,4,8,128]{3,2,1,0:T(8,128)}) %all-reduce.146.cloned.1.call-update) | async-done | bytes 65552 | tf_op jit(solution)/shard_map/psum | solution.py:151
  190.4 329.8 %while.15 = (s32[]{:T(128)}, f32[2,4,4,8,128]{4,3,2,1,0:T(8,128)S(1)}, f32[4,4,8,128]{3,2,1,0:T(8,128)S(1)}, f32[2,4,4,8,128]{4,3,2,1,0:T(8,128)S(1)}, s32[]{:T(...) while((s32[]{:T(128)}, ...), condition=%wide.region_1.2_spmd.clone.clone.clone, body=%wide.region_0.1_spmd.sunk.clone.clone.clone.sunk | while | flops 4505655 | bytes 22770104 | solution.py:161
  192.5 5.6 %collective-permute-done = f32[2,4,4,8,128]{4,3,2,1,0:T(8,128)S(1)} collective-permute-done((f32[2,4,4,8,128]{4,3,2,1,0:T(8,128)S(1)}, f32[2,4,4,8,128]{4,3,2,1,0:T(8,128)S(1)}, u32[]{:S(2)}, u32[]{:S(2)}) %collective-permute-start) | collective-permute-done | bytes 131104 | tf_op jit(solution)/shard_map/while/body/eval_jaxpr/ppermute | solution.py:47
  204.5 7.0 %collective-permute-done.2 = f32[2,4,4,8,128]{4,3,2,1,0:T(8,128)S(1)} collective-permute-done((f32[2,4,4,8,128]{4,3,2,1,0:T(8,128)S(1)}, f32[2,4,4,8,128]{4,3,2,1,0:T(8,128)S(1)}, u32[]{:S(2)}, u32[]{:S(2)}) %collective-permute-start.2) | collective-permute-done | bytes 131104 | tf_op jit(solution)/shard_map/while/body/eval_jaxpr/ppermute | solution.py:35
  215.3 5.6 %collective-permute-done = f32[2,4,4,8,128]{4,3,2,1,0:T(8,128)S(1)} collective-permute-done((f32[2,4,4,8,128]{4,3,2,1,0:T(8,128)S(1)}, f32[2,4,4,8,128]{4,3,2,1,0:T(8,128)S(1)}, u32[]{:S(2)}, u32[]{:S(2)}) %collective-permute-start) | collective-permute-done | bytes 131104 | tf_op jit(solution)/shard_map/while/body/eval_jaxpr/ppermute | solution.py:47
  226.7 5.2 collective-permute-done.2
  235.8 5.6 %collective-permute-done = f32[2,4,4,8,128]{4,3,2,1,0:T(8,128)S(1)} collective-permute-done((f32[2,4,4,8,128]{4,3,2,1,0:T(8,128)S(1)}, f32[2,4,4,8,128]{4,3,2,1,0:T(8,128)S(1)}, u32[]{:S(2)}, u32[]{:S(2)}) %collective-permute-start) | collective-permute-done | bytes 131104 | tf_op jit(solution)/shard_map/while/body/eval_jaxpr/ppermute | solution.py:47
  247.2 5.2 collective-permute-done.2
  256.3 5.6 %collective-permute-done = f32[2,4,4,8,128]{4,3,2,1,0:T(8,128)S(1)} collective-permute-done((f32[2,4,4,8,128]{4,3,2,1,0:T(8,128)S(1)}, f32[2,4,4,8,128]{4,3,2,1,0:T(8,128)S(1)}, u32[]{:S(2)}, u32[]{:S(2)}) %collective-permute-start) | collective-permute-done | bytes 131104 | tf_op jit(solution)/shard_map/while/body/eval_jaxpr/ppermute | solution.py:47
  267.6 5.2 collective-permute-done.2
  276.7 5.6 %collective-permute-done = f32[2,4,4,8,128]{4,3,2,1,0:T(8,128)S(1)} collective-permute-done((f32[2,4,4,8,128]{4,3,2,1,0:T(8,128)S(1)}, f32[2,4,4,8,128]{4,3,2,1,0:T(8,128)S(1)}, u32[]{:S(2)}, u32[]{:S(2)}) %collective-permute-start) | collective-permute-done | bytes 131104 | tf_op jit(solution)/shard_map/while/body/eval_jaxpr/ppermute | solution.py:47
  288.4 5.0 collective-permute-done.2
  297.2 5.6 %collective-permute-done = f32[2,4,4,8,128]{4,3,2,1,0:T(8,128)S(1)} collective-permute-done((f32[2,4,4,8,128]{4,3,2,1,0:T(8,128)S(1)}, f32[2,4,4,8,128]{4,3,2,1,0:T(8,128)S(1)}, u32[]{:S(2)}, u32[]{:S(2)}) %collective-permute-start) | collective-permute-done | bytes 131104 | tf_op jit(solution)/shard_map/while/body/eval_jaxpr/ppermute | solution.py:47
  308.8 5.0 collective-permute-done.2
  317.6 5.6 %collective-permute-done = f32[2,4,4,8,128]{4,3,2,1,0:T(8,128)S(1)} collective-permute-done((f32[2,4,4,8,128]{4,3,2,1,0:T(8,128)S(1)}, f32[2,4,4,8,128]{4,3,2,1,0:T(8,128)S(1)}, u32[]{:S(2)}, u32[]{:S(2)}) %collective-permute-start) | collective-permute-done | bytes 131104 | tf_op jit(solution)/shard_map/while/body/eval_jaxpr/ppermute | solution.py:47
  329.3 5.0 collective-permute-done.2
  338.1 5.6 %collective-permute-done = f32[2,4,4,8,128]{4,3,2,1,0:T(8,128)S(1)} collective-permute-done((f32[2,4,4,8,128]{4,3,2,1,0:T(8,128)S(1)}, f32[2,4,4,8,128]{4,3,2,1,0:T(8,128)S(1)}, u32[]{:S(2)}, u32[]{:S(2)}) %collective-permute-start) | collective-permute-done | bytes 131104 | tf_op jit(solution)/shard_map/while/body/eval_jaxpr/ppermute | solution.py:47
  349.8 5.0 collective-permute-done.2
  358.6 5.6 %collective-permute-done = f32[2,4,4,8,128]{4,3,2,1,0:T(8,128)S(1)} collective-permute-done((f32[2,4,4,8,128]{4,3,2,1,0:T(8,128)S(1)}, f32[2,4,4,8,128]{4,3,2,1,0:T(8,128)S(1)}, u32[]{:S(2)}, u32[]{:S(2)}) %collective-permute-start) | collective-permute-done | bytes 131104 | tf_op jit(solution)/shard_map/while/body/eval_jaxpr/ppermute | solution.py:47
  379.0 5.6 %collective-permute-done = f32[2,4,4,8,128]{4,3,2,1,0:T(8,128)S(1)} collective-permute-done((f32[2,4,4,8,128]{4,3,2,1,0:T(8,128)S(1)}, f32[2,4,4,8,128]{4,3,2,1,0:T(8,128)S(1)}, u32[]{:S(2)}, u32[]{:S(2)}) %collective-permute-start) | collective-permute-done | bytes 131104 | tf_op jit(solution)/shard_map/while/body/eval_jaxpr/ppermute | solution.py:47
  399.5 5.6 %collective-permute-done = f32[2,4,4,8,128]{4,3,2,1,0:T(8,128)S(1)} collective-permute-done((f32[2,4,4,8,128]{4,3,2,1,0:T(8,128)S(1)}, f32[2,4,4,8,128]{4,3,2,1,0:T(8,128)S(1)}, u32[]{:S(2)}, u32[]{:S(2)}) %collective-permute-start) | collective-permute-done | bytes 131104 | tf_op jit(solution)/shard_map/while/body/eval_jaxpr/ppermute | solution.py:47
  419.9 5.6 %collective-permute-done = f32[2,4,4,8,128]{4,3,2,1,0:T(8,128)S(1)} collective-permute-done((f32[2,4,4,8,128]{4,3,2,1,0:T(8,128)S(1)}, f32[2,4,4,8,128]{4,3,2,1,0:T(8,128)S(1)}, u32[]{:S(2)}, u32[]{:S(2)}) %collective-permute-start) | collective-permute-done | bytes 131104 | tf_op jit(solution)/shard_map/while/body/eval_jaxpr/ppermute | solution.py:47
  440.4 5.6 %collective-permute-done = f32[2,4,4,8,128]{4,3,2,1,0:T(8,128)S(1)} collective-permute-done((f32[2,4,4,8,128]{4,3,2,1,0:T(8,128)S(1)}, f32[2,4,4,8,128]{4,3,2,1,0:T(8,128)S(1)}, u32[]{:S(2)}, u32[]{:S(2)}) %collective-permute-start) | collective-permute-done | bytes 131104 | tf_op jit(solution)/shard_map/while/body/eval_jaxpr/ppermute | solution.py:47
  460.9 5.6 %collective-permute-done = f32[2,4,4,8,128]{4,3,2,1,0:T(8,128)S(1)} collective-permute-done((f32[2,4,4,8,128]{4,3,2,1,0:T(8,128)S(1)}, f32[2,4,4,8,128]{4,3,2,1,0:T(8,128)S(1)}, u32[]{:S(2)}, u32[]{:S(2)}) %collective-permute-start) | collective-permute-done | bytes 131104 | tf_op jit(solution)/shard_map/while/body/eval_jaxpr/ppermute | solution.py:47
  481.3 5.6 %collective-permute-done = f32[2,4,4,8,128]{4,3,2,1,0:T(8,128)S(1)} collective-permute-done((f32[2,4,4,8,128]{4,3,2,1,0:T(8,128)S(1)}, f32[2,4,4,8,128]{4,3,2,1,0:T(8,128)S(1)}, u32[]{:S(2)}, u32[]{:S(2)}) %collective-permute-start) | collective-permute-done | bytes 131104 | tf_op jit(solution)/shard_map/while/body/eval_jaxpr/ppermute | solution.py:47
  501.8 5.6 %collective-permute-done = f32[2,4,4,8,128]{4,3,2,1,0:T(8,128)S(1)} collective-permute-done((f32[2,4,4,8,128]{4,3,2,1,0:T(8,128)S(1)}, f32[2,4,4,8,128]{4,3,2,1,0:T(8,128)S(1)}, u32[]{:S(2)}, u32[]{:S(2)}) %collective-permute-start) | collective-permute-done | bytes 131104 | tf_op jit(solution)/shard_map/while/body/eval_jaxpr/ppermute | solution.py:47
  (727 shorter events, 239.1 us)
Async XLA Ops:
  7.2 183.3 %all-reduce.146.cloned.1.call-start = ((), (), s32[]{:S(2)}) async-start(), calls=%async_computation | async-start | bytes 131072 | tf_op jit(solution)/shard_map/psum | solution.py:151
  7.2 8.8 %collective-permute-start.3 = (f32[2,4,4,8,128]{4,3,2,1,0:T(8,128)}, f32[2,4,4,8,128]{4,3,2,1,0:T(8,128)S(1)}, u32[]{:S(2)}, u32[]{:S(2)}) collective-permute-start(f32[2,4,4,8,128]{4,3,2,1,0:T(8,128)} %bitcast.253), channel_id=1, source_target_pairs={{32,0},{64,32},{96,64},{128,96},{160,128},{192,160},{224,192},{256... | collective-permute-start | bytes 393224 | tf_op jit(solution)/shard_map/ppermute | solution.py:47
  16.1 9.0 %collective-permute-start.4 = (f32[2,4,4,8,128]{4,3,2,1,0:T(8,128)S(1)}, f32[2,4,4,8,128]{4,3,2,1,0:T(8,128)S(1)}, u32[]{:S(2)}, u32[]{:S(2)}) collective-permute-start(f32[2,4,4,8,128]{4,3,2,1,0:T(8,128)S(1)} %pad_maximum_fusion.14), channel_id=1, source_target_pairs={{0,1},{1,2},{2,3},{3,4},{4,5},{5,6},{6,7},{7,8},{8,9},{9,10},{10,1... | collective-permute-start | bytes 393224 | tf_op jit(solution)/shard_map/ppermute | solution.py:35
  29.2 9.4 %collective-permute-start.6 = (f32[2,4,4,8,128]{4,3,2,1,0:T(8,128)S(1)}, f32[2,4,4,8,128]{4,3,2,1,0:T(8,128)S(1)}, u32[]{:S(2)}, u32[]{:S(2)}) collective-permute-start(f32[2,4,4,8,128]{4,3,2,1,0:T(8,128)S(1)} %pad_maximum_fusion.15), channel_id=1, source_target_pairs={{0,1},{1,2},{2,3},{3,4},{4,5},{5,6},{6,7},{7,8},{8,9},{9,10},{10,1... | collective-permute-start | bytes 393224 | tf_op jit(solution)/shard_map/ppermute | solution.py:35
  31.1 9.1 %collective-permute-start.7 = (f32[2,4,4,8,128]{4,3,2,1,0:T(8,128)S(1)}, f32[2,4,4,8,128]{4,3,2,1,0:T(8,128)S(1)}, u32[]{:S(2)}, u32[]{:S(2)}) collective-permute-start(f32[2,4,4,8,128]{4,3,2,1,0:T(8,128)S(1)} %pad_maximum_fusion.15), channel_id=1, source_target_pairs={{1,0},{2,1},{3,2},{4,3},{5,4},{6,5},{7,6},{8,7},{9,8},{10,9},{11,1... | collective-permute-start | bytes 393224 | tf_op jit(solution)/shard_map/ppermute | solution.py:37
  42.1 10.4 %collective-permute-start.8 = (f32[2,4,4,8,128]{4,3,2,1,0:T(8,128)S(1)}, f32[2,4,4,8,128]{4,3,2,1,0:T(8,128)S(1)}, u32[]{:S(2)}, u32[]{:S(2)}) collective-permute-start(f32[2,4,4,8,128]{4,3,2,1,0:T(8,128)S(1)} %pad_maximum_fusion.16), channel_id=1, source_target_pairs={{0,1},{1,2},{2,3},{3,4},{4,5},{5,6},{6,7},{7,8},{8,9},{9,10},{10,1... | collective-permute-start | bytes 393224 | tf_op jit(solution)/shard_map/ppermute | solution.py:35
  44.0 10.2 %collective-permute-start.9 = (f32[2,4,4,8,128]{4,3,2,1,0:T(8,128)S(1)}, f32[2,4,4,8,128]{4,3,2,1,0:T(8,128)S(1)}, u32[]{:S(2)}, u32[]{:S(2)}) collective-permute-start(f32[2,4,4,8,128]{4,3,2,1,0:T(8,128)S(1)} %pad_maximum_fusion.16), channel_id=1, source_target_pairs={{1,0},{2,1},{3,2},{4,3},{5,4},{6,5},{7,6},{8,7},{9,8},{10,9},{11,1... | collective-permute-start | bytes 393224 | tf_op jit(solution)/shard_map/ppermute | solution.py:37
  56.1 10.7 %collective-permute-start.10 = (f32[2,4,4,8,128]{4,3,2,1,0:T(8,128)S(1)}, f32[2,4,4,8,128]{4,3,2,1,0:T(8,128)S(1)}, u32[]{:S(2)}, u32[]{:S(2)}) collective-permute-start(f32[2,4,4,8,128]{4,3,2,1,0:T(8,128)S(1)} %pad_maximum_fusion.17), channel_id=1, source_target_pairs={{0,1},{1,2},{2,3},{3,4},{4,5},{5,6},{6,7},{7,8},{8,9},{9,10},{10,1... | collective-permute-start | bytes 393224 | tf_op jit(solution)/shard_map/ppermute | solution.py:35
  58.1 9.7 %collective-permute-start.11 = (f32[2,4,4,8,128]{4,3,2,1,0:T(8,128)S(1)}, f32[2,4,4,8,128]{4,3,2,1,0:T(8,128)S(1)}, u32[]{:S(2)}, u32[]{:S(2)}) collective-permute-start(f32[2,4,4,8,128]{4,3,2,1,0:T(8,128)S(1)} %pad_maximum_fusion.17), channel_id=1, source_target_pairs={{1,0},{2,1},{3,2},{4,3},{5,4},{6,5},{7,6},{8,7},{9,8},{10,9},{11,1... | collective-permute-start | bytes 393224 | tf_op jit(solution)/shard_map/ppermute | solution.py:37
  70.3 8.9 %collective-permute-start.12 = (f32[2,4,4,8,128]{4,3,2,1,0:T(8,128)S(1)}, f32[2,4,4,8,128]{4,3,2,1,0:T(8,128)S(1)}, u32[]{:S(2)}, u32[]{:S(2)}) collective-permute-start(f32[2,4,4,8,128]{4,3,2,1,0:T(8,128)S(1)} %pad_maximum_fusion.18), channel_id=1, source_target_pairs={{32,0},{64,32},{96,64},{128,96},{160,128},{192,160},{224,192},{256... | collective-permute-start | bytes 393224 | tf_op jit(solution)/shard_map/ppermute | solution.py:47
  79.3 9.7 %collective-permute-start.13 = (f32[2,4,4,8,128]{4,3,2,1,0:T(8,128)S(1)}, f32[2,4,4,8,128]{4,3,2,1,0:T(8,128)S(1)}, u32[]{:S(2)}, u32[]{:S(2)}) collective-permute-start(f32[2,4,4,8,128]{4,3,2,1,0:T(8,128)S(1)} %pad_maximum_fusion.19), channel_id=1, source_target_pairs={{0,1},{1,2},{2,3},{3,4},{4,5},{5,6},{6,7},{7,8},{8,9},{9,10},{10,1... | collective-permute-start | bytes 393224 | tf_op jit(solution)/shard_map/ppermute | solution.py:35
  81.2 9.3 %collective-permute-start.14 = (f32[2,4,4,8,128]{4,3,2,1,0:T(8,128)S(1)}, f32[2,4,4,8,128]{4,3,2,1,0:T(8,128)S(1)}, u32[]{:S(2)}, u32[]{:S(2)}) collective-permute-start(f32[2,4,4,8,128]{4,3,2,1,0:T(8,128)S(1)} %pad_maximum_fusion.19), channel_id=1, source_target_pairs={{1,0},{2,1},{3,2},{4,3},{5,4},{6,5},{7,6},{8,7},{9,8},{10,9},{11,1... | collective-permute-start | bytes 393224 | tf_op jit(solution)/shard_map/ppermute | solution.py:37
  190.4 7.6 %collective-permute-start = (f32[2,4,4,8,128]{4,3,2,1,0:T(8,128)S(1)}, f32[2,4,4,8,128]{4,3,2,1,0:T(8,128)S(1)}, u32[]{:S(2)}, u32[]{:S(2)}) collective-permute-start(f32[2,4,4,8,128]{4,3,2,1,0:T(8,128)S(1)} %broadcast_select_fusion.2), channel_id=1, source_target_pairs={{32,0},{64,32},{96,64},{128,96},{160,128},{192,160},{224,192},{256... | collective-permute-start | bytes 393224 | tf_op jit(solution)/shard_map/while/body/eval_jaxpr/ppermute | solution.py:47
  202.5 9.0 %collective-permute-start.2 = (f32[2,4,4,8,128]{4,3,2,1,0:T(8,128)S(1)}, f32[2,4,4,8,128]{4,3,2,1,0:T(8,128)S(1)}, u32[]{:S(2)}, u32[]{:S(2)}) collective-permute-start(f32[2,4,4,8,128]{4,3,2,1,0:T(8,128)S(1)} %pad_maximum_fusion.28), channel_id=1, source_target_pairs={{0,1},{1,2},{2,3},{3,4},{4,5},{5,6},{6,7},{7,8},{8,9},{9,10},{10,1... | collective-permute-start | bytes 393224 | tf_op jit(solution)/shard_map/while/body/eval_jaxpr/ppermute | solution.py:35
  213.4 7.5 %collective-permute-start = (f32[2,4,4,8,128]{4,3,2,1,0:T(8,128)S(1)}, f32[2,4,4,8,128]{4,3,2,1,0:T(8,128)S(1)}, u32[]{:S(2)}, u32[]{:S(2)}) collective-permute-start(f32[2,4,4,8,128]{4,3,2,1,0:T(8,128)S(1)} %broadcast_select_fusion.2), channel_id=1, source_target_pairs={{32,0},{64,32},{96,64},{128,96},{160,128},{192,160},{224,192},{256... | collective-permute-start | bytes 393224 | tf_op jit(solution)/shard_map/while/body/eval_jaxpr/ppermute | solution.py:47
  222.9 9.0 %collective-permute-start.2 = (f32[2,4,4,8,128]{4,3,2,1,0:T(8,128)S(1)}, f32[2,4,4,8,128]{4,3,2,1,0:T(8,128)S(1)}, u32[]{:S(2)}, u32[]{:S(2)}) collective-permute-start(f32[2,4,4,8,128]{4,3,2,1,0:T(8,128)S(1)} %pad_maximum_fusion.28), channel_id=1, source_target_pairs={{0,1},{1,2},{2,3},{3,4},{4,5},{5,6},{6,7},{7,8},{8,9},{9,10},{10,1... | collective-permute-start | bytes 393224 | tf_op jit(solution)/shard_map/while/body/eval_jaxpr/ppermute | solution.py:35
  233.9 7.5 %collective-permute-start = (f32[2,4,4,8,128]{4,3,2,1,0:T(8,128)S(1)}, f32[2,4,4,8,128]{4,3,2,1,0:T(8,128)S(1)}, u32[]{:S(2)}, u32[]{:S(2)}) collective-permute-start(f32[2,4,4,8,128]{4,3,2,1,0:T(8,128)S(1)} %broadcast_select_fusion.2), channel_id=1, source_target_pairs={{32,0},{64,32},{96,64},{128,96},{160,128},{192,160},{224,192},{256... | collective-permute-start | bytes 393224 | tf_op jit(solution)/shard_map/while/body/eval_jaxpr/ppermute | solution.py:47
  243.4 9.0 %collective-permute-start.2 = (f32[2,4,4,8,128]{4,3,2,1,0:T(8,128)S(1)}, f32[2,4,4,8,128]{4,3,2,1,0:T(8,128)S(1)}, u32[]{:S(2)}, u32[]{:S(2)}) collective-permute-start(f32[2,4,4,8,128]{4,3,2,1,0:T(8,128)S(1)} %pad_maximum_fusion.28), channel_id=1, source_target_pairs={{0,1},{1,2},{2,3},{3,4},{4,5},{5,6},{6,7},{7,8},{8,9},{9,10},{10,1... | collective-permute-start | bytes 393224 | tf_op jit(solution)/shard_map/while/body/eval_jaxpr/ppermute | solution.py:35
  254.3 7.5 %collective-permute-start = (f32[2,4,4,8,128]{4,3,2,1,0:T(8,128)S(1)}, f32[2,4,4,8,128]{4,3,2,1,0:T(8,128)S(1)}, u32[]{:S(2)}, u32[]{:S(2)}) collective-permute-start(f32[2,4,4,8,128]{4,3,2,1,0:T(8,128)S(1)} %broadcast_select_fusion.2), channel_id=1, source_target_pairs={{32,0},{64,32},{96,64},{128,96},{160,128},{192,160},{224,192},{256... | collective-permute-start | bytes 393224 | tf_op jit(solution)/shard_map/while/body/eval_jaxpr/ppermute | solution.py:47
  263.8 9.0 %collective-permute-start.2 = (f32[2,4,4,8,128]{4,3,2,1,0:T(8,128)S(1)}, f32[2,4,4,8,128]{4,3,2,1,0:T(8,128)S(1)}, u32[]{:S(2)}, u32[]{:S(2)}) collective-permute-start(f32[2,4,4,8,128]{4,3,2,1,0:T(8,128)S(1)} %pad_maximum_fusion.28), channel_id=1, source_target_pairs={{0,1},{1,2},{2,3},{3,4},{4,5},{5,6},{6,7},{7,8},{8,9},{9,10},{10,1... | collective-permute-start | bytes 393224 | tf_op jit(solution)/shard_map/while/body/eval_jaxpr/ppermute | solution.py:35
  284.3 9.0 %collective-permute-start.2 = (f32[2,4,4,8,128]{4,3,2,1,0:T(8,128)S(1)}, f32[2,4,4,8,128]{4,3,2,1,0:T(8,128)S(1)}, u32[]{:S(2)}, u32[]{:S(2)}) collective-permute-start(f32[2,4,4,8,128]{4,3,2,1,0:T(8,128)S(1)} %pad_maximum_fusion.28), channel_id=1, source_target_pairs={{0,1},{1,2},{2,3},{3,4},{4,5},{5,6},{6,7},{7,8},{8,9},{9,10},{10,1... | collective-permute-start | bytes 393224 | tf_op jit(solution)/shard_map/while/body/eval_jaxpr/ppermute | solution.py:35
  304.8 9.0 %collective-permute-start.2 = (f32[2,4,4,8,128]{4,3,2,1,0:T(8,128)S(1)}, f32[2,4,4,8,128]{4,3,2,1,0:T(8,128)S(1)}, u32[]{:S(2)}, u32[]{:S(2)}) collective-permute-start(f32[2,4,4,8,128]{4,3,2,1,0:T(8,128)S(1)} %pad_maximum_fusion.28), channel_id=1, source_target_pairs={{0,1},{1,2},{2,3},{3,4},{4,5},{5,6},{6,7},{7,8},{8,9},{9,10},{10,1... | collective-permute-start | bytes 393224 | tf_op jit(solution)/shard_map/while/body/eval_jaxpr/ppermute | solution.py:35
  325.2 9.0 %collective-permute-start.2 = (f32[2,4,4,8,128]{4,3,2,1,0:T(8,128)S(1)}, f32[2,4,4,8,128]{4,3,2,1,0:T(8,128)S(1)}, u32[]{:S(2)}, u32[]{:S(2)}) collective-permute-start(f32[2,4,4,8,128]{4,3,2,1,0:T(8,128)S(1)} %pad_maximum_fusion.28), channel_id=1, source_target_pairs={{0,1},{1,2},{2,3},{3,4},{4,5},{5,6},{6,7},{7,8},{8,9},{9,10},{10,1... | collective-permute-start | bytes 393224 | tf_op jit(solution)/shard_map/while/body/eval_jaxpr/ppermute | solution.py:35
  345.7 9.0 %collective-permute-start.2 = (f32[2,4,4,8,128]{4,3,2,1,0:T(8,128)S(1)}, f32[2,4,4,8,128]{4,3,2,1,0:T(8,128)S(1)}, u32[]{:S(2)}, u32[]{:S(2)}) collective-permute-start(f32[2,4,4,8,128]{4,3,2,1,0:T(8,128)S(1)} %pad_maximum_fusion.28), channel_id=1, source_target_pairs={{0,1},{1,2},{2,3},{3,4},{4,5},{5,6},{6,7},{7,8},{8,9},{9,10},{10,1... | collective-permute-start | bytes 393224 | tf_op jit(solution)/shard_map/while/body/eval_jaxpr/ppermute | solution.py:35
  366.1 9.0 %collective-permute-start.2 = (f32[2,4,4,8,128]{4,3,2,1,0:T(8,128)S(1)}, f32[2,4,4,8,128]{4,3,2,1,0:T(8,128)S(1)}, u32[]{:S(2)}, u32[]{:S(2)}) collective-permute-start(f32[2,4,4,8,128]{4,3,2,1,0:T(8,128)S(1)} %pad_maximum_fusion.28), channel_id=1, source_target_pairs={{0,1},{1,2},{2,3},{3,4},{4,5},{5,6},{6,7},{7,8},{8,9},{9,10},{10,1... | collective-permute-start | bytes 393224 | tf_op jit(solution)/shard_map/while/body/eval_jaxpr/ppermute | solution.py:35
  386.6 9.0 %collective-permute-start.2 = (f32[2,4,4,8,128]{4,3,2,1,0:T(8,128)S(1)}, f32[2,4,4,8,128]{4,3,2,1,0:T(8,128)S(1)}, u32[]{:S(2)}, u32[]{:S(2)}) collective-permute-start(f32[2,4,4,8,128]{4,3,2,1,0:T(8,128)S(1)} %pad_maximum_fusion.28), channel_id=1, source_target_pairs={{0,1},{1,2},{2,3},{3,4},{4,5},{5,6},{6,7},{7,8},{8,9},{9,10},{10,1... | collective-permute-start | bytes 393224 | tf_op jit(solution)/shard_map/while/body/eval_jaxpr/ppermute | solution.py:35
  407.1 9.0 %collective-permute-start.2 = (f32[2,4,4,8,128]{4,3,2,1,0:T(8,128)S(1)}, f32[2,4,4,8,128]{4,3,2,1,0:T(8,128)S(1)}, u32[]{:S(2)}, u32[]{:S(2)}) collective-permute-start(f32[2,4,4,8,128]{4,3,2,1,0:T(8,128)S(1)} %pad_maximum_fusion.28), channel_id=1, source_target_pairs={{0,1},{1,2},{2,3},{3,4},{4,5},{5,6},{6,7},{7,8},{8,9},{9,10},{10,1... | collective-permute-start | bytes 393224 | tf_op jit(solution)/shard_map/while/body/eval_jaxpr/ppermute | solution.py:35
  427.5 9.0 %collective-permute-start.2 = (f32[2,4,4,8,128]{4,3,2,1,0:T(8,128)S(1)}, f32[2,4,4,8,128]{4,3,2,1,0:T(8,128)S(1)}, u32[]{:S(2)}, u32[]{:S(2)}) collective-permute-start(f32[2,4,4,8,128]{4,3,2,1,0:T(8,128)S(1)} %pad_maximum_fusion.28), channel_id=1, source_target_pairs={{0,1},{1,2},{2,3},{3,4},{4,5},{5,6},{6,7},{7,8},{8,9},{9,10},{10,1... | collective-permute-start | bytes 393224 | tf_op jit(solution)/shard_map/while/body/eval_jaxpr/ppermute | solution.py:35
  448.0 9.0 %collective-permute-start.2 = (f32[2,4,4,8,128]{4,3,2,1,0:T(8,128)S(1)}, f32[2,4,4,8,128]{4,3,2,1,0:T(8,128)S(1)}, u32[]{:S(2)}, u32[]{:S(2)}) collective-permute-start(f32[2,4,4,8,128]{4,3,2,1,0:T(8,128)S(1)} %pad_maximum_fusion.28), channel_id=1, source_target_pairs={{0,1},{1,2},{2,3},{3,4},{4,5},{5,6},{6,7},{7,8},{8,9},{9,10},{10,1... | collective-permute-start | bytes 393224 | tf_op jit(solution)/shard_map/while/body/eval_jaxpr/ppermute | solution.py:35
  468.4 9.0 %collective-permute-start.2 = (f32[2,4,4,8,128]{4,3,2,1,0:T(8,128)S(1)}, f32[2,4,4,8,128]{4,3,2,1,0:T(8,128)S(1)}, u32[]{:S(2)}, u32[]{:S(2)}) collective-permute-start(f32[2,4,4,8,128]{4,3,2,1,0:T(8,128)S(1)} %pad_maximum_fusion.28), channel_id=1, source_target_pairs={{0,1},{1,2},{2,3},{3,4},{4,5},{5,6},{6,7},{7,8},{8,9},{9,10},{10,1... | collective-permute-start | bytes 393224 | tf_op jit(solution)/shard_map/while/body/eval_jaxpr/ppermute | solution.py:35
  488.9 9.0 %collective-permute-start.2 = (f32[2,4,4,8,128]{4,3,2,1,0:T(8,128)S(1)}, f32[2,4,4,8,128]{4,3,2,1,0:T(8,128)S(1)}, u32[]{:S(2)}, u32[]{:S(2)}) collective-permute-start(f32[2,4,4,8,128]{4,3,2,1,0:T(8,128)S(1)} %pad_maximum_fusion.28), channel_id=1, source_target_pairs={{0,1},{1,2},{2,3},{3,4},{4,5},{5,6},{6,7},{7,8},{8,9},{9,10},{10,1... | collective-permute-start | bytes 393224 | tf_op jit(solution)/shard_map/while/body/eval_jaxpr/ppermute | solution.py:35
  509.4 9.0 %collective-permute-start.2 = (f32[2,4,4,8,128]{4,3,2,1,0:T(8,128)S(1)}, f32[2,4,4,8,128]{4,3,2,1,0:T(8,128)S(1)}, u32[]{:S(2)}, u32[]{:S(2)}) collective-permute-start(f32[2,4,4,8,128]{4,3,2,1,0:T(8,128)S(1)} %pad_maximum_fusion.28), channel_id=1, source_target_pairs={{0,1},{1,2},{2,3},{3,4},{4,5},{5,6},{6,7},{7,8},{8,9},{9,10},{10,1... | collective-permute-start | bytes 393224 | tf_op jit(solution)/shard_map/while/body/eval_jaxpr/ppermute | solution.py:35
  (37 other events, 545.4 us)
Sparse Core Ops, SparseCore 0:
  88.8 101.6 all-reduce.145
where the time goes:
time: 531 us; the launch traced here: 528 us
  waiting for transfers between devices  300 us (56%)
  starting transfers between devices  167 us (31%)
  other arithmetic  25.2 us (5%)
  local copies, waits for them, and re-layouts  16.7 us (3%)
  between operations  15.1 us (3%)
    ppermute x18, waiting for transfers between devices, passed_along(): lax.ppermute(value, axis, [(source, source + steps) for source in range(i...  99.8 us
    psum x1, waiting for transfers between devices, on_device(): gradient = lax.psum(time_step * running, 'tm')  98 us
    ppermute x21, waiting for transfers between devices, with_halo(): lax.ppermute(tail, axis, [(i, (i + 1) % count) for i in range(ends)])  86.2 us
    ppermute x21, starting transfers between devices, with_halo(): lax.ppermute(head, axis, [((i + 1) % count, i) for i in range(ends)])  67.4 us
    ppermute x21, starting transfers between devices, with_halo(): lax.ppermute(tail, axis, [(i, (i + 1) % count) for i in range(ends)])  63.2 us
    ppermute x18, starting transfers between devices, passed_along(): lax.ppermute(value, axis, [(source, source + steps) for source in range(i...  36.7 us
    ppermute x21, waiting for transfers between devices, with_halo(): lax.ppermute(head, axis, [((i + 1) % count, i) for i in range(ends)])  15.5 us
    slice x252, local copies, waits for them, and re-layouts, from_below(): retained = lax.slice_in_dim(field, 0, extent - 1, axis=axis)  13.8 us
  transfers between devices with their start and end apart: 61, of which 60 were waited for; matrix products, arithmetic and copies ran while one was open for 1% of the time, Pallas kernels for 0%

commit v1 on v0

v1 whole, which is shorter than its diff:
```python
import jax
import jax.numpy as jnp
from jax import lax
from jax.experimental import pallas as pl
from jax.experimental.pallas import tpu as pltpu
from jax.sharding import PartitionSpec as P

SWEEPS = 4
FIELDS = 4
WIDTH = 4

diffusion = (2.4, 1.2, 0.6, 4.0)
fibre_weight = 128.0
reaction = (
    (-14.4, 7.2, -4.8, 2.4),
    (4.8, -19.2, 7.2, -4.8),
    (-7.2, 2.4, -12.0, 7.2),
    (4.8, -7.2, 2.4, -38.4),
)
self_rates = (-14.4, -19.2, -12.0, -38.4)
masses = (1.0, 1.0, 1.0, 0.0)
fine_rate = 3.0
coarse_rate = 0.75
time_step = 0.5
operator_scale = 0.0078125
state_weight = 0.1
gain_weight = 0.25

AXES = ("tm", "space")
SLAB = (FIELDS, WIDTH, 8, 128)


def column(values):
    return jnp.array(values, jnp.float32).reshape(4, 1, 1, 1)


def make_diagonal(state, source_gain, rate):
    stencil_total = (2.0 * fibre_weight + 4.0) * column(diffusion)
    spatial = operator_scale * (stencil_total - column(self_rates))
    return (
        rate * column(masses) + spatial + state_weight * state * state - gain_weight * source_gain
    )


class Stencil:
    def __init__(self):
        row = lax.broadcasted_iota(jnp.int32, (8, 128), 0)
        lane = lax.broadcasted_iota(jnp.int32, (8, 128), 1)
        self.first_row, self.last_row = row == 0, row == 7
        self.first_lane, self.last_lane = lane == 0, lane == 127

    def cross(self, cell):
        rows = jnp.where(self.first_row, 0.0, pltpu.roll(cell, 1, 0)) + jnp.where(
            self.last_row, 0.0, pltpu.roll(cell, 7, 0)
        )
        lanes = jnp.where(self.first_lane, 0.0, pltpu.roll(cell, 1, 1)) + jnp.where(
            self.last_lane, 0.0, pltpu.roll(cell, 127, 1)
        )
        return rows + lanes

    def sweep(self, below, here, above, start, inverse):
        fresh = []
        for f in range(FIELDS):
            spread = (operator_scale * fibre_weight * diffusion[f]) * (below[f] + above[f])
            spread = spread + (operator_scale * diffusion[f]) * self.cross(here[f])
            for g in range(FIELDS):
                if g != f:
                    spread = spread + (operator_scale * reaction[g][f]) * here[g]
            fresh.append(start[f] + inverse[f] * spread)
        return fresh


def solve(stencil, right, inverse, count, scratch, emit):
    base, ping, pong = scratch
    for layer in range(count):
        for f in range(FIELDS):
            value = right(f, layer)
            if value is None:
                base[f, layer] = jnp.zeros((8, 128), jnp.float32)
            else:
                base[f, layer] = value * inverse(f, layer)
    source = base
    for sweep in range(1, SWEEPS + 1):
        target = ping if sweep % 2 else pong
        for layer in range(sweep, count - sweep):
            below, here, above = (
                [source[f, layer + shift] for f in range(FIELDS)] for shift in (-1, 0, 1)
            )
            start = [base[f, layer] for f in range(FIELDS)]
            factor = [inverse(f, layer) for f in range(FIELDS)]
            fresh = stencil.sweep(below, here, above, start, factor)
            if sweep == SWEEPS:
                emit(layer - SWEEPS, fresh)
            else:
                for f in range(FIELDS):
                    target[f, layer] = fresh[f]
        source = target


def layers_of(pieces):
    return lambda f, layer: pieces[layer // WIDTH][f, layer % WIDTH]


def masses_only(pieces):
    read = layers_of(pieces)
    return lambda f, layer: read(f, layer) if masses[f] else None


def vmem(shape):
    return pltpu.VMEM(shape, jnp.float32)


def call(body, outs, *operands, smem=0, layers=0, flops=0):
    spec = pl.BlockSpec(memory_space=pltpu.VMEM)
    return pl.pallas_call(
        body,
        in_specs=[pl.BlockSpec(memory_space=pltpu.SMEM)] * smem + [spec] * (len(operands) - smem),
        out_specs=[spec] * len(outs),
        out_shape=[jax.ShapeDtypeStruct(shape, jnp.float32) for shape in outs],
        scratch_shapes=[vmem((FIELDS, layers, 8, 128))] * 3,
        compiler_params=pltpu.CompilerParams(vmem_limit_bytes=24 * 1024 * 1024),
        cost_estimate=pl.CostEstimate(flops=flops, bytes_accessed=1 << 20, transcendentals=0),
    )(*operands)


def fine_step(step, right, right_low, right_high, inv, inv_low, inv_high, states, source, previous, total):
    first, last = total is None, step == 0

    def body(*refs):
        refs = list(refs)
        r0, rl, rh, i0, il, ih, u, prev = refs[:8]
        rest = refs[8:]
        src = None if last else rest.pop(0)
        old = None if first else rest.pop(0)
        out, grad = rest[:2]
        more = rest[2:-3]
        scratch = rest[-3:]
        stencil = Stencil()
        right_at = layers_of([rl, r0, rh])
        pieces = [il, i0, ih]

        def inverse(f, layer):
            return pieces[layer // WIDTH][step, f, layer % WIDTH]

        def emit(layer, x):
            for f in range(FIELDS):
                out[f, layer] = x[f]
                term = x[f] * u[f, layer]
                grad[f, layer] = term if first else old[f, layer] + term
                if not last:
                    r = src[f, layer]
                    if masses[f]:
                        r = r + (4.0 * x[f] - prev[f, layer])
                    more[0][f, layer] = r
                else:
                    z3, z6, z7 = more
                    z7[3 + f, layer] = x[f]
                    if masses[f]:
                        z = x[f] - 0.25 * prev[f, layer]
                        z3[f, layer] = z
                        z6[f, layer] = z
                        z7[f, layer] = z
                        z6[3 + f, layer] = x[f]

        solve(stencil, right_at, inverse, 3 * WIDTH, scratch, emit)

    operands = [right, right_low, right_high, inv, inv_low, inv_high, states, previous]
    operands += [] if last else [source]
    operands += [] if first else [total]
    outs = [SLAB, SLAB] + ([carry(3), carry(6), carry(7)] if last else [SLAB])
    return call(body, outs, *operands, layers=3 * WIDTH, flops=28 * 4 * 1024 * 20)


def carry(count):
    return (count, WIDTH, 8, 128)


def offsets_step(z_five, inv_five, inv_three, own_three, pair_odd, pair_even):
    def body(*refs):
        z, iv, ie, zo, (x0, x1, even) = refs[0:5], refs[5:10], refs[10], refs[11:14], refs[14:17]
        v, pairs = refs[17:19]
        scratch = refs[19:]
        stencil = Stencil()

        def emit_odd(layer, q):
            slab, at = layer // WIDTH, layer % WIDTH
            for f in range(FIELDS):
                if masses[f]:
                    v[f, layer] = zo[slab][f, at] - 0.875 * q[f] + 0.125 * z[slab + 1][3 + f, at]
                if slab == 1:
                    pairs[0, 0, f, at] = x0[f, at] - q[f]
                    pairs[0, 1, f, at] = x1[f, at] - 0.5 * (q[f] + z[2][3 + f, at])

        def emit_even(layer, q):
            for f in range(FIELDS):
                pairs[1, 0, f, layer] = even[0, f, layer] - q[f]
                pairs[1, 1, f, layer] = even[1, f, layer] - 0.5 * (q[f] + x0[f, layer])

        inv_at = lambda f, layer: ie[layer // WIDTH, f, layer % WIDTH]
        solve(stencil, masses_only(z), layers_of(iv), 5 * WIDTH, scratch, emit_odd)
        solve(stencil, masses_only(zo), inv_at, 3 * WIDTH, scratch, emit_even)

    return call(
        body,
        [(3, 3 * WIDTH, 8, 128), (2, 2) + SLAB],
        *z_five, *inv_five, inv_three, *own_three, *pair_odd, pair_even,
        layers=5 * WIDTH, flops=88 * 4 * 1024 * 20,
    )


def chip_step(turn, place, z_five, inv_five, inv_three, v_three, offsets, done, grad):
    with_done, with_grad, with_z = done is not None, grad is not None, z_five is not None

    def body(*refs):
        refs = list(refs)
        spot = refs.pop(0)
        z = [refs.pop(0) for _ in range(5)] if with_z else None
        iv = [refs.pop(0) for _ in range(5)]
        ie, v, o = refs.pop(0), refs.pop(0), refs.pop(0)
        before = refs.pop(0) if with_done else None
        g = [refs.pop(0) for _ in range(2)] if with_grad else None
        z3, z6, z7, pairs = refs[:4]
        sums = refs[4] if with_grad else None
        middle, scratch = refs[-4], refs[-3:]
        if with_grad:
            sums[...] = g[0][...] + g[1][...]
        mine = spot[0] == turn

        @pl.when(jnp.logical_not(mine))
        def _():
            pairs[...] = before[...] if with_done else jnp.zeros_like(pairs)
            z3[...] = jnp.zeros_like(z3)
            z6[...] = jnp.zeros_like(z6)
            z7[...] = jnp.zeros_like(z7)

        @pl.when(mine)
        def _():
            stencil = Stencil()
            zero = jnp.zeros((8, 128), jnp.float32)

            def emit_odd(layer, q):
                slab, at = layer // WIDTH, layer % WIDTH
                for f in range(FIELDS):
                    own = slab == 1
                    c0 = z[slab + 1][3 + f, at] if with_z and (own or masses[f]) else zero
                    if masses[f]:
                        middle[f, layer] = 0.875 * q[f] - 0.125 * c0 + v[f, layer]
                    if own:
                        pairs[0, 0, f, at] = q[f] + o[0, 0, f, at]
                        pairs[0, 1, f, at] = 0.5 * (q[f] + c0) + o[0, 1, f, at]

            def emit_even(layer, q):
                for f in range(FIELDS):
                    c0 = q[f] + o[1, 0, f, layer]
                    c1 = 0.5 * (q[f] + pairs[0, 0, f, layer]) + o[1, 1, f, layer]
                    pairs[1, 0, f, layer] = c0
                    pairs[1, 1, f, layer] = c1
                    z7[3 + f, layer] = c0
                    if masses[f]:
                        carried = c0 - 0.25 * c1
                        z3[f, layer] = carried
                        z6[f, layer] = carried
                        z7[f, layer] = carried
                        z6[3 + f, layer] = c0

            if with_z:
                right = masses_only(z)
            else:
                right = lambda f, layer: zero if masses[f] else None
            middle_at = lambda f, layer: middle[f, layer] if masses[f] else None
            inv_at = lambda f, layer: ie[layer // WIDTH, f, layer % WIDTH]
            solve(stencil, right, layers_of(iv), 5 * WIDTH, scratch, emit_odd)
            solve(stencil, middle_at, inv_at, 3 * WIDTH, scratch, emit_even)

    spec = pl.BlockSpec(memory_space=pltpu.VMEM)
    operands = [place] + (list(z_five) if with_z else []) + list(inv_five) + [inv_three, v_three, offsets]
    operands += [done] if with_done else []
    operands += list(grad) if with_grad else []
    outs = [carry(3), carry(6), carry(7), (2, 2) + SLAB] + ([SLAB] if with_grad else [])
    return pl.pallas_call(
        body,
        in_specs=[pl.BlockSpec(memory_space=pltpu.SMEM)] + [spec] * (len(operands) - 1),
        out_specs=[spec] * len(outs),
        out_shape=[jax.ShapeDtypeStruct(shape, jnp.float32) for shape in outs],
        scratch_shapes=[vmem((3, 3 * WIDTH, 8, 128))] + [vmem((FIELDS, 5 * WIDTH, 8, 128))] * 3,
        compiler_params=pltpu.CompilerParams(vmem_limit_bytes=24 * 1024 * 1024),
        cost_estimate=pl.CostEstimate(flops=88 * 4 * 1024 * 20, bytes_accessed=1 << 20, transcendentals=0),
    )(*operands)


def routes(times, slabs, moved, chosen=None):
    pairs = []
    for k in range(times):
        for s in range(slabs):
            target = moved(k, s)
            if target is None or (chosen is not None and not chosen(k)):
                continue
            k2, s2 = target
            if 0 <= k2 < times and 0 <= s2 < slabs:
                pairs.append((k * slabs + s, k2 * slabs + s2))
    return pairs


def send(value, pairs):
    return lax.ppermute(value, AXES, pairs)


def program(times, slabs):
    chips = times // 2

    def shift(count):
        return routes(times, slabs, lambda k, s: (k, s + count))

    right_one, left_one, right_two, left_two = shift(1), shift(-1), shift(2), shift(-2)
    earlier = routes(times, slabs, lambda k, s: (k - 1, s))
    even_to_odd = routes(times, slabs, lambda k, s: (k + 1, s), lambda k: k % 2 == 0)
    odd_to_even = routes(times, slabs, lambda k, s: (k - 1, s), lambda k: k % 2 == 1)
    reach = (2, 1, 0, -1, -2)
    relaxed_routes = [
        routes(times, slabs, lambda k, s, d=d: (k - 1, s + d), lambda k: k % 2 == 0) for d in reach
    ]

    def hop_routes(hop):
        group = [h for h in range(1, chips) if (h - hop) % 4 == 0]
        senders = [2 * (chips - h) + 1 for h in group]
        return [
            routes(times, slabs, lambda k, s, d=d: (k - 2, s + d), lambda k: k in senders)
            for d in reach
        ]

    def on_device(forward_states, adjoint_source, source_gain, guess_pairs):
        states = forward_states.astype(jnp.float32)
        inverses = jnp.stack(
            [1.0 / make_diagonal(states[n], source_gain, fine_rate) for n in range(4)]
            + [1.0 / make_diagonal(states[0], source_gain, coarse_rate)]
        )
        ahead = send(guess_pairs[0], earlier)
        inv_low, inv_high = send(inverses, right_one), send(inverses, left_one)
        right = adjoint_source[3] + column(masses) * (4.0 * ahead[0] - ahead[1])
        coarse = inverses[4]
        coarse_low2, coarse_high2 = send(coarse, right_two), send(coarse, left_two)
        inv_five = [coarse_low2, inv_low[4], coarse, inv_high[4], coarse_high2]
        inv_three = send(jnp.stack([inv_low[4], coarse, inv_high[4]]), even_to_odd)

        previous, total = ahead[0], None
        adjoints = [None] * 4
        for n in (3, 2, 1, 0):
            low, high = send(right, right_one), send(right, left_one)
            source = adjoint_source[n - 1] if n else None
            x, total, *more = fine_step(
                n, right, low, high, inverses, inv_low, inv_high, states[n], source, previous, total
            )
            adjoints[n] = x
            previous = x
            if n:
                right = more[0]
        z3, z6, z7 = more
        total = time_step * total

        z_low, z_high = send(z3, right_one), send(z3, left_one)
        pair_even = send(jnp.stack([adjoints[0], adjoints[1]]), even_to_odd)
        payload = (z3, z6, z7, z6, z3)
        z_five = [send(part, path) for part, path in zip(payload, relaxed_routes)]
        v, offsets = offsets_step(
            z_five, inv_five, inv_three, (z_low, z3, z_high), (adjoints[0], adjoints[1]), pair_even
        )

        place = (lax.axis_index("tm").astype(jnp.int32)).reshape(1)
        stages = []
        far = 1
        while far < chips:
            stages.append(
                routes(times, slabs, lambda k, s, d=far: (2 * ((k // 2) ^ d), s), lambda k: k % 2 == 0)
            )
            far *= 2
        stages = [odd_to_even] + stages
        z_five, done, grad, hop = None, None, total, 0
        while hop < chips or stages:
            added = None
            if hop and stages:
                added = (grad, send(grad, stages.pop(0)))
            if hop < chips:
                if hop:
                    z_five = [send(part, path) for part, path in zip(payload, hop_routes(hop))]
                z3, z6, z7, done, *sums = chip_step(
                    times - 1 - 2 * hop, place, z_five, inv_five, inv_three, v, offsets, done, added
                )
                payload = (z3, z6, z7, z6, z3)
                if sums:
                    grad = sums[0]
            elif added:
                grad = added[0] + added[1]
            hop += 1

        even = lax.axis_index("tm") % 2 == 0
        grad_odd = send(grad, even_to_odd)
        gradient = jnp.where(even, grad, grad_odd)
        done_even = send(done[1], odd_to_even)
        corrected = jnp.where(even, done_even, done[0])
        return corrected[None], gradient

    return on_device


def solution(mesh):
    placed = (
        P("tm", None, "space", None, None),
        P("tm", None, "space", None, None),
        P(None, "space", None, None),
        P("tm", None, None, "space", None, None),
    )
    return jax.shard_map(
        program(mesh.shape["tm"], mesh.shape["space"]),
        mesh=mesh,
        in_specs=placed,
        out_specs=(P("tm", None, None, "space", None, None), P(None, "space", None, None)),
        check_vma=False,
    )
```

time: 531 us -> 216 us (0.41)
  the two profiles are of different devices: /device:TPU:225 before, /device:TPU:41 now
where the time goes in v1:
time: 216 us; the launch traced here: 215 us
  starting transfers between devices  113 us (52%)
  waiting for transfers between devices  91.4 us (42%)
  Pallas kernels  4.7 us (2%)
  other arithmetic  2.81 us (1%)
    ppermute x63, starting transfers between devices, send(): return lax.ppermute(value, AXES, pairs)  113 us
    ppermute x63, waiting for transfers between devices, send(): return lax.ppermute(value, AXES, pairs)  91.4 us
  transfers between devices with their start and end apart: 63, of which 9 were waited for; matrix products, arithmetic and copies ran while one was open for 0% of the time, Pallas kernels for 2%

profile of v1, /device:TPU:41, one launch (start us, length us, event | category | flops | bytes accessed | tf_op | source)
XLA Modules:
  0.0 214.7 jit_solution(11359610477226766734)
XLA Ops:
  2.7 3.3 %collective-permute-start.1 = (f32[5,4,4,8,128]{4,3,2,1,0:T(8,128)S(1)}, f32[5,4,4,8,128]{4,3,2,1,0:T(8,128)S(1)}, u32[]{:S(2)}, u32[]{:S(2)}) collective-permute-start(f32[5,4,4,8,128]{4,3,2,1,0:T(8,128)S(1)} %get-tuple-element.100.refs_3_), channel_id=1, source_target_pairs={{0,1},{1,2},{2,3},{3,4},{4,5},{5,6},{6,7},{7,8},{8,9},{9,10},{10,1... | collective-permute-start | bytes 983048 | tf_op jit(solution)/shard_map/ppermute | solution.py:305
  5.9 4.3 %collective-permute-start.2 = (f32[5,4,4,8,128]{4,3,2,1,0:T(8,128)S(1)}, f32[5,4,4,8,128]{4,3,2,1,0:T(8,128)S(1)}, u32[]{:S(2)}, u32[]{:S(2)}) collective-permute-start(f32[5,4,4,8,128]{4,3,2,1,0:T(8,128)S(1)} %get-tuple-element.100.refs_3_), channel_id=1, source_target_pairs={{1,0},{2,1},{3,2},{4,3},{5,4},{6,5},{7,6},{8,7},{9,8},{10,9},{11,1... | collective-permute-start | bytes 983048 | tf_op jit(solution)/shard_map/ppermute | solution.py:305
  10.2 3.1 %collective-permute-start.5 = (f32[2,4,4,8,128]{4,3,2,1,0:T(8,128)S(1)}, f32[2,4,4,8,128]{4,3,2,1,0:T(8,128)S(1)}, u32[]{:S(2)}, u32[]{:S(2)}) collective-permute-start(f32[2,4,4,8,128]{4,3,2,1,0:T(8,128)S(1)} %bitcast.74), channel_id=1, source_target_pairs={{32,0},{33,1},{34,2},{35,3},{36,4},{37,5},{38,6},{39,7},{40,8},{41... | collective-permute-start | bytes 393224 | tf_op jit(solution)/shard_map/ppermute | solution.py:305
  13.4 4.6 %collective-permute-done.5 = f32[2,4,4,8,128]{4,3,2,1,0:T(8,128)S(1)} collective-permute-done((f32[2,4,4,8,128]{4,3,2,1,0:T(8,128)S(1)}, f32[2,4,4,8,128]{4,3,2,1,0:T(8,128)S(1)}, u32[]{:S(2)}, u32[]{:S(2)}) %collective-permute-start.5) | collective-permute-done | bytes 131104 | tf_op jit(solution)/shard_map/ppermute | solution.py:305
  18.1 1.9 collective-permute-start.6
  20.0 18.2 %collective-permute-start.7 = (f32[4,4,8,128]{3,2,1,0:T(8,128)S(1)}, f32[4,4,8,128]{3,2,1,0:T(8,128)S(1)}, u32[]{:S(2)}, u32[]{:S(2)}) collective-permute-start(f32[4,4,8,128]{3,2,1,0:T(8,128)S(1)} %fusion.18.refs_0_), channel_id=1, source_target_pairs={{1,0},{2,1},{3,2},{4,3},{5,4},{6,5},{7,6},{8,7},{9,8},{10,9},{11,1... | collective-permute-start | bytes 196616 | tf_op jit(solution)/shard_map/ppermute | solution.py:305
  38.2 3.3 %collective-permute-done.7.refs_2_ = f32[4,4,8,128]{3,2,1,0:T(8,128)S(1)} collective-permute-done((f32[4,4,8,128]{3,2,1,0:T(8,128)S(1)}, f32[4,4,8,128]{3,2,1,0:T(8,128)S(1)}, u32[]{:S(2)}, u32[]{:S(2)}) %collective-permute-start.7) | collective-permute-done | bytes 65568 | tf_op jit(solution)/shard_map/ppermute | solution.py:305
  41.9 3.1 %collective-permute-start.8 = (f32[4,4,8,128]{3,2,1,0:T(8,128)S(1)}, f32[4,4,8,128]{3,2,1,0:T(8,128)S(1)}, u32[]{:S(2)}, u32[]{:S(2)}) collective-permute-start(f32[4,4,8,128]{3,2,1,0:T(8,128)S(1)} %get-tuple-element.51.refs_0_), channel_id=1, source_target_pairs={{0,1},{1,2},{2,3},{3,4},{4,5},{5,6},{6,7},{7,8},{8,9},{9,10},{10,1... | collective-permute-start | bytes 196616 | tf_op jit(solution)/shard_map/ppermute | solution.py:305
  45.1 4.3 %collective-permute-start.9 = (f32[4,4,8,128]{3,2,1,0:T(8,128)S(1)}, f32[4,4,8,128]{3,2,1,0:T(8,128)S(1)}, u32[]{:S(2)}, u32[]{:S(2)}) collective-permute-start(f32[4,4,8,128]{3,2,1,0:T(8,128)S(1)} %get-tuple-element.51.refs_0_), channel_id=1, source_target_pairs={{1,0},{2,1},{3,2},{4,3},{5,4},{6,5},{7,6},{8,7},{9,8},{10,9},{11,1... | collective-permute-start | bytes 196616 | tf_op jit(solution)/shard_map/ppermute | solution.py:305
  51.1 2.2 %collective-permute-start.10 = (f32[4,4,8,128]{3,2,1,0:T(8,128)S(1)}, f32[4,4,8,128]{3,2,1,0:T(8,128)S(1)}, u32[]{:S(2)}, u32[]{:S(2)}) collective-permute-start(f32[4,4,8,128]{3,2,1,0:T(8,128)S(1)} %get-tuple-element.54.refs_0_), channel_id=1, source_target_pairs={{0,1},{1,2},{2,3},{3,4},{4,5},{5,6},{6,7},{7,8},{8,9},{9,10},{10,1... | collective-permute-start | bytes 196616 | tf_op jit(solution)/shard_map/ppermute | solution.py:305
  53.3 5.5 %collective-permute-start.11 = (f32[4,4,8,128]{3,2,1,0:T(8,128)S(1)}, f32[4,4,8,128]{3,2,1,0:T(8,128)S(1)}, u32[]{:S(2)}, u32[]{:S(2)}) collective-permute-start(f32[4,4,8,128]{3,2,1,0:T(8,128)S(1)} %get-tuple-element.54.refs_0_), channel_id=1, source_target_pairs={{1,0},{2,1},{3,2},{4,3},{5,4},{6,5},{7,6},{8,7},{9,8},{10,9},{11,1... | collective-permute-start | bytes 196616 | tf_op jit(solution)/shard_map/ppermute | solution.py:305
  60.5 2.2 %collective-permute-start.12 = (f32[4,4,8,128]{3,2,1,0:T(8,128)S(1)}, f32[4,4,8,128]{3,2,1,0:T(8,128)S(1)}, u32[]{:S(2)}, u32[]{:S(2)}) collective-permute-start(f32[4,4,8,128]{3,2,1,0:T(8,128)S(1)} %get-tuple-element.57.refs_0_), channel_id=1, source_target_pairs={{0,1},{1,2},{2,3},{3,4},{4,5},{5,6},{6,7},{7,8},{8,9},{9,10},{10,1... | collective-permute-start | bytes 196616 | tf_op jit(solution)/shard_map/ppermute | solution.py:305
  62.8 5.5 %collective-permute-start.13 = (f32[4,4,8,128]{3,2,1,0:T(8,128)S(1)}, f32[4,4,8,128]{3,2,1,0:T(8,128)S(1)}, u32[]{:S(2)}, u32[]{:S(2)}) collective-permute-start(f32[4,4,8,128]{3,2,1,0:T(8,128)S(1)} %get-tuple-element.57.refs_0_), channel_id=1, source_target_pairs={{1,0},{2,1},{3,2},{4,3},{5,4},{6,5},{7,6},{8,7},{9,8},{10,9},{11,1... | collective-permute-start | bytes 196616 | tf_op jit(solution)/shard_map/ppermute | solution.py:305
  68.2 2.3 %collective-permute-start = (f32[4,4,8,128]{3,2,1,0:T(8,128)S(1)}, f32[4,4,8,128]{3,2,1,0:T(8,128)S(1)}, u32[]{:S(2)}, u32[]{:S(2)}) collective-permute-start(f32[4,4,8,128]{3,2,1,0:T(8,128)S(1)} %get-tuple-element.101.refs_7_.refs_3_.refs_8_), channel_id=1, source_target_pairs={{0,2},{1,3},{2,4},{3,5},{4,6},{5,7},{6,8},{7,9},{8,10},{9,11},{10,... | collective-permute-start | bytes 196616 | tf_op jit(solution)/shard_map/ppermute | solution.py:305
  70.5 5.4 %collective-permute-start.3 = (f32[4,4,8,128]{3,2,1,0:T(8,128)S(1)}, f32[4,4,8,128]{3,2,1,0:T(8,128)S(1)}, u32[]{:S(2)}, u32[]{:S(2)}) collective-permute-start(f32[4,4,8,128]{3,2,1,0:T(8,128)S(1)} %get-tuple-element.101.refs_7_.refs_3_.refs_8_), channel_id=1, source_target_pairs={{2,0},{3,1},{4,2},{5,3},{6,4},{7,5},{8,6},{9,7},{10,8},{11,9},{12,... | collective-permute-start | bytes 196616 | tf_op jit(solution)/shard_map/ppermute | solution.py:305
  76.4 1.3 collective-permute-start.14
  77.7 1.3 collective-permute-start.18
  79.0 1.9 collective-permute-start.19
  81.0 1.3 collective-permute-start.15
  83.6 4.8 %collective-permute-done.14.refs_0_ = f32[3,4,8,128]{3,2,1,0:T(8,128)S(1)} collective-permute-done((f32[3,4,8,128]{3,2,1,0:T(8,128)S(1)}, f32[3,4,8,128]{3,2,1,0:T(8,128)S(1)}, u32[]{:S(2)}, u32[]{:S(2)}) %collective-permute-start.14) | collective-permute-done | bytes 49184 | tf_op jit(solution)/shard_map/ppermute | solution.py:305
  88.3 3.6 %collective-permute-start.20 = (f32[3,4,8,128]{3,2,1,0:T(8,128)S(1)}, f32[3,4,8,128]{3,2,1,0:T(8,128)S(1)}, u32[]{:S(2)}, u32[]{:S(2)}) collective-permute-start(f32[3,4,8,128]{3,2,1,0:T(8,128)S(1)} %get-tuple-element.60.refs_12_), channel_id=1, source_target_pairs={{1,0},{2,1},{3,2},{4,3},{5,4},{6,5},{7,6},{8,7},{9,8},{10,9},{11,1... | collective-permute-start | bytes 147464 | tf_op jit(solution)/shard_map/ppermute | solution.py:305
  94.6 2.4 %collective-permute-start.27 = (f32[4,4,8,128]{3,2,1,0:T(8,128)S(1)}, f32[4,4,8,128]{3,2,1,0:T(8,128)S(1)}, u32[]{:S(2)}, u32[]{:S(2)}) collective-permute-start(f32[4,4,8,128]{3,2,1,0:T(8,128)S(1)} %broadcast_multiply_fusion.refs_15_), channel_id=1, source_target_pairs={{32,0},{33,1},{34,2},{35,3},{36,4},{37,5},{38,6},{39,7},{40,8},{41... | collective-permute-start | bytes 196616 | tf_op jit(solution)/shard_map/ppermute | solution.py:305
  97.1 3.5 %collective-permute-done.16.refs_2_ = f32[7,4,8,128]{3,2,1,0:T(8,128)S(1)} collective-permute-done((f32[7,4,8,128]{3,2,1,0:T(8,128)S(1)}, f32[7,4,8,128]{3,2,1,0:T(8,128)S(1)}, u32[]{:S(2)}, u32[]{:S(2)}) %collective-permute-start.16) | collective-permute-done | bytes 114720 | tf_op jit(solution)/shard_map/ppermute | solution.py:305
  115.2 30.8 %collective-permute-done.34.refs_1_ = f32[3,4,8,128]{3,2,1,0:T(8,128)S(1)} collective-permute-done((f32[3,4,8,128]{3,2,1,0:T(8,128)S(1)}, f32[3,4,8,128]{3,2,1,0:T(8,128)S(1)}, u32[]{:S(2)}, u32[]{:S(2)}) %collective-permute-start.34) | collective-permute-done | bytes 49184 | tf_op jit(solution)/shard_map/ppermute | solution.py:305
  147.3 5.9 %collective-permute-done.38.refs_5_ = f32[3,4,8,128]{3,2,1,0:T(8,128)S(1)} collective-permute-done((f32[3,4,8,128]{3,2,1,0:T(8,128)S(1)}, f32[3,4,8,128]{3,2,1,0:T(8,128)S(1)}, u32[]{:S(2)}, u32[]{:S(2)}) %collective-permute-start.38) | collective-permute-done | bytes 49184 | tf_op jit(solution)/shard_map/ppermute | solution.py:305
  164.6 1.3 collective-permute-start.58
  165.9 1.3 collective-permute-start.57
  167.2 1.3 collective-permute-start.59
  168.5 1.3 collective-permute-start.56
  171.1 36.8 %collective-permute-done.56.refs_1_ = f32[3,4,8,128]{3,2,1,0:T(8,128)S(1)} collective-permute-done((f32[3,4,8,128]{3,2,1,0:T(8,128)S(1)}, f32[3,4,8,128]{3,2,1,0:T(8,128)S(1)}, u32[]{:S(2)}, u32[]{:S(2)}) %collective-permute-start.56) | collective-permute-done | bytes 49184 | tf_op jit(solution)/shard_map/ppermute | solution.py:305
  209.2 1.7 shard_map.215
  210.9 2.1 collective-permute-start.61
  (136 shorter events, 41.2 us)
Async XLA Ops:
  2.7 38.9 %collective-permute-start.1 = (f32[5,4,4,8,128]{4,3,2,1,0:T(8,128)S(1)}, f32[5,4,4,8,128]{4,3,2,1,0:T(8,128)S(1)}, u32[]{:S(2)}, u32[]{:S(2)}) collective-permute-start(f32[5,4,4,8,128]{4,3,2,1,0:T(8,128)S(1)} %get-tuple-element.100.refs_3_), channel_id=1, source_target_pairs={{0,1},{1,2},{2,3},{3,4},{4,5},{5,6},{6,7},{7,8},{8,9},{9,10},{10,1... | collective-permute-start | bytes 983048 | tf_op jit(solution)/shard_map/ppermute | solution.py:305
  5.9 35.6 %collective-permute-start.2 = (f32[5,4,4,8,128]{4,3,2,1,0:T(8,128)S(1)}, f32[5,4,4,8,128]{4,3,2,1,0:T(8,128)S(1)}, u32[]{:S(2)}, u32[]{:S(2)}) collective-permute-start(f32[5,4,4,8,128]{4,3,2,1,0:T(8,128)S(1)} %get-tuple-element.100.refs_3_), channel_id=1, source_target_pairs={{1,0},{2,1},{3,2},{4,3},{5,4},{6,5},{7,6},{8,7},{9,8},{10,9},{11,1... | collective-permute-start | bytes 983048 | tf_op jit(solution)/shard_map/ppermute | solution.py:305
  10.2 7.8 %collective-permute-start.5 = (f32[2,4,4,8,128]{4,3,2,1,0:T(8,128)S(1)}, f32[2,4,4,8,128]{4,3,2,1,0:T(8,128)S(1)}, u32[]{:S(2)}, u32[]{:S(2)}) collective-permute-start(f32[2,4,4,8,128]{4,3,2,1,0:T(8,128)S(1)} %bitcast.74), channel_id=1, source_target_pairs={{32,0},{33,1},{34,2},{35,3},{36,4},{37,5},{38,6},{39,7},{40,8},{41... | collective-permute-start | bytes 393224 | tf_op jit(solution)/shard_map/ppermute | solution.py:305
  18.1 20.1 %collective-permute-start.6 = (f32[4,4,8,128]{3,2,1,0:T(8,128)S(1)}, f32[4,4,8,128]{3,2,1,0:T(8,128)S(1)}, u32[]{:S(2)}, u32[]{:S(2)}) collective-permute-start(f32[4,4,8,128]{3,2,1,0:T(8,128)S(1)} %fusion.18.refs_0_), channel_id=1, source_target_pairs={{0,1},{1,2},{2,3},{3,4},{4,5},{5,6},{6,7},{7,8},{8,9},{9,10},{10,1... | collective-permute-start | bytes 196616 | tf_op jit(solution)/shard_map/ppermute | solution.py:305
  20.0 21.6 %collective-permute-start.7 = (f32[4,4,8,128]{3,2,1,0:T(8,128)S(1)}, f32[4,4,8,128]{3,2,1,0:T(8,128)S(1)}, u32[]{:S(2)}, u32[]{:S(2)}) collective-permute-start(f32[4,4,8,128]{3,2,1,0:T(8,128)S(1)} %fusion.18.refs_0_), channel_id=1, source_target_pairs={{1,0},{2,1},{3,2},{4,3},{5,4},{6,5},{7,6},{8,7},{9,8},{10,9},{11,1... | collective-permute-start | bytes 196616 | tf_op jit(solution)/shard_map/ppermute | solution.py:305
  41.9 7.4 %collective-permute-start.8 = (f32[4,4,8,128]{3,2,1,0:T(8,128)S(1)}, f32[4,4,8,128]{3,2,1,0:T(8,128)S(1)}, u32[]{:S(2)}, u32[]{:S(2)}) collective-permute-start(f32[4,4,8,128]{3,2,1,0:T(8,128)S(1)} %get-tuple-element.51.refs_0_), channel_id=1, source_target_pairs={{0,1},{1,2},{2,3},{3,4},{4,5},{5,6},{6,7},{7,8},{8,9},{9,10},{10,1... | collective-permute-start | bytes 196616 | tf_op jit(solution)/shard_map/ppermute | solution.py:305
  51.1 9.1 %collective-permute-start.10 = (f32[4,4,8,128]{3,2,1,0:T(8,128)S(1)}, f32[4,4,8,128]{3,2,1,0:T(8,128)S(1)}, u32[]{:S(2)}, u32[]{:S(2)}) collective-permute-start(f32[4,4,8,128]{3,2,1,0:T(8,128)S(1)} %get-tuple-element.54.refs_0_), channel_id=1, source_target_pairs={{0,1},{1,2},{2,3},{3,4},{4,5},{5,6},{6,7},{7,8},{8,9},{9,10},{10,1... | collective-permute-start | bytes 196616 | tf_op jit(solution)/shard_map/ppermute | solution.py:305
  53.3 6.8 %collective-permute-start.11 = (f32[4,4,8,128]{3,2,1,0:T(8,128)S(1)}, f32[4,4,8,128]{3,2,1,0:T(8,128)S(1)}, u32[]{:S(2)}, u32[]{:S(2)}) collective-permute-start(f32[4,4,8,128]{3,2,1,0:T(8,128)S(1)} %get-tuple-element.54.refs_0_), channel_id=1, source_target_pairs={{1,0},{2,1},{3,2},{4,3},{5,4},{6,5},{7,6},{8,7},{9,8},{10,9},{11,1... | collective-permute-start | bytes 196616 | tf_op jit(solution)/shard_map/ppermute | solution.py:305
  58.8 23.4 %collective-permute-start.4 = (f32[3,4,4,8,128]{4,3,2,1,0:T(8,128)S(1)}, f32[3,4,4,8,128]{4,3,2,1,0:T(8,128)S(1)}, u32[]{:S(2)}, u32[]{:S(2)}) collective-permute-start(f32[3,4,4,8,128]{4,3,2,1,0:T(8,128)S(1)} %pad_maximum_fusion), channel_id=1, source_target_pairs={{0,32},{1,33},{2,34},{3,35},{4,36},{5,37},{6,38},{7,39},{8,40},{9,... | collective-permute-start | bytes 589832 | tf_op jit(solution)/shard_map/ppermute | solution.py:305
  60.5 15.4 %collective-permute-start.12 = (f32[4,4,8,128]{3,2,1,0:T(8,128)S(1)}, f32[4,4,8,128]{3,2,1,0:T(8,128)S(1)}, u32[]{:S(2)}, u32[]{:S(2)}) collective-permute-start(f32[4,4,8,128]{3,2,1,0:T(8,128)S(1)} %get-tuple-element.57.refs_0_), channel_id=1, source_target_pairs={{0,1},{1,2},{2,3},{3,4},{4,5},{5,6},{6,7},{7,8},{8,9},{9,10},{10,1... | collective-permute-start | bytes 196616 | tf_op jit(solution)/shard_map/ppermute | solution.py:305
  62.8 13.2 %collective-permute-start.13 = (f32[4,4,8,128]{3,2,1,0:T(8,128)S(1)}, f32[4,4,8,128]{3,2,1,0:T(8,128)S(1)}, u32[]{:S(2)}, u32[]{:S(2)}) collective-permute-start(f32[4,4,8,128]{3,2,1,0:T(8,128)S(1)} %get-tuple-element.57.refs_0_), channel_id=1, source_target_pairs={{1,0},{2,1},{3,2},{4,3},{5,4},{6,5},{7,6},{8,7},{9,8},{10,9},{11,1... | collective-permute-start | bytes 196616 | tf_op jit(solution)/shard_map/ppermute | solution.py:305
  68.2 10.7 %collective-permute-start = (f32[4,4,8,128]{3,2,1,0:T(8,128)S(1)}, f32[4,4,8,128]{3,2,1,0:T(8,128)S(1)}, u32[]{:S(2)}, u32[]{:S(2)}) collective-permute-start(f32[4,4,8,128]{3,2,1,0:T(8,128)S(1)} %get-tuple-element.101.refs_7_.refs_3_.refs_8_), channel_id=1, source_target_pairs={{0,2},{1,3},{2,4},{3,5},{4,6},{5,7},{6,8},{7,9},{8,10},{9,11},{10,... | collective-permute-start | bytes 196616 | tf_op jit(solution)/shard_map/ppermute | solution.py:305
  70.5 10.4 %collective-permute-start.3 = (f32[4,4,8,128]{3,2,1,0:T(8,128)S(1)}, f32[4,4,8,128]{3,2,1,0:T(8,128)S(1)}, u32[]{:S(2)}, u32[]{:S(2)}) collective-permute-start(f32[4,4,8,128]{3,2,1,0:T(8,128)S(1)} %get-tuple-element.101.refs_7_.refs_3_.refs_8_), channel_id=1, source_target_pairs={{2,0},{3,1},{4,2},{5,3},{6,4},{7,5},{8,6},{9,7},{10,8},{11,9},{12,... | collective-permute-start | bytes 196616 | tf_op jit(solution)/shard_map/ppermute | solution.py:305
  76.4 12.0 %collective-permute-start.14 = (f32[3,4,8,128]{3,2,1,0:T(8,128)S(1)}, f32[3,4,8,128]{3,2,1,0:T(8,128)S(1)}, u32[]{:S(2)}, u32[]{:S(2)}) collective-permute-start(f32[3,4,8,128]{3,2,1,0:T(8,128)S(1)} %get-tuple-element.60.refs_12_), channel_id=1, source_target_pairs={{64,34},{65,35},{66,36},{67,37},{68,38},{69,39},{70,40},{71,41},{7... | collective-permute-start | bytes 147464 | tf_op jit(solution)/shard_map/ppermute | solution.py:305
  77.7 14.3 %collective-permute-start.18 = (f32[3,4,8,128]{3,2,1,0:T(8,128)S(1)}, f32[3,4,8,128]{3,2,1,0:T(8,128)S(1)}, u32[]{:S(2)}, u32[]{:S(2)}) collective-permute-start(f32[3,4,8,128]{3,2,1,0:T(8,128)S(1)} %get-tuple-element.60.refs_12_), channel_id=1, source_target_pairs={{66,32},{67,33},{68,34},{69,35},{70,36},{71,37},{72,38},{73,39},{7... | collective-permute-start | bytes 147464 | tf_op jit(solution)/shard_map/ppermute | solution.py:305
  79.0 14.3 %collective-permute-start.19 = (f32[3,4,8,128]{3,2,1,0:T(8,128)S(1)}, f32[3,4,8,128]{3,2,1,0:T(8,128)S(1)}, u32[]{:S(2)}, u32[]{:S(2)}) collective-permute-start(f32[3,4,8,128]{3,2,1,0:T(8,128)S(1)} %get-tuple-element.60.refs_12_), channel_id=1, source_target_pairs={{0,1},{1,2},{2,3},{3,4},{4,5},{5,6},{6,7},{7,8},{8,9},{9,10},{10,1... | collective-permute-start | bytes 147464 | tf_op jit(solution)/shard_map/ppermute | solution.py:305
  81.0 16.1 %collective-permute-start.15 = (f32[6,4,8,128]{3,2,1,0:T(8,128)S(1)}, f32[6,4,8,128]{3,2,1,0:T(8,128)S(1)}, u32[]{:S(2)}, u32[]{:S(2)}) collective-permute-start(f32[6,4,8,128]{3,2,1,0:T(8,128)S(1)} %get-tuple-element.61), channel_id=1, source_target_pairs={{64,33},{65,34},{66,35},{67,36},{68,37},{69,38},{70,39},{71,40},{7... | collective-permute-start | bytes 294920 | tf_op jit(solution)/shard_map/ppermute | solution.py:305
  82.3 14.8 %collective-permute-start.17 = (f32[6,4,8,128]{3,2,1,0:T(8,128)S(1)}, f32[6,4,8,128]{3,2,1,0:T(8,128)S(1)}, u32[]{:S(2)}, u32[]{:S(2)}) collective-permute-start(f32[6,4,8,128]{3,2,1,0:T(8,128)S(1)} %get-tuple-element.61), channel_id=1, source_target_pairs={{65,32},{66,33},{67,34},{68,35},{69,36},{70,37},{71,38},{72,39},{7... | collective-permute-start | bytes 294920 | tf_op jit(solution)/shard_map/ppermute | solution.py:305
  92.0 8.6 %collective-permute-start.21 = (f32[2,4,4,8,128]{4,3,2,1,0:T(8,128)S(1)}, f32[2,4,4,8,128]{4,3,2,1,0:T(8,128)S(1)}, u32[]{:S(2)}, u32[]{:S(2)}) collective-permute-start(f32[2,4,4,8,128]{4,3,2,1,0:T(8,128)S(1)} %pad_maximum_fusion.1), channel_id=1, source_target_pairs={{0,32},{1,33},{2,34},{3,35},{4,36},{5,37},{6,38},{7,39},{8,40},{9,... | collective-permute-start | bytes 393224 | tf_op jit(solution)/shard_map/ppermute | solution.py:305
  93.3 7.3 %collective-permute-start.16 = (f32[7,4,8,128]{3,2,1,0:T(8,128)S(1)}, f32[7,4,8,128]{3,2,1,0:T(8,128)S(1)}, u32[]{:S(2)}, u32[]{:S(2)}) collective-permute-start(f32[7,4,8,128]{3,2,1,0:T(8,128)S(1)} %get-tuple-element.62), channel_id=1, source_target_pairs={{64,32},{65,33},{66,34},{67,35},{68,36},{69,37},{70,38},{71,39},{7... | collective-permute-start | bytes 344072 | tf_op jit(solution)/shard_map/ppermute | solution.py:305
  94.6 9.7 %collective-permute-start.27 = (f32[4,4,8,128]{3,2,1,0:T(8,128)S(1)}, f32[4,4,8,128]{3,2,1,0:T(8,128)S(1)}, u32[]{:S(2)}, u32[]{:S(2)}) collective-permute-start(f32[4,4,8,128]{3,2,1,0:T(8,128)S(1)} %broadcast_multiply_fusion.refs_15_), channel_id=1, source_target_pairs={{32,0},{33,1},{34,2},{35,3},{36,4},{37,5},{38,6},{39,7},{40,8},{41... | collective-permute-start | bytes 196616 | tf_op jit(solution)/shard_map/ppermute | solution.py:305
  109.3 43.9 %collective-permute-start.36 = (f32[7,4,8,128]{3,2,1,0:T(8,128)S(1)}, f32[7,4,8,128]{3,2,1,0:T(8,128)S(1)}, u32[]{:S(2)}, u32[]{:S(2)}) collective-permute-start(f32[7,4,8,128]{3,2,1,0:T(8,128)S(1)} %get-tuple-element.78), channel_id=1, source_target_pairs={{96,32},{97,33},{98,34},{99,35},{100,36},{101,37},{102,38},{103,39... | collective-permute-start | bytes 344072 | tf_op jit(solution)/shard_map/ppermute | solution.py:305
  110.6 35.4 %collective-permute-start.34 = (f32[3,4,8,128]{3,2,1,0:T(8,128)S(1)}, f32[3,4,8,128]{3,2,1,0:T(8,128)S(1)}, u32[]{:S(2)}, u32[]{:S(2)}) collective-permute-start(f32[3,4,8,128]{3,2,1,0:T(8,128)S(1)} %get-tuple-element.76), channel_id=1, source_target_pairs={{96,34},{97,35},{98,36},{99,37},{100,38},{101,39},{102,40},{103,41... | collective-permute-start | bytes 147464 | tf_op jit(solution)/shard_map/ppermute | solution.py:305
  111.9 41.3 %collective-permute-start.35 = (f32[6,4,8,128]{3,2,1,0:T(8,128)S(1)}, f32[6,4,8,128]{3,2,1,0:T(8,128)S(1)}, u32[]{:S(2)}, u32[]{:S(2)}) collective-permute-start(f32[6,4,8,128]{3,2,1,0:T(8,128)S(1)} %get-tuple-element.77), channel_id=1, source_target_pairs={{96,33},{97,34},{98,35},{99,36},{100,37},{101,38},{102,39},{103,40... | collective-permute-start | bytes 294920 | tf_op jit(solution)/shard_map/ppermute | solution.py:305
  113.2 40.0 %collective-permute-start.37 = (f32[6,4,8,128]{3,2,1,0:T(8,128)S(1)}, f32[6,4,8,128]{3,2,1,0:T(8,128)S(1)}, u32[]{:S(2)}, u32[]{:S(2)}) collective-permute-start(f32[6,4,8,128]{3,2,1,0:T(8,128)S(1)} %get-tuple-element.77), channel_id=1, source_target_pairs={{97,32},{98,33},{99,34},{100,35},{101,36},{102,37},{103,38},{104,3... | collective-permute-start | bytes 294920 | tf_op jit(solution)/shard_map/ppermute | solution.py:305
  114.5 38.7 %collective-permute-start.39 = (f32[4,4,8,128]{3,2,1,0:T(8,128)S(1)}, f32[4,4,8,128]{3,2,1,0:T(8,128)S(1)}, u32[]{:S(2)}, u32[]{:S(2)}) collective-permute-start(f32[4,4,8,128]{3,2,1,0:T(8,128)S(1)} %get-tuple-element.80.refs_15_), channel_id=1, source_target_pairs={{0,128},{1,129},{2,130},{3,131},{4,132},{5,133},{6,134},{7,135},{8... | collective-permute-start | bytes 196616 | tf_op jit(solution)/shard_map/ppermute | solution.py:305
  146.0 7.2 %collective-permute-start.38 = (f32[3,4,8,128]{3,2,1,0:T(8,128)S(1)}, f32[3,4,8,128]{3,2,1,0:T(8,128)S(1)}, u32[]{:S(2)}, u32[]{:S(2)}) collective-permute-start(f32[3,4,8,128]{3,2,1,0:T(8,128)S(1)} %get-tuple-element.76), channel_id=1, source_target_pairs={{98,32},{99,33},{100,34},{101,35},{102,36},{103,37},{104,38},{105,... | collective-permute-start | bytes 147464 | tf_op jit(solution)/shard_map/ppermute | solution.py:305
  164.6 44.6 %collective-permute-start.58 = (f32[7,4,8,128]{3,2,1,0:T(8,128)S(1)}, f32[7,4,8,128]{3,2,1,0:T(8,128)S(1)}, u32[]{:S(2)}, u32[]{:S(2)}) collective-permute-start(f32[7,4,8,128]{3,2,1,0:T(8,128)S(1)} %get-tuple-element.96), channel_id=1, source_target_pairs={{96,32},{97,33},{98,34},{99,35},{100,36},{101,37},{102,38},{103,39... | collective-permute-start | bytes 344072 | tf_op jit(solution)/shard_map/ppermute | solution.py:305
  165.9 43.3 %collective-permute-start.57 = (f32[6,4,8,128]{3,2,1,0:T(8,128)S(1)}, f32[6,4,8,128]{3,2,1,0:T(8,128)S(1)}, u32[]{:S(2)}, u32[]{:S(2)}) collective-permute-start(f32[6,4,8,128]{3,2,1,0:T(8,128)S(1)} %get-tuple-element.95), channel_id=1, source_target_pairs={{96,33},{97,34},{98,35},{99,36},{100,37},{101,38},{102,39},{103,40... | collective-permute-start | bytes 294920 | tf_op jit(solution)/shard_map/ppermute | solution.py:305
  167.2 42.0 %collective-permute-start.59 = (f32[6,4,8,128]{3,2,1,0:T(8,128)S(1)}, f32[6,4,8,128]{3,2,1,0:T(8,128)S(1)}, u32[]{:S(2)}, u32[]{:S(2)}) collective-permute-start(f32[6,4,8,128]{3,2,1,0:T(8,128)S(1)} %get-tuple-element.95), channel_id=1, source_target_pairs={{97,32},{98,33},{99,34},{100,35},{101,36},{102,37},{103,38},{104,3... | collective-permute-start | bytes 294920 | tf_op jit(solution)/shard_map/ppermute | solution.py:305
  168.5 39.4 %collective-permute-start.56 = (f32[3,4,8,128]{3,2,1,0:T(8,128)S(1)}, f32[3,4,8,128]{3,2,1,0:T(8,128)S(1)}, u32[]{:S(2)}, u32[]{:S(2)}) collective-permute-start(f32[3,4,8,128]{3,2,1,0:T(8,128)S(1)} %get-tuple-element.94), channel_id=1, source_target_pairs={{96,34},{97,35},{98,36},{99,37},{100,38},{101,39},{102,40},{103,41... | collective-permute-start | bytes 147464 | tf_op jit(solution)/shard_map/ppermute | solution.py:305
  169.8 39.4 %collective-permute-start.60 = (f32[3,4,8,128]{3,2,1,0:T(8,128)S(1)}, f32[3,4,8,128]{3,2,1,0:T(8,128)S(1)}, u32[]{:S(2)}, u32[]{:S(2)}) collective-permute-start(f32[3,4,8,128]{3,2,1,0:T(8,128)S(1)} %get-tuple-element.94), channel_id=1, source_target_pairs={{98,32},{99,33},{100,34},{101,35},{102,36},{103,37},{104,38},{105,... | collective-permute-start | bytes 147464 | tf_op jit(solution)/shard_map/ppermute | solution.py:305
  (37 other events, 107.0 us)

commit v2 on v1

--- a/solution.py
+++ b/solution.py
@@ -152,22 +152,29 @@
                     if masses[f]:
                         r = r + (4.0 * x[f] - prev[f, layer])
                     more[0][f, layer] = r
+                    if first:
+                        more[1][f, layer] = r
                 else:
-                    z3, z6, z7 = more
+                    z7, pack = more
                     z7[3 + f, layer] = x[f]
+                    pack[0, f, layer] = x[f]
+                    pack[1, f, layer] = prev[f, layer]
                     if masses[f]:
-                        z = x[f] - 0.25 * prev[f, layer]
-                        z3[f, layer] = z
-                        z6[f, layer] = z
-                        z7[f, layer] = z
-                        z6[3 + f, layer] = x[f]
-
+                        z7[f, layer] = x[f] - 0.25 * prev[f, layer]
+
+        if first:
+            more[0][FIELDS:] = il[4]
+            more[1][FIELDS:] = ih[4]
+        if last:
+            for place in range(3):
+                more[1][2 + place] = pieces[place][4]
         solve(stencil, right_at, inverse, 3 * WIDTH, scratch, emit)
 
     operands = [right, right_low, right_high, inv, inv_low, inv_high, states, previous]
     operands += [] if last else [source]
     operands += [] if first else [total]
-    outs = [SLAB, SLAB] + ([carry(3), carry(6), carry(7)] if last else [SLAB])
+    outs = [SLAB, SLAB]
+    outs += [carry(7), (5,) + SLAB] if last else [carry(8)] * 2 if first else [SLAB]
     return call(body, outs, *operands, layers=3 * WIDTH, flops=28 * 4 * 1024 * 20)
 
 
@@ -175,11 +182,12 @@
     return (count, WIDTH, 8, 128)
 
 
-def offsets_step(z_five, inv_five, inv_three, own_three, pair_odd, pair_even):
+def offsets_step(z_three, inv_five, pack, own_three, pair_odd):
     def body(*refs):
-        z, iv, ie, zo, (x0, x1, even) = refs[0:5], refs[5:10], refs[10], refs[11:14], refs[14:17]
-        v, pairs = refs[17:19]
-        scratch = refs[19:]
+        (zl, zm, zh), iv, even, zo, (x0, x1) = refs[0:3], refs[3:8], refs[8], refs[9:12], refs[12:14]
+        v, pairs = refs[14:16]
+        scratch = refs[16:]
+        z = [zl.at[0:3], zl.at[3:9], zm, zh.at[0:6], zh.at[6:9]]
         stencil = Stencil()
 
         def emit_odd(layer, q):
@@ -196,19 +204,19 @@
                 pairs[1, 0, f, layer] = even[0, f, layer] - q[f]
                 pairs[1, 1, f, layer] = even[1, f, layer] - 0.5 * (q[f] + x0[f, layer])
 
-        inv_at = lambda f, layer: ie[layer // WIDTH, f, layer % WIDTH]
+        inv_at = lambda f, layer: even[2 + layer // WIDTH, f, layer % WIDTH]
         solve(stencil, masses_only(z), layers_of(iv), 5 * WIDTH, scratch, emit_odd)
         solve(stencil, masses_only(zo), inv_at, 3 * WIDTH, scratch, emit_even)
 
     return call(
         body,
         [(3, 3 * WIDTH, 8, 128), (2, 2) + SLAB],
-        *z_five, *inv_five, inv_three, *own_three, *pair_odd, pair_even,
+        *z_three, *inv_five, pack, *own_three, *pair_odd,
         layers=5 * WIDTH, flops=88 * 4 * 1024 * 20,
     )
 
 
-def chip_step(turn, place, z_five, inv_five, inv_three, v_three, offsets, done, grad):
+def chip_step(turn, place, z_five, inv_five, pack, v_three, offsets, done, grad):
     with_done, with_grad, with_z = done is not None, grad is not None, z_five is not None
 
     def body(*refs):
@@ -216,7 +224,7 @@
         spot = refs.pop(0)
         z = [refs.pop(0) for _ in range(5)] if with_z else None
         iv = [refs.pop(0) for _ in range(5)]
-        ie, v, o = refs.pop(0), refs.pop(0), refs.pop(0)
+        even, v, o = refs.pop(0), refs.pop(0), refs.pop(0)
         before = refs.pop(0) if with_done else None
         g = [refs.pop(0) for _ in range(2)] if with_grad else None
         z3, z6, z7, pairs = refs[:4]
@@ -268,12 +276,12 @@
             else:
                 right = lambda f, layer: zero if masses[f] else None
             middle_at = lambda f, layer: middle[f, layer] if masses[f] else None
-            inv_at = lambda f, layer: ie[layer // WIDTH, f, layer % WIDTH]
+            inv_at = lambda f, layer: even[2 + layer // WIDTH, f, layer % WIDTH]
             solve(stencil, right, layers_of(iv), 5 * WIDTH, scratch, emit_odd)
             solve(stencil, middle_at, inv_at, 3 * WIDTH, scratch, emit_even)
 
     spec = pl.BlockSpec(memory_space=pltpu.VMEM)
-    operands = [place] + (list(z_five) if with_z else []) + list(inv_five) + [inv_three, v_three, offsets]
+    operands = [place] + (list(z_five) if with_z else []) + list(inv_five) + [pack, v_three, offsets]
     operands += [done] if with_done else []
     operands += list(grad) if with_grad else []
     outs = [carry(3), carry(6), carry(7), (2, 2) + SLAB] + ([SLAB] if with_grad else [])
@@ -311,13 +319,13 @@
     def shift(count):
         return routes(times, slabs, lambda k, s: (k, s + count))
 
-    right_one, left_one, right_two, left_two = shift(1), shift(-1), shift(2), shift(-2)
+    right_one, left_one = shift(1), shift(-1)
     earlier = routes(times, slabs, lambda k, s: (k - 1, s))
     even_to_odd = routes(times, slabs, lambda k, s: (k + 1, s), lambda k: k % 2 == 0)
     odd_to_even = routes(times, slabs, lambda k, s: (k - 1, s), lambda k: k % 2 == 1)
     reach = (2, 1, 0, -1, -2)
     relaxed_routes = [
-        routes(times, slabs, lambda k, s, d=d: (k - 1, s + d), lambda k: k % 2 == 0) for d in reach
+        routes(times, slabs, lambda k, s, d=d: (k - 1, s + d), lambda k: k % 2 == 0) for d in (1, 0, -1)
     ]
 
     def hop_routes(hop):
@@ -337,15 +345,14 @@
         ahead = send(guess_pairs[0], earlier)
         inv_low, inv_high = send(inverses, right_one), send(inverses, left_one)
         right = adjoint_source[3] + column(masses) * (4.0 * ahead[0] - ahead[1])
-        coarse = inverses[4]
-        coarse_low2, coarse_high2 = send(coarse, right_two), send(coarse, left_two)
-        inv_five = [coarse_low2, inv_low[4], coarse, inv_high[4], coarse_high2]
-        inv_three = send(jnp.stack([inv_low[4], coarse, inv_high[4]]), even_to_odd)
-
         previous, total = ahead[0], None
         adjoints = [None] * 4
         for n in (3, 2, 1, 0):
-            low, high = send(right, right_one), send(right, left_one)
+            if n == 2:
+                low, high = send(more[0], right_one), send(more[1], left_one)
+                inv_five = [low[FIELDS:], inv_low[4], inverses[4], inv_high[4], high[FIELDS:]]
+            else:
+                low, high = send(right, right_one), send(right, left_one)
             source = adjoint_source[n - 1] if n else None
             x, total, *more = fine_step(
                 n, right, low, high, inverses, inv_low, inv_high, states[n], source, previous, total
@@ -354,15 +361,17 @@
             previous = x
             if n:
                 right = more[0]
-        z3, z6, z7 = more
+        z7, pack = more
         total = time_step * total
 
-        z_low, z_high = send(z3, right_one), send(z3, left_one)
-        pair_even = send(jnp.stack([adjoints[0], adjoints[1]]), even_to_odd)
-        payload = (z3, z6, z7, z6, z3)
-        z_five = [send(part, path) for part, path in zip(payload, relaxed_routes)]
+        z_low, z_high = send(z7, right_one), send(z7, left_one)
+        pack = send(pack, even_to_odd)
+        payload = (
+            jnp.concatenate([z_low[:3], z7[:6]]), z7, jnp.concatenate([z7[:6], z_high[:3]])
+        )
+        z_three = [send(part, path) for part, path in zip(payload, relaxed_routes)]
         v, offsets = offsets_step(
-            z_five, inv_five, inv_three, (z_low, z3, z_high), (adjoints[0], adjoints[1]), pair_even
+            z_three, inv_five, pack, (z_low, z7, z_high), (adjoints[0], adjoints[1])
         )
 
         place = (lax.axis_index("tm").astype(jnp.int32)).reshape(1)
@@ -377,13 +386,15 @@
         z_five, done, grad, hop = None, None, total, 0
         while hop < chips or stages:
             added = None
+            if hop and hop < chips:
+                z_five = [send(part, path) for part, path in zip(payload, hop_routes(hop))]
             if hop and stages:
-                added = (grad, send(grad, stages.pop(0)))
+                arrived = sum(part[0, 0, 0, 0] for part in z_five)
+                late = jnp.where(place[0] < 0, arrived, grad)
+                added = (grad, send(late, stages.pop(0)))
             if hop < chips:
-                if hop:
-                    z_five = [send(part, path) for part, path in zip(payload, hop_routes(hop))]
                 z3, z6, z7, done, *sums = chip_step(
-                    times - 1 - 2 * hop, place, z_five, inv_five, inv_three, v, offsets, done, added
+                    times - 1 - 2 * hop, place, z_five, inv_five, pack, v, offsets, done, added
                 )
                 payload = (z3, z6, z7, z6, z3)
                 if sums:

time: 216 us -> 216 us (level)
  the two profiles are of different devices: /device:TPU:41 before, /device:TPU:21 now
where the time goes in v2:
time: 216 us; the launch traced here: 215 us
  waiting for transfers between devices  99.5 us (46%)
  starting transfers between devices  81.7 us (38%)
  between operations  14.7 us (7%)
  local copies, waits for them, and re-layouts  11.1 us (5%)
  Pallas kernels  4.85 us (2%)
  other arithmetic  2.85 us (1%)
    ppermute x58, waiting for transfers between devices, send(): return lax.ppermute(value, AXES, pairs)  99.5 us
    ppermute x58, starting transfers between devices, send(): return lax.ppermute(value, AXES, pairs)  81.7 us
    slice x20, local copies, waits for them, and re-layouts, on_device(): arrived = sum((part[0, 0, 0, 0] for part in z_five))  10.5 us
  transfers between devices with their start and end apart: 58, of which 15 were waited for; matrix products, arithmetic and copies ran while one was open for 4% of the time, Pallas kernels for 1%

profile of v2, /device:TPU:21, one launch (start us, length us, event | category | flops | bytes accessed | tf_op | source)
XLA Modules:
  0.0 214.7 jit_solution(14945749497807086351)
XLA Ops:
  2.6 2.8 %collective-permute-start.3 = (f32[5,4,4,8,128]{4,3,2,1,0:T(8,128)S(1)}, f32[5,4,4,8,128]{4,3,2,1,0:T(8,128)S(1)}, u32[]{:S(2)}, u32[]{:S(2)}) collective-permute-start(f32[5,4,4,8,128]{4,3,2,1,0:T(8,128)S(1)} %get-tuple-element.100.refs_3_), channel_id=1, source_target_pairs={{0,1},{1,2},{2,3},{3,4},{4,5},{5,6},{6,7},{7,8},{8,9},{9,10},{10,1... | collective-permute-start | bytes 983048 | tf_op jit(solution)/shard_map/ppermute | solution.py:313
  5.4 2.5 %collective-permute-start.4 = (f32[5,4,4,8,128]{4,3,2,1,0:T(8,128)S(1)}, f32[5,4,4,8,128]{4,3,2,1,0:T(8,128)S(1)}, u32[]{:S(2)}, u32[]{:S(2)}) collective-permute-start(f32[5,4,4,8,128]{4,3,2,1,0:T(8,128)S(1)} %get-tuple-element.100.refs_3_), channel_id=1, source_target_pairs={{1,0},{2,1},{3,2},{4,3},{5,4},{6,5},{7,6},{8,7},{9,8},{10,9},{11,1... | collective-permute-start | bytes 983048 | tf_op jit(solution)/shard_map/ppermute | solution.py:313
  7.9 3.1 %collective-permute-start = (f32[2,4,4,8,128]{4,3,2,1,0:T(8,128)S(1)}, f32[2,4,4,8,128]{4,3,2,1,0:T(8,128)S(1)}, u32[]{:S(2)}, u32[]{:S(2)}) collective-permute-start(f32[2,4,4,8,128]{4,3,2,1,0:T(8,128)S(1)} %bitcast.73), channel_id=1, source_target_pairs={{32,0},{33,1},{34,2},{35,3},{36,4},{37,5},{38,6},{39,7},{40,8},{41... | collective-permute-start | bytes 393224 | tf_op jit(solution)/shard_map/ppermute | solution.py:313
  11.1 4.9 %collective-permute-done = f32[2,4,4,8,128]{4,3,2,1,0:T(8,128)S(1)} collective-permute-done((f32[2,4,4,8,128]{4,3,2,1,0:T(8,128)S(1)}, f32[2,4,4,8,128]{4,3,2,1,0:T(8,128)S(1)}, u32[]{:S(2)}, u32[]{:S(2)}) %collective-permute-start) | collective-permute-done | bytes 131104 | tf_op jit(solution)/shard_map/ppermute | solution.py:313
  16.0 2.8 %collective-permute-start.1 = (f32[4,4,8,128]{3,2,1,0:T(8,128)S(1)}, f32[4,4,8,128]{3,2,1,0:T(8,128)S(1)}, u32[]{:S(2)}, u32[]{:S(2)}) collective-permute-start(f32[4,4,8,128]{3,2,1,0:T(8,128)S(1)} %fusion.18.refs_0_), channel_id=1, source_target_pairs={{0,1},{1,2},{2,3},{3,4},{4,5},{5,6},{6,7},{7,8},{8,9},{9,10},{10,1... | collective-permute-start | bytes 196616 | tf_op jit(solution)/shard_map/ppermute | solution.py:313
  18.9 2.5 %collective-permute-start.2 = (f32[4,4,8,128]{3,2,1,0:T(8,128)S(1)}, f32[4,4,8,128]{3,2,1,0:T(8,128)S(1)}, u32[]{:S(2)}, u32[]{:S(2)}) collective-permute-start(f32[4,4,8,128]{3,2,1,0:T(8,128)S(1)} %fusion.18.refs_0_), channel_id=1, source_target_pairs={{1,0},{2,1},{3,2},{4,3},{5,4},{6,5},{7,6},{8,7},{9,8},{10,9},{11,1... | collective-permute-start | bytes 196616 | tf_op jit(solution)/shard_map/ppermute | solution.py:313
  21.3 4.1 %collective-permute-done.2.refs_2_ = f32[4,4,8,128]{3,2,1,0:T(8,128)S(1)} collective-permute-done((f32[4,4,8,128]{3,2,1,0:T(8,128)S(1)}, f32[4,4,8,128]{3,2,1,0:T(8,128)S(1)}, u32[]{:S(2)}, u32[]{:S(2)}) %collective-permute-start.2) | collective-permute-done | bytes 65568 | tf_op jit(solution)/shard_map/ppermute | solution.py:313
  25.8 5.5 %collective-permute-start.5 = (f32[8,4,8,128]{3,2,1,0:T(8,128)S(1)}, f32[8,4,8,128]{3,2,1,0:T(8,128)S(1)}, u32[]{:S(2)}, u32[]{:S(2)}) collective-permute-start(f32[8,4,8,128]{3,2,1,0:T(8,128)S(1)} %get-tuple-element.51.refs_0_), channel_id=1, source_target_pairs={{0,1},{1,2},{2,3},{3,4},{4,5},{5,6},{6,7},{7,8},{8,9},{9,10},{10,1... | collective-permute-start | bytes 393224 | tf_op jit(solution)/shard_map/ppermute | solution.py:313
  31.3 1.9 collective-permute-start.6
  33.3 4.1 %collective-permute-done.6.refs_2_ = f32[8,4,8,128]{3,2,1,0:T(8,128)S(1)} collective-permute-done((f32[8,4,8,128]{3,2,1,0:T(8,128)S(1)}, f32[8,4,8,128]{3,2,1,0:T(8,128)S(1)}, u32[]{:S(2)}, u32[]{:S(2)}) %collective-permute-start.6) | collective-permute-done | bytes 131104 | tf_op jit(solution)/shard_map/ppermute | solution.py:313
  37.7 3.8 %collective-permute-start.7 = (f32[4,4,8,128]{3,2,1,0:T(8,128)S(1)}, f32[4,4,8,128]{3,2,1,0:T(8,128)S(1)}, u32[]{:S(2)}, u32[]{:S(2)}) collective-permute-start(f32[4,4,8,128]{3,2,1,0:T(8,128)S(1)} %get-tuple-element.55.refs_0_), channel_id=1, source_target_pairs={{0,1},{1,2},{2,3},{3,4},{4,5},{5,6},{6,7},{7,8},{8,9},{9,10},{10,1... | collective-permute-start | bytes 196616 | tf_op jit(solution)/shard_map/ppermute | solution.py:313
  41.5 1.9 collective-permute-start.8
  43.7 3.7 %collective-permute-done.8.refs_2_ = f32[4,4,8,128]{3,2,1,0:T(8,128)S(1)} collective-permute-done((f32[4,4,8,128]{3,2,1,0:T(8,128)S(1)}, f32[4,4,8,128]{3,2,1,0:T(8,128)S(1)}, u32[]{:S(2)}, u32[]{:S(2)}) %collective-permute-start.8) | collective-permute-done | bytes 65568 | tf_op jit(solution)/shard_map/ppermute | solution.py:313
  47.9 4.6 %collective-permute-start.9 = (f32[4,4,8,128]{3,2,1,0:T(8,128)S(1)}, f32[4,4,8,128]{3,2,1,0:T(8,128)S(1)}, u32[]{:S(2)}, u32[]{:S(2)}) collective-permute-start(f32[4,4,8,128]{3,2,1,0:T(8,128)S(1)} %get-tuple-element.58.refs_0_), channel_id=1, source_target_pairs={{0,1},{1,2},{2,3},{3,4},{4,5},{5,6},{6,7},{7,8},{8,9},{9,10},{10,1... | collective-permute-start | bytes 196616 | tf_op jit(solution)/shard_map/ppermute | solution.py:313
  52.4 1.9 collective-permute-start.10
  54.4 3.8 %collective-permute-done.10.refs_2_ = f32[4,4,8,128]{3,2,1,0:T(8,128)S(1)} collective-permute-done((f32[4,4,8,128]{3,2,1,0:T(8,128)S(1)}, f32[4,4,8,128]{3,2,1,0:T(8,128)S(1)}, u32[]{:S(2)}, u32[]{:S(2)}) %collective-permute-start.10) | collective-permute-done | bytes 65568 | tf_op jit(solution)/shard_map/ppermute | solution.py:313
  58.6 1.9 collective-permute-start.15
  60.6 5.5 %collective-permute-start.12 = (f32[7,4,8,128]{3,2,1,0:T(8,128)S(1)}, f32[7,4,8,128]{3,2,1,0:T(8,128)S(1)}, u32[]{:S(2)}, u32[]{:S(2)}) collective-permute-start(f32[7,4,8,128]{3,2,1,0:T(8,128)S(1)} %get-tuple-element.62.refs_10_), channel_id=1, source_target_pairs={{0,1},{1,2},{2,3},{3,4},{4,5},{5,6},{6,7},{7,8},{8,9},{9,10},{10,1... | collective-permute-start | bytes 344072 | tf_op jit(solution)/shard_map/ppermute | solution.py:313
  68.7 1.3 collective-permute-start.13
  70.0 1.3 collective-permute-start.16
  71.4 4.1 %collective-permute-done.14.refs_1_ = f32[7,4,8,128]{3,2,1,0:T(8,128)S(1)} collective-permute-done((f32[7,4,8,128]{3,2,1,0:T(8,128)S(1)}, f32[7,4,8,128]{3,2,1,0:T(8,128)S(1)}, u32[]{:S(2)}, u32[]{:S(2)}) %collective-permute-start.14) | collective-permute-done | bytes 114720 | tf_op jit(solution)/shard_map/ppermute | solution.py:313
  75.5 1.9 collective-permute-done.13.refs_0_
  77.4 6.0 %collective-permute-done.16.refs_2_ = f32[9,4,8,128]{3,2,1,0:T(8,128)S(1)} collective-permute-done((f32[9,4,8,128]{3,2,1,0:T(8,128)S(1)}, f32[9,4,8,128]{3,2,1,0:T(8,128)S(1)}, u32[]{:S(2)}, u32[]{:S(2)}) %collective-permute-start.16) | collective-permute-done | bytes 147488 | tf_op jit(solution)/shard_map/ppermute | solution.py:313
  93.8 1.3 collective-permute-start.22
  106.1 1.3 collective-permute-start.31
  107.4 1.3 collective-permute-start.30
  108.7 1.3 collective-permute-start.32
  112.6 26.8 %collective-permute-done.29.refs_1_ = f32[3,4,8,128]{3,2,1,0:T(8,128)S(1)} collective-permute-done((f32[3,4,8,128]{3,2,1,0:T(8,128)S(1)}, f32[3,4,8,128]{3,2,1,0:T(8,128)S(1)}, u32[]{:S(2)}, u32[]{:S(2)}) %collective-permute-start.29) | collective-permute-done | bytes 49184 | tf_op jit(solution)/shard_map/ppermute | solution.py:313
  139.9 5.1 %collective-permute-done.33.refs_5_ = f32[3,4,8,128]{3,2,1,0:T(8,128)S(1)} collective-permute-done((f32[3,4,8,128]{3,2,1,0:T(8,128)S(1)}, f32[3,4,8,128]{3,2,1,0:T(8,128)S(1)}, u32[]{:S(2)}, u32[]{:S(2)}) %collective-permute-start.33) | collective-permute-done | bytes 49184 | tf_op jit(solution)/shard_map/ppermute | solution.py:313
  174.8 33.0 %collective-permute-done.51.refs_1_ = f32[3,4,8,128]{3,2,1,0:T(8,128)S(1)} collective-permute-done((f32[3,4,8,128]{3,2,1,0:T(8,128)S(1)}, f32[3,4,8,128]{3,2,1,0:T(8,128)S(1)}, u32[]{:S(2)}, u32[]{:S(2)}) %collective-permute-start.51) | collective-permute-done | bytes 49184 | tf_op jit(solution)/shard_map/ppermute | solution.py:313
  209.6 1.7 shard_map.215
  211.3 1.7 collective-permute-start.56
  (153 shorter events, 50.6 us)
Async XLA Ops:
  2.6 22.9 %collective-permute-start.3 = (f32[5,4,4,8,128]{4,3,2,1,0:T(8,128)S(1)}, f32[5,4,4,8,128]{4,3,2,1,0:T(8,128)S(1)}, u32[]{:S(2)}, u32[]{:S(2)}) collective-permute-start(f32[5,4,4,8,128]{4,3,2,1,0:T(8,128)S(1)} %get-tuple-element.100.refs_3_), channel_id=1, source_target_pairs={{0,1},{1,2},{2,3},{3,4},{4,5},{5,6},{6,7},{7,8},{8,9},{9,10},{10,1... | collective-permute-start | bytes 983048 | tf_op jit(solution)/shard_map/ppermute | solution.py:313
  5.4 20.0 %collective-permute-start.4 = (f32[5,4,4,8,128]{4,3,2,1,0:T(8,128)S(1)}, f32[5,4,4,8,128]{4,3,2,1,0:T(8,128)S(1)}, u32[]{:S(2)}, u32[]{:S(2)}) collective-permute-start(f32[5,4,4,8,128]{4,3,2,1,0:T(8,128)S(1)} %get-tuple-element.100.refs_3_), channel_id=1, source_target_pairs={{1,0},{2,1},{3,2},{4,3},{5,4},{6,5},{7,6},{8,7},{9,8},{10,9},{11,1... | collective-permute-start | bytes 983048 | tf_op jit(solution)/shard_map/ppermute | solution.py:313
  7.9 8.1 %collective-permute-start = (f32[2,4,4,8,128]{4,3,2,1,0:T(8,128)S(1)}, f32[2,4,4,8,128]{4,3,2,1,0:T(8,128)S(1)}, u32[]{:S(2)}, u32[]{:S(2)}) collective-permute-start(f32[2,4,4,8,128]{4,3,2,1,0:T(8,128)S(1)} %bitcast.73), channel_id=1, source_target_pairs={{32,0},{33,1},{34,2},{35,3},{36,4},{37,5},{38,6},{39,7},{40,8},{41... | collective-permute-start | bytes 393224 | tf_op jit(solution)/shard_map/ppermute | solution.py:313
  16.0 5.3 %collective-permute-start.1 = (f32[4,4,8,128]{3,2,1,0:T(8,128)S(1)}, f32[4,4,8,128]{3,2,1,0:T(8,128)S(1)}, u32[]{:S(2)}, u32[]{:S(2)}) collective-permute-start(f32[4,4,8,128]{3,2,1,0:T(8,128)S(1)} %fusion.18.refs_0_), channel_id=1, source_target_pairs={{0,1},{1,2},{2,3},{3,4},{4,5},{5,6},{6,7},{7,8},{8,9},{9,10},{10,1... | collective-permute-start | bytes 196616 | tf_op jit(solution)/shard_map/ppermute | solution.py:313
  18.9 6.6 %collective-permute-start.2 = (f32[4,4,8,128]{3,2,1,0:T(8,128)S(1)}, f32[4,4,8,128]{3,2,1,0:T(8,128)S(1)}, u32[]{:S(2)}, u32[]{:S(2)}) collective-permute-start(f32[4,4,8,128]{3,2,1,0:T(8,128)S(1)} %fusion.18.refs_0_), channel_id=1, source_target_pairs={{1,0},{2,1},{3,2},{4,3},{5,4},{6,5},{7,6},{8,7},{9,8},{10,9},{11,1... | collective-permute-start | bytes 196616 | tf_op jit(solution)/shard_map/ppermute | solution.py:313
  25.8 7.4 %collective-permute-start.5 = (f32[8,4,8,128]{3,2,1,0:T(8,128)S(1)}, f32[8,4,8,128]{3,2,1,0:T(8,128)S(1)}, u32[]{:S(2)}, u32[]{:S(2)}) collective-permute-start(f32[8,4,8,128]{3,2,1,0:T(8,128)S(1)} %get-tuple-element.51.refs_0_), channel_id=1, source_target_pairs={{0,1},{1,2},{2,3},{3,4},{4,5},{5,6},{6,7},{7,8},{8,9},{9,10},{10,1... | collective-permute-start | bytes 393224 | tf_op jit(solution)/shard_map/ppermute | solution.py:313
  31.3 6.0 %collective-permute-start.6 = (f32[8,4,8,128]{3,2,1,0:T(8,128)S(1)}, f32[8,4,8,128]{3,2,1,0:T(8,128)S(1)}, u32[]{:S(2)}, u32[]{:S(2)}) collective-permute-start(f32[8,4,8,128]{3,2,1,0:T(8,128)S(1)} %get-tuple-element.52), channel_id=1, source_target_pairs={{1,0},{2,1},{3,2},{4,3},{5,4},{6,5},{7,6},{8,7},{9,8},{10,9},{11,1... | collective-permute-start | bytes 393224 | tf_op jit(solution)/shard_map/ppermute | solution.py:313
  37.7 6.0 %collective-permute-start.7 = (f32[4,4,8,128]{3,2,1,0:T(8,128)S(1)}, f32[4,4,8,128]{3,2,1,0:T(8,128)S(1)}, u32[]{:S(2)}, u32[]{:S(2)}) collective-permute-start(f32[4,4,8,128]{3,2,1,0:T(8,128)S(1)} %get-tuple-element.55.refs_0_), channel_id=1, source_target_pairs={{0,1},{1,2},{2,3},{3,4},{4,5},{5,6},{6,7},{7,8},{8,9},{9,10},{10,1... | collective-permute-start | bytes 196616 | tf_op jit(solution)/shard_map/ppermute | solution.py:313
  41.5 6.0 %collective-permute-start.8 = (f32[4,4,8,128]{3,2,1,0:T(8,128)S(1)}, f32[4,4,8,128]{3,2,1,0:T(8,128)S(1)}, u32[]{:S(2)}, u32[]{:S(2)}) collective-permute-start(f32[4,4,8,128]{3,2,1,0:T(8,128)S(1)} %get-tuple-element.55.refs_0_), channel_id=1, source_target_pairs={{1,0},{2,1},{3,2},{4,3},{5,4},{6,5},{7,6},{8,7},{9,8},{10,9},{11,1... | collective-permute-start | bytes 196616 | tf_op jit(solution)/shard_map/ppermute | solution.py:313
  47.9 6.5 %collective-permute-start.9 = (f32[4,4,8,128]{3,2,1,0:T(8,128)S(1)}, f32[4,4,8,128]{3,2,1,0:T(8,128)S(1)}, u32[]{:S(2)}, u32[]{:S(2)}) collective-permute-start(f32[4,4,8,128]{3,2,1,0:T(8,128)S(1)} %get-tuple-element.58.refs_0_), channel_id=1, source_target_pairs={{0,1},{1,2},{2,3},{3,4},{4,5},{5,6},{6,7},{7,8},{8,9},{9,10},{10,1... | collective-permute-start | bytes 196616 | tf_op jit(solution)/shard_map/ppermute | solution.py:313
  52.4 5.8 %collective-permute-start.10 = (f32[4,4,8,128]{3,2,1,0:T(8,128)S(1)}, f32[4,4,8,128]{3,2,1,0:T(8,128)S(1)}, u32[]{:S(2)}, u32[]{:S(2)}) collective-permute-start(f32[4,4,8,128]{3,2,1,0:T(8,128)S(1)} %get-tuple-element.58.refs_0_), channel_id=1, source_target_pairs={{1,0},{2,1},{3,2},{4,3},{5,4},{6,5},{7,6},{8,7},{9,8},{10,9},{11,1... | collective-permute-start | bytes 196616 | tf_op jit(solution)/shard_map/ppermute | solution.py:313
  58.6 10.0 %collective-permute-start.15 = (f32[7,4,8,128]{3,2,1,0:T(8,128)S(1)}, f32[7,4,8,128]{3,2,1,0:T(8,128)S(1)}, u32[]{:S(2)}, u32[]{:S(2)}) collective-permute-start(f32[7,4,8,128]{3,2,1,0:T(8,128)S(1)} %get-tuple-element.62.refs_10_), channel_id=1, source_target_pairs={{1,0},{2,1},{3,2},{4,3},{5,4},{6,5},{7,6},{8,7},{9,8},{10,9},{11,1... | collective-permute-start | bytes 344072 | tf_op jit(solution)/shard_map/ppermute | solution.py:313
  60.6 8.1 %collective-permute-start.12 = (f32[7,4,8,128]{3,2,1,0:T(8,128)S(1)}, f32[7,4,8,128]{3,2,1,0:T(8,128)S(1)}, u32[]{:S(2)}, u32[]{:S(2)}) collective-permute-start(f32[7,4,8,128]{3,2,1,0:T(8,128)S(1)} %get-tuple-element.62.refs_10_), channel_id=1, source_target_pairs={{0,1},{1,2},{2,3},{3,4},{4,5},{5,6},{6,7},{7,8},{8,9},{9,10},{10,1... | collective-permute-start | bytes 344072 | tf_op jit(solution)/shard_map/ppermute | solution.py:313
  66.1 9.4 %collective-permute-start.14 = (f32[7,4,8,128]{3,2,1,0:T(8,128)S(1)}, f32[7,4,8,128]{3,2,1,0:T(8,128)S(1)}, u32[]{:S(2)}, u32[]{:S(2)}) collective-permute-start(f32[7,4,8,128]{3,2,1,0:T(8,128)S(1)} %get-tuple-element.62.refs_10_), channel_id=1, source_target_pairs={{64,32},{65,33},{66,34},{67,35},{68,36},{69,37},{70,38},{71,39},{7... | collective-permute-start | bytes 344072 | tf_op jit(solution)/shard_map/ppermute | solution.py:313
  67.4 16.0 %collective-permute-start.11 = (f32[5,4,4,8,128]{4,3,2,1,0:T(8,128)S(1)}, f32[5,4,4,8,128]{4,3,2,1,0:T(8,128)S(1)}, u32[]{:S(2)}, u32[]{:S(2)}) collective-permute-start(f32[5,4,4,8,128]{4,3,2,1,0:T(8,128)S(1)} %get-tuple-element.61), channel_id=1, source_target_pairs={{0,32},{1,33},{2,34},{3,35},{4,36},{5,37},{6,38},{7,39},{8,40},{9,... | collective-permute-start | bytes 983048 | tf_op jit(solution)/shard_map/ppermute | solution.py:313
  68.7 8.6 %collective-permute-start.13 = (f32[9,4,8,128]{3,2,1,0:T(8,128)S(1)}, f32[9,4,8,128]{3,2,1,0:T(8,128)S(1)}, u32[]{:S(2)}, u32[]{:S(2)}) collective-permute-start(f32[9,4,8,128]{3,2,1,0:T(8,128)S(1)} %get-tuple-element.111), channel_id=1, source_target_pairs={{64,33},{65,34},{66,35},{67,36},{68,37},{69,38},{70,39},{71,40},{7... | collective-permute-start | bytes 442376 | tf_op jit(solution)/shard_map/ppermute | solution.py:313
  70.0 13.4 %collective-permute-start.16 = (f32[9,4,8,128]{3,2,1,0:T(8,128)S(1)}, f32[9,4,8,128]{3,2,1,0:T(8,128)S(1)}, u32[]{:S(2)}, u32[]{:S(2)}) collective-permute-start(f32[9,4,8,128]{3,2,1,0:T(8,128)S(1)} %get-tuple-element.110), channel_id=1, source_target_pairs={{65,32},{66,33},{67,34},{68,35},{69,36},{70,37},{71,38},{72,39},{7... | collective-permute-start | bytes 442376 | tf_op jit(solution)/shard_map/ppermute | solution.py:313
  84.5 6.8 %collective-permute-start.19 = (f32[7,4,8,128]{3,2,1,0:T(8,128)S(1)}, f32[7,4,8,128]{3,2,1,0:T(8,128)S(1)}, u32[]{:S(2)}, u32[]{:S(2)}) collective-permute-start(f32[7,4,8,128]{3,2,1,0:T(8,128)S(1)} %get-tuple-element.68), channel_id=1, source_target_pairs={{224,160},{225,161},{226,162},{227,163},{228,164},{229,165},{230,1... | collective-permute-start | bytes 344072 | tf_op jit(solution)/shard_map/ppermute | solution.py:313
  96.0 6.8 %collective-permute-start.25 = (f32[7,4,8,128]{3,2,1,0:T(8,128)S(1)}, f32[7,4,8,128]{3,2,1,0:T(8,128)S(1)}, u32[]{:S(2)}, u32[]{:S(2)}) collective-permute-start(f32[7,4,8,128]{3,2,1,0:T(8,128)S(1)} %get-tuple-element.73), channel_id=1, source_target_pairs={{160,96},{161,97},{162,98},{163,99},{164,100},{165,101},{166,102},... | collective-permute-start | bytes 344072 | tf_op jit(solution)/shard_map/ppermute | solution.py:313
  106.1 41.8 %collective-permute-start.31 = (f32[7,4,8,128]{3,2,1,0:T(8,128)S(1)}, f32[7,4,8,128]{3,2,1,0:T(8,128)S(1)}, u32[]{:S(2)}, u32[]{:S(2)}) collective-permute-start(f32[7,4,8,128]{3,2,1,0:T(8,128)S(1)} %get-tuple-element.78), channel_id=1, source_target_pairs={{96,32},{97,33},{98,34},{99,35},{100,36},{101,37},{102,38},{103,39... | collective-permute-start | bytes 344072 | tf_op jit(solution)/shard_map/ppermute | solution.py:313
  107.4 38.1 %collective-permute-start.30 = (f32[6,4,8,128]{3,2,1,0:T(8,128)S(1)}, f32[6,4,8,128]{3,2,1,0:T(8,128)S(1)}, u32[]{:S(2)}, u32[]{:S(2)}) collective-permute-start(f32[6,4,8,128]{3,2,1,0:T(8,128)S(1)} %get-tuple-element.77), channel_id=1, source_target_pairs={{96,33},{97,34},{98,35},{99,36},{100,37},{101,38},{102,39},{103,40... | collective-permute-start | bytes 294920 | tf_op jit(solution)/shard_map/ppermute | solution.py:313
  108.7 38.6 %collective-permute-start.32 = (f32[6,4,8,128]{3,2,1,0:T(8,128)S(1)}, f32[6,4,8,128]{3,2,1,0:T(8,128)S(1)}, u32[]{:S(2)}, u32[]{:S(2)}) collective-permute-start(f32[6,4,8,128]{3,2,1,0:T(8,128)S(1)} %get-tuple-element.77), channel_id=1, source_target_pairs={{97,32},{98,33},{99,34},{100,35},{101,36},{102,37},{103,38},{104,3... | collective-permute-start | bytes 294920 | tf_op jit(solution)/shard_map/ppermute | solution.py:313
  110.0 29.4 %collective-permute-start.29 = (f32[3,4,8,128]{3,2,1,0:T(8,128)S(1)}, f32[3,4,8,128]{3,2,1,0:T(8,128)S(1)}, u32[]{:S(2)}, u32[]{:S(2)}) collective-permute-start(f32[3,4,8,128]{3,2,1,0:T(8,128)S(1)} %get-tuple-element.76), channel_id=1, source_target_pairs={{96,34},{97,35},{98,36},{99,37},{100,38},{101,39},{102,40},{103,41... | collective-permute-start | bytes 147464 | tf_op jit(solution)/shard_map/ppermute | solution.py:313
  111.3 33.7 %collective-permute-start.33 = (f32[3,4,8,128]{3,2,1,0:T(8,128)S(1)}, f32[3,4,8,128]{3,2,1,0:T(8,128)S(1)}, u32[]{:S(2)}, u32[]{:S(2)}) collective-permute-start(f32[3,4,8,128]{3,2,1,0:T(8,128)S(1)} %get-tuple-element.76), channel_id=1, source_target_pairs={{98,32},{99,33},{100,34},{101,35},{102,36},{103,37},{104,38},{105,... | collective-permute-start | bytes 147464 | tf_op jit(solution)/shard_map/ppermute | solution.py:313
  151.1 6.8 %collective-permute-start.37 = (f32[7,4,8,128]{3,2,1,0:T(8,128)S(1)}, f32[7,4,8,128]{3,2,1,0:T(8,128)S(1)}, u32[]{:S(2)}, u32[]{:S(2)}) collective-permute-start(f32[7,4,8,128]{3,2,1,0:T(8,128)S(1)} %get-tuple-element.83), channel_id=1, source_target_pairs={{288,224},{289,225},{290,226},{291,227},{292,228},{293,229},{294,2... | collective-permute-start | bytes 344072 | tf_op jit(solution)/shard_map/ppermute | solution.py:313
  152.5 4.9 %collective-permute-start.38 = (f32[6,4,8,128]{3,2,1,0:T(8,128)S(1)}, f32[6,4,8,128]{3,2,1,0:T(8,128)S(1)}, u32[]{:S(2)}, u32[]{:S(2)}) collective-permute-start(f32[6,4,8,128]{3,2,1,0:T(8,128)S(1)} %get-tuple-element.82), channel_id=1, source_target_pairs={{289,224},{290,225},{291,226},{292,227},{293,228},{294,229},{295,2... | collective-permute-start | bytes 294920 | tf_op jit(solution)/shard_map/ppermute | solution.py:313
  168.3 41.2 %collective-permute-start.53 = (f32[7,4,8,128]{3,2,1,0:T(8,128)S(1)}, f32[7,4,8,128]{3,2,1,0:T(8,128)S(1)}, u32[]{:S(2)}, u32[]{:S(2)}) collective-permute-start(f32[7,4,8,128]{3,2,1,0:T(8,128)S(1)} %get-tuple-element.96), channel_id=1, source_target_pairs={{96,32},{97,33},{98,34},{99,35},{100,36},{101,37},{102,38},{103,39... | collective-permute-start | bytes 344072 | tf_op jit(solution)/shard_map/ppermute | solution.py:313
  169.6 39.9 %collective-permute-start.52 = (f32[6,4,8,128]{3,2,1,0:T(8,128)S(1)}, f32[6,4,8,128]{3,2,1,0:T(8,128)S(1)}, u32[]{:S(2)}, u32[]{:S(2)}) collective-permute-start(f32[6,4,8,128]{3,2,1,0:T(8,128)S(1)} %get-tuple-element.95), channel_id=1, source_target_pairs={{96,33},{97,34},{98,35},{99,36},{100,37},{101,38},{102,39},{103,40... | collective-permute-start | bytes 294920 | tf_op jit(solution)/shard_map/ppermute | solution.py:313
  170.9 38.6 %collective-permute-start.54 = (f32[6,4,8,128]{3,2,1,0:T(8,128)S(1)}, f32[6,4,8,128]{3,2,1,0:T(8,128)S(1)}, u32[]{:S(2)}, u32[]{:S(2)}) collective-permute-start(f32[6,4,8,128]{3,2,1,0:T(8,128)S(1)} %get-tuple-element.95), channel_id=1, source_target_pairs={{97,32},{98,33},{99,34},{100,35},{101,36},{102,37},{103,38},{104,3... | collective-permute-start | bytes 294920 | tf_op jit(solution)/shard_map/ppermute | solution.py:313
  172.2 35.6 %collective-permute-start.51 = (f32[3,4,8,128]{3,2,1,0:T(8,128)S(1)}, f32[3,4,8,128]{3,2,1,0:T(8,128)S(1)}, u32[]{:S(2)}, u32[]{:S(2)}) collective-permute-start(f32[3,4,8,128]{3,2,1,0:T(8,128)S(1)} %get-tuple-element.94), channel_id=1, source_target_pairs={{96,34},{97,35},{98,36},{99,37},{100,38},{101,39},{102,40},{103,41... | collective-permute-start | bytes 147464 | tf_op jit(solution)/shard_map/ppermute | solution.py:313
  173.5 36.0 %collective-permute-start.55 = (f32[3,4,8,128]{3,2,1,0:T(8,128)S(1)}, f32[3,4,8,128]{3,2,1,0:T(8,128)S(1)}, u32[]{:S(2)}, u32[]{:S(2)}) collective-permute-start(f32[3,4,8,128]{3,2,1,0:T(8,128)S(1)} %get-tuple-element.94), channel_id=1, source_target_pairs={{98,32},{99,33},{100,34},{101,35},{102,36},{103,37},{104,38},{105,... | collective-permute-start | bytes 147464 | tf_op jit(solution)/shard_map/ppermute | solution.py:313
  207.9 5.1 %collective-permute-start.57 = (f32[4,4,8,128]{3,2,1,0:T(8,128)S(1)}, f32[4,4,8,128]{3,2,1,0:T(8,128)S(1)}, u32[]{:S(2)}, u32[]{:S(2)}) collective-permute-start(f32[4,4,8,128]{3,2,1,0:T(8,128)S(1)} %get-tuple-element.99), channel_id=1, source_target_pairs={{0,32},{1,33},{2,34},{3,35},{4,36},{5,37},{6,38},{7,39},{8,40},{9,... | collective-permute-start | bytes 196616 | tf_op jit(solution)/shard_map/ppermute | solution.py:313
  (32 other events, 81.5 us)

commit v3 on v2

--- a/solution.py
+++ b/solution.py
@@ -123,24 +123,22 @@
     )(*operands)
 
 
-def fine_step(step, right, right_low, right_high, inv, inv_low, inv_high, states, source, previous, total):
-    first, last = total is None, step == 0
+def fine_step(step, own, low, high, states, previous, total, source=None, factor=None, coarse=None):
+    first, second, last = total is None, step == 2, step == 0
 
     def body(*refs):
         refs = list(refs)
-        r0, rl, rh, i0, il, ih, u, prev = refs[:8]
-        rest = refs[8:]
-        src = None if last else rest.pop(0)
-        old = None if first else rest.pop(0)
-        out, grad = rest[:2]
-        more = rest[2:-3]
-        scratch = rest[-3:]
+        r0, rl, rh, u, prev = [refs.pop(0) for _ in range(5)]
+        src, inv = (None, None) if last else [refs.pop(0) for _ in range(2)]
+        factors = [refs.pop(0) for _ in range(3)] if last else None
+        old = None if first else refs.pop(0)
+        out, grad = refs[:2]
+        more, scratch = refs[2:-3], refs[-3:]
         stencil = Stencil()
-        right_at = layers_of([rl, r0, rh])
-        pieces = [il, i0, ih]
+        pieces = [rl, r0, rh]
 
         def inverse(f, layer):
-            return pieces[layer // WIDTH][step, f, layer % WIDTH]
+            return pieces[layer // WIDTH][FIELDS + f, layer % WIDTH]
 
         def emit(layer, x):
             for f in range(FIELDS):
@@ -151,9 +149,8 @@
                     r = src[f, layer]
                     if masses[f]:
                         r = r + (4.0 * x[f] - prev[f, layer])
-                    more[0][f, layer] = r
-                    if first:
-                        more[1][f, layer] = r
+                    for part in more:
+                        part[f, layer] = r
                 else:
                     z7, pack = more
                     z7[3 + f, layer] = x[f]
@@ -162,19 +159,22 @@
                     if masses[f]:
                         z7[f, layer] = x[f] - 0.25 * prev[f, layer]
 
-        if first:
-            more[0][FIELDS:] = il[4]
-            more[1][FIELDS:] = ih[4]
         if last:
             for place in range(3):
-                more[1][2 + place] = pieces[place][4]
-        solve(stencil, right_at, inverse, 3 * WIDTH, scratch, emit)
-
-    operands = [right, right_low, right_high, inv, inv_low, inv_high, states, previous]
-    operands += [] if last else [source]
+                more[1][2 + place] = factors[place][2 * FIELDS :]
+        else:
+            for part in more:
+                part[FIELDS : 2 * FIELDS] = inv[...]
+        if first:
+            more[0][2 * FIELDS :] = rl[2 * FIELDS :]
+            more[1][2 * FIELDS :] = rh[2 * FIELDS :]
+        solve(stencil, layers_of(pieces), inverse, 3 * WIDTH, scratch, emit)
+
+    operands = [own, low, high, states, previous]
+    operands += list(coarse) if last else [source, factor]
     operands += [] if first else [total]
     outs = [SLAB, SLAB]
-    outs += [carry(7), (5,) + SLAB] if last else [carry(8)] * 2 if first else [SLAB]
+    outs += [carry(7), (5,) + SLAB] if last else [carry(12)] * 2 if first else [carry(8)]
     return call(body, outs, *operands, layers=3 * WIDTH, flops=28 * 4 * 1024 * 20)
 
 
@@ -338,29 +338,25 @@
 
     def on_device(forward_states, adjoint_source, source_gain, guess_pairs):
         states = forward_states.astype(jnp.float32)
-        inverses = jnp.stack(
-            [1.0 / make_diagonal(states[n], source_gain, fine_rate) for n in range(4)]
-            + [1.0 / make_diagonal(states[0], source_gain, coarse_rate)]
-        )
         ahead = send(guess_pairs[0], earlier)
-        inv_low, inv_high = send(inverses, right_one), send(inverses, left_one)
+        inverses = [1.0 / make_diagonal(states[n], source_gain, fine_rate) for n in range(4)]
+        coarse = 1.0 / make_diagonal(states[0], source_gain, coarse_rate)
         right = adjoint_source[3] + column(masses) * (4.0 * ahead[0] - ahead[1])
+        up = down = jnp.concatenate([right, inverses[3], coarse])
         previous, total = ahead[0], None
-        adjoints = [None] * 4
+        adjoints, exchanged = [None] * 4, []
         for n in (3, 2, 1, 0):
-            if n == 2:
-                low, high = send(more[0], right_one), send(more[1], left_one)
-                inv_five = [low[FIELDS:], inv_low[4], inverses[4], inv_high[4], high[FIELDS:]]
+            low, high = send(up, right_one), send(down, left_one)
+            exchanged.append((low, up, high))
+            if n:
+                rest = dict(source=adjoint_source[n - 1], factor=inverses[n - 1])
             else:
-                low, high = send(right, right_one), send(right, left_one)
-            source = adjoint_source[n - 1] if n else None
-            x, total, *more = fine_step(
-                n, right, low, high, inverses, inv_low, inv_high, states[n], source, previous, total
-            )
-            adjoints[n] = x
-            previous = x
-            if n:
-                right = more[0]
+                rest = dict(coarse=exchanged[0])
+            x, total, *more = fine_step(n, up, low, high, states[n], previous, total, **rest)
+            adjoints[n] = previous = x
+            up, down = more[0], more[-1]
+        (low, own, high), (low_two, _, high_two) = exchanged[:2]
+        inv_five = [part[2 * FIELDS :] for part in (low_two, low, own, high, high_two)]
         z7, pack = more
         total = time_step * total
 
@@ -389,7 +385,7 @@
             if hop and hop < chips:
                 z_five = [send(part, path) for part, path in zip(payload, hop_routes(hop))]
             if hop and stages:
-                arrived = sum(part[0, 0, 0, 0] for part in z_five)
+                arrived = sum(part[:1] if part.shape[0] < 4 else part[:4] for part in z_five)
                 late = jnp.where(place[0] < 0, arrived, grad)
                 added = (grad, send(late, stages.pop(0)))
             if hop < chips:

time: 216 us -> 181 us (0.84)
  the two profiles are of different devices: /device:TPU:21 before, /device:TPU:25 now
where the time goes in v3:
time: 181 us; the launch traced here: 180 us
  waiting for transfers between devices  88.1 us (49%)
  starting transfers between devices  81.9 us (45%)
  Pallas kernels  4.68 us (3%)
  other arithmetic  2.58 us (1%)
    ppermute x56, waiting for transfers between devices, send(): return lax.ppermute(value, AXES, pairs)  88.1 us
    ppermute x56, starting transfers between devices, send(): return lax.ppermute(value, AXES, pairs)  81.9 us
  transfers between devices with their start and end apart: 56, of which 21 were waited for; matrix products, arithmetic and copies ran while one was open for 1% of the time, Pallas kernels for 1%

profile of v3, /device:TPU:25, one launch (start us, length us, event | category | flops | bytes accessed | tf_op | source)
XLA Modules:
  0.0 179.8 jit_solution(1956613868556976436)
XLA Ops:
  0.6 2.7 %collective-permute-start = (f32[2,4,4,8,128]{4,3,2,1,0:T(8,128)}, f32[2,4,4,8,128]{4,3,2,1,0:T(8,128)S(1)}, u32[]{:S(2)}, u32[]{:S(2)}) collective-permute-start(f32[2,4,4,8,128]{4,3,2,1,0:T(8,128)} %bitcast.64), channel_id=1, source_target_pairs={{32,0},{33,1},{34,2},{35,3},{36,4},{37,5},{38,6},{39,7},{40,8},{41... | collective-permute-start | bytes 393224 | tf_op jit(solution)/shard_map/ppermute | solution.py:313
  5.3 2.9 %collective-permute-done = f32[2,4,4,8,128]{4,3,2,1,0:T(8,128)S(1)} collective-permute-done((f32[2,4,4,8,128]{4,3,2,1,0:T(8,128)}, f32[2,4,4,8,128]{4,3,2,1,0:T(8,128)S(1)}, u32[]{:S(2)}, u32[]{:S(2)}) %collective-permute-start) | collective-permute-done | bytes 131104 | tf_op jit(solution)/shard_map/ppermute | solution.py:313
  8.3 3.1 %collective-permute-start.1 = (f32[12,4,8,128]{3,2,1,0:T(8,128)S(1)}, f32[12,4,8,128]{3,2,1,0:T(8,128)S(1)}, u32[]{:S(2)}, u32[]{:S(2)}) collective-permute-start(f32[12,4,8,128]{3,2,1,0:T(8,128)S(1)} %pad_maximum_fusion.refs_0_.refs_6_), channel_id=1, source_target_pairs={{0,1},{1,2},{2,3},{3,4},{4,5},{5,6},{6,7},{7,8},{8,9},{9,10},{10,1... | collective-permute-start | bytes 589832 | tf_op jit(solution)/shard_map/ppermute | solution.py:313
  11.4 4.3 %collective-permute-start.2 = (f32[12,4,8,128]{3,2,1,0:T(8,128)S(1)}, f32[12,4,8,128]{3,2,1,0:T(8,128)S(1)}, u32[]{:S(2)}, u32[]{:S(2)}) collective-permute-start(f32[12,4,8,128]{3,2,1,0:T(8,128)S(1)} %pad_maximum_fusion.refs_0_.refs_6_), channel_id=1, source_target_pairs={{1,0},{2,1},{3,2},{4,3},{5,4},{6,5},{7,6},{8,7},{9,8},{10,9},{11,1... | collective-permute-start | bytes 589832 | tf_op jit(solution)/shard_map/ppermute | solution.py:313
  16.8 1.5 collective-permute-done.2.refs_2_.refs_7_
  18.7 2.7 %collective-permute-start.3 = (f32[12,4,8,128]{3,2,1,0:T(8,128)S(1)}, f32[12,4,8,128]{3,2,1,0:T(8,128)S(1)}, u32[]{:S(2)}, u32[]{:S(2)}) collective-permute-start(f32[12,4,8,128]{3,2,1,0:T(8,128)S(1)} %get-tuple-element.51.refs_0_), channel_id=1, source_target_pairs={{0,1},{1,2},{2,3},{3,4},{4,5},{5,6},{6,7},{7,8},{8,9},{9,10},{10,1... | collective-permute-start | bytes 589832 | tf_op jit(solution)/shard_map/ppermute | solution.py:313
  21.4 5.2 %collective-permute-start.4 = (f32[12,4,8,128]{3,2,1,0:T(8,128)S(1)}, f32[12,4,8,128]{3,2,1,0:T(8,128)S(1)}, u32[]{:S(2)}, u32[]{:S(2)}) collective-permute-start(f32[12,4,8,128]{3,2,1,0:T(8,128)S(1)} %get-tuple-element.52), channel_id=1, source_target_pairs={{1,0},{2,1},{3,2},{4,3},{5,4},{6,5},{7,6},{8,7},{9,8},{10,9},{11,1... | collective-permute-start | bytes 589832 | tf_op jit(solution)/shard_map/ppermute | solution.py:313
  26.6 1.8 %collective-permute-done.3.refs_1_ = f32[12,4,8,128]{3,2,1,0:T(8,128)S(1)} collective-permute-done((f32[12,4,8,128]{3,2,1,0:T(8,128)S(1)}, f32[12,4,8,128]{3,2,1,0:T(8,128)S(1)}, u32[]{:S(2)}, u32[]{:S(2)}) %collective-permute-start.3) | collective-permute-done | bytes 196640 | tf_op jit(solution)/shard_map/ppermute | solution.py:313
  28.4 1.8 collective-permute-done.4.refs_2_
  30.5 5.7 %collective-permute-start.5 = (f32[8,4,8,128]{3,2,1,0:T(8,128)S(1)}, f32[8,4,8,128]{3,2,1,0:T(8,128)S(1)}, u32[]{:S(2)}, u32[]{:S(2)}) collective-permute-start(f32[8,4,8,128]{3,2,1,0:T(8,128)S(1)} %get-tuple-element.55.refs_0_), channel_id=1, source_target_pairs={{0,1},{1,2},{2,3},{3,4},{4,5},{5,6},{6,7},{7,8},{8,9},{9,10},{10,1... | collective-permute-start | bytes 393224 | tf_op jit(solution)/shard_map/ppermute | solution.py:313
  36.3 2.1 %collective-permute-start.6 = (f32[8,4,8,128]{3,2,1,0:T(8,128)S(1)}, f32[8,4,8,128]{3,2,1,0:T(8,128)S(1)}, u32[]{:S(2)}, u32[]{:S(2)}) collective-permute-start(f32[8,4,8,128]{3,2,1,0:T(8,128)S(1)} %get-tuple-element.55.refs_0_), channel_id=1, source_target_pairs={{1,0},{2,1},{3,2},{4,3},{5,4},{6,5},{7,6},{8,7},{9,8},{10,9},{11,1... | collective-permute-start | bytes 393224 | tf_op jit(solution)/shard_map/ppermute | solution.py:313
  38.4 1.6 collective-permute-done.5.refs_1_
  40.0 3.6 %collective-permute-done.6.refs_2_ = f32[8,4,8,128]{3,2,1,0:T(8,128)S(1)} collective-permute-done((f32[8,4,8,128]{3,2,1,0:T(8,128)S(1)}, f32[8,4,8,128]{3,2,1,0:T(8,128)S(1)}, u32[]{:S(2)}, u32[]{:S(2)}) %collective-permute-start.6) | collective-permute-done | bytes 131104 | tf_op jit(solution)/shard_map/ppermute | solution.py:313
  44.0 5.3 %collective-permute-start.7 = (f32[8,4,8,128]{3,2,1,0:T(8,128)S(1)}, f32[8,4,8,128]{3,2,1,0:T(8,128)S(1)}, u32[]{:S(2)}, u32[]{:S(2)}) collective-permute-start(f32[8,4,8,128]{3,2,1,0:T(8,128)S(1)} %get-tuple-element.58.refs_0_), channel_id=1, source_target_pairs={{0,1},{1,2},{2,3},{3,4},{4,5},{5,6},{6,7},{7,8},{8,9},{9,10},{10,1... | collective-permute-start | bytes 393224 | tf_op jit(solution)/shard_map/ppermute | solution.py:313
  49.3 2.1 %collective-permute-start.8 = (f32[8,4,8,128]{3,2,1,0:T(8,128)S(1)}, f32[8,4,8,128]{3,2,1,0:T(8,128)S(1)}, u32[]{:S(2)}, u32[]{:S(2)}) collective-permute-start(f32[8,4,8,128]{3,2,1,0:T(8,128)S(1)} %get-tuple-element.58.refs_0_), channel_id=1, source_target_pairs={{1,0},{2,1},{3,2},{4,3},{5,4},{6,5},{7,6},{8,7},{9,8},{10,9},{11,1... | collective-permute-start | bytes 393224 | tf_op jit(solution)/shard_map/ppermute | solution.py:313
  52.3 3.2 %collective-permute-done.8.refs_2_ = f32[8,4,8,128]{3,2,1,0:T(8,128)S(1)} collective-permute-done((f32[8,4,8,128]{3,2,1,0:T(8,128)S(1)}, f32[8,4,8,128]{3,2,1,0:T(8,128)S(1)}, u32[]{:S(2)}, u32[]{:S(2)}) %collective-permute-start.8) | collective-permute-done | bytes 131104 | tf_op jit(solution)/shard_map/ppermute | solution.py:313
  56.0 5.6 %collective-permute-start.10 = (f32[7,4,8,128]{3,2,1,0:T(8,128)S(1)}, f32[7,4,8,128]{3,2,1,0:T(8,128)S(1)}, u32[]{:S(2)}, u32[]{:S(2)}) collective-permute-start(f32[7,4,8,128]{3,2,1,0:T(8,128)S(1)} %get-tuple-element.62.refs_10_), channel_id=1, source_target_pairs={{0,1},{1,2},{2,3},{3,4},{4,5},{5,6},{6,7},{7,8},{8,9},{9,10},{10,1... | collective-permute-start | bytes 344072 | tf_op jit(solution)/shard_map/ppermute | solution.py:313
  61.5 1.9 %collective-permute-start.13 = (f32[7,4,8,128]{3,2,1,0:T(8,128)S(1)}, f32[7,4,8,128]{3,2,1,0:T(8,128)S(1)}, u32[]{:S(2)}, u32[]{:S(2)}) collective-permute-start(f32[7,4,8,128]{3,2,1,0:T(8,128)S(1)} %get-tuple-element.62.refs_10_), channel_id=1, source_target_pairs={{1,0},{2,1},{3,2},{4,3},{5,4},{6,5},{7,6},{8,7},{9,8},{10,9},{11,1... | collective-permute-start | bytes 344072 | tf_op jit(solution)/shard_map/ppermute | solution.py:313
  63.5 1.3 collective-permute-start.9
  64.8 2.3 %collective-permute-done.13.refs_11_ = f32[7,4,8,128]{3,2,1,0:T(8,128)S(1)} collective-permute-done((f32[7,4,8,128]{3,2,1,0:T(8,128)S(1)}, f32[7,4,8,128]{3,2,1,0:T(8,128)S(1)}, u32[]{:S(2)}, u32[]{:S(2)}) %collective-permute-start.13) | collective-permute-done | bytes 114720 | tf_op jit(solution)/shard_map/ppermute | solution.py:313
  67.1 1.3 collective-permute-start.11
  68.4 1.3 collective-permute-start.14
  69.7 1.3 collective-permute-start.12
  71.1 8.5 %collective-permute-done.12.refs_1_ = f32[7,4,8,128]{3,2,1,0:T(8,128)S(1)} collective-permute-done((f32[7,4,8,128]{3,2,1,0:T(8,128)S(1)}, f32[7,4,8,128]{3,2,1,0:T(8,128)S(1)}, u32[]{:S(2)}, u32[]{:S(2)}) %collective-permute-start.12) | collective-permute-done | bytes 114720 | tf_op jit(solution)/shard_map/ppermute | solution.py:313
  79.7 2.0 %collective-permute-done.14.refs_2_ = f32[9,4,8,128]{3,2,1,0:T(8,128)S(1)} collective-permute-done((f32[9,4,8,128]{3,2,1,0:T(8,128)S(1)}, f32[9,4,8,128]{3,2,1,0:T(8,128)S(1)}, u32[]{:S(2)}, u32[]{:S(2)}) %collective-permute-start.14) | collective-permute-done | bytes 147488 | tf_op jit(solution)/shard_map/ppermute | solution.py:313
  86.2 1.3 collective-permute-start.20
  92.6 1.3 collective-permute-start.31
  99.1 20.2 %collective-permute-done.31.refs_5_ = f32[3,4,8,128]{3,2,1,0:T(8,128)S(1)} collective-permute-done((f32[3,4,8,128]{3,2,1,0:T(8,128)S(1)}, f32[3,4,8,128]{3,2,1,0:T(8,128)S(1)}, u32[]{:S(2)}, u32[]{:S(2)}) %collective-permute-start.31) | collective-permute-done | bytes 49184 | tf_op jit(solution)/shard_map/ppermute | solution.py:313
  120.5 3.8 %collective-permute-done.29.refs_3_ = f32[7,4,8,128]{3,2,1,0:T(8,128)S(1)} collective-permute-done((f32[7,4,8,128]{3,2,1,0:T(8,128)S(1)}, f32[7,4,8,128]{3,2,1,0:T(8,128)S(1)}, u32[]{:S(2)}, u32[]{:S(2)}) %collective-permute-start.29) | collective-permute-done | bytes 114720 | tf_op jit(solution)/shard_map/ppermute | solution.py:313
  142.9 30.1 %collective-permute-done.49.refs_1_ = f32[3,4,8,128]{3,2,1,0:T(8,128)S(1)} collective-permute-done((f32[3,4,8,128]{3,2,1,0:T(8,128)S(1)}, f32[3,4,8,128]{3,2,1,0:T(8,128)S(1)}, u32[]{:S(2)}, u32[]{:S(2)}) %collective-permute-start.49) | collective-permute-done | bytes 49184 | tf_op jit(solution)/shard_map/ppermute | solution.py:313
  174.7 1.7 shard_map.215
  176.4 1.8 collective-permute-start.54
  (132 shorter events, 43.0 us)
Async XLA Ops:
  0.6 7.5 %collective-permute-start = (f32[2,4,4,8,128]{4,3,2,1,0:T(8,128)}, f32[2,4,4,8,128]{4,3,2,1,0:T(8,128)S(1)}, u32[]{:S(2)}, u32[]{:S(2)}) collective-permute-start(f32[2,4,4,8,128]{4,3,2,1,0:T(8,128)} %bitcast.64), channel_id=1, source_target_pairs={{32,0},{33,1},{34,2},{35,3},{36,4},{37,5},{38,6},{39,7},{40,8},{41... | collective-permute-start | bytes 393224 | tf_op jit(solution)/shard_map/ppermute | solution.py:313
  8.3 8.5 %collective-permute-start.1 = (f32[12,4,8,128]{3,2,1,0:T(8,128)S(1)}, f32[12,4,8,128]{3,2,1,0:T(8,128)S(1)}, u32[]{:S(2)}, u32[]{:S(2)}) collective-permute-start(f32[12,4,8,128]{3,2,1,0:T(8,128)S(1)} %pad_maximum_fusion.refs_0_.refs_6_), channel_id=1, source_target_pairs={{0,1},{1,2},{2,3},{3,4},{4,5},{5,6},{6,7},{7,8},{8,9},{9,10},{10,1... | collective-permute-start | bytes 589832 | tf_op jit(solution)/shard_map/ppermute | solution.py:313
  11.4 6.9 %collective-permute-start.2 = (f32[12,4,8,128]{3,2,1,0:T(8,128)S(1)}, f32[12,4,8,128]{3,2,1,0:T(8,128)S(1)}, u32[]{:S(2)}, u32[]{:S(2)}) collective-permute-start(f32[12,4,8,128]{3,2,1,0:T(8,128)S(1)} %pad_maximum_fusion.refs_0_.refs_6_), channel_id=1, source_target_pairs={{1,0},{2,1},{3,2},{4,3},{5,4},{6,5},{7,6},{8,7},{9,8},{10,9},{11,1... | collective-permute-start | bytes 589832 | tf_op jit(solution)/shard_map/ppermute | solution.py:313
  18.7 9.7 %collective-permute-start.3 = (f32[12,4,8,128]{3,2,1,0:T(8,128)S(1)}, f32[12,4,8,128]{3,2,1,0:T(8,128)S(1)}, u32[]{:S(2)}, u32[]{:S(2)}) collective-permute-start(f32[12,4,8,128]{3,2,1,0:T(8,128)S(1)} %get-tuple-element.51.refs_0_), channel_id=1, source_target_pairs={{0,1},{1,2},{2,3},{3,4},{4,5},{5,6},{6,7},{7,8},{8,9},{9,10},{10,1... | collective-permute-start | bytes 589832 | tf_op jit(solution)/shard_map/ppermute | solution.py:313
  21.4 8.8 %collective-permute-start.4 = (f32[12,4,8,128]{3,2,1,0:T(8,128)S(1)}, f32[12,4,8,128]{3,2,1,0:T(8,128)S(1)}, u32[]{:S(2)}, u32[]{:S(2)}) collective-permute-start(f32[12,4,8,128]{3,2,1,0:T(8,128)S(1)} %get-tuple-element.52), channel_id=1, source_target_pairs={{1,0},{2,1},{3,2},{4,3},{5,4},{6,5},{7,6},{8,7},{9,8},{10,9},{11,1... | collective-permute-start | bytes 589832 | tf_op jit(solution)/shard_map/ppermute | solution.py:313
  30.5 9.5 %collective-permute-start.5 = (f32[8,4,8,128]{3,2,1,0:T(8,128)S(1)}, f32[8,4,8,128]{3,2,1,0:T(8,128)S(1)}, u32[]{:S(2)}, u32[]{:S(2)}) collective-permute-start(f32[8,4,8,128]{3,2,1,0:T(8,128)S(1)} %get-tuple-element.55.refs_0_), channel_id=1, source_target_pairs={{0,1},{1,2},{2,3},{3,4},{4,5},{5,6},{6,7},{7,8},{8,9},{9,10},{10,1... | collective-permute-start | bytes 393224 | tf_op jit(solution)/shard_map/ppermute | solution.py:313
  36.3 7.3 %collective-permute-start.6 = (f32[8,4,8,128]{3,2,1,0:T(8,128)S(1)}, f32[8,4,8,128]{3,2,1,0:T(8,128)S(1)}, u32[]{:S(2)}, u32[]{:S(2)}) collective-permute-start(f32[8,4,8,128]{3,2,1,0:T(8,128)S(1)} %get-tuple-element.55.refs_0_), channel_id=1, source_target_pairs={{1,0},{2,1},{3,2},{4,3},{5,4},{6,5},{7,6},{8,7},{9,8},{10,9},{11,1... | collective-permute-start | bytes 393224 | tf_op jit(solution)/shard_map/ppermute | solution.py:313
  44.0 8.3 %collective-permute-start.7 = (f32[8,4,8,128]{3,2,1,0:T(8,128)S(1)}, f32[8,4,8,128]{3,2,1,0:T(8,128)S(1)}, u32[]{:S(2)}, u32[]{:S(2)}) collective-permute-start(f32[8,4,8,128]{3,2,1,0:T(8,128)S(1)} %get-tuple-element.58.refs_0_), channel_id=1, source_target_pairs={{0,1},{1,2},{2,3},{3,4},{4,5},{5,6},{6,7},{7,8},{8,9},{9,10},{10,1... | collective-permute-start | bytes 393224 | tf_op jit(solution)/shard_map/ppermute | solution.py:313
  49.3 6.2 %collective-permute-start.8 = (f32[8,4,8,128]{3,2,1,0:T(8,128)S(1)}, f32[8,4,8,128]{3,2,1,0:T(8,128)S(1)}, u32[]{:S(2)}, u32[]{:S(2)}) collective-permute-start(f32[8,4,8,128]{3,2,1,0:T(8,128)S(1)} %get-tuple-element.58.refs_0_), channel_id=1, source_target_pairs={{1,0},{2,1},{3,2},{4,3},{5,4},{6,5},{7,6},{8,7},{9,8},{10,9},{11,1... | collective-permute-start | bytes 393224 | tf_op jit(solution)/shard_map/ppermute | solution.py:313
  56.0 8.8 %collective-permute-start.10 = (f32[7,4,8,128]{3,2,1,0:T(8,128)S(1)}, f32[7,4,8,128]{3,2,1,0:T(8,128)S(1)}, u32[]{:S(2)}, u32[]{:S(2)}) collective-permute-start(f32[7,4,8,128]{3,2,1,0:T(8,128)S(1)} %get-tuple-element.62.refs_10_), channel_id=1, source_target_pairs={{0,1},{1,2},{2,3},{3,4},{4,5},{5,6},{6,7},{7,8},{8,9},{9,10},{10,1... | collective-permute-start | bytes 344072 | tf_op jit(solution)/shard_map/ppermute | solution.py:313
  61.5 5.5 %collective-permute-start.13 = (f32[7,4,8,128]{3,2,1,0:T(8,128)S(1)}, f32[7,4,8,128]{3,2,1,0:T(8,128)S(1)}, u32[]{:S(2)}, u32[]{:S(2)}) collective-permute-start(f32[7,4,8,128]{3,2,1,0:T(8,128)S(1)} %get-tuple-element.62.refs_10_), channel_id=1, source_target_pairs={{1,0},{2,1},{3,2},{4,3},{5,4},{6,5},{7,6},{8,7},{9,8},{10,9},{11,1... | collective-permute-start | bytes 344072 | tf_op jit(solution)/shard_map/ppermute | solution.py:313
  63.5 18.2 %collective-permute-start.9 = (f32[5,4,4,8,128]{4,3,2,1,0:T(8,128)S(1)}, f32[5,4,4,8,128]{4,3,2,1,0:T(8,128)S(1)}, u32[]{:S(2)}, u32[]{:S(2)}) collective-permute-start(f32[5,4,4,8,128]{4,3,2,1,0:T(8,128)S(1)} %get-tuple-element.61), channel_id=1, source_target_pairs={{0,32},{1,33},{2,34},{3,35},{4,36},{5,37},{6,38},{7,39},{8,40},{9,... | collective-permute-start | bytes 983048 | tf_op jit(solution)/shard_map/ppermute | solution.py:313
  67.1 12.6 %collective-permute-start.11 = (f32[9,4,8,128]{3,2,1,0:T(8,128)S(1)}, f32[9,4,8,128]{3,2,1,0:T(8,128)S(1)}, u32[]{:S(2)}, u32[]{:S(2)}) collective-permute-start(f32[9,4,8,128]{3,2,1,0:T(8,128)S(1)} %get-tuple-element.113), channel_id=1, source_target_pairs={{64,33},{65,34},{66,35},{67,36},{68,37},{69,38},{70,39},{71,40},{7... | collective-permute-start | bytes 442376 | tf_op jit(solution)/shard_map/ppermute | solution.py:313
  68.4 13.3 %collective-permute-start.14 = (f32[9,4,8,128]{3,2,1,0:T(8,128)S(1)}, f32[9,4,8,128]{3,2,1,0:T(8,128)S(1)}, u32[]{:S(2)}, u32[]{:S(2)}) collective-permute-start(f32[9,4,8,128]{3,2,1,0:T(8,128)S(1)} %get-tuple-element.112), channel_id=1, source_target_pairs={{65,32},{66,33},{67,34},{68,35},{69,36},{70,37},{71,38},{72,39},{7... | collective-permute-start | bytes 442376 | tf_op jit(solution)/shard_map/ppermute | solution.py:313
  69.7 9.9 %collective-permute-start.12 = (f32[7,4,8,128]{3,2,1,0:T(8,128)S(1)}, f32[7,4,8,128]{3,2,1,0:T(8,128)S(1)}, u32[]{:S(2)}, u32[]{:S(2)}) collective-permute-start(f32[7,4,8,128]{3,2,1,0:T(8,128)S(1)} %get-tuple-element.62.refs_10_), channel_id=1, source_target_pairs={{64,32},{65,33},{66,34},{67,35},{68,36},{69,37},{70,38},{71,39},{7... | collective-permute-start | bytes 344072 | tf_op jit(solution)/shard_map/ppermute | solution.py:313
  82.7 3.4 %collective-permute-start.19 = (f32[3,4,8,128]{3,2,1,0:T(8,128)S(1)}, f32[3,4,8,128]{3,2,1,0:T(8,128)S(1)}, u32[]{:S(2)}, u32[]{:S(2)}) collective-permute-start(f32[3,4,8,128]{3,2,1,0:T(8,128)S(1)} %get-tuple-element.66), channel_id=1, source_target_pairs={{226,160},{227,161},{228,162},{229,163},{230,164},{231,165},{232,1... | collective-permute-start | bytes 147464 | tf_op jit(solution)/shard_map/ppermute | solution.py:313
  88.4 3.4 %collective-permute-start.25 = (f32[3,4,8,128]{3,2,1,0:T(8,128)S(1)}, f32[3,4,8,128]{3,2,1,0:T(8,128)S(1)}, u32[]{:S(2)}, u32[]{:S(2)}) collective-permute-start(f32[3,4,8,128]{3,2,1,0:T(8,128)S(1)} %get-tuple-element.71), channel_id=1, source_target_pairs={{162,96},{163,97},{164,98},{165,99},{166,100},{167,101},{168,102},... | collective-permute-start | bytes 147464 | tf_op jit(solution)/shard_map/ppermute | solution.py:313
  92.6 26.7 %collective-permute-start.31 = (f32[3,4,8,128]{3,2,1,0:T(8,128)S(1)}, f32[3,4,8,128]{3,2,1,0:T(8,128)S(1)}, u32[]{:S(2)}, u32[]{:S(2)}) collective-permute-start(f32[3,4,8,128]{3,2,1,0:T(8,128)S(1)} %get-tuple-element.76), channel_id=1, source_target_pairs={{98,32},{99,33},{100,34},{101,35},{102,36},{103,37},{104,38},{105,... | collective-permute-start | bytes 147464 | tf_op jit(solution)/shard_map/ppermute | solution.py:313
  93.9 25.7 %collective-permute-start.28 = (f32[6,4,8,128]{3,2,1,0:T(8,128)S(1)}, f32[6,4,8,128]{3,2,1,0:T(8,128)S(1)}, u32[]{:S(2)}, u32[]{:S(2)}) collective-permute-start(f32[6,4,8,128]{3,2,1,0:T(8,128)S(1)} %get-tuple-element.77), channel_id=1, source_target_pairs={{96,33},{97,34},{98,35},{99,36},{100,37},{101,38},{102,39},{103,40... | collective-permute-start | bytes 294920 | tf_op jit(solution)/shard_map/ppermute | solution.py:313
  95.2 25.3 %collective-permute-start.30 = (f32[6,4,8,128]{3,2,1,0:T(8,128)S(1)}, f32[6,4,8,128]{3,2,1,0:T(8,128)S(1)}, u32[]{:S(2)}, u32[]{:S(2)}) collective-permute-start(f32[6,4,8,128]{3,2,1,0:T(8,128)S(1)} %get-tuple-element.77), channel_id=1, source_target_pairs={{97,32},{98,33},{99,34},{100,35},{101,36},{102,37},{103,38},{104,3... | collective-permute-start | bytes 294920 | tf_op jit(solution)/shard_map/ppermute | solution.py:313
  96.5 22.8 %collective-permute-start.27 = (f32[3,4,8,128]{3,2,1,0:T(8,128)S(1)}, f32[3,4,8,128]{3,2,1,0:T(8,128)S(1)}, u32[]{:S(2)}, u32[]{:S(2)}) collective-permute-start(f32[3,4,8,128]{3,2,1,0:T(8,128)S(1)} %get-tuple-element.76), channel_id=1, source_target_pairs={{96,34},{97,35},{98,36},{99,37},{100,38},{101,39},{102,40},{103,41... | collective-permute-start | bytes 147464 | tf_op jit(solution)/shard_map/ppermute | solution.py:313
  97.8 26.4 %collective-permute-start.29 = (f32[7,4,8,128]{3,2,1,0:T(8,128)S(1)}, f32[7,4,8,128]{3,2,1,0:T(8,128)S(1)}, u32[]{:S(2)}, u32[]{:S(2)}) collective-permute-start(f32[7,4,8,128]{3,2,1,0:T(8,128)S(1)} %get-tuple-element.78), channel_id=1, source_target_pairs={{96,32},{97,33},{98,34},{99,35},{100,36},{101,37},{102,38},{103,39... | collective-permute-start | bytes 344072 | tf_op jit(solution)/shard_map/ppermute | solution.py:313
  125.0 3.4 %collective-permute-start.37 = (f32[3,4,8,128]{3,2,1,0:T(8,128)S(1)}, f32[3,4,8,128]{3,2,1,0:T(8,128)S(1)}, u32[]{:S(2)}, u32[]{:S(2)}) collective-permute-start(f32[3,4,8,128]{3,2,1,0:T(8,128)S(1)} %get-tuple-element.81), channel_id=1, source_target_pairs={{290,224},{291,225},{292,226},{293,227},{294,228},{295,229},{296,2... | collective-permute-start | bytes 147464 | tf_op jit(solution)/shard_map/ppermute | solution.py:313
  129.3 3.6 %collective-permute-start.41 = (f32[7,4,8,128]{3,2,1,0:T(8,128)S(1)}, f32[7,4,8,128]{3,2,1,0:T(8,128)S(1)}, u32[]{:S(2)}, u32[]{:S(2)}) collective-permute-start(f32[7,4,8,128]{3,2,1,0:T(8,128)S(1)} %get-tuple-element.88), channel_id=1, source_target_pairs={{224,160},{225,161},{226,162},{227,163},{228,164},{229,165},{230,1... | collective-permute-start | bytes 344072 | tf_op jit(solution)/shard_map/ppermute | solution.py:313
  129.9 2.9 %collective-permute-start.40 = (f32[6,4,8,128]{3,2,1,0:T(8,128)S(1)}, f32[6,4,8,128]{3,2,1,0:T(8,128)S(1)}, u32[]{:S(2)}, u32[]{:S(2)}) collective-permute-start(f32[6,4,8,128]{3,2,1,0:T(8,128)S(1)} %get-tuple-element.87), channel_id=1, source_target_pairs={{224,161},{225,162},{226,163},{227,164},{228,165},{229,166},{230,1... | collective-permute-start | bytes 294920 | tf_op jit(solution)/shard_map/ppermute | solution.py:313
  132.9 3.4 %collective-permute-start.46 = (f32[7,4,8,128]{3,2,1,0:T(8,128)S(1)}, f32[7,4,8,128]{3,2,1,0:T(8,128)S(1)}, u32[]{:S(2)}, u32[]{:S(2)}) collective-permute-start(f32[7,4,8,128]{3,2,1,0:T(8,128)S(1)} %get-tuple-element.92), channel_id=1, source_target_pairs={{160,96},{161,97},{162,98},{163,99},{164,100},{165,101},{166,102},... | collective-permute-start | bytes 344072 | tf_op jit(solution)/shard_map/ppermute | solution.py:313
  136.4 38.3 %collective-permute-start.51 = (f32[7,4,8,128]{3,2,1,0:T(8,128)S(1)}, f32[7,4,8,128]{3,2,1,0:T(8,128)S(1)}, u32[]{:S(2)}, u32[]{:S(2)}) collective-permute-start(f32[7,4,8,128]{3,2,1,0:T(8,128)S(1)} %get-tuple-element.96), channel_id=1, source_target_pairs={{96,32},{97,33},{98,34},{99,35},{100,36},{101,37},{102,38},{103,39... | collective-permute-start | bytes 344072 | tf_op jit(solution)/shard_map/ppermute | solution.py:313
  137.7 37.0 %collective-permute-start.50 = (f32[6,4,8,128]{3,2,1,0:T(8,128)S(1)}, f32[6,4,8,128]{3,2,1,0:T(8,128)S(1)}, u32[]{:S(2)}, u32[]{:S(2)}) collective-permute-start(f32[6,4,8,128]{3,2,1,0:T(8,128)S(1)} %get-tuple-element.95), channel_id=1, source_target_pairs={{96,33},{97,34},{98,35},{99,36},{100,37},{101,38},{102,39},{103,40... | collective-permute-start | bytes 294920 | tf_op jit(solution)/shard_map/ppermute | solution.py:313
  139.0 35.7 %collective-permute-start.52 = (f32[6,4,8,128]{3,2,1,0:T(8,128)S(1)}, f32[6,4,8,128]{3,2,1,0:T(8,128)S(1)}, u32[]{:S(2)}, u32[]{:S(2)}) collective-permute-start(f32[6,4,8,128]{3,2,1,0:T(8,128)S(1)} %get-tuple-element.95), channel_id=1, source_target_pairs={{97,32},{98,33},{99,34},{100,35},{101,36},{102,37},{103,38},{104,3... | collective-permute-start | bytes 294920 | tf_op jit(solution)/shard_map/ppermute | solution.py:313
  140.3 32.7 %collective-permute-start.49 = (f32[3,4,8,128]{3,2,1,0:T(8,128)S(1)}, f32[3,4,8,128]{3,2,1,0:T(8,128)S(1)}, u32[]{:S(2)}, u32[]{:S(2)}) collective-permute-start(f32[3,4,8,128]{3,2,1,0:T(8,128)S(1)} %get-tuple-element.94), channel_id=1, source_target_pairs={{96,34},{97,35},{98,36},{99,37},{100,38},{101,39},{102,40},{103,41... | collective-permute-start | bytes 147464 | tf_op jit(solution)/shard_map/ppermute | solution.py:313
  141.6 33.1 %collective-permute-start.53 = (f32[3,4,8,128]{3,2,1,0:T(8,128)S(1)}, f32[3,4,8,128]{3,2,1,0:T(8,128)S(1)}, u32[]{:S(2)}, u32[]{:S(2)}) collective-permute-start(f32[3,4,8,128]{3,2,1,0:T(8,128)S(1)} %get-tuple-element.94), channel_id=1, source_target_pairs={{98,32},{99,33},{100,34},{101,35},{102,36},{103,37},{104,38},{105,... | collective-permute-start | bytes 147464 | tf_op jit(solution)/shard_map/ppermute | solution.py:313
  173.1 5.1 %collective-permute-start.55 = (f32[4,4,8,128]{3,2,1,0:T(8,128)S(1)}, f32[4,4,8,128]{3,2,1,0:T(8,128)S(1)}, u32[]{:S(2)}, u32[]{:S(2)}) collective-permute-start(f32[4,4,8,128]{3,2,1,0:T(8,128)S(1)} %get-tuple-element.99), channel_id=1, source_target_pairs={{0,32},{1,33},{2,34},{3,35},{4,36},{5,37},{6,38},{7,39},{8,40},{9,... | collective-permute-start | bytes 196616 | tf_op jit(solution)/shard_map/ppermute | solution.py:313
  (29 other events, 48.4 us)

commit v4 on v3

--- a/solution.py
+++ b/solution.py
@@ -130,7 +130,7 @@
         refs = list(refs)
         r0, rl, rh, u, prev = [refs.pop(0) for _ in range(5)]
         src, inv = (None, None) if last else [refs.pop(0) for _ in range(2)]
-        factors = [refs.pop(0) for _ in range(3)] if last else None
+        factors = [refs.pop(0) for _ in range(4)][:3] if last else None
         old = None if first else refs.pop(0)
         out, grad = refs[:2]
         more, scratch = refs[2:-3], refs[-3:]
@@ -182,53 +182,53 @@
     return (count, WIDTH, 8, 128)
 
 
-def offsets_step(z_three, inv_five, pack, own_three, pair_odd):
-    def body(*refs):
-        (zl, zm, zh), iv, even, zo, (x0, x1) = refs[0:3], refs[3:8], refs[8], refs[9:12], refs[12:14]
-        v, pairs = refs[14:16]
-        scratch = refs[16:]
-        z = [zl.at[0:3], zl.at[3:9], zm, zh.at[0:6], zh.at[6:9]]
+def offsets_step(pack, z_low, z_own, z_high, even_low, even_high, prior):
+    def body(even, zl, z0, zh, el, eh, before, offset, ahead, own, *scratch):
         stencil = Stencil()
-
-        def emit_odd(layer, q):
-            slab, at = layer // WIDTH, layer % WIDTH
-            for f in range(FIELDS):
-                if masses[f]:
-                    v[f, layer] = zo[slab][f, at] - 0.875 * q[f] + 0.125 * z[slab + 1][3 + f, at]
-                if slab == 1:
-                    pairs[0, 0, f, at] = x0[f, at] - q[f]
-                    pairs[0, 1, f, at] = x1[f, at] - 0.5 * (q[f] + z[2][3 + f, at])
+        for f in range(3):
+            own[f] = even[0, f] - 0.25 * even[1, f]
 
         def emit_even(layer, q):
             for f in range(FIELDS):
-                pairs[1, 0, f, layer] = even[0, f, layer] - q[f]
-                pairs[1, 1, f, layer] = even[1, f, layer] - 0.5 * (q[f] + x0[f, layer])
-
-        inv_at = lambda f, layer: even[2 + layer // WIDTH, f, layer % WIDTH]
-        solve(stencil, masses_only(z), layers_of(iv), 5 * WIDTH, scratch, emit_odd)
-        solve(stencil, masses_only(zo), inv_at, 3 * WIDTH, scratch, emit_even)
-
-    return call(
+                offset[0, f, layer] = even[0, f, layer] - q[f]
+                offset[1, f, layer] = even[1, f, layer] - 0.5 * (q[f] + z0[3 + f, layer])
+
+        def emit_before(layer, q):
+            for f in range(FIELDS):
+                ahead[f, layer] = q[f]
+
+        inv_even = lambda f, layer: even[2 + layer // WIDTH, f, layer % WIDTH]
+        inv_before = lambda f, layer: before[layer // WIDTH, f, layer % WIDTH]
+        solve(stencil, masses_only([zl, z0, zh]), inv_even, 3 * WIDTH, scratch, emit_even)
+        solve(stencil, masses_only([el, own, eh]), inv_before, 3 * WIDTH, scratch, emit_before)
+
+    spec = pl.BlockSpec(memory_space=pltpu.VMEM)
+    return pl.pallas_call(
         body,
-        [(3, 3 * WIDTH, 8, 128), (2, 2) + SLAB],
-        *z_three, *inv_five, pack, *own_three, *pair_odd,
-        layers=5 * WIDTH, flops=88 * 4 * 1024 * 20,
-    )
-
-
-def chip_step(turn, place, z_five, inv_five, pack, v_three, offsets, done, grad):
-    with_done, with_grad, with_z = done is not None, grad is not None, z_five is not None
+        in_specs=[spec] * 7,
+        out_specs=[spec] * 2,
+        out_shape=[jax.ShapeDtypeStruct(shape, jnp.float32) for shape in ((2,) + SLAB, SLAB)],
+        scratch_shapes=[vmem(carry(3))] + [vmem((FIELDS, 3 * WIDTH, 8, 128))] * 3,
+        compiler_params=pltpu.CompilerParams(vmem_limit_bytes=24 * 1024 * 1024),
+        cost_estimate=pl.CostEstimate(flops=56 * 4 * 1024 * 20, bytes_accessed=1 << 20, transcendentals=0),
+    )(pack, z_low, z_own, z_high, even_low, even_high, prior)
+
+
+def chip_step(turn, place, arrived, inv_five, pack, own_three, late, offset, ahead, done, grad):
+    with_done, with_grad, with_z = done is not None, grad is not None, arrived is not None
 
     def body(*refs):
         refs = list(refs)
         spot = refs.pop(0)
         z = [refs.pop(0) for _ in range(5)] if with_z else None
         iv = [refs.pop(0) for _ in range(5)]
-        even, v, o = refs.pop(0), refs.pop(0), refs.pop(0)
-        before = refs.pop(0) if with_done else None
+        even = refs.pop(0)
+        zo = [refs.pop(0) for _ in range(3)]
+        x1, o, qa = [refs.pop(0) for _ in range(3)]
+        before = [refs.pop(0) for _ in range(2)] if with_done else None
         g = [refs.pop(0) for _ in range(2)] if with_grad else None
-        z3, z6, z7, pairs = refs[:4]
-        sums = refs[4] if with_grad else None
+        z3, z6, z11, odd_pair, even_pair = refs[:5]
+        sums = refs[5] if with_grad else None
         middle, scratch = refs[-4], refs[-3:]
         if with_grad:
             sums[...] = g[0][...] + g[1][...]
@@ -236,10 +236,11 @@
 
         @pl.when(jnp.logical_not(mine))
         def _():
-            pairs[...] = before[...] if with_done else jnp.zeros_like(pairs)
+            odd_pair[...] = before[0][...] if with_done else jnp.zeros_like(odd_pair)
+            even_pair[...] = before[1][...] if with_done else jnp.zeros_like(even_pair)
             z3[...] = jnp.zeros_like(z3)
             z6[...] = jnp.zeros_like(z6)
-            z7[...] = jnp.zeros_like(z7)
+            z11[...] = jnp.zeros_like(z11)
 
         @pl.when(mine)
         def _():
@@ -249,27 +250,34 @@
             def emit_odd(layer, q):
                 slab, at = layer // WIDTH, layer % WIDTH
                 for f in range(FIELDS):
-                    own = slab == 1
-                    c0 = z[slab + 1][3 + f, at] if with_z and (own or masses[f]) else zero
-                    if masses[f]:
-                        middle[f, layer] = 0.875 * q[f] - 0.125 * c0 + v[f, layer]
-                    if own:
-                        pairs[0, 0, f, at] = q[f] + o[0, 0, f, at]
-                        pairs[0, 1, f, at] = 0.5 * (q[f] + c0) + o[0, 1, f, at]
+                    if slab == 1:
+                        solved = z[2][3 + f, at] if with_z else zero
+                        change = z[2][7 + f, at] if with_z else zero
+                        c0 = q[f] + (zo[1][3 + f, at] - solved)
+                        c1 = x1[f, at] + 0.5 * ((q[f] - solved) + change)
+                        odd_pair[0, f, at] = c0
+                        odd_pair[1, f, at] = c1
+                        if masses[f]:
+                            middle[f, layer] = c0 - 0.25 * c1
+                    elif masses[f]:
+                        y = z[slab + 1][3 + f, at] if with_z else zero
+                        middle[f, layer] = 0.875 * q[f] + y + zo[slab][f, at]
 
             def emit_even(layer, q):
                 for f in range(FIELDS):
-                    c0 = q[f] + o[1, 0, f, layer]
-                    c1 = 0.5 * (q[f] + pairs[0, 0, f, layer]) + o[1, 1, f, layer]
-                    pairs[1, 0, f, layer] = c0
-                    pairs[1, 1, f, layer] = c1
-                    z7[3 + f, layer] = c0
+                    c0 = q[f] + o[0, f, layer]
+                    c1 = 0.5 * (q[f] + odd_pair[0, f, layer]) + o[1, f, layer]
+                    change = c0 - even[0, f, layer]
+                    even_pair[0, f, layer] = c0
+                    even_pair[1, f, layer] = c1
+                    z11[3 + f, layer] = qa[f, layer]
+                    z11[7 + f, layer] = change
                     if masses[f]:
                         carried = c0 - 0.25 * c1
                         z3[f, layer] = carried
                         z6[f, layer] = carried
-                        z7[f, layer] = carried
-                        z6[3 + f, layer] = c0
+                        z11[f, layer] = carried
+                        z6[3 + f, layer] = -0.875 * qa[f, layer] - 0.125 * change
 
             if with_z:
                 right = masses_only(z)
@@ -281,10 +289,11 @@
             solve(stencil, middle_at, inv_at, 3 * WIDTH, scratch, emit_even)
 
     spec = pl.BlockSpec(memory_space=pltpu.VMEM)
-    operands = [place] + (list(z_five) if with_z else []) + list(inv_five) + [pack, v_three, offsets]
-    operands += [done] if with_done else []
+    operands = [place] + (list(arrived) if with_z else []) + list(inv_five) + [pack]
+    operands += list(own_three) + [late, offset, ahead]
+    operands += list(done) if with_done else []
     operands += list(grad) if with_grad else []
-    outs = [carry(3), carry(6), carry(7), (2, 2) + SLAB] + ([SLAB] if with_grad else [])
+    outs = [carry(3), carry(6), carry(11), (2,) + SLAB, (2,) + SLAB] + ([SLAB] if with_grad else [])
     return pl.pallas_call(
         body,
         in_specs=[pl.BlockSpec(memory_space=pltpu.SMEM)] + [spec] * (len(operands) - 1),
@@ -324,9 +333,12 @@
     even_to_odd = routes(times, slabs, lambda k, s: (k + 1, s), lambda k: k % 2 == 0)
     odd_to_even = routes(times, slabs, lambda k, s: (k - 1, s), lambda k: k % 2 == 1)
     reach = (2, 1, 0, -1, -2)
-    relaxed_routes = [
-        routes(times, slabs, lambda k, s, d=d: (k - 1, s + d), lambda k: k % 2 == 0) for d in (1, 0, -1)
-    ]
+    odd, even = (lambda k: k % 2 == 1), (lambda k: k % 2 == 0)
+    odd_right, odd_left = (routes(times, slabs, lambda k, s, d=d: (k, s + d), odd) for d in (1, -1))
+    even_right, even_left = (
+        routes(times, slabs, lambda k, s, d=d: (k + 1, s + d), even) for d in (1, -1)
+    )
+    later = routes(times, slabs, lambda k, s: (k + 2, s), odd)
 
     def hop_routes(hop):
         group = [h for h in range(1, chips) if (h - hop) % 4 == 0]
@@ -351,7 +363,9 @@
             if n:
                 rest = dict(source=adjoint_source[n - 1], factor=inverses[n - 1])
             else:
-                rest = dict(coarse=exchanged[0])
+                far = [part[2 * FIELDS :] for part in exchanged[0]]
+                prior = send(jnp.stack(far), later)
+                rest = dict(coarse=(*exchanged[0], prior))
             x, total, *more = fine_step(n, up, low, high, states[n], previous, total, **rest)
             adjoints[n] = previous = x
             up, down = more[0], more[-1]
@@ -360,15 +374,12 @@
         z7, pack = more
         total = time_step * total
 
-        z_low, z_high = send(z7, right_one), send(z7, left_one)
+        z3 = z7[:3]
+        z_low, z_high = send(z3, odd_right), send(z3, odd_left)
+        even_low, even_high = send(z3, even_right), send(z3, even_left)
         pack = send(pack, even_to_odd)
-        payload = (
-            jnp.concatenate([z_low[:3], z7[:6]]), z7, jnp.concatenate([z7[:6], z_high[:3]])
-        )
-        z_three = [send(part, path) for part, path in zip(payload, relaxed_routes)]
-        v, offsets = offsets_step(
-            z_three, inv_five, pack, (z_low, z7, z_high), (adjoints[0], adjoints[1])
-        )
+        own_three = (z_low, z7, z_high)
+        offset, before = offsets_step(pack, *own_three, even_low, even_high, prior)
 
         place = (lax.axis_index("tm").astype(jnp.int32)).reshape(1)
         stages = []
@@ -378,33 +389,31 @@
                 routes(times, slabs, lambda k, s, d=far: (2 * ((k // 2) ^ d), s), lambda k: k % 2 == 0)
             )
             far *= 2
-        stages = [odd_to_even] + stages
-        z_five, done, grad, hop = None, None, total, 0
+        stages = [odd_to_even] + stages + [even_to_odd]
+        is_even = lax.axis_index("tm") % 2 == 0
+        arrived, done, grad, hop = None, None, total, 0
         while hop < chips or stages:
             added = None
             if hop and hop < chips:
-                z_five = [send(part, path) for part, path in zip(payload, hop_routes(hop))]
+                arrived = [send(part, path) for part, path in zip(payload, hop_routes(hop))]
             if hop and stages:
-                arrived = sum(part[:1] if part.shape[0] < 4 else part[:4] for part in z_five)
-                late = jnp.where(place[0] < 0, arrived, grad)
-                added = (grad, send(late, stages.pop(0)))
+                mark = sum(part[:1] if part.shape[0] < 4 else part[:4] for part in arrived)
+                received = send(jnp.where(place[0] < 0, mark, grad), stages.pop(0))
+                added = (grad if stages else jnp.where(is_even, grad, 0.0), received)
             if hop < chips:
-                z3, z6, z7, done, *sums = chip_step(
-                    times - 1 - 2 * hop, place, z_five, inv_five, pack, v, offsets, done, added
+                z3, z6, z11, odd_pair, even_pair, *sums = chip_step(
+                    times - 1 - 2 * hop, place, arrived, inv_five, pack, own_three, adjoints[1],
+                    offset, before, done, added,
                 )
-                payload = (z3, z6, z7, z6, z3)
+                payload, done = (z3, z6, z11, z6, z3), (odd_pair, even_pair)
                 if sums:
                     grad = sums[0]
             elif added:
                 grad = added[0] + added[1]
             hop += 1
 
-        even = lax.axis_index("tm") % 2 == 0
-        grad_odd = send(grad, even_to_odd)
-        gradient = jnp.where(even, grad, grad_odd)
-        done_even = send(done[1], odd_to_even)
-        corrected = jnp.where(even, done_even, done[0])
-        return corrected[None], gradient
+        corrected = jnp.where(is_even, send(done[1], odd_to_even), done[0])
+        return corrected[None], grad
 
     return on_device
 

time: 181 us -> 182 us (level)
  the two profiles are of different devices: /device:TPU:25 before, /device:TPU:17 now
where the time goes in v4:
time: 182 us; the launch traced here: 181 us
  starting transfers between devices  85.2 us (47%)
  waiting for transfers between devices  84.7 us (47%)
  Pallas kernels  5.94 us (3%)
  other arithmetic  1.95 us (1%)
    ppermute x56, starting transfers between devices, send(): return lax.ppermute(value, AXES, pairs)  85.2 us
    ppermute x56, waiting for transfers between devices, send(): return lax.ppermute(value, AXES, pairs)  84.7 us
  transfers between devices with their start and end apart: 56, of which 16 were waited for; matrix products, arithmetic and copies ran while one was open for 1% of the time, Pallas kernels for 0%

profile of v4, /device:TPU:17, one launch (start us, length us, event | category | flops | bytes accessed | tf_op | source)
XLA Modules:
  0.0 181.1 jit_solution(805329094862463461)
XLA Ops:
  0.6 2.6 %collective-permute-start = (f32[2,4,4,8,128]{4,3,2,1,0:T(8,128)}, f32[2,4,4,8,128]{4,3,2,1,0:T(8,128)S(1)}, u32[]{:S(2)}, u32[]{:S(2)}) collective-permute-start(f32[2,4,4,8,128]{4,3,2,1,0:T(8,128)} %bitcast.68), channel_id=1, source_target_pairs={{32,0},{33,1},{34,2},{35,3},{36,4},{37,5},{38,6},{39,7},{40,8},{41... | collective-permute-start | bytes 393224 | tf_op jit(solution)/shard_map/ppermute | solution.py:322
  6.0 2.1 %collective-permute-done = f32[2,4,4,8,128]{4,3,2,1,0:T(8,128)S(1)} collective-permute-done((f32[2,4,4,8,128]{4,3,2,1,0:T(8,128)}, f32[2,4,4,8,128]{4,3,2,1,0:T(8,128)S(1)}, u32[]{:S(2)}, u32[]{:S(2)}) %collective-permute-start) | collective-permute-done | bytes 131104 | tf_op jit(solution)/shard_map/ppermute | solution.py:322
  8.1 3.1 %collective-permute-start.1 = (f32[12,4,8,128]{3,2,1,0:T(8,128)S(1)}, f32[12,4,8,128]{3,2,1,0:T(8,128)S(1)}, u32[]{:S(2)}, u32[]{:S(2)}) collective-permute-start(f32[12,4,8,128]{3,2,1,0:T(8,128)S(1)} %pad_maximum_fusion.refs_0_.refs_6_), channel_id=1, source_target_pairs={{0,1},{1,2},{2,3},{3,4},{4,5},{5,6},{6,7},{7,8},{8,9},{9,10},{10,1... | collective-permute-start | bytes 589832 | tf_op jit(solution)/shard_map/ppermute | solution.py:322
  11.3 4.3 %collective-permute-start.2 = (f32[12,4,8,128]{3,2,1,0:T(8,128)S(1)}, f32[12,4,8,128]{3,2,1,0:T(8,128)S(1)}, u32[]{:S(2)}, u32[]{:S(2)}) collective-permute-start(f32[12,4,8,128]{3,2,1,0:T(8,128)S(1)} %pad_maximum_fusion.refs_0_.refs_6_), channel_id=1, source_target_pairs={{1,0},{2,1},{3,2},{4,3},{5,4},{6,5},{7,6},{8,7},{9,8},{10,9},{11,1... | collective-permute-start | bytes 589832 | tf_op jit(solution)/shard_map/ppermute | solution.py:322
  15.6 1.6 collective-permute-done.1.refs_1_.refs_5_
  17.2 1.8 collective-permute-done.2.refs_2_.refs_7_
  19.3 2.7 %collective-permute-start.3 = (f32[12,4,8,128]{3,2,1,0:T(8,128)S(1)}, f32[12,4,8,128]{3,2,1,0:T(8,128)S(1)}, u32[]{:S(2)}, u32[]{:S(2)}) collective-permute-start(f32[12,4,8,128]{3,2,1,0:T(8,128)S(1)} %get-tuple-element.59.refs_0_), channel_id=1, source_target_pairs={{0,1},{1,2},{2,3},{3,4},{4,5},{5,6},{6,7},{7,8},{8,9},{9,10},{10,1... | collective-permute-start | bytes 589832 | tf_op jit(solution)/shard_map/ppermute | solution.py:322
  22.0 5.2 %collective-permute-start.4 = (f32[12,4,8,128]{3,2,1,0:T(8,128)S(1)}, f32[12,4,8,128]{3,2,1,0:T(8,128)S(1)}, u32[]{:S(2)}, u32[]{:S(2)}) collective-permute-start(f32[12,4,8,128]{3,2,1,0:T(8,128)S(1)} %get-tuple-element.60), channel_id=1, source_target_pairs={{1,0},{2,1},{3,2},{4,3},{5,4},{6,5},{7,6},{8,7},{9,8},{10,9},{11,1... | collective-permute-start | bytes 589832 | tf_op jit(solution)/shard_map/ppermute | solution.py:322
  27.2 2.7 %collective-permute-done.3.refs_1_ = f32[12,4,8,128]{3,2,1,0:T(8,128)S(1)} collective-permute-done((f32[12,4,8,128]{3,2,1,0:T(8,128)S(1)}, f32[12,4,8,128]{3,2,1,0:T(8,128)S(1)}, u32[]{:S(2)}, u32[]{:S(2)}) %collective-permute-start.3) | collective-permute-done | bytes 196640 | tf_op jit(solution)/shard_map/ppermute | solution.py:322
  29.9 1.8 collective-permute-done.4.refs_2_
  32.1 3.4 %collective-permute-start.5 = (f32[8,4,8,128]{3,2,1,0:T(8,128)S(1)}, f32[8,4,8,128]{3,2,1,0:T(8,128)S(1)}, u32[]{:S(2)}, u32[]{:S(2)}) collective-permute-start(f32[8,4,8,128]{3,2,1,0:T(8,128)S(1)} %get-tuple-element.63.refs_0_), channel_id=1, source_target_pairs={{0,1},{1,2},{2,3},{3,4},{4,5},{5,6},{6,7},{7,8},{8,9},{9,10},{10,1... | collective-permute-start | bytes 393224 | tf_op jit(solution)/shard_map/ppermute | solution.py:322
  35.5 4.5 %collective-permute-start.6 = (f32[8,4,8,128]{3,2,1,0:T(8,128)S(1)}, f32[8,4,8,128]{3,2,1,0:T(8,128)S(1)}, u32[]{:S(2)}, u32[]{:S(2)}) collective-permute-start(f32[8,4,8,128]{3,2,1,0:T(8,128)S(1)} %get-tuple-element.63.refs_0_), channel_id=1, source_target_pairs={{1,0},{2,1},{3,2},{4,3},{5,4},{6,5},{7,6},{8,7},{9,8},{10,9},{11,1... | collective-permute-start | bytes 393224 | tf_op jit(solution)/shard_map/ppermute | solution.py:322
  40.0 4.6 %collective-permute-start.9 = (f32[3,4,4,8,128]{4,3,2,1,0:T(8,128)S(1)}, f32[3,4,4,8,128]{4,3,2,1,0:T(8,128)S(1)}, u32[]{:S(2)}, u32[]{:S(2)}) collective-permute-start(f32[3,4,4,8,128]{4,3,2,1,0:T(8,128)S(1)} %pad_maximum_fusion.1), channel_id=1, source_target_pairs={{32,96},{33,97},{34,98},{35,99},{36,100},{37,101},{38,102},{39,103... | collective-permute-start | bytes 589832 | tf_op jit(solution)/shard_map/ppermute | solution.py:322
  45.1 1.9 %collective-permute-start.7 = (f32[8,4,8,128]{3,2,1,0:T(8,128)S(1)}, f32[8,4,8,128]{3,2,1,0:T(8,128)S(1)}, u32[]{:S(2)}, u32[]{:S(2)}) collective-permute-start(f32[8,4,8,128]{3,2,1,0:T(8,128)S(1)} %get-tuple-element.66.refs_0_), channel_id=1, source_target_pairs={{0,1},{1,2},{2,3},{3,4},{4,5},{5,6},{6,7},{7,8},{8,9},{9,10},{10,1... | collective-permute-start | bytes 393224 | tf_op jit(solution)/shard_map/ppermute | solution.py:322
  47.0 5.5 %collective-permute-start.8 = (f32[8,4,8,128]{3,2,1,0:T(8,128)S(1)}, f32[8,4,8,128]{3,2,1,0:T(8,128)S(1)}, u32[]{:S(2)}, u32[]{:S(2)}) collective-permute-start(f32[8,4,8,128]{3,2,1,0:T(8,128)S(1)} %get-tuple-element.66.refs_0_), channel_id=1, source_target_pairs={{1,0},{2,1},{3,2},{4,3},{5,4},{6,5},{7,6},{8,7},{9,8},{10,9},{11,1... | collective-permute-start | bytes 393224 | tf_op jit(solution)/shard_map/ppermute | solution.py:322
  52.5 1.9 %collective-permute-done.7.refs_1_ = f32[8,4,8,128]{3,2,1,0:T(8,128)S(1)} collective-permute-done((f32[8,4,8,128]{3,2,1,0:T(8,128)S(1)}, f32[8,4,8,128]{3,2,1,0:T(8,128)S(1)}, u32[]{:S(2)}, u32[]{:S(2)}) %collective-permute-start.7) | collective-permute-done | bytes 131104 | tf_op jit(solution)/shard_map/ppermute | solution.py:322
  57.9 1.9 %collective-permute-start.11 = (f32[3,4,8,128]{3,2,1,0:T(8,128)S(1)}, f32[3,4,8,128]{3,2,1,0:T(8,128)S(1)}, u32[]{:S(2)}, u32[]{:S(2)}) collective-permute-start(f32[3,4,8,128]{3,2,1,0:T(8,128)S(1)} %slice.142), channel_id=1, source_target_pairs={{32,33},{33,34},{34,35},{35,36},{36,37},{37,38},{38,39},{39,40},{4... | collective-permute-start | bytes 147464 | tf_op jit(solution)/shard_map/ppermute | solution.py:322
  59.9 6.2 %collective-permute-start.12 = (f32[3,4,8,128]{3,2,1,0:T(8,128)S(1)}, f32[3,4,8,128]{3,2,1,0:T(8,128)S(1)}, u32[]{:S(2)}, u32[]{:S(2)}) collective-permute-start(f32[3,4,8,128]{3,2,1,0:T(8,128)S(1)} %slice.142), channel_id=1, source_target_pairs={{33,32},{34,33},{35,34},{36,35},{37,36},{38,37},{39,38},{40,39},{4... | collective-permute-start | bytes 147464 | tf_op jit(solution)/shard_map/ppermute | solution.py:322
  66.1 1.3 collective-permute-start.13
  67.4 1.3 collective-permute-start.14
  68.8 4.9 %collective-permute-done.13.el = f32[3,4,8,128]{3,2,1,0:T(8,128)S(1)} collective-permute-done((f32[3,4,8,128]{3,2,1,0:T(8,128)S(1)}, f32[3,4,8,128]{3,2,1,0:T(8,128)S(1)}, u32[]{:S(2)}, u32[]{:S(2)}) %collective-permute-start.13) | collective-permute-done | bytes 49184 | tf_op jit(solution)/shard_map/ppermute | solution.py:322
  77.9 1.3 collective-permute-start.20
  90.9 20.8 %collective-permute-done.31.refs_5_ = f32[3,4,8,128]{3,2,1,0:T(8,128)S(1)} collective-permute-done((f32[3,4,8,128]{3,2,1,0:T(8,128)S(1)}, f32[3,4,8,128]{3,2,1,0:T(8,128)S(1)}, u32[]{:S(2)}, u32[]{:S(2)}) %collective-permute-start.31) | collective-permute-done | bytes 49184 | tf_op jit(solution)/shard_map/ppermute | solution.py:322
  112.2 3.7 %collective-permute-done.29.refs_3_ = f32[11,4,8,128]{3,2,1,0:T(8,128)S(1)} collective-permute-done((f32[11,4,8,128]{3,2,1,0:T(8,128)S(1)}, f32[11,4,8,128]{3,2,1,0:T(8,128)S(1)}, u32[]{:S(2)}, u32[]{:S(2)}) %collective-permute-start.29) | collective-permute-done | bytes 180256 | tf_op jit(solution)/shard_map/ppermute | solution.py:322
  124.4 1.3 collective-permute-start.44
  125.7 6.7 %collective-permute-done.44.refs_21_ = f32[4,4,8,128]{3,2,1,0:T(8,128)S(1)} collective-permute-done((f32[4,4,8,128]{3,2,1,0:T(8,128)S(1)}, f32[4,4,8,128]{3,2,1,0:T(8,128)S(1)}, u32[]{:S(2)}, u32[]{:S(2)}) %collective-permute-start.44) | collective-permute-done | bytes 65568 | tf_op jit(solution)/shard_map/ppermute | solution.py:322
  136.7 1.3 collective-permute-start.52
  138.0 1.3 collective-permute-start.51
  139.3 1.3 collective-permute-start.53
  143.2 27.6 %collective-permute-done.50.refs_1_ = f32[3,4,8,128]{3,2,1,0:T(8,128)S(1)} collective-permute-done((f32[3,4,8,128]{3,2,1,0:T(8,128)S(1)}, f32[3,4,8,128]{3,2,1,0:T(8,128)S(1)}, u32[]{:S(2)}, u32[]{:S(2)}) %collective-permute-start.50) | collective-permute-done | bytes 49184 | tf_op jit(solution)/shard_map/ppermute | solution.py:322
  170.8 5.6 %collective-permute-done.54.refs_5_ = f32[3,4,8,128]{3,2,1,0:T(8,128)S(1)} collective-permute-done((f32[3,4,8,128]{3,2,1,0:T(8,128)S(1)}, f32[3,4,8,128]{3,2,1,0:T(8,128)S(1)}, u32[]{:S(2)}, u32[]{:S(2)}) %collective-permute-start.54) | collective-permute-done | bytes 49184 | tf_op jit(solution)/shard_map/ppermute | solution.py:322
  176.4 1.8 shard_map.215
  (132 shorter events, 41.6 us)
Async XLA Ops:
  0.6 7.4 %collective-permute-start = (f32[2,4,4,8,128]{4,3,2,1,0:T(8,128)}, f32[2,4,4,8,128]{4,3,2,1,0:T(8,128)S(1)}, u32[]{:S(2)}, u32[]{:S(2)}) collective-permute-start(f32[2,4,4,8,128]{4,3,2,1,0:T(8,128)} %bitcast.68), channel_id=1, source_target_pairs={{32,0},{33,1},{34,2},{35,3},{36,4},{37,5},{38,6},{39,7},{40,8},{41... | collective-permute-start | bytes 393224 | tf_op jit(solution)/shard_map/ppermute | solution.py:322
  8.1 9.0 %collective-permute-start.1 = (f32[12,4,8,128]{3,2,1,0:T(8,128)S(1)}, f32[12,4,8,128]{3,2,1,0:T(8,128)S(1)}, u32[]{:S(2)}, u32[]{:S(2)}) collective-permute-start(f32[12,4,8,128]{3,2,1,0:T(8,128)S(1)} %pad_maximum_fusion.refs_0_.refs_6_), channel_id=1, source_target_pairs={{0,1},{1,2},{2,3},{3,4},{4,5},{5,6},{6,7},{7,8},{8,9},{9,10},{10,1... | collective-permute-start | bytes 589832 | tf_op jit(solution)/shard_map/ppermute | solution.py:322
  11.3 7.7 %collective-permute-start.2 = (f32[12,4,8,128]{3,2,1,0:T(8,128)S(1)}, f32[12,4,8,128]{3,2,1,0:T(8,128)S(1)}, u32[]{:S(2)}, u32[]{:S(2)}) collective-permute-start(f32[12,4,8,128]{3,2,1,0:T(8,128)S(1)} %pad_maximum_fusion.refs_0_.refs_6_), channel_id=1, source_target_pairs={{1,0},{2,1},{3,2},{4,3},{5,4},{6,5},{7,6},{8,7},{9,8},{10,9},{11,1... | collective-permute-start | bytes 589832 | tf_op jit(solution)/shard_map/ppermute | solution.py:322
  19.3 10.6 %collective-permute-start.3 = (f32[12,4,8,128]{3,2,1,0:T(8,128)S(1)}, f32[12,4,8,128]{3,2,1,0:T(8,128)S(1)}, u32[]{:S(2)}, u32[]{:S(2)}) collective-permute-start(f32[12,4,8,128]{3,2,1,0:T(8,128)S(1)} %get-tuple-element.59.refs_0_), channel_id=1, source_target_pairs={{0,1},{1,2},{2,3},{3,4},{4,5},{5,6},{6,7},{7,8},{8,9},{9,10},{10,1... | collective-permute-start | bytes 589832 | tf_op jit(solution)/shard_map/ppermute | solution.py:322
  22.0 9.7 %collective-permute-start.4 = (f32[12,4,8,128]{3,2,1,0:T(8,128)S(1)}, f32[12,4,8,128]{3,2,1,0:T(8,128)S(1)}, u32[]{:S(2)}, u32[]{:S(2)}) collective-permute-start(f32[12,4,8,128]{3,2,1,0:T(8,128)S(1)} %get-tuple-element.60), channel_id=1, source_target_pairs={{1,0},{2,1},{3,2},{4,3},{5,4},{6,5},{7,6},{8,7},{9,8},{10,9},{11,1... | collective-permute-start | bytes 589832 | tf_op jit(solution)/shard_map/ppermute | solution.py:322
  32.1 12.6 %collective-permute-start.5 = (f32[8,4,8,128]{3,2,1,0:T(8,128)S(1)}, f32[8,4,8,128]{3,2,1,0:T(8,128)S(1)}, u32[]{:S(2)}, u32[]{:S(2)}) collective-permute-start(f32[8,4,8,128]{3,2,1,0:T(8,128)S(1)} %get-tuple-element.63.refs_0_), channel_id=1, source_target_pairs={{0,1},{1,2},{2,3},{3,4},{4,5},{5,6},{6,7},{7,8},{8,9},{9,10},{10,1... | collective-permute-start | bytes 393224 | tf_op jit(solution)/shard_map/ppermute | solution.py:322
  35.5 9.2 %collective-permute-start.6 = (f32[8,4,8,128]{3,2,1,0:T(8,128)S(1)}, f32[8,4,8,128]{3,2,1,0:T(8,128)S(1)}, u32[]{:S(2)}, u32[]{:S(2)}) collective-permute-start(f32[8,4,8,128]{3,2,1,0:T(8,128)S(1)} %get-tuple-element.63.refs_0_), channel_id=1, source_target_pairs={{1,0},{2,1},{3,2},{4,3},{5,4},{6,5},{7,6},{8,7},{9,8},{10,9},{11,1... | collective-permute-start | bytes 393224 | tf_op jit(solution)/shard_map/ppermute | solution.py:322
  40.0 12.5 %collective-permute-start.9 = (f32[3,4,4,8,128]{4,3,2,1,0:T(8,128)S(1)}, f32[3,4,4,8,128]{4,3,2,1,0:T(8,128)S(1)}, u32[]{:S(2)}, u32[]{:S(2)}) collective-permute-start(f32[3,4,4,8,128]{4,3,2,1,0:T(8,128)S(1)} %pad_maximum_fusion.1), channel_id=1, source_target_pairs={{32,96},{33,97},{34,98},{35,99},{36,100},{37,101},{38,102},{39,103... | collective-permute-start | bytes 589832 | tf_op jit(solution)/shard_map/ppermute | solution.py:322
  45.1 9.4 %collective-permute-start.7 = (f32[8,4,8,128]{3,2,1,0:T(8,128)S(1)}, f32[8,4,8,128]{3,2,1,0:T(8,128)S(1)}, u32[]{:S(2)}, u32[]{:S(2)}) collective-permute-start(f32[8,4,8,128]{3,2,1,0:T(8,128)S(1)} %get-tuple-element.66.refs_0_), channel_id=1, source_target_pairs={{0,1},{1,2},{2,3},{3,4},{4,5},{5,6},{6,7},{7,8},{8,9},{9,10},{10,1... | collective-permute-start | bytes 393224 | tf_op jit(solution)/shard_map/ppermute | solution.py:322
  47.0 8.6 %collective-permute-start.8 = (f32[8,4,8,128]{3,2,1,0:T(8,128)S(1)}, f32[8,4,8,128]{3,2,1,0:T(8,128)S(1)}, u32[]{:S(2)}, u32[]{:S(2)}) collective-permute-start(f32[8,4,8,128]{3,2,1,0:T(8,128)S(1)} %get-tuple-element.66.refs_0_), channel_id=1, source_target_pairs={{1,0},{2,1},{3,2},{4,3},{5,4},{6,5},{7,6},{8,7},{9,8},{10,9},{11,1... | collective-permute-start | bytes 393224 | tf_op jit(solution)/shard_map/ppermute | solution.py:322
  56.6 17.0 %collective-permute-start.10 = (f32[5,4,4,8,128]{4,3,2,1,0:T(8,128)S(1)}, f32[5,4,4,8,128]{4,3,2,1,0:T(8,128)S(1)}, u32[]{:S(2)}, u32[]{:S(2)}) collective-permute-start(f32[5,4,4,8,128]{4,3,2,1,0:T(8,128)S(1)} %get-tuple-element.69), channel_id=1, source_target_pairs={{0,32},{1,33},{2,34},{3,35},{4,36},{5,37},{6,38},{7,39},{8,40},{9,... | collective-permute-start | bytes 983048 | tf_op jit(solution)/shard_map/ppermute | solution.py:322
  57.9 10.8 %collective-permute-start.11 = (f32[3,4,8,128]{3,2,1,0:T(8,128)S(1)}, f32[3,4,8,128]{3,2,1,0:T(8,128)S(1)}, u32[]{:S(2)}, u32[]{:S(2)}) collective-permute-start(f32[3,4,8,128]{3,2,1,0:T(8,128)S(1)} %slice.142), channel_id=1, source_target_pairs={{32,33},{33,34},{34,35},{35,36},{36,37},{37,38},{38,39},{39,40},{4... | collective-permute-start | bytes 147464 | tf_op jit(solution)/shard_map/ppermute | solution.py:322
  59.9 8.9 %collective-permute-start.12 = (f32[3,4,8,128]{3,2,1,0:T(8,128)S(1)}, f32[3,4,8,128]{3,2,1,0:T(8,128)S(1)}, u32[]{:S(2)}, u32[]{:S(2)}) collective-permute-start(f32[3,4,8,128]{3,2,1,0:T(8,128)S(1)} %slice.142), channel_id=1, source_target_pairs={{33,32},{34,33},{35,34},{36,35},{37,36},{38,37},{39,38},{40,39},{4... | collective-permute-start | bytes 147464 | tf_op jit(solution)/shard_map/ppermute | solution.py:322
  66.1 7.5 %collective-permute-start.13 = (f32[3,4,8,128]{3,2,1,0:T(8,128)S(1)}, f32[3,4,8,128]{3,2,1,0:T(8,128)S(1)}, u32[]{:S(2)}, u32[]{:S(2)}) collective-permute-start(f32[3,4,8,128]{3,2,1,0:T(8,128)S(1)} %slice.142), channel_id=1, source_target_pairs={{0,33},{1,34},{2,35},{3,36},{4,37},{5,38},{6,39},{7,40},{8,41},{9,... | collective-permute-start | bytes 147464 | tf_op jit(solution)/shard_map/ppermute | solution.py:322
  67.4 6.2 %collective-permute-start.14 = (f32[3,4,8,128]{3,2,1,0:T(8,128)S(1)}, f32[3,4,8,128]{3,2,1,0:T(8,128)S(1)}, u32[]{:S(2)}, u32[]{:S(2)}) collective-permute-start(f32[3,4,8,128]{3,2,1,0:T(8,128)S(1)} %slice.142), channel_id=1, source_target_pairs={{1,32},{2,33},{3,34},{4,35},{5,36},{6,37},{7,38},{8,39},{9,40},{10... | collective-permute-start | bytes 147464 | tf_op jit(solution)/shard_map/ppermute | solution.py:322
  74.4 3.4 %collective-permute-start.19 = (f32[3,4,8,128]{3,2,1,0:T(8,128)S(1)}, f32[3,4,8,128]{3,2,1,0:T(8,128)S(1)}, u32[]{:S(2)}, u32[]{:S(2)}) collective-permute-start(f32[3,4,8,128]{3,2,1,0:T(8,128)S(1)} %get-tuple-element.73), channel_id=1, source_target_pairs={{226,160},{227,161},{228,162},{229,163},{230,164},{231,165},{232,1... | collective-permute-start | bytes 147464 | tf_op jit(solution)/shard_map/ppermute | solution.py:322
  75.1 2.7 %collective-permute-start.16 = (f32[6,4,8,128]{3,2,1,0:T(8,128)S(1)}, f32[6,4,8,128]{3,2,1,0:T(8,128)S(1)}, u32[]{:S(2)}, u32[]{:S(2)}) collective-permute-start(f32[6,4,8,128]{3,2,1,0:T(8,128)S(1)} %get-tuple-element.74), channel_id=1, source_target_pairs={{224,161},{225,162},{226,163},{227,164},{228,165},{229,166},{230,1... | collective-permute-start | bytes 294920 | tf_op jit(solution)/shard_map/ppermute | solution.py:322
  80.1 3.4 %collective-permute-start.25 = (f32[3,4,8,128]{3,2,1,0:T(8,128)S(1)}, f32[3,4,8,128]{3,2,1,0:T(8,128)S(1)}, u32[]{:S(2)}, u32[]{:S(2)}) collective-permute-start(f32[3,4,8,128]{3,2,1,0:T(8,128)S(1)} %get-tuple-element.79), channel_id=1, source_target_pairs={{162,96},{163,97},{164,98},{165,99},{166,100},{167,101},{168,102},... | collective-permute-start | bytes 147464 | tf_op jit(solution)/shard_map/ppermute | solution.py:322
  84.4 27.3 %collective-permute-start.31 = (f32[3,4,8,128]{3,2,1,0:T(8,128)S(1)}, f32[3,4,8,128]{3,2,1,0:T(8,128)S(1)}, u32[]{:S(2)}, u32[]{:S(2)}) collective-permute-start(f32[3,4,8,128]{3,2,1,0:T(8,128)S(1)} %get-tuple-element.85), channel_id=1, source_target_pairs={{98,32},{99,33},{100,34},{101,35},{102,36},{103,37},{104,38},{105,... | collective-permute-start | bytes 147464 | tf_op jit(solution)/shard_map/ppermute | solution.py:322
  85.7 26.1 %collective-permute-start.28 = (f32[6,4,8,128]{3,2,1,0:T(8,128)S(1)}, f32[6,4,8,128]{3,2,1,0:T(8,128)S(1)}, u32[]{:S(2)}, u32[]{:S(2)}) collective-permute-start(f32[6,4,8,128]{3,2,1,0:T(8,128)S(1)} %get-tuple-element.86), channel_id=1, source_target_pairs={{96,33},{97,34},{98,35},{99,36},{100,37},{101,38},{102,39},{103,40... | collective-permute-start | bytes 294920 | tf_op jit(solution)/shard_map/ppermute | solution.py:322
  87.0 25.2 %collective-permute-start.30 = (f32[6,4,8,128]{3,2,1,0:T(8,128)S(1)}, f32[6,4,8,128]{3,2,1,0:T(8,128)S(1)}, u32[]{:S(2)}, u32[]{:S(2)}) collective-permute-start(f32[6,4,8,128]{3,2,1,0:T(8,128)S(1)} %get-tuple-element.86), channel_id=1, source_target_pairs={{97,32},{98,33},{99,34},{100,35},{101,36},{102,37},{103,38},{104,3... | collective-permute-start | bytes 294920 | tf_op jit(solution)/shard_map/ppermute | solution.py:322
  88.3 23.4 %collective-permute-start.27 = (f32[3,4,8,128]{3,2,1,0:T(8,128)S(1)}, f32[3,4,8,128]{3,2,1,0:T(8,128)S(1)}, u32[]{:S(2)}, u32[]{:S(2)}) collective-permute-start(f32[3,4,8,128]{3,2,1,0:T(8,128)S(1)} %get-tuple-element.85), channel_id=1, source_target_pairs={{96,34},{97,35},{98,36},{99,37},{100,38},{101,39},{102,40},{103,41... | collective-permute-start | bytes 147464 | tf_op jit(solution)/shard_map/ppermute | solution.py:322
  89.6 26.3 %collective-permute-start.29 = (f32[11,4,8,128]{3,2,1,0:T(8,128)S(1)}, f32[11,4,8,128]{3,2,1,0:T(8,128)S(1)}, u32[]{:S(2)}, u32[]{:S(2)}) collective-permute-start(f32[11,4,8,128]{3,2,1,0:T(8,128)S(1)} %get-tuple-element.87), channel_id=1, source_target_pairs={{96,32},{97,33},{98,34},{99,35},{100,36},{101,37},{102,38},{103,39... | collective-permute-start | bytes 540680 | tf_op jit(solution)/shard_map/ppermute | solution.py:322
  116.6 3.4 %collective-permute-start.37 = (f32[3,4,8,128]{3,2,1,0:T(8,128)S(1)}, f32[3,4,8,128]{3,2,1,0:T(8,128)S(1)}, u32[]{:S(2)}, u32[]{:S(2)}) collective-permute-start(f32[3,4,8,128]{3,2,1,0:T(8,128)S(1)} %get-tuple-element.91), channel_id=1, source_target_pairs={{290,224},{291,225},{292,226},{293,227},{294,228},{295,229},{296,2... | collective-permute-start | bytes 147464 | tf_op jit(solution)/shard_map/ppermute | solution.py:322
  120.9 3.4 %collective-permute-start.39 = (f32[3,4,8,128]{3,2,1,0:T(8,128)S(1)}, f32[3,4,8,128]{3,2,1,0:T(8,128)S(1)}, u32[]{:S(2)}, u32[]{:S(2)}) collective-permute-start(f32[3,4,8,128]{3,2,1,0:T(8,128)S(1)} %get-tuple-element.97), channel_id=1, source_target_pairs={{224,162},{225,163},{226,164},{227,165},{228,166},{229,167},{230,1... | collective-permute-start | bytes 147464 | tf_op jit(solution)/shard_map/ppermute | solution.py:322
  124.4 8.0 %collective-permute-start.44 = (f32[4,4,8,128]{3,2,1,0:T(8,128)S(1)}, f32[4,4,8,128]{3,2,1,0:T(8,128)S(1)}, u32[]{:S(2)}, u32[]{:S(2)}) collective-permute-start(f32[4,4,8,128]{3,2,1,0:T(8,128)S(1)} %get-tuple-element.132), channel_id=1, source_target_pairs={{0,32},{1,33},{2,34},{3,35},{4,36},{5,37},{6,38},{7,39},{8,40},{9,... | collective-permute-start | bytes 196616 | tf_op jit(solution)/shard_map/ppermute | solution.py:322
  133.2 3.4 %collective-permute-start.47 = (f32[11,4,8,128]{3,2,1,0:T(8,128)S(1)}, f32[11,4,8,128]{3,2,1,0:T(8,128)S(1)}, u32[]{:S(2)}, u32[]{:S(2)}) collective-permute-start(f32[11,4,8,128]{3,2,1,0:T(8,128)S(1)} %get-tuple-element.105), channel_id=1, source_target_pairs={{160,96},{161,97},{162,98},{163,99},{164,100},{165,101},{166,102},... | collective-permute-start | bytes 540680 | tf_op jit(solution)/shard_map/ppermute | solution.py:322
  136.7 39.7 %collective-permute-start.52 = (f32[11,4,8,128]{3,2,1,0:T(8,128)S(1)}, f32[11,4,8,128]{3,2,1,0:T(8,128)S(1)}, u32[]{:S(2)}, u32[]{:S(2)}) collective-permute-start(f32[11,4,8,128]{3,2,1,0:T(8,128)S(1)} %get-tuple-element.110), channel_id=1, source_target_pairs={{96,32},{97,33},{98,34},{99,35},{100,36},{101,37},{102,38},{103,39... | collective-permute-start | bytes 540680 | tf_op jit(solution)/shard_map/ppermute | solution.py:322
  138.0 38.4 %collective-permute-start.51 = (f32[6,4,8,128]{3,2,1,0:T(8,128)S(1)}, f32[6,4,8,128]{3,2,1,0:T(8,128)S(1)}, u32[]{:S(2)}, u32[]{:S(2)}) collective-permute-start(f32[6,4,8,128]{3,2,1,0:T(8,128)S(1)} %get-tuple-element.109), channel_id=1, source_target_pairs={{96,33},{97,34},{98,35},{99,36},{100,37},{101,38},{102,39},{103,40... | collective-permute-start | bytes 294920 | tf_op jit(solution)/shard_map/ppermute | solution.py:322
  139.3 37.1 %collective-permute-start.53 = (f32[6,4,8,128]{3,2,1,0:T(8,128)S(1)}, f32[6,4,8,128]{3,2,1,0:T(8,128)S(1)}, u32[]{:S(2)}, u32[]{:S(2)}) collective-permute-start(f32[6,4,8,128]{3,2,1,0:T(8,128)S(1)} %get-tuple-element.109), channel_id=1, source_target_pairs={{97,32},{98,33},{99,34},{100,35},{101,36},{102,37},{103,38},{104,3... | collective-permute-start | bytes 294920 | tf_op jit(solution)/shard_map/ppermute | solution.py:322
  140.6 30.2 %collective-permute-start.50 = (f32[3,4,8,128]{3,2,1,0:T(8,128)S(1)}, f32[3,4,8,128]{3,2,1,0:T(8,128)S(1)}, u32[]{:S(2)}, u32[]{:S(2)}) collective-permute-start(f32[3,4,8,128]{3,2,1,0:T(8,128)S(1)} %get-tuple-element.108), channel_id=1, source_target_pairs={{96,34},{97,35},{98,36},{99,37},{100,38},{101,39},{102,40},{103,41... | collective-permute-start | bytes 147464 | tf_op jit(solution)/shard_map/ppermute | solution.py:322
  141.9 34.5 %collective-permute-start.54 = (f32[3,4,8,128]{3,2,1,0:T(8,128)S(1)}, f32[3,4,8,128]{3,2,1,0:T(8,128)S(1)}, u32[]{:S(2)}, u32[]{:S(2)}) collective-permute-start(f32[3,4,8,128]{3,2,1,0:T(8,128)S(1)} %get-tuple-element.108), channel_id=1, source_target_pairs={{98,32},{99,33},{100,34},{101,35},{102,36},{103,37},{104,38},{105,... | collective-permute-start | bytes 147464 | tf_op jit(solution)/shard_map/ppermute | solution.py:322
  (29 other events, 43.9 us)

commit v5 on v4

v5 whole, which is shorter than its diff:
```python
import jax
import jax.numpy as jnp
from jax import lax
from jax.experimental import pallas as pl
from jax.experimental.pallas import tpu as pltpu
from jax.sharding import PartitionSpec as P

SWEEPS = 4
FIELDS = 4
WIDTH = 4

diffusion = (2.4, 1.2, 0.6, 4.0)
fibre_weight = 128.0
reaction = (
    (-14.4, 7.2, -4.8, 2.4),
    (4.8, -19.2, 7.2, -4.8),
    (-7.2, 2.4, -12.0, 7.2),
    (4.8, -7.2, 2.4, -38.4),
)
self_rates = (-14.4, -19.2, -12.0, -38.4)
masses = (1.0, 1.0, 1.0, 0.0)
fine_rate = 3.0
coarse_rate = 0.75
time_step = 0.5
operator_scale = 0.0078125
state_weight = 0.1
gain_weight = 0.25

AXES = ("tm", "space")
SLAB = (FIELDS, WIDTH, 8, 128)


def column(values):
    return jnp.array(values, jnp.float32).reshape(4, 1, 1, 1)


def make_diagonal(state, source_gain, rate):
    stencil_total = (2.0 * fibre_weight + 4.0) * column(diffusion)
    spatial = operator_scale * (stencil_total - column(self_rates))
    return (
        rate * column(masses) + spatial + state_weight * state * state - gain_weight * source_gain
    )


class Stencil:
    def __init__(self):
        row = lax.broadcasted_iota(jnp.int32, (8, 128), 0)
        lane = lax.broadcasted_iota(jnp.int32, (8, 128), 1)
        self.first_row, self.last_row = row == 0, row == 7
        self.first_lane, self.last_lane = lane == 0, lane == 127

    def cross(self, cell):
        rows = jnp.where(self.first_row, 0.0, pltpu.roll(cell, 1, 0)) + jnp.where(
            self.last_row, 0.0, pltpu.roll(cell, 7, 0)
        )
        lanes = jnp.where(self.first_lane, 0.0, pltpu.roll(cell, 1, 1)) + jnp.where(
            self.last_lane, 0.0, pltpu.roll(cell, 127, 1)
        )
        return rows + lanes

    def sweep(self, below, here, above, start, inverse):
        fresh = []
        for f in range(FIELDS):
            spread = (operator_scale * fibre_weight * diffusion[f]) * (below[f] + above[f])
            spread = spread + (operator_scale * diffusion[f]) * self.cross(here[f])
            for g in range(FIELDS):
                if g != f:
                    spread = spread + (operator_scale * reaction[g][f]) * here[g]
            fresh.append(start[f] + inverse[f] * spread)
        return fresh


def solve(stencil, right, inverse, lowest, slabs, count, scratch, emit):
    base, ping, pong = scratch
    cut = [lax.rem(lowest + (slabs + at), slabs) == 0 for at in range(count)]
    count = count * WIDTH
    for layer in range(count):
        for f in range(FIELDS):
            value = right(f, layer)
            if value is None:
                base[f, layer] = jnp.zeros((8, 128), jnp.float32)
            else:
                base[f, layer] = value * inverse(f, layer)
    source = base
    for sweep in range(1, SWEEPS + 1):
        target = ping if sweep % 2 else pong
        for layer in range(sweep, count - sweep):
            below, here, above = (
                [source[f, layer + shift] for f in range(FIELDS)] for shift in (-1, 0, 1)
            )
            if layer % WIDTH == 0:
                below = [jnp.where(cut[layer // WIDTH], 0.0, cell) for cell in below]
            if layer % WIDTH == WIDTH - 1:
                above = [jnp.where(cut[layer // WIDTH + 1], 0.0, cell) for cell in above]
            start = [base[f, layer] for f in range(FIELDS)]
            factor = [inverse(f, layer) for f in range(FIELDS)]
            fresh = stencil.sweep(below, here, above, start, factor)
            if sweep == SWEEPS:
                emit(layer - SWEEPS, fresh)
            else:
                for f in range(FIELDS):
                    target[f, layer] = fresh[f]
        source = target


def layers_of(pieces):
    return lambda f, layer: pieces[layer // WIDTH][f, layer % WIDTH]


def masses_only(pieces):
    read = layers_of(pieces)
    return lambda f, layer: read(f, layer) if masses[f] else None


def vmem(shape):
    return pltpu.VMEM(shape, jnp.float32)


def call(body, outs, *operands, smem=0, layers=0, flops=0):
    spec = pl.BlockSpec(memory_space=pltpu.VMEM)
    return pl.pallas_call(
        body,
        in_specs=[pl.BlockSpec(memory_space=pltpu.SMEM)] * smem + [spec] * (len(operands) - smem),
        out_specs=[spec] * len(outs),
        out_shape=[jax.ShapeDtypeStruct(shape, jnp.float32) for shape in outs],
        scratch_shapes=[vmem((FIELDS, layers, 8, 128))] * 3,
        compiler_params=pltpu.CompilerParams(vmem_limit_bytes=24 * 1024 * 1024),
        cost_estimate=pl.CostEstimate(flops=flops, bytes_accessed=1 << 20, transcendentals=0),
    )(*operands)


def fine_step(step, place, slabs, own, low, high, states, previous, total, source=None, factor=None, coarse=None):
    first, second, last = total is None, step == 2, step == 0

    def body(*refs):
        refs = list(refs)
        spot = refs.pop(0)
        r0, rl, rh, u, prev = [refs.pop(0) for _ in range(5)]
        src, inv = (None, None) if last else [refs.pop(0) for _ in range(2)]
        factors = [refs.pop(0) for _ in range(5)][:4] if last else None
        old = None if first else refs.pop(0)
        out = None if last else refs.pop(0)
        grad, more, scratch = refs[0], refs[1:-3], refs[-3:]
        stencil = Stencil()
        pieces = [rl, r0, rh]

        def inverse(f, layer):
            return pieces[layer // WIDTH][FIELDS + f, layer % WIDTH]

        def emit(layer, x):
            for f in range(FIELDS):
                if not last:
                    out[f, layer] = x[f]
                term = x[f] * u[f, layer]
                grad[f, layer] = term if first else old[f, layer] + term
                if not last:
                    r = src[f, layer]
                    if masses[f]:
                        r = r + (4.0 * x[f] - prev[f, layer])
                    for part in more:
                        part[f, layer] = r
                else:
                    z7, pack = more
                    z7[3 + f, layer] = x[f]
                    pack[0, f, layer] = x[f]
                    pack[1, f, layer] = prev[f, layer]
                    if masses[f]:
                        z7[f, layer] = x[f] - 0.25 * prev[f, layer]

        if last:
            for place in range(4):
                more[1][2 + place] = factors[place][2 * FIELDS :]
        else:
            for part in more:
                part[FIELDS : 2 * FIELDS] = inv[...]
        if first:
            more[0][2 * FIELDS :] = rl[2 * FIELDS :]
        if first or second:
            more[1][2 * FIELDS :] = rh[2 * FIELDS :]
        solve(stencil, layers_of(pieces), inverse, spot[1] - 1, slabs, 3, scratch, emit)

    operands = [place, own, low, high, states, previous]
    operands += list(coarse) if last else [source, factor]
    operands += [] if first else [total]
    outs = [SLAB, carry(7), (6,) + SLAB] if last else [SLAB, SLAB]
    outs += [] if last else [carry(12)] * 2 if first else [carry(8), carry(12)] if second else [carry(8)]
    return call(body, outs, *operands, smem=1, layers=3 * WIDTH, flops=28 * 4 * 1024 * 20)


def carry(count):
    return (count, WIDTH, 8, 128)


def offsets_step(place, slabs, even, four, prior):
    def body(spot, pack, z0, z1, z2, z3, before, own, ahead, *scratch):
        stencil = Stencil()
        z = [z0, z1, z2, z3]

        def emit_to(target):
            def emit(layer, q):
                for f in range(FIELDS):
                    target[f, layer] = q[f]

            return emit

        inv_own = lambda f, layer: pack[2 + layer // WIDTH, f, layer % WIDTH]
        inv_before = lambda f, layer: before[layer // WIDTH, f, layer % WIDTH]
        z_own = [part.at[0:3] for part in z]
        z_even = [part.at[3:6] for part in z]
        lowest = spot[1] - 1
        solve(stencil, masses_only(z_own), inv_own, lowest, slabs, 4, scratch, emit_to(own))
        solve(stencil, masses_only(z_even), inv_before, lowest, slabs, 4, scratch, emit_to(ahead))

    wide = (FIELDS, 2 * WIDTH, 8, 128)
    operands = (place, even, *four, prior)
    return call(body, [wide, wide], *operands, smem=1, layers=4 * WIDTH, flops=88 * 4 * 1024 * 20)


def chip_step(turn, place, slabs, arrived, inv_six, even, four, pair, own, ahead, done, grad):
    with_done, with_grad, with_z = done is not None, grad is not None, arrived is not None

    def body(*refs):
        refs = list(refs)
        take = lambda count: [refs.pop(0) for _ in range(count)]
        (spot,) = take(1)
        za, zb, zc = take(3) if with_z else [None] * 3
        iv = take(6)
        (pack,) = take(1)
        zr = take(4)
        z7, x1, qe, qa = take(4)
        before = take(2) if with_done else None
        g = take(2) if with_grad else None
        up, down, straight, odd_pair, even_pair = take(5)
        sums = take(1)[0] if with_grad else None
        middle, moved, *scratch = refs
        if with_grad:
            sums[...] = g[0][...] + g[1][...]
        mine = spot[0] == turn

        @pl.when(jnp.logical_not(mine))
        def _():
            odd_pair[...] = before[0][...] if with_done else jnp.zeros_like(odd_pair)
            even_pair[...] = before[1][...] if with_done else jnp.zeros_like(even_pair)
            for part in (up, down, straight):
                part[...] = jnp.zeros_like(part)

        @pl.when(mine)
        def _():
            stencil = Stencil()
            zero = jnp.zeros((8, 128), jnp.float32)
            read = lambda ref, f, at: ref[f, at] if with_z else zero

            def emit_odd(layer, q):
                slab, at = layer // WIDTH, layer % WIDTH
                for f in range(FIELDS):
                    if slab == 1:
                        solved, change = read(zb, 6 + f, at), read(zb, 13 + f, at)
                        c0 = q[f] + (z7[3 + f, at] - solved)
                        c1 = x1[f, at] + 0.5 * ((q[f] - solved) + change)
                        odd_pair[0, f, at] = c0
                        odd_pair[1, f, at] = c1
                        if masses[f]:
                            middle[f, layer] = c0 - 0.25 * c1
                    elif masses[f] and slab == 2:
                        solved, change = read(zb, 10 + f, at), read(zb, 17 + f, at)
                        moved[f, at] = q[f] - solved
                        middle[f, layer] = zr[2][f, at] + 0.875 * (q[f] - solved) - 0.125 * change
                    elif masses[f]:
                        y = read(za if slab == 0 else zc, 6 + f, at)
                        middle[f, layer] = 0.875 * q[f] + y + zr[slab][f, at]

            def emit_even(layer, q):
                slab, at = layer // WIDTH, layer % WIDTH
                for f in range(FIELDS):
                    if slab == 0:
                        c0 = q[f] + (pack[0, f, at] - qe[f, layer])
                        c1 = 0.5 * (q[f] + odd_pair[0, f, at]) + (
                            pack[1, f, at] - 0.5 * (qe[f, layer] + z7[3 + f, at])
                        )
                        even_pair[0, f, at] = c0
                        even_pair[1, f, at] = c1
                        change, z = c0 - pack[0, f, at], c0 - 0.25 * c1
                        straight[6 + f, at] = qa[f, layer]
                        straight[13 + f, at] = change
                    elif masses[f]:
                        change = q[f] - qe[f, layer]
                        z = zr[2][3 + f, at] + 0.875 * change - 0.125 * moved[f, at]
                        straight[10 + f, at] = qa[f, layer]
                        straight[17 + f, at] = change
                    if masses[f]:
                        for part in (up, down, straight):
                            part[3 * slab + f, at] = z
                        y = -0.875 * qa[f, layer] - 0.125 * change
                        (up if slab else down)[6 + f, at] = y

            if with_z:
                z = [za.at[0:3], za.at[3:6], zb.at[0:3], zb.at[3:6], zc.at[0:3], zc.at[3:6]]
                right = masses_only(z)
            else:
                right = lambda f, layer: zero if masses[f] else None
            middle_at = lambda f, layer: middle[f, layer] if masses[f] else None
            inv_at = lambda f, layer: pack[2 + layer // WIDTH, f, layer % WIDTH]
            solve(stencil, right, layers_of(iv), spot[1] - 2, slabs, 6, scratch, emit_odd)
            solve(stencil, middle_at, inv_at, spot[1] - 1, slabs, 4, scratch, emit_even)

    spec = pl.BlockSpec(memory_space=pltpu.VMEM)
    operands = [place] + (list(arrived) if with_z else []) + list(inv_six) + [even]
    operands += list(four) + list(pair) + [own, ahead]
    operands += list(done) if with_done else []
    operands += list(grad) if with_grad else []
    outs = [carry(9), carry(9), carry(20), (2,) + SLAB, (2,) + SLAB] + ([SLAB] if with_grad else [])
    return pl.pallas_call(
        body,
        in_specs=[pl.BlockSpec(memory_space=pltpu.SMEM)] + [spec] * (len(operands) - 1),
        out_specs=[spec] * len(outs),
        out_shape=[jax.ShapeDtypeStruct(shape, jnp.float32) for shape in outs],
        scratch_shapes=[vmem((3, 4 * WIDTH, 8, 128)), vmem(carry(3))]
        + [vmem((FIELDS, 6 * WIDTH, 8, 128))] * 3,
        compiler_params=pltpu.CompilerParams(vmem_limit_bytes=24 * 1024 * 1024),
        cost_estimate=pl.CostEstimate(flops=120 * 4 * 1024 * 20, bytes_accessed=1 << 20, transcendentals=0),
    )(*operands)


def routes(times, slabs, moved, chosen=None):
    pairs = []
    for k in range(times):
        for s in range(slabs):
            target = moved(k, s)
            if target is None or (chosen is not None and not chosen(k)):
                continue
            k2, s2 = target
            if 0 <= k2 < times:
                pairs.append((k * slabs + s, k2 * slabs + s2 % slabs))
    return pairs


def send(value, pairs):
    return lax.ppermute(value, AXES, pairs)


def program(times, slabs):
    chips = times // 2

    def shift(count):
        return routes(times, slabs, lambda k, s: (k, s + count))

    right_one, left_one = shift(1), shift(-1)
    earlier = routes(times, slabs, lambda k, s: (k - 1, s))
    even_to_odd = routes(times, slabs, lambda k, s: (k + 1, s), lambda k: k % 2 == 0)
    odd_to_even = routes(times, slabs, lambda k, s: (k - 1, s), lambda k: k % 2 == 1)
    odd, even = (lambda k: k % 2 == 1), (lambda k: k % 2 == 0)
    odd_right, odd_left, odd_left_two = (
        routes(times, slabs, lambda k, s, d=d: (k, s + d), odd) for d in (1, -1, -2)
    )
    later = routes(times, slabs, lambda k, s: (k + 2, s), odd)

    def hop_routes(hop):
        sender = 2 * (chips - hop) + 1
        return [
            routes(times, slabs, lambda k, s, d=d: (k - 2, s + d), lambda k: k == sender)
            for d in (2, 0, -2)
        ]

    def on_device(forward_states, adjoint_source, source_gain, guess_pairs):
        place = jnp.stack([lax.axis_index("tm"), lax.axis_index("space")]).astype(jnp.int32)
        states = forward_states.astype(jnp.float32)
        ahead = send(guess_pairs[0], earlier)
        inverses = [1.0 / make_diagonal(states[n], source_gain, fine_rate) for n in range(4)]
        coarse = 1.0 / make_diagonal(states[0], source_gain, coarse_rate)
        right = adjoint_source[3] + column(masses) * (4.0 * ahead[0] - ahead[1])
        up = down = jnp.concatenate([right, inverses[3], coarse])
        previous, total = ahead[0], None
        exchanged = []
        for n in (3, 2, 1, 0):
            low, high = send(up, right_one), send(down, left_one)
            exchanged.append((low, up, high))
            if n == 0:
                far = [part[2 * FIELDS :] for part in (*exchanged[0], exchanged[1][2])]
                prior = send(jnp.stack(far), later)
                rest = dict(coarse=(*exchanged[0], exchanged[1][2], prior))
            else:
                rest = dict(source=adjoint_source[n - 1], factor=inverses[n - 1])
            step = fine_step(n, place, slabs, up, low, high, states[n], previous, total, **rest)
            if n:
                previous, total, up, *more = step
                down = more[0] if more else up
        total, z7, even_pack = step
        total = time_step * total
        (low, own, high), (low_two, _, high_two), (_, _, high_three) = exchanged[:3]
        inv_six = [part[2 * FIELDS :] for part in (low_two, low, own, high, high_two, high_three)]

        even_pack = send(even_pack, even_to_odd)
        both = jnp.concatenate([z7[:3], even_pack[0, :3] - 0.25 * even_pack[1, :3]])
        four = [send(both, odd_right), both, send(both, odd_left), send(both, odd_left_two)]
        solved, ahead_solved = offsets_step(place, slabs, even_pack, four, prior)

        stages = []
        far = 1
        while far < chips:
            stages.append(
                routes(times, slabs, lambda k, s, d=far: (2 * ((k // 2) ^ d), s), lambda k: k % 2 == 0)
            )
            far *= 2
        stages = [odd_to_even] + stages + [even_to_odd]
        is_even = lax.axis_index("tm") % 2 == 0
        arrived, done, grad, hop = None, None, total, 0
        while hop < chips or stages:
            added = None
            if hop and hop < chips:
                arrived = [send(part, path) for part, path in zip(payload, hop_routes(hop))]
            if hop and stages:
                received = send(grad, stages.pop(0))
                added = (grad if stages else jnp.where(is_even, grad, 0.0), received)
            if hop < chips:
                up, down, straight, odd_pair, even_pair, *sums = chip_step(
                    times - 1 - 2 * hop, place, slabs, arrived, inv_six, even_pack, four, (z7, previous),
                    solved, ahead_solved, done, added,
                )
                payload, done = (up, straight, down), (odd_pair, even_pair)
                if sums:
                    grad = sums[0]
            elif added:
                grad = added[0] + added[1]
            hop += 1

        corrected = jnp.where(is_even, send(done[1], odd_to_even), done[0])
        return corrected[None], grad

    return on_device


def solution(mesh):
    placed = (
        P("tm", None, "space", None, None),
        P("tm", None, "space", None, None),
        P(None, "space", None, None),
        P("tm", None, None, "space", None, None),
    )
    return jax.shard_map(
        program(mesh.shape["tm"], mesh.shape["space"]),
        mesh=mesh,
        in_specs=placed,
        out_specs=(P("tm", None, None, "space", None, None), P(None, "space", None, None)),
        check_vma=False,
    )
```

time: 182 us -> 199 us (1.093)
  the two profiles are of different devices: /device:TPU:17 before, /device:TPU:1 now
where the time goes in v5:
time: 199 us; the launch traced here: 198 us
  waiting for transfers between devices  107 us (54%)
  starting transfers between devices  72.8 us (37%)
  Pallas kernels  13.3 us (7%)
    ppermute x41, waiting for transfers between devices, send(): return lax.ppermute(value, AXES, pairs)  107 us
    ppermute x41, starting transfers between devices, send(): return lax.ppermute(value, AXES, pairs)  72.8 us
    pallas_call x8, Pallas kernels, chip_step(): pl.pallas_call(body, in_specs=[pl.BlockSpec(memory_space=pltpu.SMEM)] + [...  7.97 us
    pallas_call x5, Pallas kernels, call(): pl.pallas_call(body, in_specs=[pl.BlockSpec(memory_space=pltpu.SMEM)] * s...  5.33 us
  transfers between devices with their start and end apart: 41, of which 12 were waited for; matrix products, arithmetic and copies ran while one was open for 1% of the time, Pallas kernels for 0%

profile of v5, /device:TPU:1, one launch (start us, length us, event | category | flops | bytes accessed | tf_op | source)
XLA Modules:
  0.0 198.0 jit_solution(5829284867816127945)
XLA Ops:
  0.6 8.9 %collective-permute-start = (f32[2,4,4,8,128]{4,3,2,1,0:T(8,128)}, f32[2,4,4,8,128]{4,3,2,1,0:T(8,128)S(1)}, u32[]{:S(2)}, u32[]{:S(2)}) collective-permute-start(f32[2,4,4,8,128]{4,3,2,1,0:T(8,128)} %bitcast.53), channel_id=1, source_target_pairs={{32,0},{33,1},{34,2},{35,3},{36,4},{37,5},{38,6},{39,7},{40,8},{41... | collective-permute-start | bytes 393224 | tf_op jit(solution)/shard_map/ppermute | solution.py:338
  12.2 4.2 %collective-permute-start.2 = (f32[12,4,8,128]{3,2,1,0:T(8,128)S(1)}, f32[12,4,8,128]{3,2,1,0:T(8,128)S(1)}, u32[]{:S(2)}, u32[]{:S(2)}) collective-permute-start(f32[12,4,8,128]{3,2,1,0:T(8,128)S(1)} %pad_maximum_fusion.1.refs_1_.refs_7_), channel_id=1, source_target_pairs={{0,31},{1,0},{2,1},{3,2},{4,3},{5,4},{6,5},{7,6},{8,7},{9,8},{10,9... | collective-permute-start | bytes 589832 | tf_op jit(solution)/shard_map/ppermute | solution.py:338
  16.4 1.9 collective-permute-start.1
  18.4 2.4 %collective-permute-done.2.refs_3_.refs_8_ = f32[12,4,8,128]{3,2,1,0:T(8,128)S(1)} collective-permute-done((f32[12,4,8,128]{3,2,1,0:T(8,128)S(1)}, f32[12,4,8,128]{3,2,1,0:T(8,128)S(1)}, u32[]{:S(2)}, u32[]{:S(2)}) %collective-permute-start.2) | collective-permute-done | bytes 196640 | tf_op jit(solution)/shard_map/ppermute | solution.py:338
  20.7 5.4 %collective-permute-done.1.refs_2_.refs_6_ = f32[12,4,8,128]{3,2,1,0:T(8,128)S(1)} collective-permute-done((f32[12,4,8,128]{3,2,1,0:T(8,128)S(1)}, f32[12,4,8,128]{3,2,1,0:T(8,128)S(1)}, u32[]{:S(2)}, u32[]{:S(2)}) %collective-permute-start.1) | collective-permute-done | bytes 196640 | tf_op jit(solution)/shard_map/ppermute | solution.py:338
  27.1 1.9 collective-permute-start.4
  29.0 3.4 %collective-permute-start.3 = (f32[12,4,8,128]{3,2,1,0:T(8,128)S(1)}, f32[12,4,8,128]{3,2,1,0:T(8,128)S(1)}, u32[]{:S(2)}, u32[]{:S(2)}) collective-permute-start(f32[12,4,8,128]{3,2,1,0:T(8,128)S(1)} %get-tuple-element.60.refs_1_), channel_id=1, source_target_pairs={{0,1},{1,2},{2,3},{3,4},{4,5},{5,6},{6,7},{7,8},{8,9},{9,10},{10,1... | collective-permute-start | bytes 589832 | tf_op jit(solution)/shard_map/ppermute | solution.py:338
  32.4 2.2 %collective-permute-done.4.refs_3_.refs_9_ = f32[12,4,8,128]{3,2,1,0:T(8,128)S(1)} collective-permute-done((f32[12,4,8,128]{3,2,1,0:T(8,128)S(1)}, f32[12,4,8,128]{3,2,1,0:T(8,128)S(1)}, u32[]{:S(2)}, u32[]{:S(2)}) %collective-permute-start.4) | collective-permute-done | bytes 196640 | tf_op jit(solution)/shard_map/ppermute | solution.py:338
  34.7 5.2 %collective-permute-done.3.refs_2_ = f32[12,4,8,128]{3,2,1,0:T(8,128)S(1)} collective-permute-done((f32[12,4,8,128]{3,2,1,0:T(8,128)S(1)}, f32[12,4,8,128]{3,2,1,0:T(8,128)S(1)}, u32[]{:S(2)}, u32[]{:S(2)}) %collective-permute-start.3) | collective-permute-done | bytes 196640 | tf_op jit(solution)/shard_map/ppermute | solution.py:338
  40.9 1.9 collective-permute-start.6
  42.8 6.7 %collective-permute-start.5 = (f32[12,4,8,128]{3,2,1,0:T(8,128)S(1)}, f32[12,4,8,128]{3,2,1,0:T(8,128)S(1)}, u32[]{:S(2)}, u32[]{:S(2)}) collective-permute-start(f32[12,4,8,128]{3,2,1,0:T(8,128)S(1)} %get-tuple-element.64), channel_id=1, source_target_pairs={{0,31},{1,0},{2,1},{3,2},{4,3},{5,4},{6,5},{7,6},{8,7},{9,8},{10,9... | collective-permute-start | bytes 589832 | tf_op jit(solution)/shard_map/ppermute | solution.py:338
  49.5 5.8 %collective-permute-start.9 = (f32[4,4,4,8,128]{4,3,2,1,0:T(8,128)S(1)}, f32[4,4,4,8,128]{4,3,2,1,0:T(8,128)S(1)}, u32[]{:S(2)}, u32[]{:S(2)}) collective-permute-start(f32[4,4,4,8,128]{4,3,2,1,0:T(8,128)S(1)} %pad_maximum_fusion), channel_id=1, source_target_pairs={{32,96},{33,97},{34,98},{35,99},{36,100},{37,101},{38,102},{39,103... | collective-permute-start | bytes 786440 | tf_op jit(solution)/shard_map/ppermute | solution.py:338
  56.3 5.8 %collective-permute-start.8 = (f32[8,4,8,128]{3,2,1,0:T(8,128)S(1)}, f32[8,4,8,128]{3,2,1,0:T(8,128)S(1)}, u32[]{:S(2)}, u32[]{:S(2)}) collective-permute-start(f32[8,4,8,128]{3,2,1,0:T(8,128)S(1)} %get-tuple-element.68.refs_1_), channel_id=1, source_target_pairs={{0,31},{1,0},{2,1},{3,2},{4,3},{5,4},{6,5},{7,6},{8,7},{9,8},{10,9... | collective-permute-start | bytes 393224 | tf_op jit(solution)/shard_map/ppermute | solution.py:338
  62.2 1.9 collective-permute-start.7
  64.1 7.1 %collective-permute-done.7.refs_2_ = f32[8,4,8,128]{3,2,1,0:T(8,128)S(1)} collective-permute-done((f32[8,4,8,128]{3,2,1,0:T(8,128)S(1)}, f32[8,4,8,128]{3,2,1,0:T(8,128)S(1)}, u32[]{:S(2)}, u32[]{:S(2)}) %collective-permute-start.7) | collective-permute-done | bytes 131104 | tf_op jit(solution)/shard_map/ppermute | solution.py:338
  72.2 1.3 collective-permute-start.10
  73.5 3.4 %collective-permute-done.10.pack.refs_7_.refs_10_ = f32[6,4,4,8,128]{4,3,2,1,0:T(8,128)S(1)} collective-permute-done((f32[6,4,4,8,128]{4,3,2,1,0:T(8,128)S(1)}, f32[6,4,4,8,128]{4,3,2,1,0:T(8,128)S(1)}, u32[]{:S(2)}, u32[]{:S(2)}) %collective-permute-start.10) | collective-permute-done | bytes 393248 | tf_op jit(solution)/shard_map/ppermute | solution.py:338
  76.9 1.9 collective-permute-start.13
  78.8 1.9 collective-permute-start.12
  80.7 3.4 %collective-permute-start.11 = (f32[6,4,8,128]{3,2,1,0:T(8,128)S(1)}, f32[6,4,8,128]{3,2,1,0:T(8,128)S(1)}, u32[]{:S(2)}, u32[]{:S(2)}) collective-permute-start(f32[6,4,8,128]{3,2,1,0:T(8,128)S(1)} %pad_maximum_fusion.2.z1.refs_9_.refs_12_), channel_id=1, source_target_pairs={{32,33},{33,34},{34,35},{35,36},{36,37},{37,38},{38,39},{39,40},{4... | collective-permute-start | bytes 294920 | tf_op jit(solution)/shard_map/ppermute | solution.py:338
  84.2 5.2 %collective-permute-done.11.z0.refs_8_.refs_11_ = f32[6,4,8,128]{3,2,1,0:T(8,128)S(1)} collective-permute-done((f32[6,4,8,128]{3,2,1,0:T(8,128)S(1)}, f32[6,4,8,128]{3,2,1,0:T(8,128)S(1)}, u32[]{:S(2)}, u32[]{:S(2)}) %collective-permute-start.11) | collective-permute-done | bytes 98336 | tf_op jit(solution)/shard_map/ppermute | solution.py:338
  89.4 1.5 shard_map.207
  93.7 1.3 collective-permute-start.17
  107.6 1.3 collective-permute-start.33
  110.2 27.9 %collective-permute-done.33.refs_22_ = f32[4,4,8,128]{3,2,1,0:T(8,128)S(1)} collective-permute-done((f32[4,4,8,128]{3,2,1,0:T(8,128)S(1)}, f32[4,4,8,128]{3,2,1,0:T(8,128)S(1)}, u32[]{:S(2)}, u32[]{:S(2)}) %collective-permute-start.33) | collective-permute-done | bytes 65568 | tf_op jit(solution)/shard_map/ppermute | solution.py:338
  142.1 1.3 collective-permute-start.38
  143.4 1.3 collective-permute-start.37
  144.7 1.3 collective-permute-start.39
  146.0 43.2 %collective-permute-done.37.refs_1_ = f32[9,4,8,128]{3,2,1,0:T(8,128)S(1)} collective-permute-done((f32[9,4,8,128]{3,2,1,0:T(8,128)S(1)}, f32[9,4,8,128]{3,2,1,0:T(8,128)S(1)}, u32[]{:S(2)}, u32[]{:S(2)}) %collective-permute-start.37) | collective-permute-done | bytes 147488 | tf_op jit(solution)/shard_map/ppermute | solution.py:338
  189.2 3.1 %collective-permute-done.39.refs_3_ = f32[9,4,8,128]{3,2,1,0:T(8,128)S(1)} collective-permute-done((f32[9,4,8,128]{3,2,1,0:T(8,128)S(1)}, f32[9,4,8,128]{3,2,1,0:T(8,128)S(1)}, u32[]{:S(2)}, u32[]{:S(2)}) %collective-permute-start.39) | collective-permute-done | bytes 147488 | tf_op jit(solution)/shard_map/ppermute | solution.py:338
  192.3 2.8 %shard_map.215 = (f32[9,4,8,128]{3,2,1,0:T(8,128)}, f32[9,4,8,128]{3,2,1,0:T(8,128)}, f32[20,4,8,128]{3,2,1,0:T(8,128)}, f32[2,4,4,8,128]{4,3,2,1,0:T(8,128)S(1)}, f32[2,4,4,8,128]{4,3,2,1,0:T(8,128)S(1)}) custom-call(s32[2]{0:T(128)S(1)} %pad_add_fusion.refs_0_.spot, f32[9,4,8,128]{3,2,1,0:T(8,128)S(1)} %collective-permute-done.37.refs_1_, ...), custom_call_target="tpu_custom_call" | custom-call | flops 9830400 | bytes 1048576 | tf_op jit(solution)/shard_map/pallas_call | solution.py:312
  195.0 1.3 collective-permute-start.40
  (92 shorter events, 28.4 us)
Async XLA Ops:
  0.6 10.9 %collective-permute-start = (f32[2,4,4,8,128]{4,3,2,1,0:T(8,128)}, f32[2,4,4,8,128]{4,3,2,1,0:T(8,128)S(1)}, u32[]{:S(2)}, u32[]{:S(2)}) collective-permute-start(f32[2,4,4,8,128]{4,3,2,1,0:T(8,128)} %bitcast.53), channel_id=1, source_target_pairs={{32,0},{33,1},{34,2},{35,3},{36,4},{37,5},{38,6},{39,7},{40,8},{41... | collective-permute-start | bytes 393224 | tf_op jit(solution)/shard_map/ppermute | solution.py:338
  12.2 8.5 %collective-permute-start.2 = (f32[12,4,8,128]{3,2,1,0:T(8,128)S(1)}, f32[12,4,8,128]{3,2,1,0:T(8,128)S(1)}, u32[]{:S(2)}, u32[]{:S(2)}) collective-permute-start(f32[12,4,8,128]{3,2,1,0:T(8,128)S(1)} %pad_maximum_fusion.1.refs_1_.refs_7_), channel_id=1, source_target_pairs={{0,31},{1,0},{2,1},{3,2},{4,3},{5,4},{6,5},{7,6},{8,7},{9,8},{10,9... | collective-permute-start | bytes 589832 | tf_op jit(solution)/shard_map/ppermute | solution.py:338
  16.4 9.7 %collective-permute-start.1 = (f32[12,4,8,128]{3,2,1,0:T(8,128)S(1)}, f32[12,4,8,128]{3,2,1,0:T(8,128)S(1)}, u32[]{:S(2)}, u32[]{:S(2)}) collective-permute-start(f32[12,4,8,128]{3,2,1,0:T(8,128)S(1)} %pad_maximum_fusion.1.refs_1_.refs_7_), channel_id=1, source_target_pairs={{0,1},{1,2},{2,3},{3,4},{4,5},{5,6},{6,7},{7,8},{8,9},{9,10},{10,1... | collective-permute-start | bytes 589832 | tf_op jit(solution)/shard_map/ppermute | solution.py:338
  27.1 7.6 %collective-permute-start.4 = (f32[12,4,8,128]{3,2,1,0:T(8,128)S(1)}, f32[12,4,8,128]{3,2,1,0:T(8,128)S(1)}, u32[]{:S(2)}, u32[]{:S(2)}) collective-permute-start(f32[12,4,8,128]{3,2,1,0:T(8,128)S(1)} %get-tuple-element.61), channel_id=1, source_target_pairs={{0,31},{1,0},{2,1},{3,2},{4,3},{5,4},{6,5},{7,6},{8,7},{9,8},{10,9... | collective-permute-start | bytes 589832 | tf_op jit(solution)/shard_map/ppermute | solution.py:338
  29.0 10.9 %collective-permute-start.3 = (f32[12,4,8,128]{3,2,1,0:T(8,128)S(1)}, f32[12,4,8,128]{3,2,1,0:T(8,128)S(1)}, u32[]{:S(2)}, u32[]{:S(2)}) collective-permute-start(f32[12,4,8,128]{3,2,1,0:T(8,128)S(1)} %get-tuple-element.60.refs_1_), channel_id=1, source_target_pairs={{0,1},{1,2},{2,3},{3,4},{4,5},{5,6},{6,7},{7,8},{8,9},{9,10},{10,1... | collective-permute-start | bytes 589832 | tf_op jit(solution)/shard_map/ppermute | solution.py:338
  40.9 14.5 %collective-permute-start.6 = (f32[8,4,8,128]{3,2,1,0:T(8,128)S(1)}, f32[8,4,8,128]{3,2,1,0:T(8,128)S(1)}, u32[]{:S(2)}, u32[]{:S(2)}) collective-permute-start(f32[8,4,8,128]{3,2,1,0:T(8,128)S(1)} %get-tuple-element.65.refs_1_), channel_id=1, source_target_pairs={{0,1},{1,2},{2,3},{3,4},{4,5},{5,6},{6,7},{7,8},{8,9},{9,10},{10,1... | collective-permute-start | bytes 393224 | tf_op jit(solution)/shard_map/ppermute | solution.py:338
  42.8 12.6 %collective-permute-start.5 = (f32[12,4,8,128]{3,2,1,0:T(8,128)S(1)}, f32[12,4,8,128]{3,2,1,0:T(8,128)S(1)}, u32[]{:S(2)}, u32[]{:S(2)}) collective-permute-start(f32[12,4,8,128]{3,2,1,0:T(8,128)S(1)} %get-tuple-element.64), channel_id=1, source_target_pairs={{0,31},{1,0},{2,1},{3,2},{4,3},{5,4},{6,5},{7,6},{8,7},{9,8},{10,9... | collective-permute-start | bytes 589832 | tf_op jit(solution)/shard_map/ppermute | solution.py:338
  49.5 14.6 %collective-permute-start.9 = (f32[4,4,4,8,128]{4,3,2,1,0:T(8,128)S(1)}, f32[4,4,4,8,128]{4,3,2,1,0:T(8,128)S(1)}, u32[]{:S(2)}, u32[]{:S(2)}) collective-permute-start(f32[4,4,4,8,128]{4,3,2,1,0:T(8,128)S(1)} %pad_maximum_fusion), channel_id=1, source_target_pairs={{32,96},{33,97},{34,98},{35,99},{36,100},{37,101},{38,102},{39,103... | collective-permute-start | bytes 786440 | tf_op jit(solution)/shard_map/ppermute | solution.py:338
  56.3 7.8 %collective-permute-start.8 = (f32[8,4,8,128]{3,2,1,0:T(8,128)S(1)}, f32[8,4,8,128]{3,2,1,0:T(8,128)S(1)}, u32[]{:S(2)}, u32[]{:S(2)}) collective-permute-start(f32[8,4,8,128]{3,2,1,0:T(8,128)S(1)} %get-tuple-element.68.refs_1_), channel_id=1, source_target_pairs={{0,31},{1,0},{2,1},{3,2},{4,3},{5,4},{6,5},{7,6},{8,7},{9,8},{10,9... | collective-permute-start | bytes 393224 | tf_op jit(solution)/shard_map/ppermute | solution.py:338
  62.2 9.0 %collective-permute-start.7 = (f32[8,4,8,128]{3,2,1,0:T(8,128)S(1)}, f32[8,4,8,128]{3,2,1,0:T(8,128)S(1)}, u32[]{:S(2)}, u32[]{:S(2)}) collective-permute-start(f32[8,4,8,128]{3,2,1,0:T(8,128)S(1)} %get-tuple-element.68.refs_1_), channel_id=1, source_target_pairs={{0,1},{1,2},{2,3},{3,4},{4,5},{5,6},{6,7},{7,8},{8,9},{9,10},{10,1... | collective-permute-start | bytes 393224 | tf_op jit(solution)/shard_map/ppermute | solution.py:338
  72.2 4.7 %collective-permute-start.10 = (f32[6,4,4,8,128]{4,3,2,1,0:T(8,128)S(1)}, f32[6,4,4,8,128]{4,3,2,1,0:T(8,128)S(1)}, u32[]{:S(2)}, u32[]{:S(2)}) collective-permute-start(f32[6,4,4,8,128]{4,3,2,1,0:T(8,128)S(1)} %get-tuple-element.71), channel_id=1, source_target_pairs={{0,32},{1,33},{2,34},{3,35},{4,36},{5,37},{6,38},{7,39},{8,40},{9,... | collective-permute-start | bytes 1179656 | tf_op jit(solution)/shard_map/ppermute | solution.py:338
  76.9 7.3 %collective-permute-start.13 = (f32[6,4,8,128]{3,2,1,0:T(8,128)S(1)}, f32[6,4,8,128]{3,2,1,0:T(8,128)S(1)}, u32[]{:S(2)}, u32[]{:S(2)}) collective-permute-start(f32[6,4,8,128]{3,2,1,0:T(8,128)S(1)} %pad_maximum_fusion.2.z1.refs_9_.refs_12_), channel_id=1, source_target_pairs={{32,62},{33,63},{34,32},{35,33},{36,34},{37,35},{38,36},{39,37},{4... | collective-permute-start | bytes 294920 | tf_op jit(solution)/shard_map/ppermute | solution.py:338
  78.8 5.4 %collective-permute-start.12 = (f32[6,4,8,128]{3,2,1,0:T(8,128)S(1)}, f32[6,4,8,128]{3,2,1,0:T(8,128)S(1)}, u32[]{:S(2)}, u32[]{:S(2)}) collective-permute-start(f32[6,4,8,128]{3,2,1,0:T(8,128)S(1)} %pad_maximum_fusion.2.z1.refs_9_.refs_12_), channel_id=1, source_target_pairs={{32,63},{33,32},{34,33},{35,34},{36,35},{37,36},{38,37},{39,38},{4... | collective-permute-start | bytes 294920 | tf_op jit(solution)/shard_map/ppermute | solution.py:338
  80.7 8.7 %collective-permute-start.11 = (f32[6,4,8,128]{3,2,1,0:T(8,128)S(1)}, f32[6,4,8,128]{3,2,1,0:T(8,128)S(1)}, u32[]{:S(2)}, u32[]{:S(2)}) collective-permute-start(f32[6,4,8,128]{3,2,1,0:T(8,128)S(1)} %pad_maximum_fusion.2.z1.refs_9_.refs_12_), channel_id=1, source_target_pairs={{32,33},{33,34},{34,35},{35,36},{36,37},{37,38},{38,39},{39,40},{4... | collective-permute-start | bytes 294920 | tf_op jit(solution)/shard_map/ppermute | solution.py:338
  91.6 4.3 %collective-permute-start.15 = (f32[20,4,8,128]{3,2,1,0:T(8,128)S(1)}, f32[20,4,8,128]{3,2,1,0:T(8,128)S(1)}, u32[]{:S(2)}, u32[]{:S(2)}) collective-permute-start(f32[20,4,8,128]{3,2,1,0:T(8,128)S(1)} %get-tuple-element.76), channel_id=1, source_target_pairs={{480,416},{481,417},{482,418},{483,419},{484,420},{485,421},{486,4... | collective-permute-start | bytes 983048 | tf_op jit(solution)/shard_map/ppermute | solution.py:338
  92.3 3.6 %collective-permute-start.14 = (f32[9,4,8,128]{3,2,1,0:T(8,128)S(1)}, f32[9,4,8,128]{3,2,1,0:T(8,128)S(1)}, u32[]{:S(2)}, u32[]{:S(2)}) collective-permute-start(f32[9,4,8,128]{3,2,1,0:T(8,128)S(1)} %get-tuple-element.75), channel_id=1, source_target_pairs={{480,418},{481,419},{482,420},{483,421},{484,422},{485,423},{486,4... | collective-permute-start | bytes 442376 | tf_op jit(solution)/shard_map/ppermute | solution.py:338
  93.0 2.9 %collective-permute-start.16 = (f32[9,4,8,128]{3,2,1,0:T(8,128)S(1)}, f32[9,4,8,128]{3,2,1,0:T(8,128)S(1)}, u32[]{:S(2)}, u32[]{:S(2)}) collective-permute-start(f32[9,4,8,128]{3,2,1,0:T(8,128)S(1)} %get-tuple-element.77), channel_id=1, source_target_pairs={{480,446},{481,447},{482,416},{483,417},{484,418},{485,419},{486,4... | collective-permute-start | bytes 442376 | tf_op jit(solution)/shard_map/ppermute | solution.py:338
  93.7 2.2 %collective-permute-start.17 = (f32[4,4,8,128]{3,2,1,0:T(8,128)S(1)}, f32[4,4,8,128]{3,2,1,0:T(8,128)S(1)}, u32[]{:S(2)}, u32[]{:S(2)}) collective-permute-start(f32[4,4,8,128]{3,2,1,0:T(8,128)S(1)} %broadcast_multiply_fusion.refs_21_), channel_id=1, source_target_pairs={{32,0},{33,1},{34,2},{35,3},{36,4},{37,5},{38,6},{39,7},{40,8},{41... | collective-permute-start | bytes 196616 | tf_op jit(solution)/shard_map/ppermute | solution.py:338
  96.5 2.8 %collective-permute-start.19 = (f32[20,4,8,128]{3,2,1,0:T(8,128)S(1)}, f32[20,4,8,128]{3,2,1,0:T(8,128)S(1)}, u32[]{:S(2)}, u32[]{:S(2)}) collective-permute-start(f32[20,4,8,128]{3,2,1,0:T(8,128)S(1)} %get-tuple-element.82), channel_id=1, source_target_pairs={{416,352},{417,353},{418,354},{419,355},{420,356},{421,357},{422,3... | collective-permute-start | bytes 983048 | tf_op jit(solution)/shard_map/ppermute | solution.py:338
  97.2 2.0 %collective-permute-start.18 = (f32[9,4,8,128]{3,2,1,0:T(8,128)S(1)}, f32[9,4,8,128]{3,2,1,0:T(8,128)S(1)}, u32[]{:S(2)}, u32[]{:S(2)}) collective-permute-start(f32[9,4,8,128]{3,2,1,0:T(8,128)S(1)} %get-tuple-element.81), channel_id=1, source_target_pairs={{416,354},{417,355},{418,356},{419,357},{420,358},{421,359},{422,3... | collective-permute-start | bytes 442376 | tf_op jit(solution)/shard_map/ppermute | solution.py:338
  99.9 2.8 %collective-permute-start.23 = (f32[20,4,8,128]{3,2,1,0:T(8,128)S(1)}, f32[20,4,8,128]{3,2,1,0:T(8,128)S(1)}, u32[]{:S(2)}, u32[]{:S(2)}) collective-permute-start(f32[20,4,8,128]{3,2,1,0:T(8,128)S(1)} %get-tuple-element.88), channel_id=1, source_target_pairs={{352,288},{353,289},{354,290},{355,291},{356,292},{357,293},{358,2... | collective-permute-start | bytes 983048 | tf_op jit(solution)/shard_map/ppermute | solution.py:338
  100.6 2.0 %collective-permute-start.22 = (f32[9,4,8,128]{3,2,1,0:T(8,128)S(1)}, f32[9,4,8,128]{3,2,1,0:T(8,128)S(1)}, u32[]{:S(2)}, u32[]{:S(2)}) collective-permute-start(f32[9,4,8,128]{3,2,1,0:T(8,128)S(1)} %get-tuple-element.87), channel_id=1, source_target_pairs={{352,290},{353,291},{354,292},{355,293},{356,294},{357,295},{358,2... | collective-permute-start | bytes 442376 | tf_op jit(solution)/shard_map/ppermute | solution.py:338
  103.3 2.8 %collective-permute-start.27 = (f32[20,4,8,128]{3,2,1,0:T(8,128)S(1)}, f32[20,4,8,128]{3,2,1,0:T(8,128)S(1)}, u32[]{:S(2)}, u32[]{:S(2)}) collective-permute-start(f32[20,4,8,128]{3,2,1,0:T(8,128)S(1)} %get-tuple-element.94), channel_id=1, source_target_pairs={{288,224},{289,225},{290,226},{291,227},{292,228},{293,229},{294,2... | collective-permute-start | bytes 983048 | tf_op jit(solution)/shard_map/ppermute | solution.py:338
  106.9 31.2 %collective-permute-start.31 = (f32[20,4,8,128]{3,2,1,0:T(8,128)S(1)}, f32[20,4,8,128]{3,2,1,0:T(8,128)S(1)}, u32[]{:S(2)}, u32[]{:S(2)}) collective-permute-start(f32[20,4,8,128]{3,2,1,0:T(8,128)S(1)} %get-tuple-element.100), channel_id=1, source_target_pairs={{224,160},{225,161},{226,162},{227,163},{228,164},{229,165},{230,1... | collective-permute-start | bytes 983048 | tf_op jit(solution)/shard_map/ppermute | solution.py:338
  107.6 30.5 %collective-permute-start.33 = (f32[4,4,8,128]{3,2,1,0:T(8,128)S(1)}, f32[4,4,8,128]{3,2,1,0:T(8,128)S(1)}, u32[]{:S(2)}, u32[]{:S(2)}) collective-permute-start(f32[4,4,8,128]{3,2,1,0:T(8,128)S(1)} %get-tuple-element.104), channel_id=1, source_target_pairs={{0,32},{1,33},{2,34},{3,35},{4,36},{5,37},{6,38},{7,39},{8,40},{9,... | collective-permute-start | bytes 196616 | tf_op jit(solution)/shard_map/ppermute | solution.py:338
  108.9 29.2 %collective-permute-start.30 = (f32[9,4,8,128]{3,2,1,0:T(8,128)S(1)}, f32[9,4,8,128]{3,2,1,0:T(8,128)S(1)}, u32[]{:S(2)}, u32[]{:S(2)}) collective-permute-start(f32[9,4,8,128]{3,2,1,0:T(8,128)S(1)} %get-tuple-element.99), channel_id=1, source_target_pairs={{224,162},{225,163},{226,164},{227,165},{228,166},{229,167},{230,1... | collective-permute-start | bytes 442376 | tf_op jit(solution)/shard_map/ppermute | solution.py:338
  109.5 28.6 %collective-permute-start.32 = (f32[9,4,8,128]{3,2,1,0:T(8,128)S(1)}, f32[9,4,8,128]{3,2,1,0:T(8,128)S(1)}, u32[]{:S(2)}, u32[]{:S(2)}) collective-permute-start(f32[9,4,8,128]{3,2,1,0:T(8,128)S(1)} %get-tuple-element.101), channel_id=1, source_target_pairs={{224,190},{225,191},{226,160},{227,161},{228,162},{229,163},{230,1... | collective-permute-start | bytes 442376 | tf_op jit(solution)/shard_map/ppermute | solution.py:338
  139.4 2.1 %collective-permute-start.35 = (f32[20,4,8,128]{3,2,1,0:T(8,128)S(1)}, f32[20,4,8,128]{3,2,1,0:T(8,128)S(1)}, u32[]{:S(2)}, u32[]{:S(2)}) collective-permute-start(f32[20,4,8,128]{3,2,1,0:T(8,128)S(1)} %get-tuple-element.106), channel_id=1, source_target_pairs={{160,96},{161,97},{162,98},{163,99},{164,100},{165,101},{166,102},... | collective-permute-start | bytes 983048 | tf_op jit(solution)/shard_map/ppermute | solution.py:338
  142.1 50.2 %collective-permute-start.38 = (f32[20,4,8,128]{3,2,1,0:T(8,128)S(1)}, f32[20,4,8,128]{3,2,1,0:T(8,128)S(1)}, u32[]{:S(2)}, u32[]{:S(2)}) collective-permute-start(f32[20,4,8,128]{3,2,1,0:T(8,128)S(1)} %get-tuple-element.111), channel_id=1, source_target_pairs={{96,32},{97,33},{98,34},{99,35},{100,36},{101,37},{102,38},{103,39... | collective-permute-start | bytes 983048 | tf_op jit(solution)/shard_map/ppermute | solution.py:338
  143.4 45.8 %collective-permute-start.37 = (f32[9,4,8,128]{3,2,1,0:T(8,128)S(1)}, f32[9,4,8,128]{3,2,1,0:T(8,128)S(1)}, u32[]{:S(2)}, u32[]{:S(2)}) collective-permute-start(f32[9,4,8,128]{3,2,1,0:T(8,128)S(1)} %get-tuple-element.110), channel_id=1, source_target_pairs={{96,34},{97,35},{98,36},{99,37},{100,38},{101,39},{102,40},{103,41... | collective-permute-start | bytes 442376 | tf_op jit(solution)/shard_map/ppermute | solution.py:338
  144.7 47.6 %collective-permute-start.39 = (f32[9,4,8,128]{3,2,1,0:T(8,128)S(1)}, f32[9,4,8,128]{3,2,1,0:T(8,128)S(1)}, u32[]{:S(2)}, u32[]{:S(2)}) collective-permute-start(f32[9,4,8,128]{3,2,1,0:T(8,128)S(1)} %get-tuple-element.112), channel_id=1, source_target_pairs={{96,62},{97,63},{98,32},{99,33},{100,34},{101,35},{102,36},{103,37... | collective-permute-start | bytes 442376 | tf_op jit(solution)/shard_map/ppermute | solution.py:338
  195.0 2.3 %collective-permute-start.40 = (f32[2,4,4,8,128]{4,3,2,1,0:T(8,128)S(1)}, f32[2,4,4,8,128]{4,3,2,1,0:T(8,128)S(1)}, u32[]{:S(2)}, u32[]{:S(2)}) collective-permute-start(f32[2,4,4,8,128]{4,3,2,1,0:T(8,128)S(1)} %get-tuple-element.115), channel_id=1, source_target_pairs={{32,0},{33,1},{34,2},{35,3},{36,4},{37,5},{38,6},{39,7},{40,8},{41... | collective-permute-start | bytes 393224 | tf_op jit(solution)/shard_map/ppermute | solution.py:338
  (14 other events, 23.3 us)

commit v6 on v4

--- a/solution.py
+++ b/solution.py
@@ -132,8 +132,8 @@
         src, inv = (None, None) if last else [refs.pop(0) for _ in range(2)]
         factors = [refs.pop(0) for _ in range(4)][:3] if last else None
         old = None if first else refs.pop(0)
-        out, grad = refs[:2]
-        more, scratch = refs[2:-3], refs[-3:]
+        out = None if last else refs.pop(0)
+        grad, more, scratch = refs[0], refs[1:-3], refs[-3:]
         stencil = Stencil()
         pieces = [rl, r0, rh]
 
@@ -142,9 +142,14 @@
 
         def emit(layer, x):
             for f in range(FIELDS):
-                out[f, layer] = x[f]
+                if not last:
+                    out[f, layer] = x[f]
                 term = x[f] * u[f, layer]
-                grad[f, layer] = term if first else old[f, layer] + term
+                so_far = term if first else old[f, layer] + term
+                if last:
+                    so_far = time_step * so_far
+                    more[1][5, f, layer] = so_far
+                grad[f, layer] = so_far
                 if not last:
                     r = src[f, layer]
                     if masses[f]:
@@ -173,8 +178,8 @@
     operands = [own, low, high, states, previous]
     operands += list(coarse) if last else [source, factor]
     operands += [] if first else [total]
-    outs = [SLAB, SLAB]
-    outs += [carry(7), (5,) + SLAB] if last else [carry(12)] * 2 if first else [carry(8)]
+    outs = [SLAB, carry(7), (6,) + SLAB] if last else [SLAB, SLAB]
+    outs += [] if last else [carry(12)] * 2 if first else [carry(8)]
     return call(body, outs, *operands, layers=3 * WIDTH, flops=28 * 4 * 1024 * 20)
 
 
@@ -182,16 +187,14 @@
     return (count, WIDTH, 8, 128)
 
 
-def offsets_step(pack, z_low, z_own, z_high, even_low, even_high, prior):
-    def body(even, zl, z0, zh, el, eh, before, offset, ahead, own, *scratch):
+def offsets_step(pack, z_low, z_own, z_high, x0, prior):
+    def body(even, zl, z0, zh, z7, before, offset, ahead, *scratch):
         stencil = Stencil()
-        for f in range(3):
-            own[f] = even[0, f] - 0.25 * even[1, f]
 
         def emit_even(layer, q):
             for f in range(FIELDS):
                 offset[0, f, layer] = even[0, f, layer] - q[f]
-                offset[1, f, layer] = even[1, f, layer] - 0.5 * (q[f] + z0[3 + f, layer])
+                offset[1, f, layer] = even[1, f, layer] - 0.5 * (q[f] + z7[3 + f, layer])
 
         def emit_before(layer, q):
             for f in range(FIELDS):
@@ -200,21 +203,14 @@
         inv_even = lambda f, layer: even[2 + layer // WIDTH, f, layer % WIDTH]
         inv_before = lambda f, layer: before[layer // WIDTH, f, layer % WIDTH]
         solve(stencil, masses_only([zl, z0, zh]), inv_even, 3 * WIDTH, scratch, emit_even)
-        solve(stencil, masses_only([el, own, eh]), inv_before, 3 * WIDTH, scratch, emit_before)
-
-    spec = pl.BlockSpec(memory_space=pltpu.VMEM)
-    return pl.pallas_call(
-        body,
-        in_specs=[spec] * 7,
-        out_specs=[spec] * 2,
-        out_shape=[jax.ShapeDtypeStruct(shape, jnp.float32) for shape in ((2,) + SLAB, SLAB)],
-        scratch_shapes=[vmem(carry(3))] + [vmem((FIELDS, 3 * WIDTH, 8, 128))] * 3,
-        compiler_params=pltpu.CompilerParams(vmem_limit_bytes=24 * 1024 * 1024),
-        cost_estimate=pl.CostEstimate(flops=56 * 4 * 1024 * 20, bytes_accessed=1 << 20, transcendentals=0),
-    )(pack, z_low, z_own, z_high, even_low, even_high, prior)
-
-
-def chip_step(turn, place, arrived, inv_five, pack, own_three, late, offset, ahead, done, grad):
+        z_even = [part.at[3:6] for part in (zl, z0, zh)]
+        solve(stencil, masses_only(z_even), inv_before, 3 * WIDTH, scratch, emit_before)
+
+    operands = (pack, z_low, z_own, z_high, x0, prior)
+    return call(body, [(2,) + SLAB, SLAB], *operands, layers=3 * WIDTH, flops=56 * 4 * 1024 * 20)
+
+
+def chip_step(turn, place, arrived, inv_five, pack, own_three, pair, offset, ahead, done, grad):
     with_done, with_grad, with_z = done is not None, grad is not None, arrived is not None
 
     def body(*refs):
@@ -224,14 +220,13 @@
         iv = [refs.pop(0) for _ in range(5)]
         even = refs.pop(0)
         zo = [refs.pop(0) for _ in range(3)]
-        x1, o, qa = [refs.pop(0) for _ in range(3)]
+        z7, x1, o, qa = [refs.pop(0) for _ in range(4)]
         before = [refs.pop(0) for _ in range(2)] if with_done else None
         g = [refs.pop(0) for _ in range(2)] if with_grad else None
         z3, z6, z11, odd_pair, even_pair = refs[:5]
-        sums = refs[5] if with_grad else None
         middle, scratch = refs[-4], refs[-3:]
         if with_grad:
-            sums[...] = g[0][...] + g[1][...]
+            refs[5][...] = g[0][...] + g[1][...]
         mine = spot[0] == turn
 
         @pl.when(jnp.logical_not(mine))
@@ -253,7 +248,7 @@
                     if slab == 1:
                         solved = z[2][3 + f, at] if with_z else zero
                         change = z[2][7 + f, at] if with_z else zero
-                        c0 = q[f] + (zo[1][3 + f, at] - solved)
+                        c0 = q[f] + (z7[3 + f, at] - solved)
                         c1 = x1[f, at] + 0.5 * ((q[f] - solved) + change)
                         odd_pair[0, f, at] = c0
                         odd_pair[1, f, at] = c1
@@ -290,10 +285,11 @@
 
     spec = pl.BlockSpec(memory_space=pltpu.VMEM)
     operands = [place] + (list(arrived) if with_z else []) + list(inv_five) + [pack]
-    operands += list(own_three) + [late, offset, ahead]
+    operands += list(own_three) + list(pair) + [offset, ahead]
     operands += list(done) if with_done else []
     operands += list(grad) if with_grad else []
-    outs = [carry(3), carry(6), carry(11), (2,) + SLAB, (2,) + SLAB] + ([SLAB] if with_grad else [])
+    outs = [carry(3), carry(6), carry(11), (2,) + SLAB, (2,) + SLAB]
+    outs += [SLAB] if with_grad else []
     return pl.pallas_call(
         body,
         in_specs=[pl.BlockSpec(memory_space=pltpu.SMEM)] + [spec] * (len(operands) - 1),
@@ -331,13 +327,11 @@
     right_one, left_one = shift(1), shift(-1)
     earlier = routes(times, slabs, lambda k, s: (k - 1, s))
     even_to_odd = routes(times, slabs, lambda k, s: (k + 1, s), lambda k: k % 2 == 0)
+    swap = routes(times, slabs, lambda k, s: (k ^ 1, s))
     odd_to_even = routes(times, slabs, lambda k, s: (k - 1, s), lambda k: k % 2 == 1)
     reach = (2, 1, 0, -1, -2)
     odd, even = (lambda k: k % 2 == 1), (lambda k: k % 2 == 0)
     odd_right, odd_left = (routes(times, slabs, lambda k, s, d=d: (k, s + d), odd) for d in (1, -1))
-    even_right, even_left = (
-        routes(times, slabs, lambda k, s, d=d: (k + 1, s + d), even) for d in (1, -1)
-    )
     later = routes(times, slabs, lambda k, s: (k + 2, s), odd)
 
     def hop_routes(hop):
@@ -356,7 +350,7 @@
         right = adjoint_source[3] + column(masses) * (4.0 * ahead[0] - ahead[1])
         up = down = jnp.concatenate([right, inverses[3], coarse])
         previous, total = ahead[0], None
-        adjoints, exchanged = [None] * 4, []
+        exchanged = []
         for n in (3, 2, 1, 0):
             low, high = send(up, right_one), send(down, left_one)
             exchanged.append((low, up, high))
@@ -366,33 +360,30 @@
                 far = [part[2 * FIELDS :] for part in exchanged[0]]
                 prior = send(jnp.stack(far), later)
                 rest = dict(coarse=(*exchanged[0], prior))
-            x, total, *more = fine_step(n, up, low, high, states[n], previous, total, **rest)
-            adjoints[n] = previous = x
-            up, down = more[0], more[-1]
+            step = fine_step(n, up, low, high, states[n], previous, total, **rest)
+            if n:
+                previous, total, up, *more = step
+                down = more[0] if more else up
         (low, own, high), (low_two, _, high_two) = exchanged[:2]
         inv_five = [part[2 * FIELDS :] for part in (low_two, low, own, high, high_two)]
-        z7, pack = more
-        total = time_step * total
-
-        z3 = z7[:3]
-        z_low, z_high = send(z3, odd_right), send(z3, odd_left)
-        even_low, even_high = send(z3, even_right), send(z3, even_left)
-        pack = send(pack, even_to_odd)
-        own_three = (z_low, z7, z_high)
-        offset, before = offsets_step(pack, *own_three, even_low, even_high, prior)
+        total, z7, pack = step
+
+        pack = send(pack, swap)
+        grad = total + pack[5]
+        both = jnp.concatenate([z7[:3], pack[0, :3] - 0.25 * pack[1, :3]])
+        own_three = (send(both, odd_right), both, send(both, odd_left))
+        offset, before = offsets_step(pack, *own_three, z7, prior)
 
         place = (lax.axis_index("tm").astype(jnp.int32)).reshape(1)
+        is_even = lax.axis_index("tm") % 2 == 0
         stages = []
         far = 1
         while far < chips:
-            stages.append(
-                routes(times, slabs, lambda k, s, d=far: (2 * ((k // 2) ^ d), s), lambda k: k % 2 == 0)
-            )
+            stages.append(routes(times, slabs, lambda k, s, d=far: (2 * ((k // 2) ^ d), s), even))
             far *= 2
-        stages = [odd_to_even] + stages + [even_to_odd]
-        is_even = lax.axis_index("tm") % 2 == 0
-        arrived, done, grad, hop = None, None, total, 0
-        while hop < chips or stages:
+        stages.append(even_to_odd)
+        arrived, done = None, None
+        for hop in range(max(chips, len(stages) + 1)):
             added = None
             if hop and hop < chips:
                 arrived = [send(part, path) for part, path in zip(payload, hop_routes(hop))]
@@ -402,7 +393,7 @@
                 added = (grad if stages else jnp.where(is_even, grad, 0.0), received)
             if hop < chips:
                 z3, z6, z11, odd_pair, even_pair, *sums = chip_step(
-                    times - 1 - 2 * hop, place, arrived, inv_five, pack, own_three, adjoints[1],
+                    times - 1 - 2 * hop, place, arrived, inv_five, pack, own_three, (z7, previous),
                     offset, before, done, added,
                 )
                 payload, done = (z3, z6, z11, z6, z3), (odd_pair, even_pair)
@@ -410,7 +401,6 @@
                     grad = sums[0]
             elif added:
                 grad = added[0] + added[1]
-            hop += 1
 
         corrected = jnp.where(is_even, send(done[1], odd_to_even), done[0])
         return corrected[None], grad

time: 182 us -> 181 us (level)
  the two profiles are of different devices: /device:TPU:17 before, /device:TPU:23 now
where the time goes in v6:
time: 181 us; the launch traced here: 180 us
  waiting for transfers between devices  96.5 us (53%)
  starting transfers between devices  72.5 us (40%)
  Pallas kernels  5.33 us (3%)
  other arithmetic  1.95 us (1%)
    ppermute x53, waiting for transfers between devices, send(): return lax.ppermute(value, AXES, pairs)  96.5 us
    ppermute x53, starting transfers between devices, send(): return lax.ppermute(value, AXES, pairs)  72.5 us
  transfers between devices with their start and end apart: 53, of which 17 were waited for; matrix products, arithmetic and copies ran while one was open for 1% of the time, Pallas kernels for 0%

profile of v6, /device:TPU:23, one launch (start us, length us, event | category | flops | bytes accessed | tf_op | source)
XLA Modules:
  0.0 179.6 jit_solution(16704586768418227435)
XLA Ops:
  0.6 2.6 %collective-permute-start = (f32[2,4,4,8,128]{4,3,2,1,0:T(8,128)}, f32[2,4,4,8,128]{4,3,2,1,0:T(8,128)S(1)}, u32[]{:S(2)}, u32[]{:S(2)}) collective-permute-start(f32[2,4,4,8,128]{4,3,2,1,0:T(8,128)} %bitcast.71), channel_id=1, source_target_pairs={{32,0},{33,1},{34,2},{35,3},{36,4},{37,5},{38,6},{39,7},{40,8},{41... | collective-permute-start | bytes 393224 | tf_op jit(solution)/shard_map/ppermute | solution.py:318
  6.0 2.1 %collective-permute-done = f32[2,4,4,8,128]{4,3,2,1,0:T(8,128)S(1)} collective-permute-done((f32[2,4,4,8,128]{4,3,2,1,0:T(8,128)}, f32[2,4,4,8,128]{4,3,2,1,0:T(8,128)S(1)}, u32[]{:S(2)}, u32[]{:S(2)}) %collective-permute-start) | collective-permute-done | bytes 131104 | tf_op jit(solution)/shard_map/ppermute | solution.py:318
  8.1 3.1 %collective-permute-start.1 = (f32[12,4,8,128]{3,2,1,0:T(8,128)S(1)}, f32[12,4,8,128]{3,2,1,0:T(8,128)S(1)}, u32[]{:S(2)}, u32[]{:S(2)}) collective-permute-start(f32[12,4,8,128]{3,2,1,0:T(8,128)S(1)} %pad_maximum_fusion.refs_0_.refs_6_), channel_id=1, source_target_pairs={{0,1},{1,2},{2,3},{3,4},{4,5},{5,6},{6,7},{7,8},{8,9},{9,10},{10,1... | collective-permute-start | bytes 589832 | tf_op jit(solution)/shard_map/ppermute | solution.py:318
  11.3 2.2 %collective-permute-start.2 = (f32[12,4,8,128]{3,2,1,0:T(8,128)S(1)}, f32[12,4,8,128]{3,2,1,0:T(8,128)S(1)}, u32[]{:S(2)}, u32[]{:S(2)}) collective-permute-start(f32[12,4,8,128]{3,2,1,0:T(8,128)S(1)} %pad_maximum_fusion.refs_0_.refs_6_), channel_id=1, source_target_pairs={{1,0},{2,1},{3,2},{4,3},{5,4},{6,5},{7,6},{8,7},{9,8},{10,9},{11,1... | collective-permute-start | bytes 589832 | tf_op jit(solution)/shard_map/ppermute | solution.py:318
  13.5 1.6 collective-permute-done.1.refs_1_.refs_5_
  15.1 5.5 %collective-permute-done.2.refs_2_.refs_7_ = f32[12,4,8,128]{3,2,1,0:T(8,128)S(1)} collective-permute-done((f32[12,4,8,128]{3,2,1,0:T(8,128)S(1)}, f32[12,4,8,128]{3,2,1,0:T(8,128)S(1)}, u32[]{:S(2)}, u32[]{:S(2)}) %collective-permute-start.2) | collective-permute-done | bytes 196640 | tf_op jit(solution)/shard_map/ppermute | solution.py:318
  21.0 1.9 %collective-permute-start.3 = (f32[12,4,8,128]{3,2,1,0:T(8,128)S(1)}, f32[12,4,8,128]{3,2,1,0:T(8,128)S(1)}, u32[]{:S(2)}, u32[]{:S(2)}) collective-permute-start(f32[12,4,8,128]{3,2,1,0:T(8,128)S(1)} %get-tuple-element.58.refs_0_), channel_id=1, source_target_pairs={{0,1},{1,2},{2,3},{3,4},{4,5},{5,6},{6,7},{7,8},{8,9},{9,10},{10,1... | collective-permute-start | bytes 589832 | tf_op jit(solution)/shard_map/ppermute | solution.py:318
  22.9 3.4 %collective-permute-start.4 = (f32[12,4,8,128]{3,2,1,0:T(8,128)S(1)}, f32[12,4,8,128]{3,2,1,0:T(8,128)S(1)}, u32[]{:S(2)}, u32[]{:S(2)}) collective-permute-start(f32[12,4,8,128]{3,2,1,0:T(8,128)S(1)} %get-tuple-element.59), channel_id=1, source_target_pairs={{1,0},{2,1},{3,2},{4,3},{5,4},{6,5},{7,6},{8,7},{9,8},{10,9},{11,1... | collective-permute-start | bytes 589832 | tf_op jit(solution)/shard_map/ppermute | solution.py:318
  26.3 3.3 %collective-permute-done.3.refs_1_ = f32[12,4,8,128]{3,2,1,0:T(8,128)S(1)} collective-permute-done((f32[12,4,8,128]{3,2,1,0:T(8,128)S(1)}, f32[12,4,8,128]{3,2,1,0:T(8,128)S(1)}, u32[]{:S(2)}, u32[]{:S(2)}) %collective-permute-start.3) | collective-permute-done | bytes 196640 | tf_op jit(solution)/shard_map/ppermute | solution.py:318
  29.6 3.8 %collective-permute-done.4.refs_2_ = f32[12,4,8,128]{3,2,1,0:T(8,128)S(1)} collective-permute-done((f32[12,4,8,128]{3,2,1,0:T(8,128)S(1)}, f32[12,4,8,128]{3,2,1,0:T(8,128)S(1)}, u32[]{:S(2)}, u32[]{:S(2)}) %collective-permute-start.4) | collective-permute-done | bytes 196640 | tf_op jit(solution)/shard_map/ppermute | solution.py:318
  33.8 1.9 %collective-permute-start.5 = (f32[8,4,8,128]{3,2,1,0:T(8,128)S(1)}, f32[8,4,8,128]{3,2,1,0:T(8,128)S(1)}, u32[]{:S(2)}, u32[]{:S(2)}) collective-permute-start(f32[8,4,8,128]{3,2,1,0:T(8,128)S(1)} %get-tuple-element.62.refs_0_), channel_id=1, source_target_pairs={{0,1},{1,2},{2,3},{3,4},{4,5},{5,6},{6,7},{7,8},{8,9},{9,10},{10,1... | collective-permute-start | bytes 393224 | tf_op jit(solution)/shard_map/ppermute | solution.py:318
  35.7 3.4 %collective-permute-start.6 = (f32[8,4,8,128]{3,2,1,0:T(8,128)S(1)}, f32[8,4,8,128]{3,2,1,0:T(8,128)S(1)}, u32[]{:S(2)}, u32[]{:S(2)}) collective-permute-start(f32[8,4,8,128]{3,2,1,0:T(8,128)S(1)} %get-tuple-element.62.refs_0_), channel_id=1, source_target_pairs={{1,0},{2,1},{3,2},{4,3},{5,4},{6,5},{7,6},{8,7},{9,8},{10,9},{11,1... | collective-permute-start | bytes 393224 | tf_op jit(solution)/shard_map/ppermute | solution.py:318
  39.1 4.6 %collective-permute-start.9 = (f32[3,4,4,8,128]{4,3,2,1,0:T(8,128)S(1)}, f32[3,4,4,8,128]{4,3,2,1,0:T(8,128)S(1)}, u32[]{:S(2)}, u32[]{:S(2)}) collective-permute-start(f32[3,4,4,8,128]{4,3,2,1,0:T(8,128)S(1)} %pad_maximum_fusion.1), channel_id=1, source_target_pairs={{32,96},{33,97},{34,98},{35,99},{36,100},{37,101},{38,102},{39,103... | collective-permute-start | bytes 589832 | tf_op jit(solution)/shard_map/ppermute | solution.py:318
  44.8 3.5 %collective-permute-start.7 = (f32[8,4,8,128]{3,2,1,0:T(8,128)S(1)}, f32[8,4,8,128]{3,2,1,0:T(8,128)S(1)}, u32[]{:S(2)}, u32[]{:S(2)}) collective-permute-start(f32[8,4,8,128]{3,2,1,0:T(8,128)S(1)} %get-tuple-element.65.refs_0_), channel_id=1, source_target_pairs={{0,1},{1,2},{2,3},{3,4},{4,5},{5,6},{6,7},{7,8},{8,9},{9,10},{10,1... | collective-permute-start | bytes 393224 | tf_op jit(solution)/shard_map/ppermute | solution.py:318
  48.3 1.9 %collective-permute-start.8 = (f32[8,4,8,128]{3,2,1,0:T(8,128)S(1)}, f32[8,4,8,128]{3,2,1,0:T(8,128)S(1)}, u32[]{:S(2)}, u32[]{:S(2)}) collective-permute-start(f32[8,4,8,128]{3,2,1,0:T(8,128)S(1)} %get-tuple-element.65.refs_0_), channel_id=1, source_target_pairs={{1,0},{2,1},{3,2},{4,3},{5,4},{6,5},{7,6},{8,7},{9,8},{10,9},{11,1... | collective-permute-start | bytes 393224 | tf_op jit(solution)/shard_map/ppermute | solution.py:318
  50.5 5.6 %collective-permute-done.8.refs_2_ = f32[8,4,8,128]{3,2,1,0:T(8,128)S(1)} collective-permute-done((f32[8,4,8,128]{3,2,1,0:T(8,128)S(1)}, f32[8,4,8,128]{3,2,1,0:T(8,128)S(1)}, u32[]{:S(2)}, u32[]{:S(2)}) %collective-permute-start.8) | collective-permute-done | bytes 131104 | tf_op jit(solution)/shard_map/ppermute | solution.py:318
  56.5 4.6 %collective-permute-start.10 = (f32[6,4,4,8,128]{4,3,2,1,0:T(8,128)S(1)}, f32[6,4,4,8,128]{4,3,2,1,0:T(8,128)S(1)}, u32[]{:S(2)}, u32[]{:S(2)}) collective-permute-start(f32[6,4,4,8,128]{4,3,2,1,0:T(8,128)S(1)} %get-tuple-element.68), channel_id=1, source_target_pairs={{0,32},{1,33},{2,34},{3,35},{4,36},{5,37},{6,38},{7,39},{8,40},{9,... | collective-permute-start | bytes 1179656 | tf_op jit(solution)/shard_map/ppermute | solution.py:318
  61.2 1.3 collective-permute-done.10.even.refs_6_.refs_11_
  62.5 2.8 %collective-permute-start.11 = (f32[6,4,8,128]{3,2,1,0:T(8,128)S(1)}, f32[6,4,8,128]{3,2,1,0:T(8,128)S(1)}, u32[]{:S(2)}, u32[]{:S(2)}) collective-permute-start(f32[6,4,8,128]{3,2,1,0:T(8,128)S(1)} %pad_maximum_fusion.2.z0.refs_8_.refs_13_), channel_id=1, source_target_pairs={{32,33},{33,34},{34,35},{35,36},{36,37},{37,38},{38,39},{39,40},{4... | collective-permute-start | bytes 294920 | tf_op jit(solution)/shard_map/ppermute | solution.py:318
  65.3 2.5 %collective-permute-start.12 = (f32[6,4,8,128]{3,2,1,0:T(8,128)S(1)}, f32[6,4,8,128]{3,2,1,0:T(8,128)S(1)}, u32[]{:S(2)}, u32[]{:S(2)}) collective-permute-start(f32[6,4,8,128]{3,2,1,0:T(8,128)S(1)} %pad_maximum_fusion.2.z0.refs_8_.refs_13_), channel_id=1, source_target_pairs={{33,32},{34,33},{35,34},{36,35},{37,36},{38,37},{39,38},{40,39},{4... | collective-permute-start | bytes 294920 | tf_op jit(solution)/shard_map/ppermute | solution.py:318
  67.9 4.9 %collective-permute-done.12.zh.refs_9_.refs_14_ = f32[6,4,8,128]{3,2,1,0:T(8,128)S(1)} collective-permute-done((f32[6,4,8,128]{3,2,1,0:T(8,128)S(1)}, f32[6,4,8,128]{3,2,1,0:T(8,128)S(1)}, u32[]{:S(2)}, u32[]{:S(2)}) %collective-permute-start.12) | collective-permute-done | bytes 98336 | tf_op jit(solution)/shard_map/ppermute | solution.py:318
  82.1 1.3 collective-permute-start.29
  83.4 1.3 collective-permute-start.26
  84.7 1.3 collective-permute-start.28
  86.0 1.3 collective-permute-start.25
  88.6 23.9 %collective-permute-done.29.refs_5_ = f32[3,4,8,128]{3,2,1,0:T(8,128)S(1)} collective-permute-done((f32[3,4,8,128]{3,2,1,0:T(8,128)S(1)}, f32[3,4,8,128]{3,2,1,0:T(8,128)S(1)}, u32[]{:S(2)}, u32[]{:S(2)}) %collective-permute-start.29) | collective-permute-done | bytes 49184 | tf_op jit(solution)/shard_map/ppermute | solution.py:318
  112.5 2.3 %collective-permute-done.28.refs_4_ = f32[6,4,8,128]{3,2,1,0:T(8,128)S(1)} collective-permute-done((f32[6,4,8,128]{3,2,1,0:T(8,128)S(1)}, f32[6,4,8,128]{3,2,1,0:T(8,128)S(1)}, u32[]{:S(2)}, u32[]{:S(2)}) %collective-permute-start.28) | collective-permute-done | bytes 98336 | tf_op jit(solution)/shard_map/ppermute | solution.py:318
  119.5 1.3 collective-permute-start.36
  120.8 1.8 %collective-permute-done.36.refs_22_ = f32[4,4,8,128]{3,2,1,0:T(8,128)S(1)} collective-permute-done((f32[4,4,8,128]{3,2,1,0:T(8,128)S(1)}, f32[4,4,8,128]{3,2,1,0:T(8,128)S(1)}, u32[]{:S(2)}, u32[]{:S(2)}) %collective-permute-start.36) | collective-permute-done | bytes 65568 | tf_op jit(solution)/shard_map/ppermute | solution.py:318
  137.0 34.5 %collective-permute-done.47.refs_1_ = f32[3,4,8,128]{3,2,1,0:T(8,128)S(1)} collective-permute-done((f32[3,4,8,128]{3,2,1,0:T(8,128)S(1)}, f32[3,4,8,128]{3,2,1,0:T(8,128)S(1)}, u32[]{:S(2)}, u32[]{:S(2)}) %collective-permute-start.47) | collective-permute-done | bytes 49184 | tf_op jit(solution)/shard_map/ppermute | solution.py:318
  171.5 3.5 %collective-permute-done.51.refs_5_ = f32[3,4,8,128]{3,2,1,0:T(8,128)S(1)} collective-permute-done((f32[3,4,8,128]{3,2,1,0:T(8,128)S(1)}, f32[3,4,8,128]{3,2,1,0:T(8,128)S(1)}, u32[]{:S(2)}, u32[]{:S(2)}) %collective-permute-start.51) | collective-permute-done | bytes 49184 | tf_op jit(solution)/shard_map/ppermute | solution.py:318
  174.9 1.8 shard_map.215
  (125 shorter events, 37.3 us)
Async XLA Ops:
  0.6 7.4 %collective-permute-start = (f32[2,4,4,8,128]{4,3,2,1,0:T(8,128)}, f32[2,4,4,8,128]{4,3,2,1,0:T(8,128)S(1)}, u32[]{:S(2)}, u32[]{:S(2)}) collective-permute-start(f32[2,4,4,8,128]{4,3,2,1,0:T(8,128)} %bitcast.71), channel_id=1, source_target_pairs={{32,0},{33,1},{34,2},{35,3},{36,4},{37,5},{38,6},{39,7},{40,8},{41... | collective-permute-start | bytes 393224 | tf_op jit(solution)/shard_map/ppermute | solution.py:318
  8.1 6.9 %collective-permute-start.1 = (f32[12,4,8,128]{3,2,1,0:T(8,128)S(1)}, f32[12,4,8,128]{3,2,1,0:T(8,128)S(1)}, u32[]{:S(2)}, u32[]{:S(2)}) collective-permute-start(f32[12,4,8,128]{3,2,1,0:T(8,128)S(1)} %pad_maximum_fusion.refs_0_.refs_6_), channel_id=1, source_target_pairs={{0,1},{1,2},{2,3},{3,4},{4,5},{5,6},{6,7},{7,8},{8,9},{9,10},{10,1... | collective-permute-start | bytes 589832 | tf_op jit(solution)/shard_map/ppermute | solution.py:318
  11.3 9.3 %collective-permute-start.2 = (f32[12,4,8,128]{3,2,1,0:T(8,128)S(1)}, f32[12,4,8,128]{3,2,1,0:T(8,128)S(1)}, u32[]{:S(2)}, u32[]{:S(2)}) collective-permute-start(f32[12,4,8,128]{3,2,1,0:T(8,128)S(1)} %pad_maximum_fusion.refs_0_.refs_6_), channel_id=1, source_target_pairs={{1,0},{2,1},{3,2},{4,3},{5,4},{6,5},{7,6},{8,7},{9,8},{10,9},{11,1... | collective-permute-start | bytes 589832 | tf_op jit(solution)/shard_map/ppermute | solution.py:318
  21.0 8.6 %collective-permute-start.3 = (f32[12,4,8,128]{3,2,1,0:T(8,128)S(1)}, f32[12,4,8,128]{3,2,1,0:T(8,128)S(1)}, u32[]{:S(2)}, u32[]{:S(2)}) collective-permute-start(f32[12,4,8,128]{3,2,1,0:T(8,128)S(1)} %get-tuple-element.58.refs_0_), channel_id=1, source_target_pairs={{0,1},{1,2},{2,3},{3,4},{4,5},{5,6},{6,7},{7,8},{8,9},{9,10},{10,1... | collective-permute-start | bytes 589832 | tf_op jit(solution)/shard_map/ppermute | solution.py:318
  22.9 10.5 %collective-permute-start.4 = (f32[12,4,8,128]{3,2,1,0:T(8,128)S(1)}, f32[12,4,8,128]{3,2,1,0:T(8,128)S(1)}, u32[]{:S(2)}, u32[]{:S(2)}) collective-permute-start(f32[12,4,8,128]{3,2,1,0:T(8,128)S(1)} %get-tuple-element.59), channel_id=1, source_target_pairs={{1,0},{2,1},{3,2},{4,3},{5,4},{6,5},{7,6},{8,7},{9,8},{10,9},{11,1... | collective-permute-start | bytes 589832 | tf_op jit(solution)/shard_map/ppermute | solution.py:318
  33.8 10.0 %collective-permute-start.5 = (f32[8,4,8,128]{3,2,1,0:T(8,128)S(1)}, f32[8,4,8,128]{3,2,1,0:T(8,128)S(1)}, u32[]{:S(2)}, u32[]{:S(2)}) collective-permute-start(f32[8,4,8,128]{3,2,1,0:T(8,128)S(1)} %get-tuple-element.62.refs_0_), channel_id=1, source_target_pairs={{0,1},{1,2},{2,3},{3,4},{4,5},{5,6},{6,7},{7,8},{8,9},{9,10},{10,1... | collective-permute-start | bytes 393224 | tf_op jit(solution)/shard_map/ppermute | solution.py:318
  35.7 8.7 %collective-permute-start.6 = (f32[8,4,8,128]{3,2,1,0:T(8,128)S(1)}, f32[8,4,8,128]{3,2,1,0:T(8,128)S(1)}, u32[]{:S(2)}, u32[]{:S(2)}) collective-permute-start(f32[8,4,8,128]{3,2,1,0:T(8,128)S(1)} %get-tuple-element.62.refs_0_), channel_id=1, source_target_pairs={{1,0},{2,1},{3,2},{4,3},{5,4},{6,5},{7,6},{8,7},{9,8},{10,9},{11,1... | collective-permute-start | bytes 393224 | tf_op jit(solution)/shard_map/ppermute | solution.py:318
  39.1 11.1 %collective-permute-start.9 = (f32[3,4,4,8,128]{4,3,2,1,0:T(8,128)S(1)}, f32[3,4,4,8,128]{4,3,2,1,0:T(8,128)S(1)}, u32[]{:S(2)}, u32[]{:S(2)}) collective-permute-start(f32[3,4,4,8,128]{4,3,2,1,0:T(8,128)S(1)} %pad_maximum_fusion.1), channel_id=1, source_target_pairs={{32,96},{33,97},{34,98},{35,99},{36,100},{37,101},{38,102},{39,103... | collective-permute-start | bytes 589832 | tf_op jit(solution)/shard_map/ppermute | solution.py:318
  44.8 5.7 %collective-permute-start.7 = (f32[8,4,8,128]{3,2,1,0:T(8,128)S(1)}, f32[8,4,8,128]{3,2,1,0:T(8,128)S(1)}, u32[]{:S(2)}, u32[]{:S(2)}) collective-permute-start(f32[8,4,8,128]{3,2,1,0:T(8,128)S(1)} %get-tuple-element.65.refs_0_), channel_id=1, source_target_pairs={{0,1},{1,2},{2,3},{3,4},{4,5},{5,6},{6,7},{7,8},{8,9},{9,10},{10,1... | collective-permute-start | bytes 393224 | tf_op jit(solution)/shard_map/ppermute | solution.py:318
  48.3 7.8 %collective-permute-start.8 = (f32[8,4,8,128]{3,2,1,0:T(8,128)S(1)}, f32[8,4,8,128]{3,2,1,0:T(8,128)S(1)}, u32[]{:S(2)}, u32[]{:S(2)}) collective-permute-start(f32[8,4,8,128]{3,2,1,0:T(8,128)S(1)} %get-tuple-element.65.refs_0_), channel_id=1, source_target_pairs={{1,0},{2,1},{3,2},{4,3},{5,4},{6,5},{7,6},{8,7},{9,8},{10,9},{11,1... | collective-permute-start | bytes 393224 | tf_op jit(solution)/shard_map/ppermute | solution.py:318
  56.5 6.0 %collective-permute-start.10 = (f32[6,4,4,8,128]{4,3,2,1,0:T(8,128)S(1)}, f32[6,4,4,8,128]{4,3,2,1,0:T(8,128)S(1)}, u32[]{:S(2)}, u32[]{:S(2)}) collective-permute-start(f32[6,4,4,8,128]{4,3,2,1,0:T(8,128)S(1)} %get-tuple-element.68), channel_id=1, source_target_pairs={{0,32},{1,33},{2,34},{3,35},{4,36},{5,37},{6,38},{7,39},{8,40},{9,... | collective-permute-start | bytes 1179656 | tf_op jit(solution)/shard_map/ppermute | solution.py:318
  62.5 5.4 %collective-permute-start.11 = (f32[6,4,8,128]{3,2,1,0:T(8,128)S(1)}, f32[6,4,8,128]{3,2,1,0:T(8,128)S(1)}, u32[]{:S(2)}, u32[]{:S(2)}) collective-permute-start(f32[6,4,8,128]{3,2,1,0:T(8,128)S(1)} %pad_maximum_fusion.2.z0.refs_8_.refs_13_), channel_id=1, source_target_pairs={{32,33},{33,34},{34,35},{35,36},{36,37},{37,38},{38,39},{39,40},{4... | collective-permute-start | bytes 294920 | tf_op jit(solution)/shard_map/ppermute | solution.py:318
  65.3 7.5 %collective-permute-start.12 = (f32[6,4,8,128]{3,2,1,0:T(8,128)S(1)}, f32[6,4,8,128]{3,2,1,0:T(8,128)S(1)}, u32[]{:S(2)}, u32[]{:S(2)}) collective-permute-start(f32[6,4,8,128]{3,2,1,0:T(8,128)S(1)} %pad_maximum_fusion.2.z0.refs_8_.refs_13_), channel_id=1, source_target_pairs={{33,32},{34,33},{35,34},{36,35},{37,36},{38,37},{39,38},{40,39},{4... | collective-permute-start | bytes 294920 | tf_op jit(solution)/shard_map/ppermute | solution.py:318
  73.6 3.4 %collective-permute-start.17 = (f32[3,4,8,128]{3,2,1,0:T(8,128)S(1)}, f32[3,4,8,128]{3,2,1,0:T(8,128)S(1)}, u32[]{:S(2)}, u32[]{:S(2)}) collective-permute-start(f32[3,4,8,128]{3,2,1,0:T(8,128)S(1)} %get-tuple-element.72), channel_id=1, source_target_pairs={{226,160},{227,161},{228,162},{229,163},{230,164},{231,165},{232,1... | collective-permute-start | bytes 147464 | tf_op jit(solution)/shard_map/ppermute | solution.py:318
  74.2 2.7 %collective-permute-start.14 = (f32[6,4,8,128]{3,2,1,0:T(8,128)S(1)}, f32[6,4,8,128]{3,2,1,0:T(8,128)S(1)}, u32[]{:S(2)}, u32[]{:S(2)}) collective-permute-start(f32[6,4,8,128]{3,2,1,0:T(8,128)S(1)} %get-tuple-element.73), channel_id=1, source_target_pairs={{224,161},{225,162},{226,163},{227,164},{228,165},{229,166},{230,1... | collective-permute-start | bytes 294920 | tf_op jit(solution)/shard_map/ppermute | solution.py:318
  77.8 3.4 %collective-permute-start.23 = (f32[3,4,8,128]{3,2,1,0:T(8,128)S(1)}, f32[3,4,8,128]{3,2,1,0:T(8,128)S(1)}, u32[]{:S(2)}, u32[]{:S(2)}) collective-permute-start(f32[3,4,8,128]{3,2,1,0:T(8,128)S(1)} %get-tuple-element.78), channel_id=1, source_target_pairs={{162,96},{163,97},{164,98},{165,99},{166,100},{167,101},{168,102},... | collective-permute-start | bytes 147464 | tf_op jit(solution)/shard_map/ppermute | solution.py:318
  78.5 2.7 %collective-permute-start.20 = (f32[6,4,8,128]{3,2,1,0:T(8,128)S(1)}, f32[6,4,8,128]{3,2,1,0:T(8,128)S(1)}, u32[]{:S(2)}, u32[]{:S(2)}) collective-permute-start(f32[6,4,8,128]{3,2,1,0:T(8,128)S(1)} %get-tuple-element.79), channel_id=1, source_target_pairs={{160,97},{161,98},{162,99},{163,100},{164,101},{165,102},{166,103}... | collective-permute-start | bytes 294920 | tf_op jit(solution)/shard_map/ppermute | solution.py:318
  82.1 30.4 %collective-permute-start.29 = (f32[3,4,8,128]{3,2,1,0:T(8,128)S(1)}, f32[3,4,8,128]{3,2,1,0:T(8,128)S(1)}, u32[]{:S(2)}, u32[]{:S(2)}) collective-permute-start(f32[3,4,8,128]{3,2,1,0:T(8,128)S(1)} %get-tuple-element.84), channel_id=1, source_target_pairs={{98,32},{99,33},{100,34},{101,35},{102,36},{103,37},{104,38},{105,... | collective-permute-start | bytes 147464 | tf_op jit(solution)/shard_map/ppermute | solution.py:318
  83.4 29.1 %collective-permute-start.26 = (f32[6,4,8,128]{3,2,1,0:T(8,128)S(1)}, f32[6,4,8,128]{3,2,1,0:T(8,128)S(1)}, u32[]{:S(2)}, u32[]{:S(2)}) collective-permute-start(f32[6,4,8,128]{3,2,1,0:T(8,128)S(1)} %get-tuple-element.85), channel_id=1, source_target_pairs={{96,33},{97,34},{98,35},{99,36},{100,37},{101,38},{102,39},{103,40... | collective-permute-start | bytes 294920 | tf_op jit(solution)/shard_map/ppermute | solution.py:318
  84.7 30.2 %collective-permute-start.28 = (f32[6,4,8,128]{3,2,1,0:T(8,128)S(1)}, f32[6,4,8,128]{3,2,1,0:T(8,128)S(1)}, u32[]{:S(2)}, u32[]{:S(2)}) collective-permute-start(f32[6,4,8,128]{3,2,1,0:T(8,128)S(1)} %get-tuple-element.85), channel_id=1, source_target_pairs={{97,32},{98,33},{99,34},{100,35},{101,36},{102,37},{103,38},{104,3... | collective-permute-start | bytes 294920 | tf_op jit(solution)/shard_map/ppermute | solution.py:318
  86.0 26.5 %collective-permute-start.25 = (f32[3,4,8,128]{3,2,1,0:T(8,128)S(1)}, f32[3,4,8,128]{3,2,1,0:T(8,128)S(1)}, u32[]{:S(2)}, u32[]{:S(2)}) collective-permute-start(f32[3,4,8,128]{3,2,1,0:T(8,128)S(1)} %get-tuple-element.84), channel_id=1, source_target_pairs={{96,34},{97,35},{98,36},{99,37},{100,38},{101,39},{102,40},{103,41... | collective-permute-start | bytes 147464 | tf_op jit(solution)/shard_map/ppermute | solution.py:318
  87.3 28.0 %collective-permute-start.27 = (f32[11,4,8,128]{3,2,1,0:T(8,128)S(1)}, f32[11,4,8,128]{3,2,1,0:T(8,128)S(1)}, u32[]{:S(2)}, u32[]{:S(2)}) collective-permute-start(f32[11,4,8,128]{3,2,1,0:T(8,128)S(1)} %get-tuple-element.86), channel_id=1, source_target_pairs={{96,32},{97,33},{98,34},{99,35},{100,36},{101,37},{102,38},{103,39... | collective-permute-start | bytes 540680 | tf_op jit(solution)/shard_map/ppermute | solution.py:318
  116.0 3.4 %collective-permute-start.35 = (f32[3,4,8,128]{3,2,1,0:T(8,128)S(1)}, f32[3,4,8,128]{3,2,1,0:T(8,128)S(1)}, u32[]{:S(2)}, u32[]{:S(2)}) collective-permute-start(f32[3,4,8,128]{3,2,1,0:T(8,128)S(1)} %get-tuple-element.90), channel_id=1, source_target_pairs={{290,224},{291,225},{292,226},{293,227},{294,228},{295,229},{296,2... | collective-permute-start | bytes 147464 | tf_op jit(solution)/shard_map/ppermute | solution.py:318
  116.7 2.7 %collective-permute-start.32 = (f32[6,4,8,128]{3,2,1,0:T(8,128)S(1)}, f32[6,4,8,128]{3,2,1,0:T(8,128)S(1)}, u32[]{:S(2)}, u32[]{:S(2)}) collective-permute-start(f32[6,4,8,128]{3,2,1,0:T(8,128)S(1)} %get-tuple-element.91), channel_id=1, source_target_pairs={{288,225},{289,226},{290,227},{291,228},{292,229},{293,230},{294,2... | collective-permute-start | bytes 294920 | tf_op jit(solution)/shard_map/ppermute | solution.py:318
  119.5 3.1 %collective-permute-start.36 = (f32[4,4,8,128]{3,2,1,0:T(8,128)S(1)}, f32[4,4,8,128]{3,2,1,0:T(8,128)S(1)}, u32[]{:S(2)}, u32[]{:S(2)}) collective-permute-start(f32[4,4,8,128]{3,2,1,0:T(8,128)S(1)} %get-tuple-element.132), channel_id=1, source_target_pairs={{0,32},{1,33},{2,34},{3,35},{4,36},{5,37},{6,38},{7,39},{8,40},{9,... | collective-permute-start | bytes 196616 | tf_op jit(solution)/shard_map/ppermute | solution.py:318
  123.4 3.4 %collective-permute-start.39 = (f32[11,4,8,128]{3,2,1,0:T(8,128)S(1)}, f32[11,4,8,128]{3,2,1,0:T(8,128)S(1)}, u32[]{:S(2)}, u32[]{:S(2)}) collective-permute-start(f32[11,4,8,128]{3,2,1,0:T(8,128)S(1)} %get-tuple-element.98), channel_id=1, source_target_pairs={{224,160},{225,161},{226,162},{227,163},{228,164},{229,165},{230,1... | collective-permute-start | bytes 540680 | tf_op jit(solution)/shard_map/ppermute | solution.py:318
  127.0 3.4 %collective-permute-start.44 = (f32[11,4,8,128]{3,2,1,0:T(8,128)S(1)}, f32[11,4,8,128]{3,2,1,0:T(8,128)S(1)}, u32[]{:S(2)}, u32[]{:S(2)}) collective-permute-start(f32[11,4,8,128]{3,2,1,0:T(8,128)S(1)} %get-tuple-element.103), channel_id=1, source_target_pairs={{160,96},{161,97},{162,98},{163,99},{164,100},{165,101},{166,102},... | collective-permute-start | bytes 540680 | tf_op jit(solution)/shard_map/ppermute | solution.py:318
  130.5 44.4 %collective-permute-start.49 = (f32[11,4,8,128]{3,2,1,0:T(8,128)S(1)}, f32[11,4,8,128]{3,2,1,0:T(8,128)S(1)}, u32[]{:S(2)}, u32[]{:S(2)}) collective-permute-start(f32[11,4,8,128]{3,2,1,0:T(8,128)S(1)} %get-tuple-element.108), channel_id=1, source_target_pairs={{96,32},{97,33},{98,34},{99,35},{100,36},{101,37},{102,38},{103,39... | collective-permute-start | bytes 540680 | tf_op jit(solution)/shard_map/ppermute | solution.py:318
  131.8 43.1 %collective-permute-start.48 = (f32[6,4,8,128]{3,2,1,0:T(8,128)S(1)}, f32[6,4,8,128]{3,2,1,0:T(8,128)S(1)}, u32[]{:S(2)}, u32[]{:S(2)}) collective-permute-start(f32[6,4,8,128]{3,2,1,0:T(8,128)S(1)} %get-tuple-element.107), channel_id=1, source_target_pairs={{96,33},{97,34},{98,35},{99,36},{100,37},{101,38},{102,39},{103,40... | collective-permute-start | bytes 294920 | tf_op jit(solution)/shard_map/ppermute | solution.py:318
  133.1 41.8 %collective-permute-start.50 = (f32[6,4,8,128]{3,2,1,0:T(8,128)S(1)}, f32[6,4,8,128]{3,2,1,0:T(8,128)S(1)}, u32[]{:S(2)}, u32[]{:S(2)}) collective-permute-start(f32[6,4,8,128]{3,2,1,0:T(8,128)S(1)} %get-tuple-element.107), channel_id=1, source_target_pairs={{97,32},{98,33},{99,34},{100,35},{101,36},{102,37},{103,38},{104,3... | collective-permute-start | bytes 294920 | tf_op jit(solution)/shard_map/ppermute | solution.py:318
  134.4 37.1 %collective-permute-start.47 = (f32[3,4,8,128]{3,2,1,0:T(8,128)S(1)}, f32[3,4,8,128]{3,2,1,0:T(8,128)S(1)}, u32[]{:S(2)}, u32[]{:S(2)}) collective-permute-start(f32[3,4,8,128]{3,2,1,0:T(8,128)S(1)} %get-tuple-element.106), channel_id=1, source_target_pairs={{96,34},{97,35},{98,36},{99,37},{100,38},{101,39},{102,40},{103,41... | collective-permute-start | bytes 147464 | tf_op jit(solution)/shard_map/ppermute | solution.py:318
  135.7 39.2 %collective-permute-start.51 = (f32[3,4,8,128]{3,2,1,0:T(8,128)S(1)}, f32[3,4,8,128]{3,2,1,0:T(8,128)S(1)}, u32[]{:S(2)}, u32[]{:S(2)}) collective-permute-start(f32[3,4,8,128]{3,2,1,0:T(8,128)S(1)} %get-tuple-element.106), channel_id=1, source_target_pairs={{98,32},{99,33},{100,34},{101,35},{102,36},{103,37},{104,38},{105,... | collective-permute-start | bytes 147464 | tf_op jit(solution)/shard_map/ppermute | solution.py:318
  (26 other events, 36.0 us)

commit v7 on v6

--- a/solution.py
+++ b/solution.py
@@ -130,7 +130,7 @@
         refs = list(refs)
         r0, rl, rh, u, prev = [refs.pop(0) for _ in range(5)]
         src, inv = (None, None) if last else [refs.pop(0) for _ in range(2)]
-        factors = [refs.pop(0) for _ in range(4)][:3] if last else None
+        factors = [refs.pop(0) for _ in range(3)] if last else None
         old = None if first else refs.pop(0)
         out = None if last else refs.pop(0)
         grad, more, scratch = refs[0], refs[1:-3], refs[-3:]
@@ -210,8 +210,9 @@
     return call(body, [(2,) + SLAB, SLAB], *operands, layers=3 * WIDTH, flops=56 * 4 * 1024 * 20)
 
 
-def chip_step(turn, place, arrived, inv_five, pack, own_three, pair, offset, ahead, done, grad):
+def chip_step(turn, place, arrived, inv_five, pack, own_three, pair, offset, ahead, solved, done, grad):
     with_done, with_grad, with_z = done is not None, grad is not None, arrived is not None
+    final = turn == 1
 
     def body(*refs):
         refs = list(refs)
@@ -221,21 +222,23 @@
         even = refs.pop(0)
         zo = [refs.pop(0) for _ in range(3)]
         z7, x1, o, qa = [refs.pop(0) for _ in range(4)]
+        qs = refs.pop(0) if with_z else None
         before = [refs.pop(0) for _ in range(2)] if with_done else None
         g = [refs.pop(0) for _ in range(2)] if with_grad else None
-        z3, z6, z11, odd_pair, even_pair = refs[:5]
+        odd_pair, even_pair = refs.pop(0), refs.pop(0)
+        sums = refs.pop(0) if with_grad else None
+        z3, z6, z7_out = [None] * 3 if final else refs[:3]
         middle, scratch = refs[-4], refs[-3:]
         if with_grad:
-            refs[5][...] = g[0][...] + g[1][...]
+            sums[...] = g[0][...] + g[1][...]
         mine = spot[0] == turn
 
         @pl.when(jnp.logical_not(mine))
         def _():
             odd_pair[...] = before[0][...] if with_done else jnp.zeros_like(odd_pair)
             even_pair[...] = before[1][...] if with_done else jnp.zeros_like(even_pair)
-            z3[...] = jnp.zeros_like(z3)
-            z6[...] = jnp.zeros_like(z6)
-            z11[...] = jnp.zeros_like(z11)
+            for part in () if final else (z3, z6, z7_out):
+                part[...] = jnp.zeros_like(part)
 
         @pl.when(mine)
         def _():
@@ -246,10 +249,10 @@
                 slab, at = layer // WIDTH, layer % WIDTH
                 for f in range(FIELDS):
                     if slab == 1:
-                        solved = z[2][3 + f, at] if with_z else zero
-                        change = z[2][7 + f, at] if with_z else zero
-                        c0 = q[f] + (z7[3 + f, at] - solved)
-                        c1 = x1[f, at] + 0.5 * ((q[f] - solved) + change)
+                        before_q = qs[f, at] if with_z else zero
+                        change = z[2][3 + f, at] if with_z else zero
+                        c0 = q[f] + (z7[3 + f, at] - before_q)
+                        c1 = x1[f, at] + 0.5 * ((q[f] - before_q) + change)
                         odd_pair[0, f, at] = c0
                         odd_pair[1, f, at] = c1
                         if masses[f]:
@@ -265,13 +268,14 @@
                     change = c0 - even[0, f, layer]
                     even_pair[0, f, layer] = c0
                     even_pair[1, f, layer] = c1
-                    z11[3 + f, layer] = qa[f, layer]
-                    z11[7 + f, layer] = change
+                    if final:
+                        continue
+                    z7_out[3 + f, layer] = change
                     if masses[f]:
                         carried = c0 - 0.25 * c1
                         z3[f, layer] = carried
                         z6[f, layer] = carried
-                        z11[f, layer] = carried
+                        z7_out[f, layer] = carried
                         z6[3 + f, layer] = -0.875 * qa[f, layer] - 0.125 * change
 
             if with_z:
@@ -286,10 +290,11 @@
     spec = pl.BlockSpec(memory_space=pltpu.VMEM)
     operands = [place] + (list(arrived) if with_z else []) + list(inv_five) + [pack]
     operands += list(own_three) + list(pair) + [offset, ahead]
+    operands += [solved] if with_z else []
     operands += list(done) if with_done else []
     operands += list(grad) if with_grad else []
-    outs = [carry(3), carry(6), carry(11), (2,) + SLAB, (2,) + SLAB]
-    outs += [SLAB] if with_grad else []
+    outs = [(2,) + SLAB, (2,) + SLAB] + ([SLAB] if with_grad else [])
+    outs += [] if final else [carry(3), carry(6), carry(7)]
     return pl.pallas_call(
         body,
         in_specs=[pl.BlockSpec(memory_space=pltpu.SMEM)] + [spec] * (len(operands) - 1),
@@ -333,6 +338,7 @@
     odd, even = (lambda k: k % 2 == 1), (lambda k: k % 2 == 0)
     odd_right, odd_left = (routes(times, slabs, lambda k, s, d=d: (k, s + d), odd) for d in (1, -1))
     later = routes(times, slabs, lambda k, s: (k + 2, s), odd)
+    sooner = routes(times, slabs, lambda k, s: (k - 2, s), odd)
 
     def hop_routes(hop):
         group = [h for h in range(1, chips) if (h - hop) % 4 == 0]
@@ -357,9 +363,7 @@
             if n:
                 rest = dict(source=adjoint_source[n - 1], factor=inverses[n - 1])
             else:
-                far = [part[2 * FIELDS :] for part in exchanged[0]]
-                prior = send(jnp.stack(far), later)
-                rest = dict(coarse=(*exchanged[0], prior))
+                rest = dict(coarse=exchanged[0])
             step = fine_step(n, up, low, high, states[n], previous, total, **rest)
             if n:
                 previous, total, up, *more = step
@@ -368,11 +372,13 @@
         inv_five = [part[2 * FIELDS :] for part in (low_two, low, own, high, high_two)]
         total, z7, pack = step
 
+        prior = send(jnp.stack([part[2 * FIELDS :] for part in (low, own, high)]), later)
         pack = send(pack, swap)
         grad = total + pack[5]
         both = jnp.concatenate([z7[:3], pack[0, :3] - 0.25 * pack[1, :3]])
         own_three = (send(both, odd_right), both, send(both, odd_left))
         offset, before = offsets_step(pack, *own_three, z7, prior)
+        solved = send(before, sooner)
 
         place = (lax.axis_index("tm").astype(jnp.int32)).reshape(1)
         is_even = lax.axis_index("tm") % 2 == 0
@@ -392,13 +398,18 @@
                 received = send(jnp.where(place[0] < 0, mark, grad), stages.pop(0))
                 added = (grad if stages else jnp.where(is_even, grad, 0.0), received)
             if hop < chips:
-                z3, z6, z11, odd_pair, even_pair, *sums = chip_step(
+                odd_pair, even_pair, *more = chip_step(
                     times - 1 - 2 * hop, place, arrived, inv_five, pack, own_three, (z7, previous),
-                    offset, before, done, added,
+                    offset, before, solved if hop else None, done, added,
                 )
-                payload, done = (z3, z6, z11, z6, z3), (odd_pair, even_pair)
-                if sums:
-                    grad = sums[0]
+                if added:
+                    grad = more.pop(0)
+                if hop < chips - 1:
+                    z3, z6, z7_out = more
+                    if not hop:
+                        z3, z6, z7_out = (jnp.where(place[0] < 0, solved[:1], p) for p in more)
+                    payload = (z3, z6, z7_out, z6, z3)
+                done = (odd_pair, even_pair)
             elif added:
                 grad = added[0] + added[1]
 

time: 181 us -> 182 us (level)
  the two profiles are of different devices: /device:TPU:23 before, /device:TPU:25 now
where the time goes in v7:
time: 182 us; the launch traced here: 181 us
  waiting for transfers between devices  86.8 us (48%)
  starting transfers between devices  85.2 us (47%)
  Pallas kernels  4.59 us (3%)
  other arithmetic  1.99 us (1%)
    ppermute x54, waiting for transfers between devices, send(): return lax.ppermute(value, AXES, pairs)  86.8 us
    ppermute x54, starting transfers between devices, send(): return lax.ppermute(value, AXES, pairs)  85.2 us
  transfers between devices with their start and end apart: 54, of which 19 were waited for; matrix products, arithmetic and copies ran while one was open for 1% of the time, Pallas kernels for 0%

profile of v7, /device:TPU:25, one launch (start us, length us, event | category | flops | bytes accessed | tf_op | source)
XLA Modules:
  0.0 181.1 jit_solution(5676483968326714980)
XLA Ops:
  0.6 2.7 %collective-permute-start = (f32[2,4,4,8,128]{4,3,2,1,0:T(8,128)}, f32[2,4,4,8,128]{4,3,2,1,0:T(8,128)S(1)}, u32[]{:S(2)}, u32[]{:S(2)}) collective-permute-start(f32[2,4,4,8,128]{4,3,2,1,0:T(8,128)} %bitcast.73), channel_id=1, source_target_pairs={{32,0},{33,1},{34,2},{35,3},{36,4},{37,5},{38,6},{39,7},{40,8},{41... | collective-permute-start | bytes 393224 | tf_op jit(solution)/shard_map/ppermute | solution.py:323
  5.3 2.9 %collective-permute-done = f32[2,4,4,8,128]{4,3,2,1,0:T(8,128)S(1)} collective-permute-done((f32[2,4,4,8,128]{4,3,2,1,0:T(8,128)}, f32[2,4,4,8,128]{4,3,2,1,0:T(8,128)S(1)}, u32[]{:S(2)}, u32[]{:S(2)}) %collective-permute-start) | collective-permute-done | bytes 131104 | tf_op jit(solution)/shard_map/ppermute | solution.py:323
  8.3 3.1 %collective-permute-start.1 = (f32[12,4,8,128]{3,2,1,0:T(8,128)S(1)}, f32[12,4,8,128]{3,2,1,0:T(8,128)S(1)}, u32[]{:S(2)}, u32[]{:S(2)}) collective-permute-start(f32[12,4,8,128]{3,2,1,0:T(8,128)S(1)} %pad_maximum_fusion.refs_0_.refs_6_), channel_id=1, source_target_pairs={{0,1},{1,2},{2,3},{3,4},{4,5},{5,6},{6,7},{7,8},{8,9},{9,10},{10,1... | collective-permute-start | bytes 589832 | tf_op jit(solution)/shard_map/ppermute | solution.py:323
  11.4 4.3 %collective-permute-start.2 = (f32[12,4,8,128]{3,2,1,0:T(8,128)S(1)}, f32[12,4,8,128]{3,2,1,0:T(8,128)S(1)}, u32[]{:S(2)}, u32[]{:S(2)}) collective-permute-start(f32[12,4,8,128]{3,2,1,0:T(8,128)S(1)} %pad_maximum_fusion.refs_0_.refs_6_), channel_id=1, source_target_pairs={{1,0},{2,1},{3,2},{4,3},{5,4},{6,5},{7,6},{8,7},{9,8},{10,9},{11,1... | collective-permute-start | bytes 589832 | tf_op jit(solution)/shard_map/ppermute | solution.py:323
  16.8 1.5 collective-permute-done.2.refs_2_.refs_7_
  18.7 2.7 %collective-permute-start.3 = (f32[12,4,8,128]{3,2,1,0:T(8,128)S(1)}, f32[12,4,8,128]{3,2,1,0:T(8,128)S(1)}, u32[]{:S(2)}, u32[]{:S(2)}) collective-permute-start(f32[12,4,8,128]{3,2,1,0:T(8,128)S(1)} %get-tuple-element.58.refs_0_), channel_id=1, source_target_pairs={{0,1},{1,2},{2,3},{3,4},{4,5},{5,6},{6,7},{7,8},{8,9},{9,10},{10,1... | collective-permute-start | bytes 589832 | tf_op jit(solution)/shard_map/ppermute | solution.py:323
  21.4 5.2 %collective-permute-start.4 = (f32[12,4,8,128]{3,2,1,0:T(8,128)S(1)}, f32[12,4,8,128]{3,2,1,0:T(8,128)S(1)}, u32[]{:S(2)}, u32[]{:S(2)}) collective-permute-start(f32[12,4,8,128]{3,2,1,0:T(8,128)S(1)} %get-tuple-element.59), channel_id=1, source_target_pairs={{1,0},{2,1},{3,2},{4,3},{5,4},{6,5},{7,6},{8,7},{9,8},{10,9},{11,1... | collective-permute-start | bytes 589832 | tf_op jit(solution)/shard_map/ppermute | solution.py:323
  26.5 1.8 %collective-permute-done.3.refs_1_ = f32[12,4,8,128]{3,2,1,0:T(8,128)S(1)} collective-permute-done((f32[12,4,8,128]{3,2,1,0:T(8,128)S(1)}, f32[12,4,8,128]{3,2,1,0:T(8,128)S(1)}, u32[]{:S(2)}, u32[]{:S(2)}) %collective-permute-start.3) | collective-permute-done | bytes 196640 | tf_op jit(solution)/shard_map/ppermute | solution.py:323
  28.4 1.8 collective-permute-done.4.refs_2_
  30.5 5.7 %collective-permute-start.5 = (f32[8,4,8,128]{3,2,1,0:T(8,128)S(1)}, f32[8,4,8,128]{3,2,1,0:T(8,128)S(1)}, u32[]{:S(2)}, u32[]{:S(2)}) collective-permute-start(f32[8,4,8,128]{3,2,1,0:T(8,128)S(1)} %get-tuple-element.62.refs_0_), channel_id=1, source_target_pairs={{0,1},{1,2},{2,3},{3,4},{4,5},{5,6},{6,7},{7,8},{8,9},{9,10},{10,1... | collective-permute-start | bytes 393224 | tf_op jit(solution)/shard_map/ppermute | solution.py:323
  36.3 2.1 %collective-permute-start.6 = (f32[8,4,8,128]{3,2,1,0:T(8,128)S(1)}, f32[8,4,8,128]{3,2,1,0:T(8,128)S(1)}, u32[]{:S(2)}, u32[]{:S(2)}) collective-permute-start(f32[8,4,8,128]{3,2,1,0:T(8,128)S(1)} %get-tuple-element.62.refs_0_), channel_id=1, source_target_pairs={{1,0},{2,1},{3,2},{4,3},{5,4},{6,5},{7,6},{8,7},{9,8},{10,9},{11,1... | collective-permute-start | bytes 393224 | tf_op jit(solution)/shard_map/ppermute | solution.py:323
  38.4 1.6 collective-permute-done.5.refs_1_
  40.0 3.6 %collective-permute-done.6.refs_2_ = f32[8,4,8,128]{3,2,1,0:T(8,128)S(1)} collective-permute-done((f32[8,4,8,128]{3,2,1,0:T(8,128)S(1)}, f32[8,4,8,128]{3,2,1,0:T(8,128)S(1)}, u32[]{:S(2)}, u32[]{:S(2)}) %collective-permute-start.6) | collective-permute-done | bytes 131104 | tf_op jit(solution)/shard_map/ppermute | solution.py:323
  44.0 5.3 %collective-permute-start.7 = (f32[8,4,8,128]{3,2,1,0:T(8,128)S(1)}, f32[8,4,8,128]{3,2,1,0:T(8,128)S(1)}, u32[]{:S(2)}, u32[]{:S(2)}) collective-permute-start(f32[8,4,8,128]{3,2,1,0:T(8,128)S(1)} %get-tuple-element.65.refs_0_), channel_id=1, source_target_pairs={{0,1},{1,2},{2,3},{3,4},{4,5},{5,6},{6,7},{7,8},{8,9},{9,10},{10,1... | collective-permute-start | bytes 393224 | tf_op jit(solution)/shard_map/ppermute | solution.py:323
  49.3 2.1 %collective-permute-start.8 = (f32[8,4,8,128]{3,2,1,0:T(8,128)S(1)}, f32[8,4,8,128]{3,2,1,0:T(8,128)S(1)}, u32[]{:S(2)}, u32[]{:S(2)}) collective-permute-start(f32[8,4,8,128]{3,2,1,0:T(8,128)S(1)} %get-tuple-element.65.refs_0_), channel_id=1, source_target_pairs={{1,0},{2,1},{3,2},{4,3},{5,4},{6,5},{7,6},{8,7},{9,8},{10,9},{11,1... | collective-permute-start | bytes 393224 | tf_op jit(solution)/shard_map/ppermute | solution.py:323
  52.3 3.2 %collective-permute-done.8.refs_2_ = f32[8,4,8,128]{3,2,1,0:T(8,128)S(1)} collective-permute-done((f32[8,4,8,128]{3,2,1,0:T(8,128)S(1)}, f32[8,4,8,128]{3,2,1,0:T(8,128)S(1)}, u32[]{:S(2)}, u32[]{:S(2)}) %collective-permute-start.8) | collective-permute-done | bytes 131104 | tf_op jit(solution)/shard_map/ppermute | solution.py:323
  56.0 3.5 %collective-permute-start.9 = (f32[6,4,4,8,128]{4,3,2,1,0:T(8,128)S(1)}, f32[6,4,4,8,128]{4,3,2,1,0:T(8,128)S(1)}, u32[]{:S(2)}, u32[]{:S(2)}) collective-permute-start(f32[6,4,4,8,128]{4,3,2,1,0:T(8,128)S(1)} %get-tuple-element.68), channel_id=1, source_target_pairs={{0,32},{1,33},{2,34},{3,35},{4,36},{5,37},{6,38},{7,39},{8,40},{9,... | collective-permute-start | bytes 1179656 | tf_op jit(solution)/shard_map/ppermute | solution.py:323
  59.5 5.7 %collective-permute-start.12 = (f32[3,4,4,8,128]{4,3,2,1,0:T(8,128)S(1)}, f32[3,4,4,8,128]{4,3,2,1,0:T(8,128)S(1)}, u32[]{:S(2)}, u32[]{:S(2)}) collective-permute-start(f32[3,4,4,8,128]{4,3,2,1,0:T(8,128)S(1)} %pad_maximum_fusion.1), channel_id=1, source_target_pairs={{32,96},{33,97},{34,98},{35,99},{36,100},{37,101},{38,102},{39,103... | collective-permute-start | bytes 589832 | tf_op jit(solution)/shard_map/ppermute | solution.py:323
  65.3 5.0 %collective-permute-start.10 = (f32[6,4,8,128]{3,2,1,0:T(8,128)S(1)}, f32[6,4,8,128]{3,2,1,0:T(8,128)S(1)}, u32[]{:S(2)}, u32[]{:S(2)}) collective-permute-start(f32[6,4,8,128]{3,2,1,0:T(8,128)S(1)} %pad_maximum_fusion.2.z0.refs_8_.refs_13_), channel_id=1, source_target_pairs={{32,33},{33,34},{34,35},{35,36},{36,37},{37,38},{38,39},{39,40},{4... | collective-permute-start | bytes 294920 | tf_op jit(solution)/shard_map/ppermute | solution.py:323
  70.3 2.4 %collective-permute-start.11 = (f32[6,4,8,128]{3,2,1,0:T(8,128)S(1)}, f32[6,4,8,128]{3,2,1,0:T(8,128)S(1)}, u32[]{:S(2)}, u32[]{:S(2)}) collective-permute-start(f32[6,4,8,128]{3,2,1,0:T(8,128)S(1)} %pad_maximum_fusion.2.z0.refs_8_.refs_13_), channel_id=1, source_target_pairs={{33,32},{34,33},{35,34},{36,35},{37,36},{38,37},{39,38},{40,39},{4... | collective-permute-start | bytes 294920 | tf_op jit(solution)/shard_map/ppermute | solution.py:323
  72.8 3.1 %collective-permute-done.11.zh.refs_9_.refs_14_ = f32[6,4,8,128]{3,2,1,0:T(8,128)S(1)} collective-permute-done((f32[6,4,8,128]{3,2,1,0:T(8,128)S(1)}, f32[6,4,8,128]{3,2,1,0:T(8,128)S(1)}, u32[]{:S(2)}, u32[]{:S(2)}) %collective-permute-start.11) | collective-permute-done | bytes 98336 | tf_op jit(solution)/shard_map/ppermute | solution.py:323
  76.6 1.3 collective-permute-start.13
  78.0 4.2 %collective-permute-done.13.refs_19_ = f32[4,4,8,128]{3,2,1,0:T(8,128)S(1)} collective-permute-done((f32[4,4,8,128]{3,2,1,0:T(8,128)S(1)}, f32[4,4,8,128]{3,2,1,0:T(8,128)S(1)}, u32[]{:S(2)}, u32[]{:S(2)}) %collective-permute-start.13) | collective-permute-done | bytes 65568 | tf_op jit(solution)/shard_map/ppermute | solution.py:323
  90.8 1.3 collective-permute-start.30
  92.1 1.3 collective-permute-start.27
  93.4 1.3 collective-permute-start.29
  97.3 24.4 %collective-permute-done.30.refs_5_ = f32[3,4,8,128]{3,2,1,0:T(8,128)S(1)} collective-permute-done((f32[3,4,8,128]{3,2,1,0:T(8,128)S(1)}, f32[3,4,8,128]{3,2,1,0:T(8,128)S(1)}, u32[]{:S(2)}, u32[]{:S(2)}) %collective-permute-start.30) | collective-permute-done | bytes 49184 | tf_op jit(solution)/shard_map/ppermute | solution.py:323
  121.8 3.4 %collective-permute-done.28.refs_3_ = f32[7,4,8,128]{3,2,1,0:T(8,128)S(1)} collective-permute-done((f32[7,4,8,128]{3,2,1,0:T(8,128)S(1)}, f32[7,4,8,128]{3,2,1,0:T(8,128)S(1)}, u32[]{:S(2)}, u32[]{:S(2)}) %collective-permute-start.28) | collective-permute-done | bytes 114720 | tf_op jit(solution)/shard_map/ppermute | solution.py:323
  130.8 1.8 %collective-permute-done.37.refs_23_ = f32[4,4,8,128]{3,2,1,0:T(8,128)S(1)} collective-permute-done((f32[4,4,8,128]{3,2,1,0:T(8,128)S(1)}, f32[4,4,8,128]{3,2,1,0:T(8,128)S(1)}, u32[]{:S(2)}, u32[]{:S(2)}) %collective-permute-start.37) | collective-permute-done | bytes 65568 | tf_op jit(solution)/shard_map/ppermute | solution.py:323
  147.0 28.5 %collective-permute-done.48.refs_1_ = f32[3,4,8,128]{3,2,1,0:T(8,128)S(1)} collective-permute-done((f32[3,4,8,128]{3,2,1,0:T(8,128)S(1)}, f32[3,4,8,128]{3,2,1,0:T(8,128)S(1)}, u32[]{:S(2)}, u32[]{:S(2)}) %collective-permute-start.48) | collective-permute-done | bytes 49184 | tf_op jit(solution)/shard_map/ppermute | solution.py:323
  175.5 1.6 collective-permute-done.52.refs_5_
  178.2 1.3 collective-permute-start.53
  (130 shorter events, 39.6 us)
Async XLA Ops:
  0.6 7.5 %collective-permute-start = (f32[2,4,4,8,128]{4,3,2,1,0:T(8,128)}, f32[2,4,4,8,128]{4,3,2,1,0:T(8,128)S(1)}, u32[]{:S(2)}, u32[]{:S(2)}) collective-permute-start(f32[2,4,4,8,128]{4,3,2,1,0:T(8,128)} %bitcast.73), channel_id=1, source_target_pairs={{32,0},{33,1},{34,2},{35,3},{36,4},{37,5},{38,6},{39,7},{40,8},{41... | collective-permute-start | bytes 393224 | tf_op jit(solution)/shard_map/ppermute | solution.py:323
  8.3 8.5 %collective-permute-start.1 = (f32[12,4,8,128]{3,2,1,0:T(8,128)S(1)}, f32[12,4,8,128]{3,2,1,0:T(8,128)S(1)}, u32[]{:S(2)}, u32[]{:S(2)}) collective-permute-start(f32[12,4,8,128]{3,2,1,0:T(8,128)S(1)} %pad_maximum_fusion.refs_0_.refs_6_), channel_id=1, source_target_pairs={{0,1},{1,2},{2,3},{3,4},{4,5},{5,6},{6,7},{7,8},{8,9},{9,10},{10,1... | collective-permute-start | bytes 589832 | tf_op jit(solution)/shard_map/ppermute | solution.py:323
  11.4 6.9 %collective-permute-start.2 = (f32[12,4,8,128]{3,2,1,0:T(8,128)S(1)}, f32[12,4,8,128]{3,2,1,0:T(8,128)S(1)}, u32[]{:S(2)}, u32[]{:S(2)}) collective-permute-start(f32[12,4,8,128]{3,2,1,0:T(8,128)S(1)} %pad_maximum_fusion.refs_0_.refs_6_), channel_id=1, source_target_pairs={{1,0},{2,1},{3,2},{4,3},{5,4},{6,5},{7,6},{8,7},{9,8},{10,9},{11,1... | collective-permute-start | bytes 589832 | tf_op jit(solution)/shard_map/ppermute | solution.py:323
  18.7 9.7 %collective-permute-start.3 = (f32[12,4,8,128]{3,2,1,0:T(8,128)S(1)}, f32[12,4,8,128]{3,2,1,0:T(8,128)S(1)}, u32[]{:S(2)}, u32[]{:S(2)}) collective-permute-start(f32[12,4,8,128]{3,2,1,0:T(8,128)S(1)} %get-tuple-element.58.refs_0_), channel_id=1, source_target_pairs={{0,1},{1,2},{2,3},{3,4},{4,5},{5,6},{6,7},{7,8},{8,9},{9,10},{10,1... | collective-permute-start | bytes 589832 | tf_op jit(solution)/shard_map/ppermute | solution.py:323
  21.4 8.8 %collective-permute-start.4 = (f32[12,4,8,128]{3,2,1,0:T(8,128)S(1)}, f32[12,4,8,128]{3,2,1,0:T(8,128)S(1)}, u32[]{:S(2)}, u32[]{:S(2)}) collective-permute-start(f32[12,4,8,128]{3,2,1,0:T(8,128)S(1)} %get-tuple-element.59), channel_id=1, source_target_pairs={{1,0},{2,1},{3,2},{4,3},{5,4},{6,5},{7,6},{8,7},{9,8},{10,9},{11,1... | collective-permute-start | bytes 589832 | tf_op jit(solution)/shard_map/ppermute | solution.py:323
  30.5 9.5 %collective-permute-start.5 = (f32[8,4,8,128]{3,2,1,0:T(8,128)S(1)}, f32[8,4,8,128]{3,2,1,0:T(8,128)S(1)}, u32[]{:S(2)}, u32[]{:S(2)}) collective-permute-start(f32[8,4,8,128]{3,2,1,0:T(8,128)S(1)} %get-tuple-element.62.refs_0_), channel_id=1, source_target_pairs={{0,1},{1,2},{2,3},{3,4},{4,5},{5,6},{6,7},{7,8},{8,9},{9,10},{10,1... | collective-permute-start | bytes 393224 | tf_op jit(solution)/shard_map/ppermute | solution.py:323
  36.3 7.3 %collective-permute-start.6 = (f32[8,4,8,128]{3,2,1,0:T(8,128)S(1)}, f32[8,4,8,128]{3,2,1,0:T(8,128)S(1)}, u32[]{:S(2)}, u32[]{:S(2)}) collective-permute-start(f32[8,4,8,128]{3,2,1,0:T(8,128)S(1)} %get-tuple-element.62.refs_0_), channel_id=1, source_target_pairs={{1,0},{2,1},{3,2},{4,3},{5,4},{6,5},{7,6},{8,7},{9,8},{10,9},{11,1... | collective-permute-start | bytes 393224 | tf_op jit(solution)/shard_map/ppermute | solution.py:323
  44.0 8.3 %collective-permute-start.7 = (f32[8,4,8,128]{3,2,1,0:T(8,128)S(1)}, f32[8,4,8,128]{3,2,1,0:T(8,128)S(1)}, u32[]{:S(2)}, u32[]{:S(2)}) collective-permute-start(f32[8,4,8,128]{3,2,1,0:T(8,128)S(1)} %get-tuple-element.65.refs_0_), channel_id=1, source_target_pairs={{0,1},{1,2},{2,3},{3,4},{4,5},{5,6},{6,7},{7,8},{8,9},{9,10},{10,1... | collective-permute-start | bytes 393224 | tf_op jit(solution)/shard_map/ppermute | solution.py:323
  49.3 6.2 %collective-permute-start.8 = (f32[8,4,8,128]{3,2,1,0:T(8,128)S(1)}, f32[8,4,8,128]{3,2,1,0:T(8,128)S(1)}, u32[]{:S(2)}, u32[]{:S(2)}) collective-permute-start(f32[8,4,8,128]{3,2,1,0:T(8,128)S(1)} %get-tuple-element.65.refs_0_), channel_id=1, source_target_pairs={{1,0},{2,1},{3,2},{4,3},{5,4},{6,5},{7,6},{8,7},{9,8},{10,9},{11,1... | collective-permute-start | bytes 393224 | tf_op jit(solution)/shard_map/ppermute | solution.py:323
  56.0 9.3 %collective-permute-start.9 = (f32[6,4,4,8,128]{4,3,2,1,0:T(8,128)S(1)}, f32[6,4,4,8,128]{4,3,2,1,0:T(8,128)S(1)}, u32[]{:S(2)}, u32[]{:S(2)}) collective-permute-start(f32[6,4,4,8,128]{4,3,2,1,0:T(8,128)S(1)} %get-tuple-element.68), channel_id=1, source_target_pairs={{0,32},{1,33},{2,34},{3,35},{4,36},{5,37},{6,38},{7,39},{8,40},{9,... | collective-permute-start | bytes 1179656 | tf_op jit(solution)/shard_map/ppermute | solution.py:323
  59.5 13.2 %collective-permute-start.12 = (f32[3,4,4,8,128]{4,3,2,1,0:T(8,128)S(1)}, f32[3,4,4,8,128]{4,3,2,1,0:T(8,128)S(1)}, u32[]{:S(2)}, u32[]{:S(2)}) collective-permute-start(f32[3,4,4,8,128]{4,3,2,1,0:T(8,128)S(1)} %pad_maximum_fusion.1), channel_id=1, source_target_pairs={{32,96},{33,97},{34,98},{35,99},{36,100},{37,101},{38,102},{39,103... | collective-permute-start | bytes 589832 | tf_op jit(solution)/shard_map/ppermute | solution.py:323
  65.3 7.5 %collective-permute-start.10 = (f32[6,4,8,128]{3,2,1,0:T(8,128)S(1)}, f32[6,4,8,128]{3,2,1,0:T(8,128)S(1)}, u32[]{:S(2)}, u32[]{:S(2)}) collective-permute-start(f32[6,4,8,128]{3,2,1,0:T(8,128)S(1)} %pad_maximum_fusion.2.z0.refs_8_.refs_13_), channel_id=1, source_target_pairs={{32,33},{33,34},{34,35},{35,36},{36,37},{37,38},{38,39},{39,40},{4... | collective-permute-start | bytes 294920 | tf_op jit(solution)/shard_map/ppermute | solution.py:323
  70.3 5.6 %collective-permute-start.11 = (f32[6,4,8,128]{3,2,1,0:T(8,128)S(1)}, f32[6,4,8,128]{3,2,1,0:T(8,128)S(1)}, u32[]{:S(2)}, u32[]{:S(2)}) collective-permute-start(f32[6,4,8,128]{3,2,1,0:T(8,128)S(1)} %pad_maximum_fusion.2.z0.refs_8_.refs_13_), channel_id=1, source_target_pairs={{33,32},{34,33},{35,34},{36,35},{37,36},{38,37},{39,38},{40,39},{4... | collective-permute-start | bytes 294920 | tf_op jit(solution)/shard_map/ppermute | solution.py:323
  76.6 5.6 %collective-permute-start.13 = (f32[4,4,8,128]{3,2,1,0:T(8,128)S(1)}, f32[4,4,8,128]{3,2,1,0:T(8,128)S(1)}, u32[]{:S(2)}, u32[]{:S(2)}) collective-permute-start(f32[4,4,8,128]{3,2,1,0:T(8,128)S(1)} %get-tuple-element.70.refs_13_.refs_18_), channel_id=1, source_target_pairs={{96,32},{97,33},{98,34},{99,35},{100,36},{101,37},{102,38},{103,39... | collective-permute-start | bytes 196616 | tf_op jit(solution)/shard_map/ppermute | solution.py:323
  82.3 3.4 %collective-permute-start.15 = (f32[6,4,8,128]{3,2,1,0:T(8,128)S(1)}, f32[6,4,8,128]{3,2,1,0:T(8,128)S(1)}, u32[]{:S(2)}, u32[]{:S(2)}) collective-permute-start(f32[6,4,8,128]{3,2,1,0:T(8,128)S(1)} %broadcast_select_fusion.1), channel_id=1, source_target_pairs={{224,161},{225,162},{226,163},{227,164},{228,165},{229,166},{230,1... | collective-permute-start | bytes 294920 | tf_op jit(solution)/shard_map/ppermute | solution.py:323
  83.0 2.8 %collective-permute-start.17 = (f32[6,4,8,128]{3,2,1,0:T(8,128)S(1)}, f32[6,4,8,128]{3,2,1,0:T(8,128)S(1)}, u32[]{:S(2)}, u32[]{:S(2)}) collective-permute-start(f32[6,4,8,128]{3,2,1,0:T(8,128)S(1)} %broadcast_select_fusion.1), channel_id=1, source_target_pairs={{225,160},{226,161},{227,162},{228,163},{229,164},{230,165},{231,1... | collective-permute-start | bytes 294920 | tf_op jit(solution)/shard_map/ppermute | solution.py:323
  86.6 3.4 %collective-permute-start.24 = (f32[3,4,8,128]{3,2,1,0:T(8,128)S(1)}, f32[3,4,8,128]{3,2,1,0:T(8,128)S(1)}, u32[]{:S(2)}, u32[]{:S(2)}) collective-permute-start(f32[3,4,8,128]{3,2,1,0:T(8,128)S(1)} %get-tuple-element.78), channel_id=1, source_target_pairs={{162,96},{163,97},{164,98},{165,99},{166,100},{167,101},{168,102},... | collective-permute-start | bytes 147464 | tf_op jit(solution)/shard_map/ppermute | solution.py:323
  87.3 2.7 %collective-permute-start.21 = (f32[6,4,8,128]{3,2,1,0:T(8,128)S(1)}, f32[6,4,8,128]{3,2,1,0:T(8,128)S(1)}, u32[]{:S(2)}, u32[]{:S(2)}) collective-permute-start(f32[6,4,8,128]{3,2,1,0:T(8,128)S(1)} %get-tuple-element.79), channel_id=1, source_target_pairs={{160,97},{161,98},{162,99},{163,100},{164,101},{165,102},{166,103}... | collective-permute-start | bytes 294920 | tf_op jit(solution)/shard_map/ppermute | solution.py:323
  90.8 30.9 %collective-permute-start.30 = (f32[3,4,8,128]{3,2,1,0:T(8,128)S(1)}, f32[3,4,8,128]{3,2,1,0:T(8,128)S(1)}, u32[]{:S(2)}, u32[]{:S(2)}) collective-permute-start(f32[3,4,8,128]{3,2,1,0:T(8,128)S(1)} %get-tuple-element.84), channel_id=1, source_target_pairs={{98,32},{99,33},{100,34},{101,35},{102,36},{103,37},{104,38},{105,... | collective-permute-start | bytes 147464 | tf_op jit(solution)/shard_map/ppermute | solution.py:323
  92.1 29.7 %collective-permute-start.27 = (f32[6,4,8,128]{3,2,1,0:T(8,128)S(1)}, f32[6,4,8,128]{3,2,1,0:T(8,128)S(1)}, u32[]{:S(2)}, u32[]{:S(2)}) collective-permute-start(f32[6,4,8,128]{3,2,1,0:T(8,128)S(1)} %get-tuple-element.85), channel_id=1, source_target_pairs={{96,33},{97,34},{98,35},{99,36},{100,37},{101,38},{102,39},{103,40... | collective-permute-start | bytes 294920 | tf_op jit(solution)/shard_map/ppermute | solution.py:323
  93.4 28.4 %collective-permute-start.29 = (f32[6,4,8,128]{3,2,1,0:T(8,128)S(1)}, f32[6,4,8,128]{3,2,1,0:T(8,128)S(1)}, u32[]{:S(2)}, u32[]{:S(2)}) collective-permute-start(f32[6,4,8,128]{3,2,1,0:T(8,128)S(1)} %get-tuple-element.85), channel_id=1, source_target_pairs={{97,32},{98,33},{99,34},{100,35},{101,36},{102,37},{103,38},{104,3... | collective-permute-start | bytes 294920 | tf_op jit(solution)/shard_map/ppermute | solution.py:323
  94.7 27.0 %collective-permute-start.26 = (f32[3,4,8,128]{3,2,1,0:T(8,128)S(1)}, f32[3,4,8,128]{3,2,1,0:T(8,128)S(1)}, u32[]{:S(2)}, u32[]{:S(2)}) collective-permute-start(f32[3,4,8,128]{3,2,1,0:T(8,128)S(1)} %get-tuple-element.84), channel_id=1, source_target_pairs={{96,34},{97,35},{98,36},{99,37},{100,38},{101,39},{102,40},{103,41... | collective-permute-start | bytes 147464 | tf_op jit(solution)/shard_map/ppermute | solution.py:323
  96.0 29.2 %collective-permute-start.28 = (f32[7,4,8,128]{3,2,1,0:T(8,128)S(1)}, f32[7,4,8,128]{3,2,1,0:T(8,128)S(1)}, u32[]{:S(2)}, u32[]{:S(2)}) collective-permute-start(f32[7,4,8,128]{3,2,1,0:T(8,128)S(1)} %get-tuple-element.86), channel_id=1, source_target_pairs={{96,32},{97,33},{98,34},{99,35},{100,36},{101,37},{102,38},{103,39... | collective-permute-start | bytes 344072 | tf_op jit(solution)/shard_map/ppermute | solution.py:323
  126.0 3.4 %collective-permute-start.36 = (f32[3,4,8,128]{3,2,1,0:T(8,128)S(1)}, f32[3,4,8,128]{3,2,1,0:T(8,128)S(1)}, u32[]{:S(2)}, u32[]{:S(2)}) collective-permute-start(f32[3,4,8,128]{3,2,1,0:T(8,128)S(1)} %get-tuple-element.90), channel_id=1, source_target_pairs={{290,224},{291,225},{292,226},{293,227},{294,228},{295,229},{296,2... | collective-permute-start | bytes 147464 | tf_op jit(solution)/shard_map/ppermute | solution.py:323
  129.5 3.1 %collective-permute-start.37 = (f32[4,4,8,128]{3,2,1,0:T(8,128)S(1)}, f32[4,4,8,128]{3,2,1,0:T(8,128)S(1)}, u32[]{:S(2)}, u32[]{:S(2)}) collective-permute-start(f32[4,4,8,128]{3,2,1,0:T(8,128)S(1)} %get-tuple-element.132), channel_id=1, source_target_pairs={{0,32},{1,33},{2,34},{3,35},{4,36},{5,37},{6,38},{7,39},{8,40},{9,... | collective-permute-start | bytes 196616 | tf_op jit(solution)/shard_map/ppermute | solution.py:323
  133.3 3.4 %collective-permute-start.40 = (f32[7,4,8,128]{3,2,1,0:T(8,128)S(1)}, f32[7,4,8,128]{3,2,1,0:T(8,128)S(1)}, u32[]{:S(2)}, u32[]{:S(2)}) collective-permute-start(f32[7,4,8,128]{3,2,1,0:T(8,128)S(1)} %get-tuple-element.98), channel_id=1, source_target_pairs={{224,160},{225,161},{226,162},{227,163},{228,164},{229,165},{230,1... | collective-permute-start | bytes 344072 | tf_op jit(solution)/shard_map/ppermute | solution.py:323
  137.0 3.4 %collective-permute-start.45 = (f32[7,4,8,128]{3,2,1,0:T(8,128)S(1)}, f32[7,4,8,128]{3,2,1,0:T(8,128)S(1)}, u32[]{:S(2)}, u32[]{:S(2)}) collective-permute-start(f32[7,4,8,128]{3,2,1,0:T(8,128)S(1)} %get-tuple-element.103), channel_id=1, source_target_pairs={{160,96},{161,97},{162,98},{163,99},{164,100},{165,101},{166,102},... | collective-permute-start | bytes 344072 | tf_op jit(solution)/shard_map/ppermute | solution.py:323
  140.5 36.7 %collective-permute-start.50 = (f32[7,4,8,128]{3,2,1,0:T(8,128)S(1)}, f32[7,4,8,128]{3,2,1,0:T(8,128)S(1)}, u32[]{:S(2)}, u32[]{:S(2)}) collective-permute-start(f32[7,4,8,128]{3,2,1,0:T(8,128)S(1)} %get-tuple-element.108), channel_id=1, source_target_pairs={{96,32},{97,33},{98,34},{99,35},{100,36},{101,37},{102,38},{103,39... | collective-permute-start | bytes 344072 | tf_op jit(solution)/shard_map/ppermute | solution.py:323
  141.8 35.4 %collective-permute-start.49 = (f32[6,4,8,128]{3,2,1,0:T(8,128)S(1)}, f32[6,4,8,128]{3,2,1,0:T(8,128)S(1)}, u32[]{:S(2)}, u32[]{:S(2)}) collective-permute-start(f32[6,4,8,128]{3,2,1,0:T(8,128)S(1)} %get-tuple-element.107), channel_id=1, source_target_pairs={{96,33},{97,34},{98,35},{99,36},{100,37},{101,38},{102,39},{103,40... | collective-permute-start | bytes 294920 | tf_op jit(solution)/shard_map/ppermute | solution.py:323
  143.1 34.1 %collective-permute-start.51 = (f32[6,4,8,128]{3,2,1,0:T(8,128)S(1)}, f32[6,4,8,128]{3,2,1,0:T(8,128)S(1)}, u32[]{:S(2)}, u32[]{:S(2)}) collective-permute-start(f32[6,4,8,128]{3,2,1,0:T(8,128)S(1)} %get-tuple-element.107), channel_id=1, source_target_pairs={{97,32},{98,33},{99,34},{100,35},{101,36},{102,37},{103,38},{104,3... | collective-permute-start | bytes 294920 | tf_op jit(solution)/shard_map/ppermute | solution.py:323
  144.4 31.1 %collective-permute-start.48 = (f32[3,4,8,128]{3,2,1,0:T(8,128)S(1)}, f32[3,4,8,128]{3,2,1,0:T(8,128)S(1)}, u32[]{:S(2)}, u32[]{:S(2)}) collective-permute-start(f32[3,4,8,128]{3,2,1,0:T(8,128)S(1)} %get-tuple-element.106), channel_id=1, source_target_pairs={{96,34},{97,35},{98,36},{99,37},{100,38},{101,39},{102,40},{103,41... | collective-permute-start | bytes 147464 | tf_op jit(solution)/shard_map/ppermute | solution.py:323
  145.7 31.5 %collective-permute-start.52 = (f32[3,4,8,128]{3,2,1,0:T(8,128)S(1)}, f32[3,4,8,128]{3,2,1,0:T(8,128)S(1)}, u32[]{:S(2)}, u32[]{:S(2)}) collective-permute-start(f32[3,4,8,128]{3,2,1,0:T(8,128)S(1)} %get-tuple-element.106), channel_id=1, source_target_pairs={{98,32},{99,33},{100,34},{101,35},{102,36},{103,37},{104,38},{105,... | collective-permute-start | bytes 147464 | tf_op jit(solution)/shard_map/ppermute | solution.py:323
  (27 other events, 42.4 us)

commit v8 on v7

--- a/solution.py
+++ b/solution.py
@@ -210,7 +210,7 @@
     return call(body, [(2,) + SLAB, SLAB], *operands, layers=3 * WIDTH, flops=56 * 4 * 1024 * 20)
 
 
-def chip_step(turn, place, arrived, inv_five, pack, own_three, pair, offset, ahead, solved, done, grad):
+def chip_step(turn, place, arrived, inv_five, pack, own_three, pair, offset, ahead, solved, done, grad, mark):
     with_done, with_grad, with_z = done is not None, grad is not None, arrived is not None
     final = turn == 1
 
@@ -225,6 +225,8 @@
         qs = refs.pop(0) if with_z else None
         before = [refs.pop(0) for _ in range(2)] if with_done else None
         g = [refs.pop(0) for _ in range(2)] if with_grad else None
+        if mark is not None:
+            refs.pop(0)
         odd_pair, even_pair = refs.pop(0), refs.pop(0)
         sums = refs.pop(0) if with_grad else None
         z3, z6, z7_out = [None] * 3 if final else refs[:3]
@@ -293,6 +295,7 @@
     operands += [solved] if with_z else []
     operands += list(done) if with_done else []
     operands += list(grad) if with_grad else []
+    operands += [mark] if mark is not None else []
     outs = [(2,) + SLAB, (2,) + SLAB] + ([SLAB] if with_grad else [])
     outs += [] if final else [carry(3), carry(6), carry(7)]
     return pl.pallas_call(
@@ -390,17 +393,18 @@
         stages.append(even_to_odd)
         arrived, done = None, None
         for hop in range(max(chips, len(stages) + 1)):
-            added = None
+            added, mark = None, None
             if hop and hop < chips:
                 arrived = [send(part, path) for part, path in zip(payload, hop_routes(hop))]
+                mark = sum(part[:1] if part.shape[0] < 4 else part[:4] for part in arrived)
             if hop and stages:
-                mark = sum(part[:1] if part.shape[0] < 4 else part[:4] for part in arrived)
                 received = send(jnp.where(place[0] < 0, mark, grad), stages.pop(0))
+                mark = None
                 added = (grad if stages else jnp.where(is_even, grad, 0.0), received)
             if hop < chips:
                 odd_pair, even_pair, *more = chip_step(
                     times - 1 - 2 * hop, place, arrived, inv_five, pack, own_three, (z7, previous),
-                    offset, before, solved if hop else None, done, added,
+                    offset, before, solved if hop else None, done, added, mark,
                 )
                 if added:
                     grad = more.pop(0)

time: 182 us -> 180 us (0.989)
  waiting for transfers between devices: 86.8 us -> 84.3 us
    ppermute x54, waiting for transfers between devices: 86.8 us -> 84.3 us  [send(): return lax.ppermute(value, AXES, pairs)]
  transfers between devices with their start and end apart: 54 -> 54, of which waited for: 19 -> 21; matrix products, arithmetic and copies ran while one was open for 1% -> 1% of each run, Pallas kernels for 0% -> 0%
where the time goes in v8:
time: 180 us; the launch traced here: 179 us
  starting transfers between devices  85.2 us (47%)
  waiting for transfers between devices  84.3 us (47%)
  Pallas kernels  4.59 us (3%)
  other arithmetic  2.05 us (1%)
    ppermute x54, starting transfers between devices, send(): return lax.ppermute(value, AXES, pairs)  85.2 us
    ppermute x54, waiting for transfers between devices, send(): return lax.ppermute(value, AXES, pairs)  84.3 us
  transfers between devices with their start and end apart: 54, of which 21 were waited for; matrix products, arithmetic and copies ran while one was open for 1% of the time, Pallas kernels for 0%

profile of v8, /device:TPU:25, one launch (start us, length us, event | category | flops | bytes accessed | tf_op | source)
XLA Modules:
  0.0 178.8 jit_solution(5526463771367361041)
XLA Ops:
  0.6 2.7 %collective-permute-start = (f32[2,4,4,8,128]{4,3,2,1,0:T(8,128)}, f32[2,4,4,8,128]{4,3,2,1,0:T(8,128)S(1)}, u32[]{:S(2)}, u32[]{:S(2)}) collective-permute-start(f32[2,4,4,8,128]{4,3,2,1,0:T(8,128)} %bitcast.85), channel_id=1, source_target_pairs={{32,0},{33,1},{34,2},{35,3},{36,4},{37,5},{38,6},{39,7},{40,8},{41... | collective-permute-start | bytes 393224 | tf_op jit(solution)/shard_map/ppermute | solution.py:326
  5.3 2.9 %collective-permute-done = f32[2,4,4,8,128]{4,3,2,1,0:T(8,128)S(1)} collective-permute-done((f32[2,4,4,8,128]{4,3,2,1,0:T(8,128)}, f32[2,4,4,8,128]{4,3,2,1,0:T(8,128)S(1)}, u32[]{:S(2)}, u32[]{:S(2)}) %collective-permute-start) | collective-permute-done | bytes 131104 | tf_op jit(solution)/shard_map/ppermute | solution.py:326
  8.3 3.1 %collective-permute-start.1 = (f32[12,4,8,128]{3,2,1,0:T(8,128)S(1)}, f32[12,4,8,128]{3,2,1,0:T(8,128)S(1)}, u32[]{:S(2)}, u32[]{:S(2)}) collective-permute-start(f32[12,4,8,128]{3,2,1,0:T(8,128)S(1)} %pad_maximum_fusion.refs_0_.refs_6_), channel_id=1, source_target_pairs={{0,1},{1,2},{2,3},{3,4},{4,5},{5,6},{6,7},{7,8},{8,9},{9,10},{10,1... | collective-permute-start | bytes 589832 | tf_op jit(solution)/shard_map/ppermute | solution.py:326
  11.4 4.3 %collective-permute-start.2 = (f32[12,4,8,128]{3,2,1,0:T(8,128)S(1)}, f32[12,4,8,128]{3,2,1,0:T(8,128)S(1)}, u32[]{:S(2)}, u32[]{:S(2)}) collective-permute-start(f32[12,4,8,128]{3,2,1,0:T(8,128)S(1)} %pad_maximum_fusion.refs_0_.refs_6_), channel_id=1, source_target_pairs={{1,0},{2,1},{3,2},{4,3},{5,4},{6,5},{7,6},{8,7},{9,8},{10,9},{11,1... | collective-permute-start | bytes 589832 | tf_op jit(solution)/shard_map/ppermute | solution.py:326
  16.8 1.5 collective-permute-done.2.refs_2_.refs_7_
  18.7 2.7 %collective-permute-start.3 = (f32[12,4,8,128]{3,2,1,0:T(8,128)S(1)}, f32[12,4,8,128]{3,2,1,0:T(8,128)S(1)}, u32[]{:S(2)}, u32[]{:S(2)}) collective-permute-start(f32[12,4,8,128]{3,2,1,0:T(8,128)S(1)} %get-tuple-element.58.refs_0_), channel_id=1, source_target_pairs={{0,1},{1,2},{2,3},{3,4},{4,5},{5,6},{6,7},{7,8},{8,9},{9,10},{10,1... | collective-permute-start | bytes 589832 | tf_op jit(solution)/shard_map/ppermute | solution.py:326
  21.4 5.2 %collective-permute-start.4 = (f32[12,4,8,128]{3,2,1,0:T(8,128)S(1)}, f32[12,4,8,128]{3,2,1,0:T(8,128)S(1)}, u32[]{:S(2)}, u32[]{:S(2)}) collective-permute-start(f32[12,4,8,128]{3,2,1,0:T(8,128)S(1)} %get-tuple-element.59), channel_id=1, source_target_pairs={{1,0},{2,1},{3,2},{4,3},{5,4},{6,5},{7,6},{8,7},{9,8},{10,9},{11,1... | collective-permute-start | bytes 589832 | tf_op jit(solution)/shard_map/ppermute | solution.py:326
  26.5 1.8 %collective-permute-done.3.refs_1_ = f32[12,4,8,128]{3,2,1,0:T(8,128)S(1)} collective-permute-done((f32[12,4,8,128]{3,2,1,0:T(8,128)S(1)}, f32[12,4,8,128]{3,2,1,0:T(8,128)S(1)}, u32[]{:S(2)}, u32[]{:S(2)}) %collective-permute-start.3) | collective-permute-done | bytes 196640 | tf_op jit(solution)/shard_map/ppermute | solution.py:326
  28.4 1.8 collective-permute-done.4.refs_2_
  30.5 5.7 %collective-permute-start.5 = (f32[8,4,8,128]{3,2,1,0:T(8,128)S(1)}, f32[8,4,8,128]{3,2,1,0:T(8,128)S(1)}, u32[]{:S(2)}, u32[]{:S(2)}) collective-permute-start(f32[8,4,8,128]{3,2,1,0:T(8,128)S(1)} %get-tuple-element.62.refs_0_), channel_id=1, source_target_pairs={{0,1},{1,2},{2,3},{3,4},{4,5},{5,6},{6,7},{7,8},{8,9},{9,10},{10,1... | collective-permute-start | bytes 393224 | tf_op jit(solution)/shard_map/ppermute | solution.py:326
  36.3 2.1 %collective-permute-start.6 = (f32[8,4,8,128]{3,2,1,0:T(8,128)S(1)}, f32[8,4,8,128]{3,2,1,0:T(8,128)S(1)}, u32[]{:S(2)}, u32[]{:S(2)}) collective-permute-start(f32[8,4,8,128]{3,2,1,0:T(8,128)S(1)} %get-tuple-element.62.refs_0_), channel_id=1, source_target_pairs={{1,0},{2,1},{3,2},{4,3},{5,4},{6,5},{7,6},{8,7},{9,8},{10,9},{11,1... | collective-permute-start | bytes 393224 | tf_op jit(solution)/shard_map/ppermute | solution.py:326
  38.4 1.6 collective-permute-done.5.refs_1_
  40.0 3.6 %collective-permute-done.6.refs_2_ = f32[8,4,8,128]{3,2,1,0:T(8,128)S(1)} collective-permute-done((f32[8,4,8,128]{3,2,1,0:T(8,128)S(1)}, f32[8,4,8,128]{3,2,1,0:T(8,128)S(1)}, u32[]{:S(2)}, u32[]{:S(2)}) %collective-permute-start.6) | collective-permute-done | bytes 131104 | tf_op jit(solution)/shard_map/ppermute | solution.py:326
  44.0 5.3 %collective-permute-start.7 = (f32[8,4,8,128]{3,2,1,0:T(8,128)S(1)}, f32[8,4,8,128]{3,2,1,0:T(8,128)S(1)}, u32[]{:S(2)}, u32[]{:S(2)}) collective-permute-start(f32[8,4,8,128]{3,2,1,0:T(8,128)S(1)} %get-tuple-element.65.refs_0_), channel_id=1, source_target_pairs={{0,1},{1,2},{2,3},{3,4},{4,5},{5,6},{6,7},{7,8},{8,9},{9,10},{10,1... | collective-permute-start | bytes 393224 | tf_op jit(solution)/shard_map/ppermute | solution.py:326
  49.3 2.1 %collective-permute-start.8 = (f32[8,4,8,128]{3,2,1,0:T(8,128)S(1)}, f32[8,4,8,128]{3,2,1,0:T(8,128)S(1)}, u32[]{:S(2)}, u32[]{:S(2)}) collective-permute-start(f32[8,4,8,128]{3,2,1,0:T(8,128)S(1)} %get-tuple-element.65.refs_0_), channel_id=1, source_target_pairs={{1,0},{2,1},{3,2},{4,3},{5,4},{6,5},{7,6},{8,7},{9,8},{10,9},{11,1... | collective-permute-start | bytes 393224 | tf_op jit(solution)/shard_map/ppermute | solution.py:326
  52.3 3.2 %collective-permute-done.8.refs_2_ = f32[8,4,8,128]{3,2,1,0:T(8,128)S(1)} collective-permute-done((f32[8,4,8,128]{3,2,1,0:T(8,128)S(1)}, f32[8,4,8,128]{3,2,1,0:T(8,128)S(1)}, u32[]{:S(2)}, u32[]{:S(2)}) %collective-permute-start.8) | collective-permute-done | bytes 131104 | tf_op jit(solution)/shard_map/ppermute | solution.py:326
  56.0 3.5 %collective-permute-start.9 = (f32[6,4,4,8,128]{4,3,2,1,0:T(8,128)S(1)}, f32[6,4,4,8,128]{4,3,2,1,0:T(8,128)S(1)}, u32[]{:S(2)}, u32[]{:S(2)}) collective-permute-start(f32[6,4,4,8,128]{4,3,2,1,0:T(8,128)S(1)} %get-tuple-element.68), channel_id=1, source_target_pairs={{0,32},{1,33},{2,34},{3,35},{4,36},{5,37},{6,38},{7,39},{8,40},{9,... | collective-permute-start | bytes 1179656 | tf_op jit(solution)/shard_map/ppermute | solution.py:326
  59.5 5.7 %collective-permute-start.12 = (f32[3,4,4,8,128]{4,3,2,1,0:T(8,128)S(1)}, f32[3,4,4,8,128]{4,3,2,1,0:T(8,128)S(1)}, u32[]{:S(2)}, u32[]{:S(2)}) collective-permute-start(f32[3,4,4,8,128]{4,3,2,1,0:T(8,128)S(1)} %pad_maximum_fusion.1), channel_id=1, source_target_pairs={{32,96},{33,97},{34,98},{35,99},{36,100},{37,101},{38,102},{39,103... | collective-permute-start | bytes 589832 | tf_op jit(solution)/shard_map/ppermute | solution.py:326
  65.3 5.0 %collective-permute-start.10 = (f32[6,4,8,128]{3,2,1,0:T(8,128)S(1)}, f32[6,4,8,128]{3,2,1,0:T(8,128)S(1)}, u32[]{:S(2)}, u32[]{:S(2)}) collective-permute-start(f32[6,4,8,128]{3,2,1,0:T(8,128)S(1)} %pad_maximum_fusion.2.z0.refs_8_.refs_13_), channel_id=1, source_target_pairs={{32,33},{33,34},{34,35},{35,36},{36,37},{37,38},{38,39},{39,40},{4... | collective-permute-start | bytes 294920 | tf_op jit(solution)/shard_map/ppermute | solution.py:326
  70.3 2.4 %collective-permute-start.11 = (f32[6,4,8,128]{3,2,1,0:T(8,128)S(1)}, f32[6,4,8,128]{3,2,1,0:T(8,128)S(1)}, u32[]{:S(2)}, u32[]{:S(2)}) collective-permute-start(f32[6,4,8,128]{3,2,1,0:T(8,128)S(1)} %pad_maximum_fusion.2.z0.refs_8_.refs_13_), channel_id=1, source_target_pairs={{33,32},{34,33},{35,34},{36,35},{37,36},{38,37},{39,38},{40,39},{4... | collective-permute-start | bytes 294920 | tf_op jit(solution)/shard_map/ppermute | solution.py:326
  72.8 3.1 %collective-permute-done.11.zh.refs_9_.refs_14_ = f32[6,4,8,128]{3,2,1,0:T(8,128)S(1)} collective-permute-done((f32[6,4,8,128]{3,2,1,0:T(8,128)S(1)}, f32[6,4,8,128]{3,2,1,0:T(8,128)S(1)}, u32[]{:S(2)}, u32[]{:S(2)}) %collective-permute-start.11) | collective-permute-done | bytes 98336 | tf_op jit(solution)/shard_map/ppermute | solution.py:326
  78.0 4.2 %collective-permute-done.13.refs_19_ = f32[4,4,8,128]{3,2,1,0:T(8,128)S(1)} collective-permute-done((f32[4,4,8,128]{3,2,1,0:T(8,128)S(1)}, f32[4,4,8,128]{3,2,1,0:T(8,128)S(1)}, u32[]{:S(2)}, u32[]{:S(2)}) %collective-permute-start.13) | collective-permute-done | bytes 65568 | tf_op jit(solution)/shard_map/ppermute | solution.py:326
  97.3 24.4 %collective-permute-done.30.refs_5_ = f32[3,4,8,128]{3,2,1,0:T(8,128)S(1)} collective-permute-done((f32[3,4,8,128]{3,2,1,0:T(8,128)S(1)}, f32[3,4,8,128]{3,2,1,0:T(8,128)S(1)}, u32[]{:S(2)}, u32[]{:S(2)}) %collective-permute-start.30) | collective-permute-done | bytes 49184 | tf_op jit(solution)/shard_map/ppermute | solution.py:326
  121.8 3.4 %collective-permute-done.28.refs_3_ = f32[7,4,8,128]{3,2,1,0:T(8,128)S(1)} collective-permute-done((f32[7,4,8,128]{3,2,1,0:T(8,128)S(1)}, f32[7,4,8,128]{3,2,1,0:T(8,128)S(1)}, u32[]{:S(2)}, u32[]{:S(2)}) %collective-permute-start.28) | collective-permute-done | bytes 114720 | tf_op jit(solution)/shard_map/ppermute | solution.py:326
  130.8 1.8 %collective-permute-done.37.refs_23_ = f32[4,4,8,128]{3,2,1,0:T(8,128)S(1)} collective-permute-done((f32[4,4,8,128]{3,2,1,0:T(8,128)S(1)}, f32[4,4,8,128]{3,2,1,0:T(8,128)S(1)}, u32[]{:S(2)}, u32[]{:S(2)}) %collective-permute-start.37) | collective-permute-done | bytes 65568 | tf_op jit(solution)/shard_map/ppermute | solution.py:326
  140.6 1.3 collective-permute-start.52
  141.9 1.3 collective-permute-start.49
  143.2 1.3 collective-permute-start.51
  144.5 1.3 collective-permute-start.48
  147.1 23.3 %collective-permute-done.52.refs_5_ = f32[3,4,8,128]{3,2,1,0:T(8,128)S(1)} collective-permute-done((f32[3,4,8,128]{3,2,1,0:T(8,128)S(1)}, f32[3,4,8,128]{3,2,1,0:T(8,128)S(1)}, u32[]{:S(2)}, u32[]{:S(2)}) %collective-permute-start.52) | collective-permute-done | bytes 49184 | tf_op jit(solution)/shard_map/ppermute | solution.py:326
  171.7 3.0 %collective-permute-done.50.refs_3_ = f32[7,4,8,128]{3,2,1,0:T(8,128)S(1)} collective-permute-done((f32[7,4,8,128]{3,2,1,0:T(8,128)S(1)}, f32[7,4,8,128]{3,2,1,0:T(8,128)S(1)}, u32[]{:S(2)}, u32[]{:S(2)}) %collective-permute-start.50) | collective-permute-done | bytes 114720 | tf_op jit(solution)/shard_map/ppermute | solution.py:326
  175.8 1.3 collective-permute-start.53
  (139 shorter events, 41.0 us)
Async XLA Ops:
  0.6 7.5 %collective-permute-start = (f32[2,4,4,8,128]{4,3,2,1,0:T(8,128)}, f32[2,4,4,8,128]{4,3,2,1,0:T(8,128)S(1)}, u32[]{:S(2)}, u32[]{:S(2)}) collective-permute-start(f32[2,4,4,8,128]{4,3,2,1,0:T(8,128)} %bitcast.85), channel_id=1, source_target_pairs={{32,0},{33,1},{34,2},{35,3},{36,4},{37,5},{38,6},{39,7},{40,8},{41... | collective-permute-start | bytes 393224 | tf_op jit(solution)/shard_map/ppermute | solution.py:326
  8.3 8.5 %collective-permute-start.1 = (f32[12,4,8,128]{3,2,1,0:T(8,128)S(1)}, f32[12,4,8,128]{3,2,1,0:T(8,128)S(1)}, u32[]{:S(2)}, u32[]{:S(2)}) collective-permute-start(f32[12,4,8,128]{3,2,1,0:T(8,128)S(1)} %pad_maximum_fusion.refs_0_.refs_6_), channel_id=1, source_target_pairs={{0,1},{1,2},{2,3},{3,4},{4,5},{5,6},{6,7},{7,8},{8,9},{9,10},{10,1... | collective-permute-start | bytes 589832 | tf_op jit(solution)/shard_map/ppermute | solution.py:326
  11.4 6.9 %collective-permute-start.2 = (f32[12,4,8,128]{3,2,1,0:T(8,128)S(1)}, f32[12,4,8,128]{3,2,1,0:T(8,128)S(1)}, u32[]{:S(2)}, u32[]{:S(2)}) collective-permute-start(f32[12,4,8,128]{3,2,1,0:T(8,128)S(1)} %pad_maximum_fusion.refs_0_.refs_6_), channel_id=1, source_target_pairs={{1,0},{2,1},{3,2},{4,3},{5,4},{6,5},{7,6},{8,7},{9,8},{10,9},{11,1... | collective-permute-start | bytes 589832 | tf_op jit(solution)/shard_map/ppermute | solution.py:326
  18.7 9.7 %collective-permute-start.3 = (f32[12,4,8,128]{3,2,1,0:T(8,128)S(1)}, f32[12,4,8,128]{3,2,1,0:T(8,128)S(1)}, u32[]{:S(2)}, u32[]{:S(2)}) collective-permute-start(f32[12,4,8,128]{3,2,1,0:T(8,128)S(1)} %get-tuple-element.58.refs_0_), channel_id=1, source_target_pairs={{0,1},{1,2},{2,3},{3,4},{4,5},{5,6},{6,7},{7,8},{8,9},{9,10},{10,1... | collective-permute-start | bytes 589832 | tf_op jit(solution)/shard_map/ppermute | solution.py:326
  21.4 8.8 %collective-permute-start.4 = (f32[12,4,8,128]{3,2,1,0:T(8,128)S(1)}, f32[12,4,8,128]{3,2,1,0:T(8,128)S(1)}, u32[]{:S(2)}, u32[]{:S(2)}) collective-permute-start(f32[12,4,8,128]{3,2,1,0:T(8,128)S(1)} %get-tuple-element.59), channel_id=1, source_target_pairs={{1,0},{2,1},{3,2},{4,3},{5,4},{6,5},{7,6},{8,7},{9,8},{10,9},{11,1... | collective-permute-start | bytes 589832 | tf_op jit(solution)/shard_map/ppermute | solution.py:326
  30.5 9.5 %collective-permute-start.5 = (f32[8,4,8,128]{3,2,1,0:T(8,128)S(1)}, f32[8,4,8,128]{3,2,1,0:T(8,128)S(1)}, u32[]{:S(2)}, u32[]{:S(2)}) collective-permute-start(f32[8,4,8,128]{3,2,1,0:T(8,128)S(1)} %get-tuple-element.62.refs_0_), channel_id=1, source_target_pairs={{0,1},{1,2},{2,3},{3,4},{4,5},{5,6},{6,7},{7,8},{8,9},{9,10},{10,1... | collective-permute-start | bytes 393224 | tf_op jit(solution)/shard_map/ppermute | solution.py:326
  36.3 7.3 %collective-permute-start.6 = (f32[8,4,8,128]{3,2,1,0:T(8,128)S(1)}, f32[8,4,8,128]{3,2,1,0:T(8,128)S(1)}, u32[]{:S(2)}, u32[]{:S(2)}) collective-permute-start(f32[8,4,8,128]{3,2,1,0:T(8,128)S(1)} %get-tuple-element.62.refs_0_), channel_id=1, source_target_pairs={{1,0},{2,1},{3,2},{4,3},{5,4},{6,5},{7,6},{8,7},{9,8},{10,9},{11,1... | collective-permute-start | bytes 393224 | tf_op jit(solution)/shard_map/ppermute | solution.py:326
  44.0 8.3 %collective-permute-start.7 = (f32[8,4,8,128]{3,2,1,0:T(8,128)S(1)}, f32[8,4,8,128]{3,2,1,0:T(8,128)S(1)}, u32[]{:S(2)}, u32[]{:S(2)}) collective-permute-start(f32[8,4,8,128]{3,2,1,0:T(8,128)S(1)} %get-tuple-element.65.refs_0_), channel_id=1, source_target_pairs={{0,1},{1,2},{2,3},{3,4},{4,5},{5,6},{6,7},{7,8},{8,9},{9,10},{10,1... | collective-permute-start | bytes 393224 | tf_op jit(solution)/shard_map/ppermute | solution.py:326
  49.3 6.2 %collective-permute-start.8 = (f32[8,4,8,128]{3,2,1,0:T(8,128)S(1)}, f32[8,4,8,128]{3,2,1,0:T(8,128)S(1)}, u32[]{:S(2)}, u32[]{:S(2)}) collective-permute-start(f32[8,4,8,128]{3,2,1,0:T(8,128)S(1)} %get-tuple-element.65.refs_0_), channel_id=1, source_target_pairs={{1,0},{2,1},{3,2},{4,3},{5,4},{6,5},{7,6},{8,7},{9,8},{10,9},{11,1... | collective-permute-start | bytes 393224 | tf_op jit(solution)/shard_map/ppermute | solution.py:326
  56.0 9.3 %collective-permute-start.9 = (f32[6,4,4,8,128]{4,3,2,1,0:T(8,128)S(1)}, f32[6,4,4,8,128]{4,3,2,1,0:T(8,128)S(1)}, u32[]{:S(2)}, u32[]{:S(2)}) collective-permute-start(f32[6,4,4,8,128]{4,3,2,1,0:T(8,128)S(1)} %get-tuple-element.68), channel_id=1, source_target_pairs={{0,32},{1,33},{2,34},{3,35},{4,36},{5,37},{6,38},{7,39},{8,40},{9,... | collective-permute-start | bytes 1179656 | tf_op jit(solution)/shard_map/ppermute | solution.py:326
  59.5 13.2 %collective-permute-start.12 = (f32[3,4,4,8,128]{4,3,2,1,0:T(8,128)S(1)}, f32[3,4,4,8,128]{4,3,2,1,0:T(8,128)S(1)}, u32[]{:S(2)}, u32[]{:S(2)}) collective-permute-start(f32[3,4,4,8,128]{4,3,2,1,0:T(8,128)S(1)} %pad_maximum_fusion.1), channel_id=1, source_target_pairs={{32,96},{33,97},{34,98},{35,99},{36,100},{37,101},{38,102},{39,103... | collective-permute-start | bytes 589832 | tf_op jit(solution)/shard_map/ppermute | solution.py:326
  65.3 7.5 %collective-permute-start.10 = (f32[6,4,8,128]{3,2,1,0:T(8,128)S(1)}, f32[6,4,8,128]{3,2,1,0:T(8,128)S(1)}, u32[]{:S(2)}, u32[]{:S(2)}) collective-permute-start(f32[6,4,8,128]{3,2,1,0:T(8,128)S(1)} %pad_maximum_fusion.2.z0.refs_8_.refs_13_), channel_id=1, source_target_pairs={{32,33},{33,34},{34,35},{35,36},{36,37},{37,38},{38,39},{39,40},{4... | collective-permute-start | bytes 294920 | tf_op jit(solution)/shard_map/ppermute | solution.py:326
  70.3 5.6 %collective-permute-start.11 = (f32[6,4,8,128]{3,2,1,0:T(8,128)S(1)}, f32[6,4,8,128]{3,2,1,0:T(8,128)S(1)}, u32[]{:S(2)}, u32[]{:S(2)}) collective-permute-start(f32[6,4,8,128]{3,2,1,0:T(8,128)S(1)} %pad_maximum_fusion.2.z0.refs_8_.refs_13_), channel_id=1, source_target_pairs={{33,32},{34,33},{35,34},{36,35},{37,36},{38,37},{39,38},{40,39},{4... | collective-permute-start | bytes 294920 | tf_op jit(solution)/shard_map/ppermute | solution.py:326
  76.6 5.6 %collective-permute-start.13 = (f32[4,4,8,128]{3,2,1,0:T(8,128)S(1)}, f32[4,4,8,128]{3,2,1,0:T(8,128)S(1)}, u32[]{:S(2)}, u32[]{:S(2)}) collective-permute-start(f32[4,4,8,128]{3,2,1,0:T(8,128)S(1)} %get-tuple-element.70.refs_13_.refs_18_), channel_id=1, source_target_pairs={{96,32},{97,33},{98,34},{99,35},{100,36},{101,37},{102,38},{103,39... | collective-permute-start | bytes 196616 | tf_op jit(solution)/shard_map/ppermute | solution.py:326
  82.3 3.4 %collective-permute-start.15 = (f32[6,4,8,128]{3,2,1,0:T(8,128)S(1)}, f32[6,4,8,128]{3,2,1,0:T(8,128)S(1)}, u32[]{:S(2)}, u32[]{:S(2)}) collective-permute-start(f32[6,4,8,128]{3,2,1,0:T(8,128)S(1)} %broadcast_select_fusion.1), channel_id=1, source_target_pairs={{224,161},{225,162},{226,163},{227,164},{228,165},{229,166},{230,1... | collective-permute-start | bytes 294920 | tf_op jit(solution)/shard_map/ppermute | solution.py:326
  83.0 2.8 %collective-permute-start.17 = (f32[6,4,8,128]{3,2,1,0:T(8,128)S(1)}, f32[6,4,8,128]{3,2,1,0:T(8,128)S(1)}, u32[]{:S(2)}, u32[]{:S(2)}) collective-permute-start(f32[6,4,8,128]{3,2,1,0:T(8,128)S(1)} %broadcast_select_fusion.1), channel_id=1, source_target_pairs={{225,160},{226,161},{227,162},{228,163},{229,164},{230,165},{231,1... | collective-permute-start | bytes 294920 | tf_op jit(solution)/shard_map/ppermute | solution.py:326
  86.6 3.4 %collective-permute-start.24 = (f32[3,4,8,128]{3,2,1,0:T(8,128)S(1)}, f32[3,4,8,128]{3,2,1,0:T(8,128)S(1)}, u32[]{:S(2)}, u32[]{:S(2)}) collective-permute-start(f32[3,4,8,128]{3,2,1,0:T(8,128)S(1)} %get-tuple-element.78), channel_id=1, source_target_pairs={{162,96},{163,97},{164,98},{165,99},{166,100},{167,101},{168,102},... | collective-permute-start | bytes 147464 | tf_op jit(solution)/shard_map/ppermute | solution.py:326
  90.8 30.9 %collective-permute-start.30 = (f32[3,4,8,128]{3,2,1,0:T(8,128)S(1)}, f32[3,4,8,128]{3,2,1,0:T(8,128)S(1)}, u32[]{:S(2)}, u32[]{:S(2)}) collective-permute-start(f32[3,4,8,128]{3,2,1,0:T(8,128)S(1)} %get-tuple-element.84), channel_id=1, source_target_pairs={{98,32},{99,33},{100,34},{101,35},{102,36},{103,37},{104,38},{105,... | collective-permute-start | bytes 147464 | tf_op jit(solution)/shard_map/ppermute | solution.py:326
  92.1 29.7 %collective-permute-start.27 = (f32[6,4,8,128]{3,2,1,0:T(8,128)S(1)}, f32[6,4,8,128]{3,2,1,0:T(8,128)S(1)}, u32[]{:S(2)}, u32[]{:S(2)}) collective-permute-start(f32[6,4,8,128]{3,2,1,0:T(8,128)S(1)} %get-tuple-element.85), channel_id=1, source_target_pairs={{96,33},{97,34},{98,35},{99,36},{100,37},{101,38},{102,39},{103,40... | collective-permute-start | bytes 294920 | tf_op jit(solution)/shard_map/ppermute | solution.py:326
  93.4 28.4 %collective-permute-start.29 = (f32[6,4,8,128]{3,2,1,0:T(8,128)S(1)}, f32[6,4,8,128]{3,2,1,0:T(8,128)S(1)}, u32[]{:S(2)}, u32[]{:S(2)}) collective-permute-start(f32[6,4,8,128]{3,2,1,0:T(8,128)S(1)} %get-tuple-element.85), channel_id=1, source_target_pairs={{97,32},{98,33},{99,34},{100,35},{101,36},{102,37},{103,38},{104,3... | collective-permute-start | bytes 294920 | tf_op jit(solution)/shard_map/ppermute | solution.py:326
  94.7 27.0 %collective-permute-start.26 = (f32[3,4,8,128]{3,2,1,0:T(8,128)S(1)}, f32[3,4,8,128]{3,2,1,0:T(8,128)S(1)}, u32[]{:S(2)}, u32[]{:S(2)}) collective-permute-start(f32[3,4,8,128]{3,2,1,0:T(8,128)S(1)} %get-tuple-element.84), channel_id=1, source_target_pairs={{96,34},{97,35},{98,36},{99,37},{100,38},{101,39},{102,40},{103,41... | collective-permute-start | bytes 147464 | tf_op jit(solution)/shard_map/ppermute | solution.py:326
  96.0 29.2 %collective-permute-start.28 = (f32[7,4,8,128]{3,2,1,0:T(8,128)S(1)}, f32[7,4,8,128]{3,2,1,0:T(8,128)S(1)}, u32[]{:S(2)}, u32[]{:S(2)}) collective-permute-start(f32[7,4,8,128]{3,2,1,0:T(8,128)S(1)} %get-tuple-element.86), channel_id=1, source_target_pairs={{96,32},{97,33},{98,34},{99,35},{100,36},{101,37},{102,38},{103,39... | collective-permute-start | bytes 344072 | tf_op jit(solution)/shard_map/ppermute | solution.py:326
  126.0 3.4 %collective-permute-start.36 = (f32[3,4,8,128]{3,2,1,0:T(8,128)S(1)}, f32[3,4,8,128]{3,2,1,0:T(8,128)S(1)}, u32[]{:S(2)}, u32[]{:S(2)}) collective-permute-start(f32[3,4,8,128]{3,2,1,0:T(8,128)S(1)} %get-tuple-element.90), channel_id=1, source_target_pairs={{290,224},{291,225},{292,226},{293,227},{294,228},{295,229},{296,2... | collective-permute-start | bytes 147464 | tf_op jit(solution)/shard_map/ppermute | solution.py:326
  129.5 3.1 %collective-permute-start.37 = (f32[4,4,8,128]{3,2,1,0:T(8,128)S(1)}, f32[4,4,8,128]{3,2,1,0:T(8,128)S(1)}, u32[]{:S(2)}, u32[]{:S(2)}) collective-permute-start(f32[4,4,8,128]{3,2,1,0:T(8,128)S(1)} %get-tuple-element.132), channel_id=1, source_target_pairs={{0,32},{1,33},{2,34},{3,35},{4,36},{5,37},{6,38},{7,39},{8,40},{9,... | collective-permute-start | bytes 196616 | tf_op jit(solution)/shard_map/ppermute | solution.py:326
  133.3 3.4 %collective-permute-start.42 = (f32[3,4,8,128]{3,2,1,0:T(8,128)S(1)}, f32[3,4,8,128]{3,2,1,0:T(8,128)S(1)}, u32[]{:S(2)}, u32[]{:S(2)}) collective-permute-start(f32[3,4,8,128]{3,2,1,0:T(8,128)S(1)} %get-tuple-element.96), channel_id=1, source_target_pairs={{226,160},{227,161},{228,162},{229,163},{230,164},{231,165},{232,1... | collective-permute-start | bytes 147464 | tf_op jit(solution)/shard_map/ppermute | solution.py:326
  134.0 2.7 %collective-permute-start.39 = (f32[6,4,8,128]{3,2,1,0:T(8,128)S(1)}, f32[6,4,8,128]{3,2,1,0:T(8,128)S(1)}, u32[]{:S(2)}, u32[]{:S(2)}) collective-permute-start(f32[6,4,8,128]{3,2,1,0:T(8,128)S(1)} %get-tuple-element.97), channel_id=1, source_target_pairs={{224,161},{225,162},{226,163},{227,164},{228,165},{229,166},{230,1... | collective-permute-start | bytes 294920 | tf_op jit(solution)/shard_map/ppermute | solution.py:326
  137.0 3.4 %collective-permute-start.47 = (f32[3,4,8,128]{3,2,1,0:T(8,128)S(1)}, f32[3,4,8,128]{3,2,1,0:T(8,128)S(1)}, u32[]{:S(2)}, u32[]{:S(2)}) collective-permute-start(f32[3,4,8,128]{3,2,1,0:T(8,128)S(1)} %get-tuple-element.101), channel_id=1, source_target_pairs={{162,96},{163,97},{164,98},{165,99},{166,100},{167,101},{168,102},... | collective-permute-start | bytes 147464 | tf_op jit(solution)/shard_map/ppermute | solution.py:326
  140.6 29.8 %collective-permute-start.52 = (f32[3,4,8,128]{3,2,1,0:T(8,128)S(1)}, f32[3,4,8,128]{3,2,1,0:T(8,128)S(1)}, u32[]{:S(2)}, u32[]{:S(2)}) collective-permute-start(f32[3,4,8,128]{3,2,1,0:T(8,128)S(1)} %get-tuple-element.106), channel_id=1, source_target_pairs={{98,32},{99,33},{100,34},{101,35},{102,36},{103,37},{104,38},{105,... | collective-permute-start | bytes 147464 | tf_op jit(solution)/shard_map/ppermute | solution.py:326
  141.9 29.7 %collective-permute-start.49 = (f32[6,4,8,128]{3,2,1,0:T(8,128)S(1)}, f32[6,4,8,128]{3,2,1,0:T(8,128)S(1)}, u32[]{:S(2)}, u32[]{:S(2)}) collective-permute-start(f32[6,4,8,128]{3,2,1,0:T(8,128)S(1)} %get-tuple-element.107), channel_id=1, source_target_pairs={{96,33},{97,34},{98,35},{99,36},{100,37},{101,38},{102,39},{103,40... | collective-permute-start | bytes 294920 | tf_op jit(solution)/shard_map/ppermute | solution.py:326
  143.2 28.6 %collective-permute-start.51 = (f32[6,4,8,128]{3,2,1,0:T(8,128)S(1)}, f32[6,4,8,128]{3,2,1,0:T(8,128)S(1)}, u32[]{:S(2)}, u32[]{:S(2)}) collective-permute-start(f32[6,4,8,128]{3,2,1,0:T(8,128)S(1)} %get-tuple-element.107), channel_id=1, source_target_pairs={{97,32},{98,33},{99,34},{100,35},{101,36},{102,37},{103,38},{104,3... | collective-permute-start | bytes 294920 | tf_op jit(solution)/shard_map/ppermute | solution.py:326
  144.5 27.1 %collective-permute-start.48 = (f32[3,4,8,128]{3,2,1,0:T(8,128)S(1)}, f32[3,4,8,128]{3,2,1,0:T(8,128)S(1)}, u32[]{:S(2)}, u32[]{:S(2)}) collective-permute-start(f32[3,4,8,128]{3,2,1,0:T(8,128)S(1)} %get-tuple-element.106), channel_id=1, source_target_pairs={{96,34},{97,35},{98,36},{99,37},{100,38},{101,39},{102,40},{103,41... | collective-permute-start | bytes 147464 | tf_op jit(solution)/shard_map/ppermute | solution.py:326
  145.8 29.0 %collective-permute-start.50 = (f32[7,4,8,128]{3,2,1,0:T(8,128)S(1)}, f32[7,4,8,128]{3,2,1,0:T(8,128)S(1)}, u32[]{:S(2)}, u32[]{:S(2)}) collective-permute-start(f32[7,4,8,128]{3,2,1,0:T(8,128)S(1)} %get-tuple-element.108), channel_id=1, source_target_pairs={{96,32},{97,33},{98,34},{99,35},{100,36},{101,37},{102,38},{103,39... | collective-permute-start | bytes 344072 | tf_op jit(solution)/shard_map/ppermute | solution.py:326
  (27 other events, 42.7 us)
